TPU v7x, 32 devices: a whole 2x2x4 slice. The times are simulated.
32 devices in a mesh: seq: 16 (over z, y, core), fsdp: 2 (over x).
Axes of the slice: x: 2, y: 2, z: 4, core: 2. Of those that a mesh axis runs over, the one named last changes fastest.
Arguments:
- tokens: bfloat16 [2, 4096, 2048], P('fsdp', 'seq'), may hold values from -6 to 6
- per_layer: bfloat16 [2, 4096, 256], P('fsdp', 'seq'), may hold values from -6 to 6
- teacher: bfloat16 [2, 4096, 2048], P('fsdp', 'seq'), may hold values from -6 to 6
- cont_lengths: int32 [2, 4], replicated, may hold values from 257 to 512, as said below
- w_query: bfloat16 [2048, 2048], P(('seq', 'fsdp')), may hold values from -0.125 to 0.125
- w_kv: bfloat16 [2048, 1024], P(('seq', 'fsdp')), may hold values from -0.125 to 0.125
- w_out: bfloat16 [2048, 2048], P(('seq', 'fsdp')), may hold values from -0.125 to 0.125
- laurel_left: bfloat16 [2048, 64], P(('seq', 'fsdp')), may hold values from -0.125 to 0.125
- laurel_right: bfloat16 [64, 2048], P(None, ('seq', 'fsdp')), may hold values from -0.75 to 0.75
- pl_gate: bfloat16 [2048, 256], P(('seq', 'fsdp')), may hold values from -0.125 to 0.125
- pl_proj: bfloat16 [256, 2048], P(('seq', 'fsdp')), may hold values from -0.375 to 0.375
- norm_gains: bfloat16 [6, 2048], P(None, ('seq', 'fsdp')), may hold values from 0.25 to 1.75
- head_gains: bfloat16 [2, 256], P(None, ('seq', 'fsdp')), may hold values from 0.29882812 to 0.5
- ffn_weight: bfloat16 [8192, 3, 2048], P(('seq', 'fsdp')), may hold values from -0.125 to 0.125
Outputs:
- block_out: float32 [2, 4096, 2048], P('fsdp', 'seq')
- match_loss: float32 [], replicated
- d_tokens: float32 [2, 4096, 2048], P('fsdp', 'seq')
- d_per_layer: float32 [2, 4096, 256], P('fsdp', 'seq')
- d_w_query: float32 [2048, 2048], P(('seq', 'fsdp'))
- d_w_kv: float32 [2048, 1024], P(('seq', 'fsdp'))
- d_w_out: float32 [2048, 2048], P(('seq', 'fsdp'))
- d_laurel_left: float32 [2048, 64], P(('seq', 'fsdp'))
- d_laurel_right: float32 [64, 2048], P(None, ('seq', 'fsdp'))
- d_pl_gate: float32 [2048, 256], P(('seq', 'fsdp'))
- d_pl_proj: float32 [256, 2048], P(('seq', 'fsdp'))
- d_norm_gains: float32 [6, 2048], P(None, ('seq', 'fsdp'))
- d_head_gains: float32 [2, 256], P(None, ('seq', 'fsdp'))
- d_ffn_weight: float32 [8192, 3, 2048], P(('seq', 'fsdp'))
Inputs may be any that keep to these rules, and one draw needn't show every extreme that they name: `cont_lengths`: in every group some continuation has all 512 slots valid.
All inputs are finite; a program needn't handle non-finite values.
Results may differ from a plain program's by a relative error of at most 0.02.
Values may be sent and summed in bfloat16 or wider, within the bound.
A program may use at most 512 MiB of HBM per device.

v0:
```python
import math

import jax
import jax.numpy as jnp
from jax import lax
from jax.sharding import PartitionSpec as P

D = 2048
HEADS = 8
KV_HEADS = 2
HEAD = 256
WINDOW = 512
CONT_LEN = 512


EPSILON = 1e-06
INV_SQRT2 = 0.7071067811865476
ROPE_BASE = 10000.0


def passed_along(shard, axis, by):
    size = lax.axis_size(axis)
    pairs = [(i, i + by) for i in range(size) if 0 <= i + by < size]
    return lax.ppermute(shard, axis, pairs)


def broadcast(value, axis, source):
    kept = jnp.where(lax.axis_index(axis) == source, value, 0).astype(value.dtype)
    return lax.psum(kept, axis)


def rms_norm(values, gain):
    return values * lax.rsqrt(jnp.mean(values * values, axis=-1, keepdims=True) + EPSILON) * gain


def plain_norm(values):
    return values * lax.rsqrt(jnp.mean(values * values, axis=-1, keepdims=True) + EPSILON)


def rotate(values, places):
    half_dim = values.shape[-1] // 2
    freqs = jnp.exp(
        jnp.arange(half_dim, dtype=jnp.float32) * (-2.0 * math.log(ROPE_BASE) / values.shape[-1])
    )
    angles = places.astype(jnp.float32)[:, None, None] * freqs
    cosine = jnp.cos(angles)
    sine = jnp.sin(angles)
    first = values[..., :half_dim]
    second = values[..., half_dim:]
    return jnp.concatenate([first * cosine - second * sine, second * cosine + first * sine], -1)


def gelu_tanh(values):
    return jax.nn.gelu(values, approximate=True)


def gated_product(gate_in, up_in):
    return gelu_tanh(gate_in) * up_in


def full_dot(left, right):
    return jnp.dot(left, right, preferred_element_type=jnp.float32)


def left_dot(left, right):
    return lax.dot_general(
        left, right, (((0,), (0,)), ((), ())), preferred_element_type=jnp.float32
    )


def right_dot(left, right):
    return lax.dot_general(
        left, right, (((1,), (1,)), ((), ())), preferred_element_type=jnp.float32
    )


def body(
    tokens,
    per_layer,
    teacher,
    cont_lengths,
    w_query,
    w_kv,
    w_out,
    laurel_left,
    laurel_right,
    pl_gate,
    pl_proj,
    norm_gains,
    head_gains,
    ffn_weight,
):
    states = tokens[0].astype(jnp.float32)
    layer_in = per_layer[0].astype(jnp.float32)
    target = teacher[0].astype(jnp.float32)
    row_count = states.shape[0]
    seq_count = lax.axis_size("seq")
    group_count = lax.axis_size("fsdp")
    seq_index = lax.axis_index("seq")
    group_index = lax.axis_index("fsdp")
    half_point = seq_count // 2
    prompt_len = half_point * row_count
    win_shards = -(-WINDOW // row_count)
    cont_shards = CONT_LEN // row_count
    cont_count = prompt_len // CONT_LEN
    is_cont = seq_index >= half_point
    rel_index = seq_index - half_point
    local_shard = jnp.where(is_cont, rel_index % cont_shards, 0)
    cont_index = jnp.where(is_cont, rel_index // cont_shards, 0)
    first_place = jnp.where(is_cont, prompt_len + local_shard * row_count, seq_index * row_count)
    row_range = jnp.arange(row_count, dtype=jnp.int32)
    places = first_place + row_range
    group_lengths = jnp.sum(
        jnp.where(
            jnp.arange(group_count, dtype=jnp.int32)[:, None] == group_index, cont_lengths, 0
        ),
        axis=0,
    )
    my_length = jnp.sum(
        jnp.where(jnp.arange(cont_count, dtype=jnp.int32) == cont_index, group_lengths, 0)
    )
    valid = jnp.logical_or(
        jnp.logical_not(is_cont), local_shard * row_count + row_range < my_length
    )
    weight_mask = valid.astype(jnp.float32)
    count = jnp.float32(group_count * prompt_len) + jnp.sum(cont_lengths).astype(jnp.float32)
    total_slots = float(row_count * seq_count * group_count)
    wq, wkv, wo, lleft, lright, plg, plp, gain_rows, head_rows = (
        lax.all_gather(w_query, ("seq", "fsdp"), axis=0, tiled=True),
        lax.all_gather(w_kv, ("seq", "fsdp"), axis=0, tiled=True),
        lax.all_gather(w_out, ("seq", "fsdp"), axis=0, tiled=True),
        lax.all_gather(laurel_left, ("seq", "fsdp"), axis=0, tiled=True),
        lax.all_gather(laurel_right, ("seq", "fsdp"), axis=1, tiled=True),
        lax.all_gather(pl_gate, ("seq", "fsdp"), axis=0, tiled=True),
        lax.all_gather(pl_proj, ("seq", "fsdp"), axis=0, tiled=True),
        lax.all_gather(norm_gains, ("seq", "fsdp"), axis=1, tiled=True),
        lax.all_gather(head_gains, ("seq", "fsdp"), axis=1, tiled=True),
    )
    gains = gain_rows.astype(jnp.float32)
    head_gain = head_rows.astype(jnp.float32)
    key_cols = KV_HEADS * HEAD
    normed = rms_norm(states, gains[0])
    normed_low = normed.astype(jnp.bfloat16)
    query_raw = full_dot(normed_low, wq)
    kv_raw = full_dot(normed_low, wkv)

    def prepare(q_input, k_input, v_input, q_gain, k_gain):
        q_heads = rotate(rms_norm(q_input.reshape(row_count, HEADS, HEAD), q_gain), places)
        k_heads = rotate(rms_norm(k_input.reshape(row_count, KV_HEADS, HEAD), k_gain), places)
        v_heads = plain_norm(v_input.reshape(row_count, KV_HEADS, HEAD))
        return (q_heads, k_heads, v_heads)

    (queries, keys_new, values_new), prepare_back = jax.vjp(
        prepare, query_raw, kv_raw[:, :key_cols], kv_raw[:, key_cols:], head_gain[0], head_gain[1]
    )
    query_low = queries.astype(jnp.bfloat16)
    kv_send = jnp.concatenate(
        [
            keys_new.reshape(row_count, key_cols).astype(jnp.bfloat16),
            values_new.reshape(row_count, key_cols).astype(jnp.bfloat16),
        ],
        1,
    )

    def uses_tail(offset):
        return jnp.logical_and(is_cont, local_shard < offset)

    halo_blocks = []
    for offset in range(1, win_shards + 1):
        halo_blocks.append(passed_along(kv_send, "seq", offset))
    slots = []
    far_blocks = []
    for member in range(win_shards):
        far_blocks.append(broadcast(kv_send, "seq", half_point - win_shards + member))
    tail_stack = jnp.stack(far_blocks)
    for offset in range(1, win_shards + 1):
        pick = jnp.clip(win_shards - offset + local_shard, 0, win_shards - 1)
        far_block = lax.dynamic_index_in_dim(tail_stack, pick, 0, keepdims=False)
        slots.append(jnp.where(uses_tail(offset), far_block, halo_blocks[offset - 1]))
    keys_all = jnp.concatenate(
        [slots[win_shards - 1 - number] for number in range(win_shards)] + [kv_send], 0
    )
    key_len = keys_all.shape[0]
    key_places = first_place - win_shards * row_count + jnp.arange(key_len, dtype=jnp.int32)
    visible = (
        (key_places[None, :] <= places[:, None])
        & (places[:, None] - key_places[None, :] < WINDOW)
        & (key_places[None, :] >= 0)
    )
    group_heads = HEADS // KV_HEADS
    query_grouped = query_low.reshape(row_count, KV_HEADS, group_heads, HEAD)
    key_heads = keys_all[:, :key_cols].reshape(key_len, KV_HEADS, HEAD)
    value_heads = keys_all[:, key_cols:].reshape(key_len, KV_HEADS, HEAD)

    def masked_scores():
        scores = jnp.einsum(
            "qgjd,kgd->gjqk", query_grouped, key_heads, preferred_element_type=jnp.float32
        )
        return jnp.where(visible, scores, -1e30)

    scores_fwd = masked_scores()
    top_score = jnp.max(scores_fwd, axis=-1, keepdims=True)
    expo = jnp.exp(scores_fwd - top_score)
    totals = jnp.sum(expo, axis=-1, keepdims=True)
    probs = expo / totals
    log_total = top_score + jnp.log(totals)
    probs_low = probs.astype(jnp.bfloat16)
    context = jnp.einsum(
        "gjqk,kgd->qgjd", probs_low, value_heads, preferred_element_type=jnp.float32
    )
    context_low = context.reshape(row_count, HEADS * HEAD).astype(jnp.bfloat16)
    attn_raw = full_dot(context_low, wo)
    attn_out = rms_norm(attn_raw, gains[1])
    laurel_mid = full_dot(normed_low, lleft).astype(jnp.bfloat16)
    laurel_raw = full_dot(laurel_mid, lright)
    mixed = (states + attn_out + normed + rms_norm(laurel_raw, gains[2])) * INV_SQRT2
    ffn_in = rms_norm(mixed, gains[3]).astype(jnp.bfloat16)
    ffn_rows = lax.all_gather(ffn_in, "fsdp", axis=0, tiled=True)
    piece = lax.all_gather(ffn_weight, "seq", axis=0, tiled=True)
    gate_up = jnp.einsum("td,nkd->tkn", ffn_rows, piece[:, :2], preferred_element_type=jnp.float32)
    hidden_low = gated_product(gate_up[:, 0], gate_up[:, 1]).astype(jnp.bfloat16)
    running = full_dot(hidden_low, piece[:, 2])
    down_out = lax.psum_scatter(
        running.astype(jnp.bfloat16), "fsdp", scatter_dimension=0, tiled=True
    ).astype(jnp.float32)
    preact = gate_up
    after_ffn = mixed + rms_norm(down_out, gains[4])
    after_low = after_ffn.astype(jnp.bfloat16)
    pl_raw = full_dot(after_low, plg)
    pl_act = gelu_tanh(pl_raw)
    pl_mid = (pl_act * layer_in).astype(jnp.bfloat16)
    pl_out = full_dot(pl_mid, plp)
    result = after_ffn + rms_norm(pl_out, gains[5])
    errors = result - target
    squares = jnp.sum(weight_mask[:, None] * errors * errors)
    match_loss = lax.psum(squares, ("seq", "fsdp")) / (2.0 * D * count)
    grad_out = weight_mask[:, None] * errors * (total_slots / count)
    unused, pl_norm_back = jax.vjp(rms_norm, pl_out, gains[5])
    grad_pl_out, grad_g5 = pl_norm_back(grad_out)
    grad_pl_low = grad_pl_out.astype(jnp.bfloat16)
    grad_plp = left_dot(pl_mid, grad_pl_low)
    grad_pl_mid = right_dot(grad_pl_low, plp)
    grad_layer_in = grad_pl_mid * pl_act
    unused, gelu_back = jax.vjp(gelu_tanh, pl_raw)
    grad_pl_raw = gelu_back(grad_pl_mid * layer_in)[0].astype(jnp.bfloat16)
    grad_plg = left_dot(after_low, grad_pl_raw)
    grad_after = grad_out + right_dot(grad_pl_raw, plg)
    unused, down_norm_back = jax.vjp(rms_norm, down_out, gains[4])
    grad_down, grad_g4 = down_norm_back(grad_after)
    grad_down_low = grad_down.astype(jnp.bfloat16)
    grad_down_rows = lax.all_gather(grad_down_low, "fsdp", axis=0, tiled=True)
    piece = lax.all_gather(ffn_weight, "seq", axis=0, tiled=True)
    gate_up = preact
    activated, act_back = jax.vjp(gated_product, gate_up[:, 0], gate_up[:, 1])
    hidden_low = activated.astype(jnp.bfloat16)
    grad_hidden = right_dot(grad_down_rows, piece[:, 2])
    grad_gate, grad_up = act_back(grad_hidden)
    grad_gate_up = jnp.stack([grad_gate, grad_up], 1).astype(jnp.bfloat16)
    running = jnp.einsum(
        "tkn,nkd->td", grad_gate_up, piece[:, :2], preferred_element_type=jnp.float32
    )
    saved_rows = jnp.concatenate([grad_gate_up, hidden_low[:, None]], 1)
    grad_ffn_in = lax.psum_scatter(
        running.astype(jnp.bfloat16), "fsdp", scatter_dimension=0, tiled=True
    ).astype(jnp.float32)
    gate_up_grad = jnp.einsum(
        "tkn,td->nkd", saved_rows[:, :2], ffn_rows, preferred_element_type=jnp.float32
    )
    down_grad = jnp.einsum(
        "tn,td->nd", saved_rows[:, 2], grad_down_rows, preferred_element_type=jnp.float32
    )
    grad_ffn = lax.psum_scatter(
        jnp.concatenate([gate_up_grad, down_grad[:, None]], 1),
        "seq",
        scatter_dimension=0,
        tiled=True,
    )
    unused, mix_norm_back = jax.vjp(rms_norm, mixed, gains[3])
    grad_mixed_norm, grad_g3 = mix_norm_back(grad_ffn_in)
    grad_scaled = (grad_after + grad_mixed_norm) * INV_SQRT2
    unused, laurel_norm_back = jax.vjp(rms_norm, laurel_raw, gains[2])
    grad_laurel, grad_g2 = laurel_norm_back(grad_scaled)
    grad_laurel_low = grad_laurel.astype(jnp.bfloat16)
    grad_lright = left_dot(laurel_mid, grad_laurel_low)
    grad_mid_low = right_dot(grad_laurel_low, lright).astype(jnp.bfloat16)
    grad_lleft = left_dot(normed_low, grad_mid_low)
    unused, attn_norm_back = jax.vjp(rms_norm, attn_raw, gains[1])
    grad_attn, grad_g1 = attn_norm_back(grad_scaled)
    grad_attn_low = grad_attn.astype(jnp.bfloat16)
    grad_wo = left_dot(context_low, grad_attn_low)
    grad_context = (
        right_dot(grad_attn_low, wo)
        .astype(jnp.bfloat16)
        .reshape(row_count, KV_HEADS, group_heads, HEAD)
    )
    probs_again = jnp.exp(masked_scores() - log_total)
    grad_probs = jnp.einsum(
        "qgjd,kgd->gjqk", grad_context, value_heads, preferred_element_type=jnp.float32
    )
    grad_scores = (
        probs_again * (grad_probs - jnp.sum(probs_again * grad_probs, axis=-1, keepdims=True))
    ).astype(jnp.bfloat16)
    grad_queries = jnp.einsum(
        "gjqk,kgd->qgjd", grad_scores, key_heads, preferred_element_type=jnp.float32
    )
    grad_keys = jnp.einsum(
        "gjqk,qgjd->kgd", grad_scores, query_grouped, preferred_element_type=jnp.float32
    )
    grad_values = jnp.einsum(
        "gjqk,qgjd->kgd",
        probs_again.astype(jnp.bfloat16),
        grad_context,
        preferred_element_type=jnp.float32,
    )
    grad_kv_all = jnp.concatenate(
        [grad_keys.reshape(key_len, key_cols), grad_values.reshape(key_len, key_cols)], 1
    )
    grad_own = grad_kv_all[win_shards * row_count :]
    tail_terms = jnp.zeros((win_shards, row_count, 2 * key_cols), jnp.float32)
    for offset in range(1, win_shards + 1):
        slot_grad = grad_kv_all[
            (win_shards - offset) * row_count : (win_shards - offset + 1) * row_count
        ]
        halo_used = jnp.logical_not(uses_tail(offset))
        grad_own = grad_own + passed_along(
            jnp.where(halo_used, slot_grad, 0.0).astype(jnp.bfloat16), "seq", -offset
        ).astype(jnp.float32)
        pick = win_shards - offset + local_shard
        placed = jnp.where(uses_tail(offset), slot_grad, 0.0)
        tail_terms = tail_terms + jnp.where(
            (jnp.arange(win_shards, dtype=jnp.int32) == pick)[:, None, None], placed[None], 0.0
        )
    tail_summed = lax.psum(tail_terms, "seq")
    for member in range(win_shards):
        grad_own = grad_own + jnp.where(
            seq_index == half_point - win_shards + member, tail_summed[member], 0.0
        )
    grad_query_raw, grad_key_raw, grad_value_raw, grad_hq, grad_hk = prepare_back(
        (
            grad_queries.reshape(row_count, HEADS, HEAD),
            grad_own[:, :key_cols].reshape(row_count, KV_HEADS, HEAD),
            grad_own[:, key_cols:].reshape(row_count, KV_HEADS, HEAD),
        )
    )
    grad_query_low = grad_query_raw.astype(jnp.bfloat16)
    grad_kv_low = jnp.concatenate([grad_key_raw, grad_value_raw], 1).astype(jnp.bfloat16)
    grad_wq = left_dot(normed_low, grad_query_low)
    grad_wkv = left_dot(normed_low, grad_kv_low)
    grad_normed = (
        grad_scaled
        + right_dot(grad_mid_low, lleft)
        + right_dot(grad_query_low, wq)
        + right_dot(grad_kv_low, wkv)
    )
    unused, input_norm_back = jax.vjp(rms_norm, states, gains[0])
    grad_states, grad_g0 = input_norm_back(grad_normed)
    grad_tokens = grad_scaled + grad_states
    grad_gain_rows = jnp.stack([grad_g0, grad_g1, grad_g2, grad_g3, grad_g4, grad_g5])
    grad_head_rows = jnp.stack([grad_hq, grad_hk])
    (
        outs_wq,
        outs_wkv,
        outs_wo,
        outs_lleft,
        outs_lright,
        outs_plg,
        outs_plp,
        outs_gains,
        outs_heads,
    ) = (
        lax.psum_scatter(grad_wq, ("seq", "fsdp"), scatter_dimension=0, tiled=True),
        lax.psum_scatter(grad_wkv, ("seq", "fsdp"), scatter_dimension=0, tiled=True),
        lax.psum_scatter(grad_wo, ("seq", "fsdp"), scatter_dimension=0, tiled=True),
        lax.psum_scatter(grad_lleft, ("seq", "fsdp"), scatter_dimension=0, tiled=True),
        lax.psum_scatter(grad_lright, ("seq", "fsdp"), scatter_dimension=1, tiled=True),
        lax.psum_scatter(grad_plg, ("seq", "fsdp"), scatter_dimension=0, tiled=True),
        lax.psum_scatter(grad_plp, ("seq", "fsdp"), scatter_dimension=0, tiled=True),
        lax.psum_scatter(grad_gain_rows, ("seq", "fsdp"), scatter_dimension=1, tiled=True),
        lax.psum_scatter(grad_head_rows, ("seq", "fsdp"), scatter_dimension=1, tiled=True),
    )
    return (
        result[None],
        match_loss,
        grad_tokens[None],
        grad_layer_in[None],
        outs_wq,
        outs_wkv,
        outs_wo,
        outs_lleft,
        outs_lright,
        outs_plg,
        outs_plp,
        outs_gains,
        outs_heads,
        grad_ffn,
    )


def solution(mesh):
    placed = (
        P("fsdp", "seq", None),
        P("fsdp", "seq", None),
        P("fsdp", "seq", None),
        P(),
        P(("seq", "fsdp"), None),
        P(("seq", "fsdp"), None),
        P(("seq", "fsdp"), None),
        P(("seq", "fsdp"), None),
        P(None, ("seq", "fsdp")),
        P(("seq", "fsdp"), None),
        P(("seq", "fsdp"), None),
        P(None, ("seq", "fsdp")),
        P(None, ("seq", "fsdp")),
        P(("seq", "fsdp"), None, None),
    )
    return jax.shard_map(
        body,
        mesh=mesh,
        in_specs=placed,
        out_specs=(
            P("fsdp", "seq", None),
            P(),
            P("fsdp", "seq", None),
            P("fsdp", "seq", None),
            P(("seq", "fsdp"), None),
            P(("seq", "fsdp"), None),
            P(("seq", "fsdp"), None),
            P(("seq", "fsdp"), None),
            P(None, ("seq", "fsdp")),
            P(("seq", "fsdp"), None),
            P(("seq", "fsdp"), None),
            P(None, ("seq", "fsdp")),
            P(None, ("seq", "fsdp")),
            P(("seq", "fsdp"), None, None),
        ),
        check_vma=False,
    )
```

profile of v0, /device:TPU:0, one launch (start us, length us, event | category | flops | bytes accessed | tf_op | source)
XLA Modules:
  0.0 3697.6 jit_solution(8390201885059416440)
XLA Ops:
  8.0 69.7 %all-gather.1 = bf16[32,8,2]{1,2,0:T(2,128)(2,1)S(1)} all-gather(bf16[1,8,2]{1,2,0:T(2,128)(2,1)} %bitcast.368), channel_id=1, replica_groups=mesh['seq'=16,'fsdp'=2] {'seq','fsdp'}, dimensions={0}, use_global_device_ids=true | all-gather | bytes 1056 | tf_op jit(solution)/shard_map/all_gather | solution.py:137
  78.0 63.9 %all-gather = bf16[32,64,6]{1,2,0:T(8,128)(2,1)S(1)} all-gather(bf16[1,64,6]{1,2,0:T(8,128)(2,1)} %bitcast.367), channel_id=1, replica_groups=mesh['seq'=16,'fsdp'=2] {'seq','fsdp'}, dimensions={0}, use_global_device_ids=true | all-gather | bytes 25344 | tf_op jit(solution)/shard_map/all_gather | solution.py:136
  145.6 3.5 fusion.161
  157.3 69.3 %all_gather.43 = bf16[64,2048]{0,1:T(8,128)(2,1)S(1)} all-gather(bf16[64,64]{0,1:T(8,128)(2,1)S(1)} %copy.140), channel_id=1, replica_groups=mesh['seq'=16,'fsdp'=2] {'seq','fsdp'}, dimensions={1}, use_global_device_ids=true | all-gather | bytes 270336 | tf_op jit(solution)/shard_map/all_gather | solution.py:133
  226.6 67.8 %all_gather.42 = bf16[2048,64]{1,0:T(8,128)(2,1)S(1)} all-gather(bf16[64,64]{1,0:T(8,128)(2,1)S(1)} %copy-done.99), channel_id=1, replica_groups=mesh['seq'=16,'fsdp'=2] {'seq','fsdp'}, dimensions={0}, use_global_device_ids=true | all-gather | bytes 270336 | tf_op jit(solution)/shard_map/all_gather | solution.py:132
  296.8 2.1 collective-permute-start.1
  298.8 2.1 collective-permute-start
  303.5 20.0 collective-permute-done
  326.2 2.5 reshape.419
  330.6 4.6 all-gather.13.cloned.1.call-done
  335.2 12.5 copy.134
  347.7 5.9 multiply_reduce_fusion.12
  358.2 2.0 copy.136
  360.3 2.6 fusion.32
  367.5 54.0 %all-gather.15.cloned.1.call-done = bf16[2048,2048]{1,0:T(8,128)(2,1)} async-done(((bf16[64,2048]{1,0:T(8,128)(2,1)}), bf16[2048,2048]{1,0:T(8,128)(2,1)}) %all-gather.15.cloned.1.call-update) | async-done | bytes 8388624 | tf_op jit(solution)/shard_map/all_gather | solution.py:131
  421.5 6.0 multiply_reduce_fusion.11
  431.2 31.2 all-gather.17.cloned.1.call-done
  462.4 248.5 %all-gather.19.cloned.1.call-done = bf16[4096,3,2048]{2,0,1:T(8,128)(2,1)} async-done(((bf16[256,3,2048]{2,0,1:T(8,128)(2,1)}), bf16[4096,3,2048]{2,0,1:T(8,128)(2,1)}) %all-gather.19.cloned.1.call-update) | async-done | bytes 50331664 | tf_op jit(solution)/shard_map/all_gather | solution.py:219
  710.9 25.1 fusion.6
  736.0 21.6 fusion.50
  762.6 27.0 reduce-scatter.17.cloned.1.call-done
  792.9 53.7 %all-gather.21.cloned.1.call-done = bf16[2048,256]{1,0:T(8,128)(2,1)} async-done(((bf16[64,256]{1,0:T(8,128)(2,1)}), bf16[2048,256]{1,0:T(8,128)(2,1)}) %all-gather.21.cloned.1.call-update) | async-done | bytes 1048592 | tf_op jit(solution)/shard_map/all_gather | solution.py:134
  848.4 54.3 %all-gather.23.cloned.1.call-done = bf16[256,2048]{1,0:T(8,128)(2,1)} async-done(((bf16[8,2048]{1,0:T(8,128)(2,1)}), bf16[256,2048]{1,0:T(8,128)(2,1)}) %all-gather.23.cloned.1.call-update) | async-done | bytes 1048592 | tf_op jit(solution)/shard_map/all_gather | solution.py:135
  904.6 2.4 multiply_reduce_fusion.1
  915.5 32.1 all-gather.25.cloned.1.call-done
  947.6 20.6 fusion.40
  968.2 2.1 copy-done.30
  971.4 22.4 bitcast_convert_fusion
  994.3 31.5 convolution_bitcast_fusion
  1025.8 19.7 convolution_bitcast_fusion.1
  1045.6 2.8 fusion.73
  1048.5 4.7 multiply_reduce_fusion.2
  1056.0 5.7 convolution_convert_fusion
  1062.6 5.6 fusion.44
  1068.2 4.8 fusion.28
  1074.6 2.3 fusion.110
  1077.0 2.3 fusion.171
  1080.2 3.2 multiply_add_fusion.2
  1091.6 3.4 multiply_reduce_fusion
  1097.7 3.6 fusion.84
  1101.6 7.5 fusion.172
  1109.1 3.6 collective-permute-done.3
  1112.7 81.9 %all-reduce.10.cloned.1.call-done = f32[2,256,1024]{2,1,0:T(8,128)} async-done(((f32[2,256,1024]{2,1,0:T(8,128)}), f32[2,256,1024]{2,1,0:T(8,128)}) %all-reduce.10.cloned.1.call-update) | async-done | bytes 2097168 | tf_op jit(solution)/shard_map/psum | solution.py:333
  1194.6 2.4 fusion.98
  1206.1 3.6 fusion.115
  1210.2 2.9 fusion.71
  1214.7 65.4 %pad_maximum_fusion = f32[4096,3,2048]{0,2,1:T(8,128)} fusion(f32[4096,1,2048]{0,2,1:T(8,128)} %convolution_bitcast_fusion.1, f32[4096,2,2048]{0,2,1:T(8,128)} %convolution_bitcast_fusion), kind=kLoop, calls=%fused_computation | loop fusion | flops 25165824 | bytes 201326592 | tf_op jit(solution)/shard_map/concatenate | solution.py:273
  1281.0 3.1 fusion.153
  1284.3 3.0 fusion.174
  1287.4 2.4 fusion.157
  1290.1 5.7 fusion.114
  1295.8 9.5 fusion.103
  1305.4 9.6 fusion.173
  1315.7 40.3 %all-reduce.5 = (f32[]{:T(128)}, f32[2,256]{1,0:T(2,128)S(1)}) all-reduce(f32[]{:T(128)} %get-tuple-element.92, f32[2,256]{1,0:T(2,128)S(1)} %pad_maximum_fusion.15), channel_id=1, replica_groups=mesh['seq'=16,'fsdp'=2] {'seq','fsdp'}, use_global_device_ids=true, to_apply=%region_17.18 | all-reduce | flops 513 | bytes 4104 | tf_op jit(solution)/shard_map/psum | solution.py:236
  1358.8 3.6 fusion.86
  1362.3 102.8 %reduce-scatter.37.cloned.1.call-done = f32[64,6]{1,0:T(8,128)} async-done(((f32[2048,6]{1,0:T(8,128)}), f32[64,6]{1,0:T(8,128)}) %reduce-scatter.37.cloned.1.call-update) | async-done | bytes 1552
  1466.5 908.4 %reduce-scatter.33.cloned.1.call-done = f32[256,3,2048]{0,2,1:T(8,128)} async-done(((f32[4096,3,2048]{0,2,1:T(8,128)}), f32[256,3,2048]{0,2,1:T(8,128)}) %reduce-scatter.33.cloned.1.call-update) | async-done | bytes 6291472 | tf_op jit(solution)/shard_map/reduce_scatter | solution.py:272
  2374.9 6.6 copy.157
  2381.6 132.9 %reduce-scatter.31.cloned.1.call-done = f32[8,2048]{1,0:T(8,128)} async-done(((f32[256,2048]{1,0:T(8,128)}), f32[8,2048]{1,0:T(8,128)}) %reduce-scatter.31.cloned.1.call-update) | async-done | bytes 65552 | tf_op jit(solution)/shard_map/reduce_scatter | solution.py:377
  2514.5 136.3 %reduce-scatter.29.cloned.1.call-done = f32[64,256]{1,0:T(8,128)} async-done(((f32[2048,256]{1,0:T(8,128)}), f32[64,256]{1,0:T(8,128)}) %reduce-scatter.29.cloned.1.call-update) | async-done | bytes 65552 | tf_op jit(solution)/shard_map/reduce_scatter | solution.py:376
  2650.9 133.5 %reduce-scatter.27.cloned.1.call-done = f32[64,64]{1,0:T(8,128)} async-done(((f32[2048,64]{1,0:T(8,128)}), f32[64,64]{1,0:T(8,128)}) %reduce-scatter.27.cloned.1.call-update) | async-done | bytes 16400 | tf_op jit(solution)/shard_map/reduce_scatter | solution.py:374
  2784.4 182.1 %reduce-scatter.23.cloned.1.call-done = f32[64,1024]{1,0:T(8,128)} async-done(((f32[2048,1024]{1,0:T(8,128)}), f32[64,1024]{1,0:T(8,128)}) %reduce-scatter.23.cloned.1.call-update) | async-done | bytes 262160 | tf_op jit(solution)/shard_map/reduce_scatter | solution.py:372
  2966.5 361.0 %reduce-scatter.21.cloned.1.call-done = f32[64,2048]{1,0:T(8,128)} async-done(((f32[2048,2048]{1,0:T(8,128)}), f32[64,2048]{1,0:T(8,128)}) %reduce-scatter.21.cloned.1.call-update) | async-done | bytes 524304 | tf_op jit(solution)/shard_map/reduce_scatter | solution.py:371
  3327.5 361.6 %reduce-scatter.25.cloned.1.call-done = f32[64,2048]{1,0:T(8,128)} async-done(((f32[2048,2048]{1,0:T(8,128)}), f32[64,2048]{1,0:T(8,128)}) %reduce-scatter.25.cloned.1.call-update) | async-done | bytes 524304 | tf_op jit(solution)/shard_map/reduce_scatter | solution.py:373
  (420 shorter events, 89.5 us)
Async XLA Ops:
  7.2 136.8 %copy-start = (bf16[1,256,2048]{2,1,0:T(8,128)(2,1)S(1)}, bf16[1,256,2048]{2,1,0:T(8,128)(2,1)}, u32[]{:S(2)}) copy-start(bf16[1,256,2048]{2,1,0:T(8,128)(2,1)} %param.14) | copy-start | bytes 3145732
  7.2 138.4 %all-gather.11.cloned.1.call-start = ((), (), s32[]{:S(2)}) async-start(), calls=%async_computation.11 | async-start | bytes 4325376 | tf_op jit(solution)/shard_map/all_gather | solution.py:130
  7.9 293.3 %all-reduce.12.cloned.1.call-start = ((), (), s32[]{:S(2)}) async-start(), calls=%async_computation.31 | async-start | bytes 2097152 | tf_op jit(solution)/shard_map/psum | solution.py:29
  143.2 210.8 %copy-start.49 = (f32[256,128]{0,1:T(8,128)}, f32[256,128]{0,1:T(8,128)S(1)}, u32[]{:S(2)}) copy-start(f32[256,128]{0,1:T(8,128)S(1)} %get-tuple-element.150) | copy-start | bytes 393220
  143.2 210.8 %copy-start.51 = (f32[256,128]{0,1:T(8,128)}, f32[256,128]{0,1:T(8,128)S(1)}, u32[]{:S(2)}) copy-start(f32[256,128]{0,1:T(8,128)S(1)} %get-tuple-element.151) | copy-start | bytes 393220
  143.3 9.8 copy-start.54
  144.3 4.7 copy-start.73
  145.6 281.9 %copy-start.61 = (f32[1,2048]{1,0:T(1,128)}, f32[1,2048]{1,0:T(1,128)S(1)}, u32[]{:S(2)}) copy-start(f32[1,2048]{1,0:T(1,128)S(1)} %get-tuple-element.147) | copy-start | bytes 24580
  154.6 72.1 %copy-start.99 = (bf16[64,64]{1,0:T(8,128)(2,1)S(1)}, bf16[64,64]{1,0:T(8,128)(2,1)}, u32[]{:S(2)}) copy-start(bf16[64,64]{1,0:T(8,128)(2,1)} %param.21) | copy-start | bytes 24580
  154.6 139.8 %copy-start.74 = (f32[256]{0:T(256)S(1)}, f32[256]{0:T(256)}, u32[]{:S(2)}) copy-start(f32[256]{0:T(256)} %copy-done.73) | copy-start | bytes 3076
  155.9 179.3 %all-gather.13.cloned.1.call-start = ((), (), s32[]{:S(2)}) async-start(), calls=%async_computation.12 | async-start | bytes 8650752 | tf_op jit(solution)/shard_map/all_gather | solution.py:129
  156.6 264.8 %all-gather.15.cloned.1.call-start = ((), (), s32[]{:S(2)}) async-start(), calls=%async_computation.13 | async-start | bytes 8650752 | tf_op jit(solution)/shard_map/all_gather | solution.py:131
  157.2 305.2 %all-gather.17.cloned.1.call-start = ((), (), s32[]{:S(2)}) async-start(), calls=%async_computation.14 | async-start | bytes 3145728 | tf_op jit(solution)/shard_map/all_gather | solution.py:218
  226.6 70.1 %copy-start.26 = (bf16[64,2048]{0,1:T(8,128)(2,1)}, bf16[64,2048]{0,1:T(8,128)(2,1)S(1)}, u32[]{:S(2)}) copy-start(bf16[64,2048]{0,1:T(8,128)(2,1)S(1)} %all_gather.43) | copy-start | bytes 786436
  294.4 6.6 copy-start.122
  294.9 8.6 copy-start.67
  296.7 28.1 copy-start.109
  296.7 130.7 %copy-start.105 = (f32[256]{0:T(256)}, f32[256]{0:T(256)S(1)}, u32[]{:S(2)}) copy-start(f32[256]{0:T(256)S(1)} %fusion.131) | copy-start | bytes 3076
  296.8 6.7 collective-permute-start.1
  298.8 24.7 collective-permute-start
  301.2 62.8 %copy-start.24 = (pred[256,768]{0,1:T(8,128)(4,1)}, pred[256,768]{0,1:T(8,128)(4,1)S(1)}, u32[]{:S(2)}) copy-start(pred[256,768]{0,1:T(8,128)(4,1)S(1)} %fusion.106) | copy-start | bytes 589828
  326.2 37.9 %copy-start.36 = (bf16[768,2,256]{2,1,0:T(2,128)(2,1)}, bf16[768,2,256]{2,1,0:T(2,128)(2,1)S(1)}, u32[]{:S(2)}) copy-start(bf16[768,2,256]{2,1,0:T(2,128)(2,1)S(1)} %reshape.418) | copy-start | bytes 2359300
  347.7 5.9 copy-start.103
  354.9 5.4 copy-start.38
  367.5 59.9 %copy-start.18 = (bf16[2,256,4,256]{3,1,2,0:T(8,128)(2,1)}, bf16[2,256,4,256]{3,1,2,0:T(8,128)(2,1)S(1)}, u32[]{:S(2)}) copy-start(bf16[2,256,4,256]{3,1,2,0:T(8,128)(2,1)S(1)} %fusion.91) | copy-start | bytes 3145732
  421.5 6.0 copy-start.3
  421.5 6.0 copy-start.77
  421.5 6.1 copy-start.79
  430.5 280.4 %all-gather.19.cloned.1.call-start = ((), (), s32[]{:S(2)}) async-start(), calls=%async_computation.15 | async-start | bytes 53477376 | tf_op jit(solution)/shard_map/all_gather | solution.py:219
  431.1 358.5 %reduce-scatter.17.cloned.1.call-start = ((), (), s32[]{:S(2)}) async-start(), calls=%async_computation.16 | async-start | bytes 3145728 | tf_op jit(solution)/shard_map/reduce_scatter | solution.py:223
  757.6 89.0 %all-gather.21.cloned.1.call-start = ((), (), s32[]{:S(2)}) async-start(), calls=%async_computation.17 | async-start | bytes 1081344 | tf_op jit(solution)/shard_map/all_gather | solution.py:134
  758.4 144.3 %all-gather.23.cloned.1.call-start = ((), (), s32[]{:S(2)}) async-start(), calls=%async_computation.18 | async-start | bytes 1081344 | tf_op jit(solution)/shard_map/all_gather | solution.py:135
  759.1 188.5 %all-gather.25.cloned.1.call-start = ((), (), s32[]{:S(2)}) async-start(), calls=%async_computation.19 | async-start | bytes 3145728 | tf_op jit(solution)/shard_map/all_gather | solution.py:251
  792.9 53.8 %copy-start.16 = (bf16[256,2048]{1,0:T(8,128)(2,1)}, bf16[256,2048]{1,0:T(8,128)(2,1)S(1)}, u32[]{:S(2)}) copy-start(bf16[256,2048]{1,0:T(8,128)(2,1)S(1)} %fusion.92) | copy-start | bytes 3145732
  792.9 109.8 %copy-start.65 = (bf16[1,256,256]{2,1,0:T(8,128)(2,1)S(1)}, bf16[1,256,256]{2,1,0:T(8,128)(2,1)}, u32[]{:S(2)}) copy-start(bf16[1,256,256]{2,1,0:T(8,128)(2,1)} %param.15) | copy-start | bytes 393220
  848.3 59.4 %copy-start.40 = (f32[256,256]{1,0:T(8,128)}, f32[256,256]{1,0:T(8,128)S(1)}, u32[]{:S(2)}) copy-start(f32[256,256]{1,0:T(8,128)S(1)} %fusion.170) | copy-start | bytes 786436
  848.3 56.2 %copy-start.9 = (bf16[256,2048]{1,0:T(8,128)(2,1)S(1)}, bf16[256,2048]{1,0:T(8,128)(2,1)}, u32[]{:S(2)}) copy-start(bf16[256,2048]{1,0:T(8,128)(2,1)} %reduce-scatter.17.cloned.1.call-done) | copy-start | bytes 3145732
  848.3 56.2 %copy-start.76 = (f32[1,2048]{1,0:T(1,128)S(1)}, f32[1,2048]{1,0:T(1,128)}, u32[]{:S(2)}) copy-start(f32[1,2048]{1,0:T(1,128)} %get-tuple-element.142) | copy-start | bytes 24580
  915.3 130.2 %reduce-scatter.19.cloned.1.call-start = ((), (), s32[]{:S(2)}) async-start(), calls=%async_computation.20 | async-start | bytes 3145728 | tf_op jit(solution)/shard_map/reduce_scatter | solution.py:263
  993.9 200.7 %all-reduce.10.cloned.1.call-start = ((), (), s32[]{:S(2)}) async-start(), calls=%async_computation.21 | async-start | bytes 4194304 | tf_op jit(solution)/shard_map/psum | solution.py:333
  1025.8 19.8 copy-start.70
  1025.8 19.8 copy-start.112
  1048.5 4.7 copy-start.116
  1048.5 4.7 copy-start.110
  1048.5 4.7 copy-start.8
  1062.6 5.6 copy-start.37
  1062.6 10.3 slice-start
  1068.2 4.8 slice-start.1
  1086.7 22.4 collective-permute-start.2
  1088.0 24.7 collective-permute-start.3
  1091.0 265.0 %reduce-scatter.35.cloned.1.call-start = ((), (), s32[]{:S(2)}) async-start(), calls=%async_computation.29 | async-start | bytes 1081344
  1091.6 4.5 copy-start.68
  1101.4 363.8 %reduce-scatter.37.cloned.1.call-start = ((), (), s32[]{:S(2)}) async-start(), calls=%async_computation.30 | async-start | bytes 1081344
  1206.1 4.0 copy-start.44
  1214.6 1160.3 %reduce-scatter.33.cloned.1.call-start = ((), (), s32[]{:S(2)}) async-start(), calls=%async_computation.28 | async-start | bytes 106954752 | tf_op jit(solution)/shard_map/reduce_scatter | solution.py:272
  1280.1 4.1 copy-start.64
  1280.1 1234.4 %reduce-scatter.31.cloned.1.call-start = ((), (), s32[]{:S(2)}) async-start(), calls=%async_computation.27 | async-start | bytes 2162688 | tf_op jit(solution)/shard_map/reduce_scatter | solution.py:377
  1284.2 1366.7 %reduce-scatter.29.cloned.1.call-start = ((), (), s32[]{:S(2)}) async-start(), calls=%async_computation.26 | async-start | bytes 2162688 | tf_op jit(solution)/shard_map/reduce_scatter | solution.py:376
  1287.3 1497.1 %reduce-scatter.27.cloned.1.call-start = ((), (), s32[]{:S(2)}) async-start(), calls=%async_computation.25 | async-start | bytes 1081344 | tf_op jit(solution)/shard_map/reduce_scatter | solution.py:374
  1289.8 1676.7 %reduce-scatter.23.cloned.1.call-start = ((), (), s32[]{:S(2)}) async-start(), calls=%async_computation.23 | async-start | bytes 8650752 | tf_op jit(solution)/shard_map/reduce_scatter | solution.py:372
  1295.8 2031.7 %reduce-scatter.21.cloned.1.call-start = ((), (), s32[]{:S(2)}) async-start(), calls=%async_computation.22 | async-start | bytes 17301504 | tf_op jit(solution)/shard_map/reduce_scatter | solution.py:371
  1305.4 2383.8 %reduce-scatter.25.cloned.1.call-start = ((), (), s32[]{:S(2)}) async-start(), calls=%async_computation.24 | async-start | bytes 17301504 | tf_op jit(solution)/shard_map/reduce_scatter | solution.py:373
  1315.1 43.7 %copy-start.114 = (f32[256]{0:T(256)S(1)}, f32[256]{0:T(256)}, u32[]{:S(2)}) copy-start(f32[256]{0:T(256)} %copy-done.113) | copy-start | bytes 3076
  1315.1 43.7 %copy-start.124 = (f32[256]{0:T(256)S(1)}, f32[256]{0:T(256)}, u32[]{:S(2)}) copy-start(f32[256]{0:T(256)} %get-tuple-element.98) | copy-start | bytes 3076
  (89 other events, 202.2 us)
Sparse Core Ops, SparseCore 0:
  11.0 65.0 all-gather.10
  156.0 91.9 all-reduce.11
  251.0 84.1 all-gather.12
  338.0 83.3 all-gather.14
  430.6 31.6 all-gather.16
  463.8 247.0 all-gather.18
  757.7 31.8 reduce-scatter.16
  792.9 53.7 all-gather.20
  850.0 52.6 all-gather.22
  915.5 32.0 all-gather.24
  994.0 31.8 reduce-scatter.18
  1091.1 103.4 all-reduce.9
  1196.9 134.2 reduce-scatter.34
  1333.9 131.1 reduce-scatter.36
  1469.8 905.1 reduce-scatter.32
  2377.6 136.8 reduce-scatter.30
  2517.3 133.5 reduce-scatter.28
  2653.5 130.8 reduce-scatter.26
  2787.4 179.0 reduce-scatter.22
  2969.3 358.1 reduce-scatter.20
  3330.5 358.5 reduce-scatter.24
where the time goes:
time: 3710 us; the launch traced here: 3700 us
  waiting for transfers between devices  2930 us (79%)
  blocking collectives  311 us (8%)
  matrix products  240 us (6%)
  other arithmetic  123 us (3%)
  local copies, waits for them, and re-layouts  61.8 us (2%)
    reduce_scatter x1, waiting for transfers between devices, body(): lax.psum_scatter(jnp.concatenate([gate_up_grad, down_grad[:, None]], 1),...  908 us
    reduce_scatter x1, waiting for transfers between devices, body(): lax.psum_scatter(grad_wo, ('seq', 'fsdp'), scatter_dimension=0, tiled=True)  362 us
    reduce_scatter x1, waiting for transfers between devices, body(): lax.psum_scatter(grad_wq, ('seq', 'fsdp'), scatter_dimension=0, tiled=True)  361 us
    all_gather x1, waiting for transfers between devices, body(): piece = lax.all_gather(ffn_weight, 'seq', axis=0, tiled=True)  249 us
    reduce_scatter x1, waiting for transfers between devices, body(): lax.psum_scatter(grad_wkv, ('seq', 'fsdp'), scatter_dimension=0, tiled=True)  182 us
    reduce_scatter x1, waiting for transfers between devices, body(): lax.psum_scatter(grad_plg, ('seq', 'fsdp'), scatter_dimension=0, tiled=True)  136 us
    reduce_scatter x1, waiting for transfers between devices, body(): lax.psum_scatter(grad_lleft, ('seq', 'fsdp'), scatter_dimension=0, tiled=...  134 us
    reduce_scatter x1, waiting for transfers between devices, body(): lax.psum_scatter(grad_plp, ('seq', 'fsdp'), scatter_dimension=0, tiled=True)  133 us
  transfers between devices with their start and end apart: 25, of which 19 were waited for; matrix products, arithmetic and copies ran while one was open for 7% of the time, Pallas kernels for 0%

commit v1 on v0

v1 whole, which is shorter than its diff:
```python
import math

import jax
import jax.numpy as jnp
from jax import lax
from jax.sharding import Mesh, PartitionSpec as P

D = 2048
HEADS = 8
KV_HEADS = 2
HEAD = 256
WINDOW = 512
CONT_LEN = 512
RANK = 64
PLD = 256

EPSILON = 1e-06
INV_SQRT2 = 0.7071067811865476
ROPE_BASE = 10000.0
BF16 = jnp.bfloat16
F32 = jnp.float32


def rms_norm(values, gain):
    return values * lax.rsqrt(jnp.mean(values * values, axis=-1, keepdims=True) + EPSILON) * gain


def plain_norm(values):
    return values * lax.rsqrt(jnp.mean(values * values, axis=-1, keepdims=True) + EPSILON)


def rotate(values, places):
    half_dim = values.shape[-1] // 2
    freqs = jnp.exp(
        jnp.arange(half_dim, dtype=F32) * (-2.0 * math.log(ROPE_BASE) / values.shape[-1])
    )
    angles = places.astype(F32)[:, None, None] * freqs
    cosine = jnp.cos(angles)
    sine = jnp.sin(angles)
    first = values[..., :half_dim]
    second = values[..., half_dim:]
    return jnp.concatenate([first * cosine - second * sine, second * cosine + first * sine], -1)


def gelu_tanh(values):
    return jax.nn.gelu(values, approximate=True)


def gated_product(gate_in, up_in):
    return gelu_tanh(gate_in) * up_in


def full_dot(left, right):
    return jnp.dot(left, right, preferred_element_type=F32)


def left_dot(left, right):
    return lax.dot_general(left, right, (((0,), (0,)), ((), ())), preferred_element_type=F32)


def right_dot(left, right):
    return lax.dot_general(left, right, (((1,), (1,)), ((), ())), preferred_element_type=F32)


def ring_order(n):
    return list(range(0, n, 2)) + list(range(n - 1, 0, -2))


def ring_pairs(n, by):
    order = ring_order(n)
    return [(order[i], order[(i + by) % n]) for i in range(n)]


def ring(value, by):
    return lax.ppermute(value, "zy", ring_pairs(lax.axis_size("zy"), by))


def swap(value, axis):
    return lax.ppermute(value, axis, [(0, 1), (1, 0)])


def rows_of_four(own):
    pair = jnp.concatenate([own, swap(own, "fsdp")], 0)
    return jnp.concatenate([pair, swap(pair, "core")], 0)


def sum_of_four(partial):
    count = partial.shape[0] // 4
    low = partial[2 * count :].astype(BF16)
    pair = partial[: 2 * count] + swap(low, "core").astype(F32)
    low = pair[count:].astype(BF16)
    return pair[:count] + swap(low, "fsdp").astype(F32)


def body(
    tokens,
    per_layer,
    teacher,
    cont_lengths,
    w_query,
    w_kv,
    w_out,
    laurel_left,
    laurel_right,
    pl_gate,
    pl_proj,
    norm_gains,
    head_gains,
    ffn_weight,
):
    states = tokens[0].astype(F32)
    layer_in = per_layer[0].astype(F32)
    target = teacher[0].astype(F32)
    row_count = states.shape[0]
    chips = lax.axis_size("zy")
    seq_count = 2 * chips
    group_count = lax.axis_size("fsdp")
    shards = seq_count * group_count
    chip = lax.axis_index("zy")
    core = lax.axis_index("core")
    seq_index = chip * 2 + core
    group_index = lax.axis_index("fsdp")
    half_point = seq_count // 2
    prompt_len = half_point * row_count
    cont_shards = CONT_LEN // row_count
    cont_count = prompt_len // CONT_LEN
    is_cont = seq_index >= half_point
    rel_index = seq_index - half_point
    local_shard = jnp.where(is_cont, rel_index % cont_shards, 0)
    cont_index = jnp.where(is_cont, rel_index // cont_shards, 0)
    first_place = jnp.where(is_cont, prompt_len + local_shard * row_count, seq_index * row_count)
    row_range = jnp.arange(row_count, dtype=jnp.int32)
    places = first_place + row_range
    group_lengths = jnp.sum(
        jnp.where(
            jnp.arange(group_count, dtype=jnp.int32)[:, None] == group_index, cont_lengths, 0
        ),
        axis=0,
    )
    my_length = jnp.sum(
        jnp.where(jnp.arange(cont_count, dtype=jnp.int32) == cont_index, group_lengths, 0)
    )
    valid = jnp.logical_or(
        jnp.logical_not(is_cont), local_shard * row_count + row_range < my_length
    )
    weight_mask = valid.astype(F32)
    count = F32(group_count * prompt_len) + jnp.sum(cont_lengths).astype(F32)
    total_slots = float(row_count * seq_count * group_count)
    ring_pos = jnp.where(chip % 2 == 0, chip // 2, chips - 1 - chip // 2)

    def ring_owner(offset):
        spot = (ring_pos + offset + chips) % chips
        return jnp.where(spot < chips // 2, 2 * spot, 2 * (chips - 1 - spot) + 1)

    shard_rows = w_query.shape[0]
    key_cols = KV_HEADS * HEAD
    proj_cols = pl_proj.shape[0] * D // shard_rows
    misc_cols = RANK
    head_part = head_gains.reshape(-1, 1)
    misc = jnp.concatenate(
        [
            norm_gains.T,
            jnp.pad(head_part, ((0, shard_rows - head_part.shape[0]), (0, 0))),
            jnp.zeros((shard_rows, misc_cols - 7), BF16),
        ],
        1,
    )
    pack_a = jnp.concatenate([w_query, w_kv, laurel_left, misc], 1)
    pack_b = jnp.concatenate(
        [w_out, pl_gate, pl_proj.reshape(shard_rows, proj_cols), laurel_right.T], 1
    )
    all_axes = ("zy", "core", "fsdp")
    full_a = lax.all_gather(pack_a, all_axes, axis=0, tiled=True)
    full_b = lax.all_gather(pack_b, all_axes, axis=0, tiled=True)
    wq = full_a[:, :D]
    wkv = full_a[:, D : D + 2 * key_cols]
    lleft = full_a[:, D + 2 * key_cols : D + 2 * key_cols + RANK]
    misc_full = full_a[:, D + 2 * key_cols + RANK :]
    gains = misc_full[:, :6].T.astype(F32)
    head_n = head_gains.shape[1]
    head_gain = (
        misc_full[:, 6]
        .reshape(shards, shard_rows)[:, : 2 * head_n]
        .reshape(shards, 2, head_n)
        .transpose(1, 0, 2)
        .reshape(2, HEAD)
        .astype(F32)
    )
    wo = full_b[:, :D]
    plg = full_b[:, D : D + PLD]
    plp = full_b[:, D + PLD : D + PLD + proj_cols].reshape(PLD, D)
    lright = full_b[:, D + PLD + proj_cols :].T

    units = ffn_weight.shape[0]
    half = units // 2
    kinds = [ffn_weight[:, kind] for kind in range(3)]
    ups = [[w[:half] for w in kinds]]
    downs = [[w[half:] for w in kinds]]
    for _ in range(1, chips):
        ups.append([ring(w, 1) for w in ups[-1]])
        downs.append([ring(w, -1) for w in downs[-1]])
    parts = []
    first = 0
    while first < chips:
        length = max(1, (chips - first) // 2)
        parts.append(list(range(first, first + length)))
        first += length
    part_weights = [
        [
            jnp.concatenate([half_w for k in part for half_w in (ups[k][kind], downs[k][kind])], 0)
            for kind in range(3)
        ]
        for part in parts
    ]

    normed = rms_norm(states, gains[0])
    normed_low = normed.astype(BF16)
    query_raw = full_dot(normed_low, wq)
    kv_raw = full_dot(normed_low, wkv)

    def prepare(q_input, k_input, v_input, q_gain, k_gain):
        q_heads = rotate(rms_norm(q_input.reshape(row_count, HEADS, HEAD), q_gain), places)
        k_heads = rotate(rms_norm(k_input.reshape(row_count, KV_HEADS, HEAD), k_gain), places)
        v_heads = plain_norm(v_input.reshape(row_count, KV_HEADS, HEAD))
        return (q_heads, k_heads, v_heads)

    (queries, keys_new, values_new), prepare_back = jax.vjp(
        prepare, query_raw, kv_raw[:, :key_cols], kv_raw[:, key_cols:], head_gain[0], head_gain[1]
    )
    query_low = queries.astype(BF16)
    kv_own = jnp.concatenate(
        [
            keys_new.reshape(row_count, key_cols).astype(BF16),
            values_new.reshape(row_count, key_cols).astype(BF16),
        ],
        1,
    )

    mid = chips // 2
    chain = [(i, i + 1) for i in range(mid - 1)] + [(mid - 1, mid + 1)]
    kv_before = jnp.where(
        chip == mid,
        lax.ppermute(kv_own, "zy", [(mid - 1, mid)]),
        lax.ppermute(kv_own, "zy", chain),
    )
    spans = []
    span = 2
    while span < mid:
        spans.append(span)
        span *= 2
    for span in spans:
        moved = lax.ppermute(
            kv_before, "zy", [(mid + i, mid + i + span) for i in range(min(span, mid - span))]
        )
        fresh = jnp.logical_and(chip >= mid + span, chip < mid + 2 * span)
        kv_before = jnp.where(fresh, moved, kv_before)
    kv_other = swap(jnp.where(core == 0, kv_own, kv_before), "core")
    keys_all = jnp.concatenate([kv_before, kv_other, kv_own], 0)
    key_len = keys_all.shape[0]
    key_places = first_place - 2 * row_count + jnp.arange(key_len, dtype=jnp.int32)
    visible = (
        (key_places[None, :] <= places[:, None])
        & (places[:, None] - key_places[None, :] < WINDOW)
        & (key_places[None, :] >= 0)
    )
    group_heads = HEADS // KV_HEADS
    query_grouped = query_low.reshape(row_count, KV_HEADS, group_heads, HEAD)
    key_heads = keys_all[:, :key_cols].reshape(key_len, KV_HEADS, HEAD)
    value_heads = keys_all[:, key_cols:].reshape(key_len, KV_HEADS, HEAD)

    def masked_scores():
        scores = jnp.einsum(
            "qgjd,kgd->gjqk", query_grouped, key_heads, preferred_element_type=F32
        )
        return jnp.where(visible, scores, -1e30)

    scores_fwd = masked_scores()
    top_score = jnp.max(scores_fwd, axis=-1, keepdims=True)
    expo = jnp.exp(scores_fwd - top_score)
    totals = jnp.sum(expo, axis=-1, keepdims=True)
    probs = expo / totals
    log_total = top_score + jnp.log(totals)
    probs_low = probs.astype(BF16)
    context = jnp.einsum("gjqk,kgd->qgjd", probs_low, value_heads, preferred_element_type=F32)
    context_low = context.reshape(row_count, HEADS * HEAD).astype(BF16)
    attn_raw = full_dot(context_low, wo)
    attn_out = rms_norm(attn_raw, gains[1])
    laurel_mid = full_dot(normed_low, lleft).astype(BF16)
    laurel_raw = full_dot(laurel_mid, lright)
    mixed = (states + attn_out + normed + rms_norm(laurel_raw, gains[2])) * INV_SQRT2
    ffn_in = rms_norm(mixed, gains[3]).astype(BF16)

    ffn_rows = rows_of_four(ffn_in)
    gates, uppers, hiddens = [], [], []
    running = None
    for weights in part_weights:
        gate = right_dot(ffn_rows, weights[0])
        upper = right_dot(ffn_rows, weights[1])
        hidden = gated_product(gate, upper).astype(BF16)
        term = full_dot(hidden, weights[2])
        running = term if running is None else running + term
        gates.append(gate)
        uppers.append(upper)
        hiddens.append(hidden)
    down_out = sum_of_four(running)
    after_ffn = mixed + rms_norm(down_out, gains[4])
    after_low = after_ffn.astype(BF16)
    pl_raw = full_dot(after_low, plg)
    pl_act = gelu_tanh(pl_raw)
    pl_mid = (pl_act * layer_in).astype(BF16)
    pl_out = full_dot(pl_mid, plp)
    result = after_ffn + rms_norm(pl_out, gains[5])
    errors = result - target
    squares = jnp.sum(weight_mask[:, None] * errors * errors)

    grad_out = weight_mask[:, None] * errors * (total_slots / count)
    unused, pl_norm_back = jax.vjp(rms_norm, pl_out, gains[5])
    grad_pl_out, grad_g5 = pl_norm_back(grad_out)
    grad_pl_low = grad_pl_out.astype(BF16)
    grad_plp = left_dot(pl_mid, grad_pl_low)
    grad_pl_mid = right_dot(grad_pl_low, plp)
    grad_layer_in = grad_pl_mid * pl_act
    unused, gelu_back = jax.vjp(gelu_tanh, pl_raw)
    grad_pl_raw = gelu_back(grad_pl_mid * layer_in)[0].astype(BF16)
    grad_plg = left_dot(after_low, grad_pl_raw)
    grad_after = grad_out + right_dot(grad_pl_raw, plg)
    unused, down_norm_back = jax.vjp(rms_norm, down_out, gains[4])
    grad_down, grad_g4 = down_norm_back(grad_after)
    grad_down_low = grad_down.astype(BF16)

    grad_down_rows = rows_of_four(grad_down_low)
    grad_gates, grad_uppers = [], []
    running = None
    for weights, gate, upper in zip(part_weights, gates, uppers):
        unused, act_back = jax.vjp(gated_product, gate, upper)
        grad_gate, grad_upper = act_back(right_dot(grad_down_rows, weights[2]))
        grad_gates.append(grad_gate.astype(BF16))
        grad_uppers.append(grad_upper.astype(BF16))
        term = full_dot(grad_gates[-1], weights[0]) + full_dot(grad_uppers[-1], weights[1])
        running = term if running is None else running + term
    grad_ffn_in = sum_of_four(running)

    def unit_grads(k):
        for part, gg, gu, hid in zip(parts, grad_gates, grad_uppers, hiddens):
            if k in part:
                at = (k - part[0]) * units
                cut = slice(at, at + units)
                return [
                    left_dot(gg[:, cut], ffn_rows),
                    left_dot(gu[:, cut], ffn_rows),
                    left_dot(hid[:, cut], grad_down_rows),
                ]

    up_sums, down_sums = None, None
    for k in list(range(1, chips)) + [0]:
        terms = unit_grads(k)
        if up_sums is None:
            up_sums = [t[:half] for t in terms]
            down_sums = [t[half:] for t in terms]
        else:
            up_sums = [
                ring(s.astype(BF16), 1).astype(F32) + t[:half] for s, t in zip(up_sums, terms)
            ]
            down_sums = [
                ring(s.astype(BF16), -1).astype(F32) + t[half:] for s, t in zip(down_sums, terms)
            ]
    grad_ffn = jnp.stack(
        [jnp.concatenate([a, b], 0) for a, b in zip(up_sums, down_sums)], 1
    )

    unused, mix_norm_back = jax.vjp(rms_norm, mixed, gains[3])
    grad_mixed_norm, grad_g3 = mix_norm_back(grad_ffn_in)
    grad_scaled = (grad_after + grad_mixed_norm) * INV_SQRT2
    unused, laurel_norm_back = jax.vjp(rms_norm, laurel_raw, gains[2])
    grad_laurel, grad_g2 = laurel_norm_back(grad_scaled)
    grad_laurel_low = grad_laurel.astype(BF16)
    grad_lright_t = left_dot(grad_laurel_low, laurel_mid)
    grad_mid_low = right_dot(grad_laurel_low, lright).astype(BF16)
    grad_lleft = left_dot(normed_low, grad_mid_low)
    unused, attn_norm_back = jax.vjp(rms_norm, attn_raw, gains[1])
    grad_attn, grad_g1 = attn_norm_back(grad_scaled)
    grad_attn_low = grad_attn.astype(BF16)
    grad_wo = left_dot(context_low, grad_attn_low)
    grad_context = (
        right_dot(grad_attn_low, wo).astype(BF16).reshape(row_count, KV_HEADS, group_heads, HEAD)
    )
    probs_again = jnp.exp(masked_scores() - log_total)
    grad_probs = jnp.einsum(
        "qgjd,kgd->gjqk", grad_context, value_heads, preferred_element_type=F32
    )
    grad_scores = (
        probs_again * (grad_probs - jnp.sum(probs_again * grad_probs, axis=-1, keepdims=True))
    ).astype(BF16)
    grad_queries = jnp.einsum("gjqk,kgd->qgjd", grad_scores, key_heads, preferred_element_type=F32)
    grad_keys = jnp.einsum(
        "gjqk,qgjd->kgd", grad_scores, query_grouped, preferred_element_type=F32
    )
    grad_values = jnp.einsum(
        "gjqk,qgjd->kgd", probs_again.astype(BF16), grad_context, preferred_element_type=F32
    )
    grad_kv = jnp.concatenate(
        [grad_keys.reshape(key_len, key_cols), grad_values.reshape(key_len, key_cols)], 1
    )
    grad_before = grad_kv[:row_count]
    grad_own = grad_kv[2 * row_count :]
    returned = swap(grad_kv[row_count : 2 * row_count].astype(BF16), "core").astype(F32)
    grad_own = grad_own + jnp.where(core == 0, returned, 0.0)
    grad_before = grad_before + jnp.where(core == 0, 0.0, returned)
    for span in reversed(spans):
        back = [(mid + i + span, mid + i) for i in range(min(span, mid - span))]
        grad_before = grad_before + lax.ppermute(grad_before.astype(BF16), "zy", back).astype(F32)
    before_low = grad_before.astype(BF16)
    grad_own = (
        grad_own
        + lax.ppermute(before_low, "zy", [(b, a) for a, b in chain]).astype(F32)
        + lax.ppermute(before_low, "zy", [(mid, mid - 1)]).astype(F32)
    )
    grad_query_raw, grad_key_raw, grad_value_raw, grad_hq, grad_hk = prepare_back(
        (
            grad_queries.reshape(row_count, HEADS, HEAD),
            grad_own[:, :key_cols].reshape(row_count, KV_HEADS, HEAD),
            grad_own[:, key_cols:].reshape(row_count, KV_HEADS, HEAD),
        )
    )
    grad_query_low = grad_query_raw.astype(BF16)
    grad_kv_low = jnp.concatenate([grad_key_raw, grad_value_raw], 1).astype(BF16)
    grad_wq = left_dot(normed_low, grad_query_low)
    grad_wkv = left_dot(normed_low, grad_kv_low)
    grad_normed = (
        grad_scaled
        + right_dot(grad_mid_low, lleft)
        + right_dot(grad_query_low, wq)
        + right_dot(grad_kv_low, wkv)
    )
    unused, input_norm_back = jax.vjp(rms_norm, states, gains[0])
    grad_states, grad_g0 = input_norm_back(grad_normed)
    grad_tokens = grad_scaled + grad_states

    def scatter_sum(full):
        cols = full.shape[1]
        blocks = full.reshape(chips, 2, group_count, shard_rows, cols)
        mine = lax.dynamic_index_in_dim(blocks, core, 1, keepdims=False)
        other = lax.dynamic_index_in_dim(blocks, 1 - core, 1, keepdims=False)
        blocks = mine + swap(other.astype(BF16), "core").astype(F32)
        mine = lax.dynamic_index_in_dim(blocks, group_index, 1, keepdims=False)
        other = lax.dynamic_index_in_dim(blocks, 1 - group_index, 1, keepdims=False)
        blocks = mine + swap(other.astype(BF16), "fsdp").astype(F32)
        mid_row = shard_rows // 2
        up_sum, down_sum = None, None
        for k in list(range(1, chips)) + [0]:
            up_term = lax.dynamic_index_in_dim(blocks, ring_owner(-k), 0, False)[:mid_row]
            down_term = lax.dynamic_index_in_dim(blocks, ring_owner(k), 0, False)[mid_row:]
            if up_sum is None:
                up_sum, down_sum = up_term, down_term
            else:
                up_sum = ring(up_sum.astype(BF16), 1).astype(F32) + up_term
                down_sum = ring(down_sum.astype(BF16), -1).astype(F32) + down_term
        return jnp.concatenate([up_sum, down_sum], 0)

    head_back = jnp.stack([grad_hq, grad_hk]).reshape(2, shards, head_n).transpose(1, 0, 2)
    head_back = head_back.reshape(shards, 2 * head_n)
    head_back = jnp.pad(head_back, ((0, 0), (0, shard_rows - 2 * head_n))).reshape(-1, 1)
    gains_back = jnp.stack([grad_g0, grad_g1, grad_g2, grad_g3, grad_g4, grad_g5], 1)
    misc_back = jnp.concatenate(
        [gains_back, head_back, jnp.zeros((D, misc_cols - 7), F32)], 1
    )
    sums_b = scatter_sum(
        jnp.concatenate(
            [grad_wo, grad_plg, grad_plp.reshape(D, proj_cols), grad_lright_t], 1
        )
    )
    sums_a = scatter_sum(jnp.concatenate([grad_wq, grad_wkv, grad_lleft, misc_back], 1))

    total = jnp.broadcast_to(squares, (8, 128))
    total = total + swap(total, "core")
    total = total + swap(total, "fsdp")
    span = 1
    while span < chips:
        total = total + lax.ppermute(total, "zy", [(i, i ^ span) for i in range(chips)])
        span *= 2
    match_loss = total[0, 0] / (2.0 * D * count)

    misc_out = sums_a[:, D + 2 * key_cols + RANK :]
    return (
        result[None],
        match_loss,
        grad_tokens[None],
        grad_layer_in[None],
        sums_a[:, :D],
        sums_a[:, D : D + 2 * key_cols],
        sums_b[:, :D],
        sums_a[:, D + 2 * key_cols : D + 2 * key_cols + RANK],
        sums_b[:, D + PLD + proj_cols :].T,
        sums_b[:, D : D + PLD],
        sums_b[:, D + PLD : D + PLD + proj_cols].reshape(pl_proj.shape),
        misc_out[:, :6].T,
        misc_out[: 2 * head_n, 6].reshape(2, head_n),
        grad_ffn,
    )


def solution(mesh):
    seq, fsdp = mesh.shape["seq"], mesh.shape["fsdp"]
    fine = Mesh(mesh.devices.reshape(seq // 2, 2, fsdp), ("zy", "core", "fsdp"))
    rows = P("fsdp", ("zy", "core"), None)
    split = ("zy", "core", "fsdp")
    weights = (
        P(split, None),
        P(split, None),
        P(split, None),
        P(split, None),
        P(None, split),
        P(split, None),
        P(split, None),
        P(None, split),
        P(None, split),
        P(split, None, None),
    )
    return jax.shard_map(
        body,
        mesh=fine,
        in_specs=(rows, rows, rows, P()) + weights,
        out_specs=(rows, P(), rows, rows) + weights,
        check_vma=False,
    )
```

time: 3710 us -> 1390 us (0.37)
  waiting for transfers between devices: 2930 us -> 478 us
  blocking collectives: 311 us -> 0 us
  starting transfers between devices: 8.65 us -> 248 us
  local copies, waits for them, and re-layouts: 61.8 us -> 208 us
  matrix products: 240 us -> 288 us
    reduce_scatter x9 -> x0, waiting for transfers between devices: 2240 us -> none  [the longest x1 908 us: body(): lax.psum_scatter(jnp.concatenate([gate_up_grad, down_grad[:, None]], 1),...]
    all_gather x8 -> x2, waiting for transfers between devices: 478 us -> 0.01 us  [the longest x1 0.01 us: body(): full_a = lax.all_gather(pack_a, all_axes, axis=0, tiled=True)]
    ppermute x4 -> x137, waiting for transfers between devices: 23.6 us -> 478 us  [the longest x112 326 us: ring(): return lax.ppermute(value, 'zy', ring_pairs(lax.axis_size('zy'), by))]
    all_gather x4 -> x0, blocking collectives: 271 us -> none  [the longest x1 69.7 us: body(): lax.all_gather(head_gains, ('seq', 'fsdp'), axis=1, tiled=True)]
    ppermute x4 -> x137, starting transfers between devices: 6.76 us -> 248 us  [the longest x112 219 us: ring(): return lax.ppermute(value, 'zy', ring_pairs(lax.axis_size('zy'), by))]
    unnamed x23 -> x2, waiting for transfers between devices: 107 us -> 0.03 us
    psum x2 -> x0, waiting for transfers between devices: 81.9 us -> none  [the longest x1 81.9 us: body(): tail_summed = lax.psum(tail_terms, 'seq')]
    dot_general x6 -> x31, matrix products: 33.4 us -> 92.2 us  [left_dot(): lax.dot_general(left, right, (((0,), (0,)), ((), ())), preferred_element_...]
  transfers between devices with their start and end apart: 25 -> 139, of which waited for: 19 -> 82; matrix products, arithmetic and copies ran while one was open for 7% -> 32% of each run, Pallas kernels for 0% -> 0%
where the time goes in v1:
time: 1390 us; the launch traced here: 1380 us
  waiting for transfers between devices  478 us (34%)
  matrix products  288 us (21%)
  starting transfers between devices  248 us (18%)
  local copies, waits for them, and re-layouts  208 us (15%)
  other arithmetic  142 us (10%)
  between operations  20.3 us (1%)
    ppermute x112, waiting for transfers between devices, ring(): return lax.ppermute(value, 'zy', ring_pairs(lax.axis_size('zy'), by))  326 us
    ppermute x112, starting transfers between devices, ring(): return lax.ppermute(value, 'zy', ring_pairs(lax.axis_size('zy'), by))  219 us
    ppermute x16, waiting for transfers between devices, swap(): return lax.ppermute(value, axis, [(0, 1), (1, 0)])  149 us
    dot_general x19, matrix products, full_dot(): return jnp.dot(left, right, preferred_element_type=F32)  99.7 us
    dot_general x31, matrix products, left_dot(): lax.dot_general(left, right, (((0,), (0,)), ((), ())), preferred_element_...  92.2 us
    dot_general x19, matrix products, right_dot(): lax.dot_general(left, right, (((1,), (1,)), ((), ())), preferred_element_...  75.2 us
    unnamed x476, local copies, waits for them, and re-layouts  55.6 us
    concatenate x8, local copies, waits for them, and re-layouts, body(): jnp.concatenate([grad_wq, grad_wkv, grad_lleft, misc_back], 1)  44.4 us
  transfers between devices with their start and end apart: 139, of which 82 were waited for; matrix products, arithmetic and copies ran while one was open for 32% of the time, Pallas kernels for 0%

profile of v1, /device:TPU:0, one launch (start us, length us, event | category | flops | bytes accessed | tf_op | source)
XLA Modules:
  0.0 1384.1 jit_solution(10379318700648605663)
XLA Ops:
  32.2 9.4 collective-permute-done.6
  47.9 8.4 collective-permute-done.12
  65.0 13.6 collective-permute-done.18
  78.6 5.4 collective-permute-start.15
  86.8 6.3 collective-permute-done.8
  98.8 16.7 %collective-permute-done.14 = bf16[128,2048]{1,0:T(8,128)(2,1)S(1)} collective-permute-done((bf16[128,2048]{1,0:T(8,128)(2,1)}, bf16[128,2048]{1,0:T(8,128)(2,1)S(1)}, u32[]{:S(2)}, u32[]{:S(2)}) %collective-permute-start.14) | collective-permute-done | bytes 524320 | tf_op jit(solution)/shard_map/ppermute | solution.py:75
  115.6 12.8 collective-permute-start.11
  132.4 5.6 collective-permute-done.20
  138.0 14.8 %collective-permute-start.17 = (bf16[128,2048]{1,0:T(8,128)(2,1)S(1)}, bf16[128,2048]{1,0:T(8,128)(2,1)S(1)}, u32[]{:S(2)}, u32[]{:S(2)}) collective-permute-start(bf16[128,2048]{1,0:T(8,128)(2,1)S(1)} %collective-permute-done.15), channel_id=1, source_target_pairs={{0,4},{8,0},{16,8},{24,16},{28,24},{20,28},{12,20},{4,12},{1,5},{9... | collective-permute-start | bytes 1572872 | tf_op jit(solution)/shard_map/ppermute | solution.py:75
  154.6 5.8 collective-permute-done.10
  166.6 6.3 collective-permute-done.16
  177.9 10.5 collective-permute-done.22
  193.8 9.0 collective-permute-done.24
  207.3 17.9 %collective-permute-done.28 = bf16[128,2048]{1,0:T(8,128)(2,1)S(1)} collective-permute-done((bf16[128,2048]{1,0:T(8,128)(2,1)S(1)}, bf16[128,2048]{1,0:T(8,128)(2,1)S(1)}, u32[]{:S(2)}, u32[]{:S(2)}) %collective-permute-start.28) | collective-permute-done | bytes 524320 | tf_op jit(solution)/shard_map/ppermute | solution.py:75
  225.2 5.7 collective-permute-start.27
  232.6 7.4 collective-permute-done.32
  245.3 16.8 %collective-permute-done.26 = bf16[128,2048]{1,0:T(8,128)(2,1)} collective-permute-done((bf16[128,2048]{1,0:T(8,128)(2,1)S(1)}, bf16[128,2048]{1,0:T(8,128)(2,1)}, u32[]{:S(2)}, u32[]{:S(2)}) %collective-permute-start.26) | collective-permute-done | bytes 524320 | tf_op jit(solution)/shard_map/ppermute | solution.py:75
  262.1 11.5 collective-permute-start.35
  276.3 8.3 collective-permute-done.30
  286.4 8.0 collective-permute-done.31
  320.3 8.4 slice_bitcast_fusion
  328.7 12.3 copy.189
  341.0 5.9 multiply_reduce_fusion.17
  388.6 8.1 collective-permute-start.40
  402.6 7.4 collective-permute-done.4
  410.7 7.9 collective-permute-start.44
  431.2 7.1 collective-permute-start.47
  442.4 10.2 collective-permute-done.47
  465.6 6.0 multiply_convert_fusion.3
  472.6 5.9 fusion.307
  478.5 6.8 multiply_convert_fusion.1
  485.4 6.7 fusion.305
  498.3 8.0 add_add_fusion.1
  523.8 16.3 %collective-permute-done.49 = bf16[256,2048]{1,0:T(8,128)(2,1)} collective-permute-done((bf16[256,2048]{1,0:T(8,128)(2,1)}, bf16[256,2048]{1,0:T(8,128)(2,1)}, u32[]{:S(2)}, u32[]{:S(2)}) %collective-permute-start.49) | collective-permute-done | bytes 1048608 | tf_op jit(solution)/shard_map/ppermute | solution.py:79
  561.3 22.9 %collective-permute-done.55 = bf16[256,2048]{1,0:T(8,128)(2,1)S(1)} collective-permute-done((bf16[256,2048]{1,0:T(8,128)(2,1)S(1)}, bf16[256,2048]{1,0:T(8,128)(2,1)S(1)}, u32[]{:S(2)}, u32[]{:S(2)}) %collective-permute-start.55) | collective-permute-done | bytes 1048608 | tf_op jit(solution)/shard_map/ppermute | solution.py:79
  606.7 6.2 collective-permute-start.54
  619.9 12.4 multiply_convert_fusion
  666.8 7.0 fusion.312
  673.8 7.2 fusion.311
  681.1 7.3 fusion.314
  688.4 5.6 fusion.313
  759.3 21.2 %add_add_fusion = f32[1024,2048]{1,0:T(8,128)} fusion(f32[1024,2048]{1,0:T(8,128)} %fusion.317, f32[1024,2048]{1,0:T(8,128)} %fusion.315, f32[1024,2048]{1,0:T(8,128)S(1)} %fusion.316, f32[1024,2048]{1,0:T(8,128)} %fusion.313, f32[1024,2048]{1,0:T(8,128)} %fusion.314, f32[1024,2048]{1,0:T(8,128)} %fusion.311, f32[1024,2048]{1,0:T(8,128)} %fusion.312, ...), kind=kOutput, calls=%fused_computation.5 | convolution fusion | flops 1088421888 | bytes 68681728 | tf_op jit(solution)/shard_map/dot_general | solution.py:54
  795.0 7.0 collective-permute-done.130
  804.2 9.0 collective-permute-done.103
  817.6 6.8 collective-permute-done.117
  829.1 6.6 collective-permute-done.131
  836.8 10.0 collective-permute-done.104
  851.4 6.8 collective-permute-done.118
  862.8 6.6 collective-permute-done.132
  870.6 10.0 collective-permute-done.105
  896.5 6.6 collective-permute-done.133
  920.1 7.4 fusion.7
  927.5 5.5 fusion.26
  956.6 10.3 pad_maximum_fusion
  967.0 7.3 fusion.4
  975.7 8.1 fusion.319
  994.7 7.3 fusion.11
  1028.5 5.5 fusion.178
  1037.4 31.6 %concatenate.159 = f32[8,2,2,64,3200]{4,3,2,1,0:T(8,128)} concatenate(f32[8,2,2,64,2048]{4,3,2,1,0:T(8,128)} %fusion.319, f32[8,2,2,64,1024]{4,3,2,1,0:T(8,128)} %fusion.178, f32[8,2,2,64,64]{4,3,2,1,0:T(8,128)} %fusion.259, f32[8,2,2,64,1]{4,3,2,1,0:T(8,128)} %concatenate.169, f32[8,2,2,64,1]{4,3,2,1,0:T(8,128)} %concatenate.170, f32[8,2,2,64,1]{4,3,2,1,0:T(8,128)} %concatenate.171, ...), dimensions={4} | concatenate | bytes 52428800 | tf_op jit(solution)/shard_map/concatenate | solution.py:472
  1069.0 8.5 fusion.6
  1155.5 11.1 bitcast_add_fusion.1
  1174.3 8.1 bitcast_add_fusion
  1185.3 48.6 %collective-permute-done.80 = bf16[8,64,2624]{2,1,0:T(8,128)(2,1)} collective-permute-done((bf16[8,64,2624]{2,1,0:T(8,128)(2,1)}, bf16[8,64,2624]{2,1,0:T(8,128)(2,1)}, u32[]{:S(2)}, u32[]{:S(2)}) %collective-permute-start.80) | collective-permute-done | bytes 2687008 | tf_op jit(solution)/shard_map/ppermute | solution.py:79
  1258.0 44.8 %collective-permute-done.64 = bf16[8,64,3200]{2,1,0:T(8,128)(2,1)} collective-permute-done((bf16[8,64,3200]{2,1,0:T(8,128)(2,1)}, bf16[8,64,3200]{2,1,0:T(8,128)(2,1)}, u32[]{:S(2)}, u32[]{:S(2)}) %collective-permute-start.64) | collective-permute-done | bytes 3276832 | tf_op jit(solution)/shard_map/ppermute | solution.py:79
  (1002 shorter events, 683.6 us)
Async XLA Ops:
  7.2 289.0 %all-gather.3.cloned.1.call-start = ((), (), s32[]{:S(2)}) async-start(), calls=%async_computation | async-start | bytes 13516800 | tf_op jit(solution)/shard_map/all_gather | solution.py:173
  10.7 346.6 %all-gather.5.cloned.1.call-start = ((), (), s32[]{:S(2)}) async-start(), calls=%async_computation.1 | async-start | bytes 11354112 | tf_op jit(solution)/shard_map/all_gather | solution.py:174
  17.2 24.4 %collective-permute-start.6 = (bf16[128,2048]{1,0:T(8,128)(2,1)}, bf16[128,2048]{1,0:T(8,128)(2,1)}, u32[]{:S(2)}, u32[]{:S(2)}) collective-permute-start(bf16[128,2048]{1,0:T(8,128)(2,1)} %get-tuple-element.161), channel_id=1, source_target_pairs={{0,8},{8,16},{16,24},{24,28},{28,20},{20,12},{12,4},{4,0},{1,9},{9... | collective-permute-start | bytes 1572872 | tf_op jit(solution)/shard_map/ppermute | solution.py:75
  20.2 25.8 %collective-permute-start.7 = (bf16[128,2048]{1,0:T(8,128)(2,1)}, bf16[128,2048]{1,0:T(8,128)(2,1)}, u32[]{:S(2)}, u32[]{:S(2)}) collective-permute-start(bf16[128,2048]{1,0:T(8,128)(2,1)} %get-tuple-element.160), channel_id=1, source_target_pairs={{0,4},{8,0},{16,8},{24,16},{28,24},{20,28},{12,20},{4,12},{1,5},{9... | collective-permute-start | bytes 1572872 | tf_op jit(solution)/shard_map/ppermute | solution.py:75
  20.2 36.1 %collective-permute-start.12 = (bf16[128,2048]{1,0:T(8,128)(2,1)}, bf16[128,2048]{1,0:T(8,128)(2,1)}, u32[]{:S(2)}, u32[]{:S(2)}) collective-permute-start(bf16[128,2048]{1,0:T(8,128)(2,1)} %get-tuple-element.159), channel_id=1, source_target_pairs={{0,8},{8,16},{16,24},{24,28},{28,20},{20,12},{12,4},{4,0},{1,9},{9... | collective-permute-start | bytes 1572872 | tf_op jit(solution)/shard_map/ppermute | solution.py:75
  22.2 40.9 %collective-permute-start.13 = (bf16[128,2048]{1,0:T(8,128)(2,1)S(1)}, bf16[128,2048]{1,0:T(8,128)(2,1)}, u32[]{:S(2)}, u32[]{:S(2)}) collective-permute-start(bf16[128,2048]{1,0:T(8,128)(2,1)S(1)} %get-tuple-element.158), channel_id=1, source_target_pairs={{0,4},{8,0},{16,8},{24,16},{28,24},{20,28},{12,20},{4,12},{1,5},{9... | collective-permute-start | bytes 1572872 | tf_op jit(solution)/shard_map/ppermute | solution.py:75
  22.2 56.4 %collective-permute-start.18 = (bf16[128,2048]{1,0:T(8,128)(2,1)S(1)}, bf16[128,2048]{1,0:T(8,128)(2,1)}, u32[]{:S(2)}, u32[]{:S(2)}) collective-permute-start(bf16[128,2048]{1,0:T(8,128)(2,1)S(1)} %get-tuple-element.162), channel_id=1, source_target_pairs={{0,8},{8,16},{16,24},{24,28},{28,20},{20,12},{12,4},{4,0},{1,9},{9... | collective-permute-start | bytes 1572872 | tf_op jit(solution)/shard_map/ppermute | solution.py:75
  41.6 44.3 %collective-permute-start.19 = (bf16[128,2048]{1,0:T(8,128)(2,1)S(1)}, bf16[128,2048]{1,0:T(8,128)(2,1)S(1)}, u32[]{:S(2)}, u32[]{:S(2)}) collective-permute-start(bf16[128,2048]{1,0:T(8,128)(2,1)S(1)} %get-tuple-element.157), channel_id=1, source_target_pairs={{0,4},{8,0},{16,8},{24,16},{28,24},{20,28},{12,20},{4,12},{1,5},{9... | collective-permute-start | bytes 1572872 | tf_op jit(solution)/shard_map/ppermute | solution.py:75
  46.0 47.1 %collective-permute-start.8 = (bf16[128,2048]{1,0:T(8,128)(2,1)}, bf16[128,2048]{1,0:T(8,128)(2,1)S(1)}, u32[]{:S(2)}, u32[]{:S(2)}) collective-permute-start(bf16[128,2048]{1,0:T(8,128)(2,1)} %collective-permute-done.6), channel_id=1, source_target_pairs={{0,8},{8,16},{16,24},{24,28},{28,20},{20,12},{12,4},{4,0},{1,9},{9... | collective-permute-start | bytes 1572872 | tf_op jit(solution)/shard_map/ppermute | solution.py:75
  56.2 39.9 %collective-permute-start.9 = (bf16[128,2048]{1,0:T(8,128)(2,1)}, bf16[128,2048]{1,0:T(8,128)(2,1)S(1)}, u32[]{:S(2)}, u32[]{:S(2)}) collective-permute-start(bf16[128,2048]{1,0:T(8,128)(2,1)} %collective-permute-done.7), channel_id=1, source_target_pairs={{0,4},{8,0},{16,8},{24,16},{28,24},{20,28},{12,20},{4,12},{1,5},{9... | collective-permute-start | bytes 1572872 | tf_op jit(solution)/shard_map/ppermute | solution.py:75
  63.1 52.5 %collective-permute-start.14 = (bf16[128,2048]{1,0:T(8,128)(2,1)}, bf16[128,2048]{1,0:T(8,128)(2,1)S(1)}, u32[]{:S(2)}, u32[]{:S(2)}) collective-permute-start(bf16[128,2048]{1,0:T(8,128)(2,1)} %collective-permute-done.12), channel_id=1, source_target_pairs={{0,8},{8,16},{16,24},{24,28},{28,20},{20,12},{12,4},{4,0},{1,9},{9... | collective-permute-start | bytes 1572872 | tf_op jit(solution)/shard_map/ppermute | solution.py:75
  78.6 53.0 %collective-permute-start.15 = (bf16[128,2048]{1,0:T(8,128)(2,1)}, bf16[128,2048]{1,0:T(8,128)(2,1)S(1)}, u32[]{:S(2)}, u32[]{:S(2)}) collective-permute-start(bf16[128,2048]{1,0:T(8,128)(2,1)} %collective-permute-done.13), channel_id=1, source_target_pairs={{0,4},{8,0},{16,8},{24,16},{28,24},{20,28},{12,20},{4,12},{1,5},{9... | collective-permute-start | bytes 1572872 | tf_op jit(solution)/shard_map/ppermute | solution.py:75
  85.9 52.1 %collective-permute-start.20 = (bf16[128,2048]{1,0:T(8,128)(2,1)}, bf16[128,2048]{1,0:T(8,128)(2,1)S(1)}, u32[]{:S(2)}, u32[]{:S(2)}) collective-permute-start(bf16[128,2048]{1,0:T(8,128)(2,1)} %collective-permute-done.18), channel_id=1, source_target_pairs={{0,8},{8,16},{16,24},{24,28},{28,20},{20,12},{12,4},{4,0},{1,9},{9... | collective-permute-start | bytes 1572872 | tf_op jit(solution)/shard_map/ppermute | solution.py:75
  93.1 60.6 %collective-permute-start.21 = (bf16[128,2048]{1,0:T(8,128)(2,1)S(1)}, bf16[128,2048]{1,0:T(8,128)(2,1)S(1)}, u32[]{:S(2)}, u32[]{:S(2)}) collective-permute-start(bf16[128,2048]{1,0:T(8,128)(2,1)S(1)} %collective-permute-done.19), channel_id=1, source_target_pairs={{0,4},{8,0},{16,8},{24,16},{28,24},{20,28},{12,20},{4,12},{1,5},{9... | collective-permute-start | bytes 1572872 | tf_op jit(solution)/shard_map/ppermute | solution.py:75
  96.2 64.2 %collective-permute-start.10 = (bf16[128,2048]{1,0:T(8,128)(2,1)S(1)}, bf16[128,2048]{1,0:T(8,128)(2,1)S(1)}, u32[]{:S(2)}, u32[]{:S(2)}) collective-permute-start(bf16[128,2048]{1,0:T(8,128)(2,1)S(1)} %collective-permute-done.8), channel_id=1, source_target_pairs={{0,8},{8,16},{16,24},{24,28},{28,20},{20,12},{12,4},{4,0},{1,9},{9... | collective-permute-start | bytes 1572872 | tf_op jit(solution)/shard_map/ppermute | solution.py:75
  115.6 49.4 %collective-permute-start.11 = (bf16[128,2048]{1,0:T(8,128)(2,1)S(1)}, bf16[128,2048]{1,0:T(8,128)(2,1)S(1)}, u32[]{:S(2)}, u32[]{:S(2)}) collective-permute-start(bf16[128,2048]{1,0:T(8,128)(2,1)S(1)} %collective-permute-done.9), channel_id=1, source_target_pairs={{0,4},{8,0},{16,8},{24,16},{28,24},{20,28},{12,20},{4,12},{1,5},{9... | collective-permute-start | bytes 1572872 | tf_op jit(solution)/shard_map/ppermute | solution.py:75
  131.6 41.4 %collective-permute-start.16 = (bf16[128,2048]{1,0:T(8,128)(2,1)S(1)}, bf16[128,2048]{1,0:T(8,128)(2,1)S(1)}, u32[]{:S(2)}, u32[]{:S(2)}) collective-permute-start(bf16[128,2048]{1,0:T(8,128)(2,1)S(1)} %collective-permute-done.14), channel_id=1, source_target_pairs={{0,8},{8,16},{16,24},{24,28},{28,20},{20,12},{12,4},{4,0},{1,9},{9... | collective-permute-start | bytes 1572872 | tf_op jit(solution)/shard_map/ppermute | solution.py:75
  138.0 38.2 %collective-permute-start.17 = (bf16[128,2048]{1,0:T(8,128)(2,1)S(1)}, bf16[128,2048]{1,0:T(8,128)(2,1)S(1)}, u32[]{:S(2)}, u32[]{:S(2)}) collective-permute-start(bf16[128,2048]{1,0:T(8,128)(2,1)S(1)} %collective-permute-done.15), channel_id=1, source_target_pairs={{0,4},{8,0},{16,8},{24,16},{28,24},{20,28},{12,20},{4,12},{1,5},{9... | collective-permute-start | bytes 1572872 | tf_op jit(solution)/shard_map/ppermute | solution.py:75
  153.7 34.7 %collective-permute-start.22 = (bf16[128,2048]{1,0:T(8,128)(2,1)S(1)}, bf16[128,2048]{1,0:T(8,128)(2,1)S(1)}, u32[]{:S(2)}, u32[]{:S(2)}) collective-permute-start(bf16[128,2048]{1,0:T(8,128)(2,1)S(1)} %collective-permute-done.20), channel_id=1, source_target_pairs={{0,8},{8,16},{16,24},{24,28},{28,20},{20,12},{12,4},{4,0},{1,9},{9... | collective-permute-start | bytes 1572872 | tf_op jit(solution)/shard_map/ppermute | solution.py:75
  160.4 31.2 %collective-permute-start.23 = (bf16[128,2048]{1,0:T(8,128)(2,1)S(1)}, bf16[128,2048]{1,0:T(8,128)(2,1)S(1)}, u32[]{:S(2)}, u32[]{:S(2)}) collective-permute-start(bf16[128,2048]{1,0:T(8,128)(2,1)S(1)} %collective-permute-done.21), channel_id=1, source_target_pairs={{0,4},{8,0},{16,8},{24,16},{28,24},{20,28},{12,20},{4,12},{1,5},{9... | collective-permute-start | bytes 1572872 | tf_op jit(solution)/shard_map/ppermute | solution.py:75
  165.0 37.8 %collective-permute-start.24 = (bf16[128,2048]{1,0:T(8,128)(2,1)S(1)}, bf16[128,2048]{1,0:T(8,128)(2,1)S(1)}, u32[]{:S(2)}, u32[]{:S(2)}) collective-permute-start(bf16[128,2048]{1,0:T(8,128)(2,1)S(1)} %collective-permute-done.10), channel_id=1, source_target_pairs={{0,8},{8,16},{16,24},{24,28},{28,20},{20,12},{12,4},{4,0},{1,9},{9... | collective-permute-start | bytes 1572872 | tf_op jit(solution)/shard_map/ppermute | solution.py:75
  172.9 32.7 %collective-permute-start.25 = (bf16[128,2048]{1,0:T(8,128)(2,1)S(1)}, bf16[128,2048]{1,0:T(8,128)(2,1)S(1)}, u32[]{:S(2)}, u32[]{:S(2)}) collective-permute-start(bf16[128,2048]{1,0:T(8,128)(2,1)S(1)} %collective-permute-done.11), channel_id=1, source_target_pairs={{0,4},{8,0},{16,8},{24,16},{28,24},{20,28},{12,20},{4,12},{1,5},{9... | collective-permute-start | bytes 1572872 | tf_op jit(solution)/shard_map/ppermute | solution.py:75
  176.2 49.0 %collective-permute-start.28 = (bf16[128,2048]{1,0:T(8,128)(2,1)S(1)}, bf16[128,2048]{1,0:T(8,128)(2,1)S(1)}, u32[]{:S(2)}, u32[]{:S(2)}) collective-permute-start(bf16[128,2048]{1,0:T(8,128)(2,1)S(1)} %collective-permute-done.16), channel_id=1, source_target_pairs={{0,8},{8,16},{16,24},{24,28},{28,20},{20,12},{12,4},{4,0},{1,9},{9... | collective-permute-start | bytes 1572872 | tf_op jit(solution)/shard_map/ppermute | solution.py:75
  188.4 43.4 %collective-permute-start.29 = (bf16[128,2048]{1,0:T(8,128)(2,1)S(1)}, bf16[128,2048]{1,0:T(8,128)(2,1)S(1)}, u32[]{:S(2)}, u32[]{:S(2)}) collective-permute-start(bf16[128,2048]{1,0:T(8,128)(2,1)S(1)} %collective-permute-done.17), channel_id=1, source_target_pairs={{0,4},{8,0},{16,8},{24,16},{28,24},{20,28},{12,20},{4,12},{1,5},{9... | collective-permute-start | bytes 1572872 | tf_op jit(solution)/shard_map/ppermute | solution.py:75
  191.6 48.4 %collective-permute-start.32 = (bf16[128,2048]{1,0:T(8,128)(2,1)S(1)}, bf16[128,2048]{1,0:T(8,128)(2,1)}, u32[]{:S(2)}, u32[]{:S(2)}) collective-permute-start(bf16[128,2048]{1,0:T(8,128)(2,1)S(1)} %collective-permute-done.22), channel_id=1, source_target_pairs={{0,8},{8,16},{16,24},{24,28},{28,20},{20,12},{12,4},{4,0},{1,9},{9... | collective-permute-start | bytes 1572872 | tf_op jit(solution)/shard_map/ppermute | solution.py:75
  202.8 40.8 %collective-permute-start.33 = (bf16[128,2048]{1,0:T(8,128)(2,1)S(1)}, bf16[128,2048]{1,0:T(8,128)(2,1)}, u32[]{:S(2)}, u32[]{:S(2)}) collective-permute-start(bf16[128,2048]{1,0:T(8,128)(2,1)S(1)} %collective-permute-done.23), channel_id=1, source_target_pairs={{0,4},{8,0},{16,8},{24,16},{28,24},{20,28},{12,20},{4,12},{1,5},{9... | collective-permute-start | bytes 1572872 | tf_op jit(solution)/shard_map/ppermute | solution.py:75
  205.6 56.4 %collective-permute-start.26 = (bf16[128,2048]{1,0:T(8,128)(2,1)S(1)}, bf16[128,2048]{1,0:T(8,128)(2,1)}, u32[]{:S(2)}, u32[]{:S(2)}) collective-permute-start(bf16[128,2048]{1,0:T(8,128)(2,1)S(1)} %collective-permute-done.24), channel_id=1, source_target_pairs={{0,8},{8,16},{16,24},{24,28},{28,20},{20,12},{12,4},{4,0},{1,9},{9... | collective-permute-start | bytes 1572872 | tf_op jit(solution)/shard_map/ppermute | solution.py:75
  225.2 50.8 %collective-permute-start.27 = (bf16[128,2048]{1,0:T(8,128)(2,1)S(1)}, bf16[128,2048]{1,0:T(8,128)(2,1)S(1)}, u32[]{:S(2)}, u32[]{:S(2)}) collective-permute-start(bf16[128,2048]{1,0:T(8,128)(2,1)S(1)} %collective-permute-done.25), channel_id=1, source_target_pairs={{0,4},{8,0},{16,8},{24,16},{28,24},{20,28},{12,20},{4,12},{1,5},{9... | collective-permute-start | bytes 1572872 | tf_op jit(solution)/shard_map/ppermute | solution.py:75
  231.8 52.8 %collective-permute-start.30 = (bf16[128,2048]{1,0:T(8,128)(2,1)S(1)}, bf16[128,2048]{1,0:T(8,128)(2,1)}, u32[]{:S(2)}, u32[]{:S(2)}) collective-permute-start(bf16[128,2048]{1,0:T(8,128)(2,1)S(1)} %collective-permute-done.28), channel_id=1, source_target_pairs={{0,8},{8,16},{16,24},{24,28},{28,20},{20,12},{12,4},{4,0},{1,9},{9... | collective-permute-start | bytes 1572872 | tf_op jit(solution)/shard_map/ppermute | solution.py:75
  240.0 54.5 %collective-permute-start.31 = (bf16[128,2048]{1,0:T(8,128)(2,1)S(1)}, bf16[128,2048]{1,0:T(8,128)(2,1)S(1)}, u32[]{:S(2)}, u32[]{:S(2)}) collective-permute-start(bf16[128,2048]{1,0:T(8,128)(2,1)S(1)} %collective-permute-done.29), channel_id=1, source_target_pairs={{0,4},{8,0},{16,8},{24,16},{28,24},{20,28},{12,20},{4,12},{1,5},{9... | collective-permute-start | bytes 1572872 | tf_op jit(solution)/shard_map/ppermute | solution.py:75
  243.6 141.1 %collective-permute-start.34 = (bf16[128,2048]{1,0:T(8,128)(2,1)}, bf16[128,2048]{1,0:T(8,128)(2,1)}, u32[]{:S(2)}, u32[]{:S(2)}) collective-permute-start(bf16[128,2048]{1,0:T(8,128)(2,1)} %collective-permute-done.32), channel_id=1, source_target_pairs={{0,8},{8,16},{16,24},{24,28},{28,20},{20,12},{12,4},{4,0},{1,9},{9... | collective-permute-start | bytes 1572872 | tf_op jit(solution)/shard_map/ppermute | solution.py:75
  262.1 125.3 %collective-permute-start.35 = (bf16[128,2048]{1,0:T(8,128)(2,1)}, bf16[128,2048]{1,0:T(8,128)(2,1)}, u32[]{:S(2)}, u32[]{:S(2)}) collective-permute-start(bf16[128,2048]{1,0:T(8,128)(2,1)} %collective-permute-done.33), channel_id=1, source_target_pairs={{0,4},{8,0},{16,8},{24,16},{28,24},{20,28},{12,20},{4,12},{1,5},{9... | collective-permute-start | bytes 1572872 | tf_op jit(solution)/shard_map/ppermute | solution.py:75
  276.0 112.6 %collective-permute-start.36 = (bf16[128,2048]{1,0:T(8,128)(2,1)}, bf16[128,2048]{1,0:T(8,128)(2,1)}, u32[]{:S(2)}, u32[]{:S(2)}) collective-permute-start(bf16[128,2048]{1,0:T(8,128)(2,1)} %collective-permute-done.26), channel_id=1, source_target_pairs={{0,8},{8,16},{16,24},{24,28},{28,20},{20,12},{12,4},{4,0},{1,9},{9... | collective-permute-start | bytes 1572872 | tf_op jit(solution)/shard_map/ppermute | solution.py:75
  314.2 33.6 %collective-permute-start = (bf16[256,1024]{1,0:T(8,128)(2,1)}, bf16[256,1024]{1,0:T(8,128)(2,1)}, u32[]{:S(2)}, u32[]{:S(2)}) collective-permute-start(bf16[256,1024]{1,0:T(8,128)(2,1)} %pad_maximum_fusion.10), channel_id=1, source_target_pairs={{12,16},{13,17},{14,18},{15,19}} | collective-permute-start | bytes 1572872 | tf_op jit(solution)/shard_map/ppermute | solution.py:243
  315.6 32.3 %collective-permute-start.1 = (bf16[256,1024]{1,0:T(8,128)(2,1)}, bf16[256,1024]{1,0:T(8,128)(2,1)}, u32[]{:S(2)}, u32[]{:S(2)}) collective-permute-start(bf16[256,1024]{1,0:T(8,128)(2,1)} %pad_maximum_fusion.10), channel_id=1, source_target_pairs={{0,4},{4,8},{8,12},{12,20},{1,5},{5,9},{9,13},{13,21},{2,6},{6,10}... | collective-permute-start | bytes 1572872 | tf_op jit(solution)/shard_map/ppermute | solution.py:244
  347.8 51.2 %collective-permute-start.37 = (bf16[128,2048]{1,0:T(8,128)(2,1)}, bf16[128,2048]{1,0:T(8,128)(2,1)}, u32[]{:S(2)}, u32[]{:S(2)}) collective-permute-start(bf16[128,2048]{1,0:T(8,128)(2,1)} %copy-done.123), channel_id=1, source_target_pairs={{0,4},{8,0},{16,8},{24,16},{28,24},{20,28},{12,20},{4,12},{1,5},{9... | collective-permute-start | bytes 1572872 | tf_op jit(solution)/shard_map/ppermute | solution.py:75
  360.2 37.7 %collective-permute-start.38 = (bf16[128,2048]{1,0:T(8,128)(2,1)}, bf16[128,2048]{1,0:T(8,128)(2,1)}, u32[]{:S(2)}, u32[]{:S(2)}) collective-permute-start(bf16[128,2048]{1,0:T(8,128)(2,1)} %collective-permute-done.30), channel_id=1, source_target_pairs={{0,8},{8,16},{16,24},{24,28},{28,20},{20,12},{12,4},{4,0},{1,9},{9... | collective-permute-start | bytes 1572872 | tf_op jit(solution)/shard_map/ppermute | solution.py:75
  384.7 25.3 %collective-permute-start.4 = (bf16[256,2048]{1,0:T(8,128)(2,1)S(1)}, bf16[256,2048]{1,0:T(8,128)(2,1)S(1)}, u32[]{:S(2)}, u32[]{:S(2)}) collective-permute-start(bf16[256,2048]{1,0:T(8,128)(2,1)S(1)} %multiply_convert_fusion.4), channel_id=1, source_target_pairs={{0,1},{1,0},{2,3},{3,2},{4,5},{5,4},{6,7},{7,6},{8,9},{9,8},{10,11... | collective-permute-start | bytes 3145736 | tf_op jit(solution)/shard_map/ppermute | solution.py:79
  410.0 32.1 %collective-permute-start.43 = (bf16[128,2048]{1,0:T(8,128)(2,1)}, bf16[128,2048]{1,0:T(8,128)(2,1)S(1)}, u32[]{:S(2)}, u32[]{:S(2)}) collective-permute-start(bf16[128,2048]{1,0:T(8,128)(2,1)} %collective-permute-done.37), channel_id=1, source_target_pairs={{0,4},{8,0},{16,8},{24,16},{28,24},{20,28},{12,20},{4,12},{1,5},{9... | collective-permute-start | bytes 1572872 | tf_op jit(solution)/shard_map/ppermute | solution.py:75
  410.6 42.1 %collective-permute-start.5 = (bf16[512,2048]{1,0:T(8,128)(2,1)S(1)}, bf16[512,2048]{1,0:T(8,128)(2,1)S(1)}, u32[]{:S(2)}, u32[]{:S(2)}) collective-permute-start(bf16[512,2048]{1,0:T(8,128)(2,1)S(1)} %pad_maximum_fusion.4), channel_id=1, source_target_pairs={{0,2},{2,0},{1,3},{3,1},{4,6},{6,4},{5,7},{7,5},{8,10},{10,8},{9,1... | collective-permute-start | bytes 6291464 | tf_op jit(solution)/shard_map/ppermute | solution.py:79
  514.6 25.5 %collective-permute-start.49 = (bf16[256,2048]{1,0:T(8,128)(2,1)}, bf16[256,2048]{1,0:T(8,128)(2,1)}, u32[]{:S(2)}, u32[]{:S(2)}) collective-permute-start(bf16[256,2048]{1,0:T(8,128)(2,1)} %slice.1209), channel_id=1, source_target_pairs={{0,1},{1,0},{2,3},{3,2},{4,5},{5,4},{6,7},{7,6},{8,9},{9,8},{10,11... | collective-permute-start | bytes 3145736 | tf_op jit(solution)/shard_map/ppermute | solution.py:79
  559.7 24.4 %collective-permute-start.55 = (bf16[256,2048]{1,0:T(8,128)(2,1)S(1)}, bf16[256,2048]{1,0:T(8,128)(2,1)S(1)}, u32[]{:S(2)}, u32[]{:S(2)}) collective-permute-start(bf16[256,2048]{1,0:T(8,128)(2,1)S(1)} %fusion.62), channel_id=1, source_target_pairs={{0,1},{1,0},{2,3},{3,2},{4,5},{5,4},{6,7},{7,6},{8,9},{9,8},{10,11... | collective-permute-start | bytes 3145736 | tf_op jit(solution)/shard_map/ppermute | solution.py:79
  585.8 34.0 %collective-permute-start.56 = (bf16[512,2048]{1,0:T(8,128)(2,1)}, bf16[512,2048]{1,0:T(8,128)(2,1)}, u32[]{:S(2)}, u32[]{:S(2)}) collective-permute-start(bf16[512,2048]{1,0:T(8,128)(2,1)} %pad_maximum_fusion.5), channel_id=1, source_target_pairs={{0,2},{2,0},{1,3},{3,1},{4,6},{6,4},{5,7},{7,5},{8,10},{10,8},{9,1... | collective-permute-start | bytes 6291464 | tf_op jit(solution)/shard_map/ppermute | solution.py:79
  720.4 67.2 %collective-permute-start.102 = (bf16[128,2048]{1,0:T(8,128)(2,1)}, bf16[128,2048]{1,0:T(8,128)(2,1)}, u32[]{:S(2)}, u32[]{:S(2)}) collective-permute-start(bf16[128,2048]{1,0:T(8,128)(2,1)} %get-tuple-element.220), channel_id=1, source_target_pairs={{0,4},{8,0},{16,8},{24,16},{28,24},{20,28},{12,20},{4,12},{1,5},{9... | collective-permute-start | bytes 1572872 | tf_op jit(solution)/shard_map/ppermute | solution.py:75
  720.7 67.3 %collective-permute-start.95 = (bf16[128,2048]{1,0:T(8,128)(2,1)}, bf16[128,2048]{1,0:T(8,128)(2,1)}, u32[]{:S(2)}, u32[]{:S(2)}) collective-permute-start(bf16[128,2048]{1,0:T(8,128)(2,1)} %get-tuple-element.219), channel_id=1, source_target_pairs={{0,8},{8,16},{16,24},{24,28},{28,20},{20,12},{12,4},{4,0},{1,9},{9... | collective-permute-start | bytes 1572872 | tf_op jit(solution)/shard_map/ppermute | solution.py:75
  726.2 63.6 %collective-permute-start.109 = (bf16[128,2048]{1,0:T(8,128)(2,1)}, bf16[128,2048]{1,0:T(8,128)(2,1)}, u32[]{:S(2)}, u32[]{:S(2)}) collective-permute-start(bf16[128,2048]{1,0:T(8,128)(2,1)} %get-tuple-element.221), channel_id=1, source_target_pairs={{0,8},{8,16},{16,24},{24,28},{28,20},{20,12},{12,4},{4,0},{1,9},{9... | collective-permute-start | bytes 1572872 | tf_op jit(solution)/shard_map/ppermute | solution.py:75
  727.9 62.2 %collective-permute-start.116 = (bf16[128,2048]{1,0:T(8,128)(2,1)}, bf16[128,2048]{1,0:T(8,128)(2,1)}, u32[]{:S(2)}, u32[]{:S(2)}) collective-permute-start(bf16[128,2048]{1,0:T(8,128)(2,1)} %get-tuple-element.222), channel_id=1, source_target_pairs={{0,4},{8,0},{16,8},{24,16},{28,24},{20,28},{12,20},{4,12},{1,5},{9... | collective-permute-start | bytes 1572872 | tf_op jit(solution)/shard_map/ppermute | solution.py:75
  732.2 61.2 %collective-permute-start.123 = (bf16[128,2048]{1,0:T(8,128)(2,1)}, bf16[128,2048]{1,0:T(8,128)(2,1)}, u32[]{:S(2)}, u32[]{:S(2)}) collective-permute-start(bf16[128,2048]{1,0:T(8,128)(2,1)} %get-tuple-element.223), channel_id=1, source_target_pairs={{0,8},{8,16},{16,24},{24,28},{28,20},{20,12},{12,4},{4,0},{1,9},{9... | collective-permute-start | bytes 1572872 | tf_op jit(solution)/shard_map/ppermute | solution.py:75
  788.0 95.9 %collective-permute-start.57 = (bf16[512,2048]{1,0:T(8,128)(2,1)S(1)}, bf16[512,2048]{1,0:T(8,128)(2,1)S(1)}, u32[]{:S(2)}, u32[]{:S(2)}) collective-permute-start(bf16[512,2048]{1,0:T(8,128)(2,1)S(1)} %slice.1206), channel_id=1, source_target_pairs={{0,2},{2,0},{1,3},{3,1},{4,6},{6,4},{5,7},{7,5},{8,10},{10,8},{9,1... | collective-permute-start | bytes 6291464 | tf_op jit(solution)/shard_map/ppermute | solution.py:79
  816.1 30.8 %collective-permute-start.104 = (bf16[128,2048]{1,0:T(8,128)(2,1)S(1)}, bf16[128,2048]{1,0:T(8,128)(2,1)S(1)}, u32[]{:S(2)}, u32[]{:S(2)}) collective-permute-start(bf16[128,2048]{1,0:T(8,128)(2,1)S(1)} %get-tuple-element.178), channel_id=1, source_target_pairs={{0,4},{8,0},{16,8},{24,16},{28,24},{20,28},{12,20},{4,12},{1,5},{9... | collective-permute-start | bytes 1572872 | tf_op jit(solution)/shard_map/ppermute | solution.py:75
  850.5 30.1 %collective-permute-start.105 = (bf16[128,2048]{1,0:T(8,128)(2,1)S(1)}, bf16[128,2048]{1,0:T(8,128)(2,1)S(1)}, u32[]{:S(2)}, u32[]{:S(2)}) collective-permute-start(bf16[128,2048]{1,0:T(8,128)(2,1)S(1)} %get-tuple-element.176), channel_id=1, source_target_pairs={{0,4},{8,0},{16,8},{24,16},{28,24},{20,28},{12,20},{4,12},{1,5},{9... | collective-permute-start | bytes 1572872 | tf_op jit(solution)/shard_map/ppermute | solution.py:75
  861.8 24.1 %collective-permute-start.112 = (bf16[128,2048]{1,0:T(8,128)(2,1)S(1)}, bf16[128,2048]{1,0:T(8,128)(2,1)S(1)}, u32[]{:S(2)}, u32[]{:S(2)}) collective-permute-start(bf16[128,2048]{1,0:T(8,128)(2,1)S(1)} %get-tuple-element.189), channel_id=1, source_target_pairs={{0,8},{8,16},{16,24},{24,28},{28,20},{20,12},{12,4},{4,0},{1,9},{9... | collective-permute-start | bytes 1572872 | tf_op jit(solution)/shard_map/ppermute | solution.py:75
  883.9 193.6 %collective-permute-start.106 = (bf16[128,2048]{1,0:T(8,128)(2,1)}, bf16[128,2048]{1,0:T(8,128)(2,1)}, u32[]{:S(2)}, u32[]{:S(2)}) collective-permute-start(bf16[128,2048]{1,0:T(8,128)(2,1)} %get-tuple-element.174), channel_id=1, source_target_pairs={{0,4},{8,0},{16,8},{24,16},{28,24},{20,28},{12,20},{4,12},{1,5},{9... | collective-permute-start | bytes 1572872 | tf_op jit(solution)/shard_map/ppermute | solution.py:75
  885.9 193.0 %collective-permute-start.99 = (bf16[128,2048]{1,0:T(8,128)(2,1)}, bf16[128,2048]{1,0:T(8,128)(2,1)}, u32[]{:S(2)}, u32[]{:S(2)}) collective-permute-start(bf16[128,2048]{1,0:T(8,128)(2,1)} %get-tuple-element.173), channel_id=1, source_target_pairs={{0,8},{8,16},{16,24},{24,28},{28,20},{20,12},{12,4},{4,0},{1,9},{9... | collective-permute-start | bytes 1572872 | tf_op jit(solution)/shard_map/ppermute | solution.py:75
  895.5 184.9 %collective-permute-start.113 = (bf16[128,2048]{1,0:T(8,128)(2,1)}, bf16[128,2048]{1,0:T(8,128)(2,1)}, u32[]{:S(2)}, u32[]{:S(2)}) collective-permute-start(bf16[128,2048]{1,0:T(8,128)(2,1)} %get-tuple-element.187), channel_id=1, source_target_pairs={{0,8},{8,16},{16,24},{24,28},{28,20},{20,12},{12,4},{4,0},{1,9},{9... | collective-permute-start | bytes 1572872 | tf_op jit(solution)/shard_map/ppermute | solution.py:75
  949.7 24.6 %collective-permute-start.59 = (bf16[256,1024]{1,0:T(8,128)(2,1)S(1)}, bf16[256,1024]{1,0:T(8,128)(2,1)S(1)}, u32[]{:S(2)}, u32[]{:S(2)}) collective-permute-start(bf16[256,1024]{1,0:T(8,128)(2,1)S(1)} %fusion.89), channel_id=1, source_target_pairs={{0,2},{2,0},{1,3},{3,1},{4,6},{6,4},{5,7},{7,5},{8,10},{10,8},{9,1... | collective-permute-start | bytes 1572872 | tf_op jit(solution)/shard_map/ppermute | solution.py:79
  1002.1 80.2 %collective-permute-start.120 = (bf16[128,2048]{1,0:T(8,128)(2,1)}, bf16[128,2048]{1,0:T(8,128)(2,1)}, u32[]{:S(2)}, u32[]{:S(2)}) collective-permute-start(bf16[128,2048]{1,0:T(8,128)(2,1)} %get-tuple-element.188), channel_id=1, source_target_pairs={{0,4},{8,0},{16,8},{24,16},{28,24},{20,28},{12,20},{4,12},{1,5},{9... | collective-permute-start | bytes 1572872 | tf_op jit(solution)/shard_map/ppermute | solution.py:75
  1004.7 150.7 %collective-permute-start.79 = (bf16[8,2,64,2624]{3,2,1,0:T(8,128)(2,1)}, bf16[8,2,64,2624]{3,2,1,0:T(8,128)(2,1)}, u32[]{:S(2)}, u32[]{:S(2)}) collective-permute-start(bf16[8,2,64,2624]{3,2,1,0:T(8,128)(2,1)} %fusion.11), channel_id=1, source_target_pairs={{0,2},{2,0},{1,3},{3,1},{4,6},{6,4},{5,7},{7,5},{8,10},{10,8},{9,1... | collective-permute-start | bytes 16121864 | tf_op jit(solution)/shard_map/ppermute | solution.py:79
  1078.8 95.4 %collective-permute-start.63 = (bf16[8,2,64,3200]{3,2,1,0:T(8,128)(2,1)}, bf16[8,2,64,3200]{3,2,1,0:T(8,128)(2,1)}, u32[]{:S(2)}, u32[]{:S(2)}) collective-permute-start(bf16[8,2,64,3200]{3,2,1,0:T(8,128)(2,1)} %fusion.6), channel_id=1, source_target_pairs={{0,2},{2,0},{1,3},{3,1},{4,6},{6,4},{5,7},{7,5},{8,10},{10,8},{9,1... | collective-permute-start | bytes 19660808 | tf_op jit(solution)/shard_map/ppermute | solution.py:79
  1143.9 27.8 %collective-permute-start.129 = (bf16[128,2048]{1,0:T(8,128)(2,1)}, bf16[128,2048]{1,0:T(8,128)(2,1)S(1)}, u32[]{:S(2)}, u32[]{:S(2)}) collective-permute-start(bf16[128,2048]{1,0:T(8,128)(2,1)} %get-tuple-element.197), channel_id=1, source_target_pairs={{0,8},{8,16},{16,24},{24,28},{28,20},{20,12},{12,4},{4,0},{1,9},{9... | collective-permute-start | bytes 1572872 | tf_op jit(solution)/shard_map/ppermute | solution.py:75
  1171.0 62.9 %collective-permute-start.80 = (bf16[8,64,2624]{2,1,0:T(8,128)(2,1)}, bf16[8,64,2624]{2,1,0:T(8,128)(2,1)}, u32[]{:S(2)}, u32[]{:S(2)}) collective-permute-start(bf16[8,64,2624]{2,1,0:T(8,128)(2,1)} %fusion.32), channel_id=1, source_target_pairs={{0,1},{1,0},{2,3},{3,2},{4,5},{5,4},{6,7},{7,6},{8,9},{9,8},{10,11... | collective-permute-start | bytes 8060936 | tf_op jit(solution)/shard_map/ppermute | solution.py:79
  1184.6 118.1 %collective-permute-start.64 = (bf16[8,64,3200]{2,1,0:T(8,128)(2,1)}, bf16[8,64,3200]{2,1,0:T(8,128)(2,1)}, u32[]{:S(2)}, u32[]{:S(2)}) collective-permute-start(bf16[8,64,3200]{2,1,0:T(8,128)(2,1)} %fusion.25), channel_id=1, source_target_pairs={{0,1},{1,0},{2,3},{3,2},{4,5},{5,4},{6,7},{7,6},{8,9},{9,8},{10,11... | collective-permute-start | bytes 9830408 | tf_op jit(solution)/shard_map/ppermute | solution.py:79
  1254.3 51.3 %collective-permute-start.82 = (bf16[32,2624]{1,0:T(8,128)(2,1)S(1)}, bf16[32,2624]{1,0:T(8,128)(2,1)S(1)}, u32[]{:S(2)}, u32[]{:S(2)}) collective-permute-start(bf16[32,2624]{1,0:T(8,128)(2,1)S(1)} %get-tuple-element.146), channel_id=1, source_target_pairs={{0,8},{8,16},{16,24},{24,28},{28,20},{20,12},{12,4},{4,0},{1,9},{9... | collective-permute-start | bytes 503816 | tf_op jit(solution)/shard_map/ppermute | solution.py:75
  1258.0 47.6 %collective-permute-start.90 = (bf16[32,2624]{1,0:T(8,128)(2,1)S(1)}, bf16[32,2624]{1,0:T(8,128)(2,1)S(1)}, u32[]{:S(2)}, u32[]{:S(2)}) collective-permute-start(bf16[32,2624]{1,0:T(8,128)(2,1)S(1)} %get-tuple-element.145), channel_id=1, source_target_pairs={{0,4},{8,0},{16,8},{24,16},{28,24},{20,28},{12,20},{4,12},{1,5},{9... | collective-permute-start | bytes 503816 | tf_op jit(solution)/shard_map/ppermute | solution.py:75
  (293 other events, 4872.3 us)
Sparse Core Ops, SparseCore 0:
  11.4 151.6 all-gather.2
  166.1 133.4 all-gather.4

commit v2 on v1

v2 whole, which is shorter than its diff:
```python
import functools
import math

import jax
import jax.numpy as jnp
from jax import lax
from jax.experimental import pallas as pl
from jax.experimental.pallas import tpu as pltpu
from jax.sharding import Mesh, PartitionSpec as P

D = 2048
HEADS = 8
KV_HEADS = 2
HEAD = 256
WINDOW = 512
CONT_LEN = 512
RANK = 64
PLD = 256

EPSILON = 1e-06
INV_SQRT2 = 0.7071067811865476
ROPE_BASE = 10000.0
BF16 = jnp.bfloat16
F32 = jnp.float32


def rms_norm(values, gain):
    return values * lax.rsqrt(jnp.mean(values * values, axis=-1, keepdims=True) + EPSILON) * gain


def plain_norm(values):
    return values * lax.rsqrt(jnp.mean(values * values, axis=-1, keepdims=True) + EPSILON)


def rotate(values, places):
    half_dim = values.shape[-1] // 2
    freqs = jnp.exp(
        jnp.arange(half_dim, dtype=F32) * (-2.0 * math.log(ROPE_BASE) / values.shape[-1])
    )
    angles = places.astype(F32)[:, None, None] * freqs
    cosine = jnp.cos(angles)
    sine = jnp.sin(angles)
    first = values[..., :half_dim]
    second = values[..., half_dim:]
    return jnp.concatenate([first * cosine - second * sine, second * cosine + first * sine], -1)


def gelu_tanh(values):
    return jax.nn.gelu(values, approximate=True)


def gated_product(gate_in, up_in):
    return gelu_tanh(gate_in) * up_in


def full_dot(left, right):
    return jnp.dot(left, right, preferred_element_type=F32)


def left_dot(left, right):
    return lax.dot_general(left, right, (((0,), (0,)), ((), ())), preferred_element_type=F32)


def right_dot(left, right):
    return lax.dot_general(left, right, (((1,), (1,)), ((), ())), preferred_element_type=F32)


def ring_order(n):
    return list(range(0, n, 2)) + list(range(n - 1, 0, -2))


def ring_pairs(n, by):
    order = ring_order(n)
    return [(order[i], order[(i + by) % n]) for i in range(n)]


def ring(value, by):
    return lax.ppermute(value, "zy", ring_pairs(lax.axis_size("zy"), by))


def swap(value, axis):
    return lax.ppermute(value, axis, [(0, 1), (1, 0)])


MESH = pl.DeviceIdType.MESH


def ring_chip(spot, chips):
    spot = lax.rem(spot, chips)
    return jnp.where(spot < chips // 2, 2 * spot, 2 * (chips - 1 - spot) + 1)


def ring_spot(chip, chips):
    return jnp.where(lax.rem(chip, 2) == 0, chip // 2, chips - 1 - chip // 2)


def gather_kernel(chips, streams, shard, full, ring_send, ring_recv, x_send, x_recv, core_send, core_recv, own_sem):
    chip = lax.axis_index("zy")
    core = lax.axis_index("core")
    side = lax.axis_index("fsdp")
    spot = ring_spot(chip, chips)
    rows = shard.shape[0]

    def neighbour(by):
        return {"zy": ring_chip(spot + chips + by, chips)}

    other_core = {"core": 1 - core}
    other_side = {"fsdp": 1 - side}

    barrier = pltpu.get_barrier_semaphore()
    for peer in (neighbour(1), neighbour(-1), other_core, other_side):
        pl.semaphore_signal(barrier, inc=1, device_id=peer, device_id_type=MESH)
    pl.semaphore_wait(barrier, 4)

    def place(owner, its_core, its_side, stream):
        row = ((owner * 2 + its_core) * 2 + its_side) * rows
        return full.at[pl.ds(pl.multiple_of(row, rows), rows), pl.ds(stream[0], stream[1])]

    def owner_at(step, stream):
        return ring_chip(spot + chips - stream[2] * step, chips)

    def send(src, dst, sems, at, peer):
        return pltpu.make_async_remote_copy(
            src_ref=src,
            dst_ref=dst,
            send_sem=sems[0].at[at],
            recv_sem=sems[1].at[at],
            device_id=peer,
            device_id_type=MESH,
        )

    ring_sems, x_sems, core_sems = (ring_send, ring_recv), (x_send, x_recv), (core_send, core_recv)

    def ring_copy(number, away, step, src=None):
        stream = streams[number]
        its_side = 1 - side if away else side
        spot_ref = place(owner_at(step, stream), core, its_side, stream)
        return send(src if src is not None else spot_ref, spot_ref, ring_sems, (number, away, step), neighbour(stream[2]))

    def ring_arrival(number, away, step):
        stream = streams[number]
        its_side = 1 - side if away else side
        spot_ref = place(owner_at(step, stream), core, its_side, stream)
        return send(spot_ref, spot_ref, ring_sems, (number, away, step - 1), neighbour(stream[2]))

    def x_copy(number, step, its_side, src=None):
        stream = streams[number]
        spot_ref = place(owner_at(step, stream), core, its_side, stream)
        return send(src if src is not None else spot_ref, spot_ref, x_sems, (number, step), other_side)

    def core_copy(number, away, step, its_core, src=None):
        stream = streams[number]
        its_side = 1 - side if away else side
        spot_ref = place(owner_at(step, stream), its_core, its_side, stream)
        return send(src if src is not None else spot_ref, spot_ref, core_sems, (number, away, step), other_core)

    def cut(stream):
        return shard.at[:, pl.ds(stream[0], stream[1])]

    own_row = ((chip * 2 + core) * 2 + side) * rows
    own = pltpu.make_async_copy(
        shard, full.at[pl.ds(pl.multiple_of(own_row, rows), rows), :], own_sem
    )
    own.start()
    numbers = range(len(streams))
    for number in numbers:
        if streams[number][3]:
            x_copy(number, 0, side, cut(streams[number])).start()
    for number in numbers:
        ring_copy(number, 0, 0, cut(streams[number])).start()
    for number in numbers:
        if not streams[number][3]:
            x_copy(number, 0, side, cut(streams[number])).start()
    for number in numbers:
        core_copy(number, 0, 0, core, cut(streams[number])).start()
    for number in numbers:
        if streams[number][3]:
            x_copy(number, 0, 1 - side).wait_recv()
            ring_copy(number, 1, 0).start()
            core_copy(number, 1, 0, core).start()

    def turn(step, carry):
        for number in numbers:
            aways = (0, 1) if streams[number][3] else (0,)
            for away in aways:
                ring_arrival(number, away, step).wait_recv()

                @pl.when(step < chips - 1)
                def _(number=number, away=away):
                    ring_copy(number, away, step).start()

                core_copy(number, away, step, core).start()
            if not streams[number][3]:
                x_copy(number, step, side).start()
        for number in numbers:
            if not streams[number][3]:
                x_copy(number, step - 1, 1 - side).wait_recv()
                core_copy(number, 1, step - 1, core).start()
        return carry

    lax.fori_loop(1, chips, turn, 0)
    for number in numbers:
        if not streams[number][3]:
            x_copy(number, chips - 1, 1 - side).wait_recv()
            core_copy(number, 1, chips - 1, core).start()
    own.wait()

    def drain(step, carry):
        for number in numbers:
            first = streams[number][3]
            for away in (0, 1):
                core_copy(number, away, step, 1 - core).wait_recv()
                core_copy(number, away, step, core).wait_send()
                if first or not away:

                    @pl.when(step < chips - 1)
                    def _(number=number, away=away):
                        ring_copy(number, away, step).wait_send()

            if not first:
                x_copy(number, step, side).wait_send()
        return carry

    lax.fori_loop(0, chips, drain, 0)
    for number in numbers:
        if streams[number][3]:
            x_copy(number, 0, side).wait_send()


def gather_all(shard, chips):
    rows, cols = shard.shape
    tiles = cols // 128
    first = int(round(tiles * 0.43)) // 2 * 2
    rest = tiles - first
    bounds = [0, first // 2, first, first + rest // 2, tiles]
    streams = tuple(
        (128 * bounds[i], 128 * (bounds[i + 1] - bounds[i]), 1 if i % 2 == 0 else -1, i < 2)
        for i in range(4)
    )
    dma = pltpu.SemaphoreType.DMA
    return pl.pallas_call(
        functools.partial(gather_kernel, chips, streams),
        out_shape=jax.ShapeDtypeStruct((rows * 4 * chips, cols), shard.dtype),
        in_specs=[pl.BlockSpec(memory_space=pl.ANY)],
        out_specs=pl.BlockSpec(memory_space=pl.ANY),
        scratch_shapes=[
            dma((4, 2, chips)),
            dma((4, 2, chips)),
            dma((4, chips)),
            dma((4, chips)),
            dma((4, 2, chips)),
            dma((4, 2, chips)),
            dma,
        ],
        compiler_params=pltpu.CompilerParams(collective_id=0, has_side_effects=True),
        cost_estimate=pl.CostEstimate(
            flops=0, bytes_accessed=2 * rows * 4 * chips * cols * 2, transcendentals=0
        ),
        name="gather_all",
    )(shard)


def sum_kernel(chips, streams, counts, *refs):
    arrays, outs, held, core_in, ring_in, x_in, sems = refs_of(counts, refs)
    load_sem, core_send, core_recv, ring_send, ring_recv, x_send, x_recv = sems
    chip = lax.axis_index("zy")
    core = lax.axis_index("core")
    side = lax.axis_index("fsdp")
    spot = ring_spot(chip, chips)
    far = 1 - side

    def neighbour(by):
        return {"zy": ring_chip(spot + chips + by, chips)}

    other_core = {"core": 1 - core}
    other_side = {"fsdp": 1 - side}
    barrier = pltpu.get_barrier_semaphore()
    for peer in (neighbour(1), neighbour(-1), other_core, other_side):
        pl.semaphore_signal(barrier, inc=1, device_id=peer, device_id_type=MESH)
    pl.semaphore_wait(barrier, 4)

    numbers = range(len(streams))

    def owner_at(number, turn):
        return ring_chip(spot + 2 * chips - streams[number][3] * turn, chips)

    def cols(number):
        return pl.ds(streams[number][1], streams[number][2])

    def remote(src, dst, send, recv, peer):
        return pltpu.make_async_remote_copy(
            src_ref=src, dst_ref=dst, send_sem=send, recv_sem=recv, device_id=peer, device_id_type=MESH
        )

    def core_copy(number, turn):
        owner = owner_at(number, turn)
        array = streams[number][0]
        return remote(
            arrays[array].at[owner, 1 - core, :, :, cols(number)],
            core_in[array].at[owner, :, :, cols(number)],
            core_send.at[number, turn - 1],
            core_recv.at[number, turn - 1],
            other_core,
        )

    def x_copy(number, turn):
        array = streams[number][0]
        first = streams[number][4]
        slot = turn - 1 if first else 0
        return remote(
            held[array].at[owner_at(number, turn), far, :, cols(number)],
            x_in[number].at[slot],
            x_send.at[number, slot],
            x_recv.at[number, slot],
            other_side,
        )

    def ring_copy(number, turn):
        array = streams[number][0]
        owner = owner_at(number, turn)
        if streams[number][4]:
            src = held[array].at[owner, pl.ds(side, 1), :, cols(number)]
        else:
            src = held[array].at[owner, :, :, cols(number)]
        return remote(
            src,
            ring_in[number].at[turn - 1],
            ring_send.at[number, turn - 1],
            ring_recv.at[number, turn - 1],
            neighbour(streams[number][3]),
        )

    loads = [
        pltpu.make_async_copy(arrays[i].at[:, core], held[i], load_sem.at[i])
        for i in range(len(arrays))
    ]

    def send_cores(turn, carry):
        for number in numbers:
            core_copy(number, turn).start()
        return carry

    lax.fori_loop(1, 2, send_cores, 0)
    for load in loads:
        load.start()
    lax.fori_loop(2, chips + 1, send_cores, 0)
    for load in loads:
        load.wait()

    def add_cores(number, turn):
        array = streams[number][0]
        owner = owner_at(number, turn)
        core_copy(number, turn).wait_recv()
        for its_side in range(2):
            held[array][owner, its_side, :, cols(number)] = (
                held[array][owner, its_side, :, cols(number)].astype(F32)
                + core_in[array][owner, its_side, :, cols(number)].astype(F32)
            ).astype(BF16)

    def begin(turn):
        for number in numbers:
            if streams[number][4]:
                add_cores(number, turn)
                x_copy(number, turn).start()

    begin(1)

    def round_trip(turn, carry):
        @pl.when(turn < chips)
        def _():
            begin(turn + 1)

        for number in numbers:
            array = streams[number][0]
            owner = owner_at(number, turn)
            if not streams[number][4]:
                add_cores(number, turn)

                @pl.when(turn > 1)
                def _(number=number, array=array, owner=owner):
                    ring_copy(number, turn - 1).wait_recv()
                    for its_side in range(2):
                        held[array][owner, its_side, :, cols(number)] = (
                            held[array][owner, its_side, :, cols(number)].astype(F32)
                            + ring_in[number][turn - 2, its_side].astype(F32)
                        ).astype(BF16)

                @pl.when(turn < chips)
                def _(number=number):
                    ring_copy(number, turn).start()

        for number in numbers:
            array = streams[number][0]
            owner = owner_at(number, turn)
            if streams[number][4]:
                x_copy(number, turn).wait_recv()

                @pl.when(turn == 1)
                def _(number=number, array=array, owner=owner):
                    held[array][owner, side, :, cols(number)] = (
                        held[array][owner, side, :, cols(number)].astype(F32)
                        + x_in[number][turn - 1].astype(F32)
                    ).astype(BF16)

                @pl.when(turn > 1)
                def _(number=number, array=array, owner=owner):
                    ring_copy(number, turn - 1).wait_recv()
                    total = (
                        held[array][owner, side, :, cols(number)].astype(F32)
                        + x_in[number][turn - 1].astype(F32)
                        + ring_in[number][turn - 2, 0].astype(F32)
                    )
                    held[array][owner, side, :, cols(number)] = total.astype(BF16)

                    @pl.when(turn == chips)
                    def _():
                        outs[array][:, cols(number)] = total

                @pl.when(turn < chips)
                def _(number=number):
                    ring_copy(number, turn).start()

        return carry

    lax.fori_loop(1, chips + 1, round_trip, 0)
    for number in numbers:
        if not streams[number][4]:
            x_copy(number, chips).start()
    for number in numbers:
        array = streams[number][0]
        if not streams[number][4]:
            x_copy(number, chips).wait_recv()
            outs[array][:, cols(number)] = held[array][chip, side, :, cols(number)].astype(
                F32
            ) + x_in[number][0].astype(F32)

    def drain(turn, carry):
        for number in numbers:
            core_copy(number, turn).wait_send()
            if streams[number][4]:
                x_copy(number, turn).wait_send()

            @pl.when(turn < chips)
            def _(number=number):
                ring_copy(number, turn).wait_send()

        return carry

    lax.fori_loop(1, chips + 1, drain, 0)
    for number in numbers:
        if not streams[number][4]:
            x_copy(number, chips).wait_send()


def refs_of(counts, refs):
    groups, at = [], 0
    for count in counts:
        groups.append(refs[at : at + count])
        at += count
    return groups


def sum_all(arrays, firsts, chips):
    rows = arrays[0].shape[0] // (4 * chips)
    streams = []
    for i, (array, first) in enumerate(zip(arrays, firsts)):
        width = array.shape[1]
        left = width // 256 * 128
        streams.append((i, 0, left, 1, first))
        streams.append((i, left, width - left, -1, first))
    streams = tuple(sorted(streams, key=lambda stream: stream[4]))
    count, number = len(arrays), len(streams)
    dma = pltpu.SemaphoreType.DMA
    vmem = pltpu.VMEM
    scratch = (
        [vmem((chips, 2, rows, a.shape[1]), BF16) for a in arrays]
        + [vmem((chips, 2, rows, a.shape[1]), BF16) for a in arrays]
        + [vmem((chips - 1, 1 if first else 2, rows, width), BF16) for _, _, width, _, first in streams]
        + [vmem((chips if first else 1, rows, width), BF16) for _, _, width, _, first in streams]
        + [dma((count,))]
        + [dma((number, chips)) for _ in range(6)]
    )
    return pl.pallas_call(
        functools.partial(
            sum_kernel, chips, streams, (count, count, count, count, number, number, 7)
        ),
        out_shape=[jax.ShapeDtypeStruct((rows, a.shape[1]), F32) for a in arrays],
        in_specs=[pl.BlockSpec(memory_space=pl.ANY)] * count,
        out_specs=[pl.BlockSpec(memory_space=pltpu.VMEM)] * count,
        scratch_shapes=scratch,
        compiler_params=pltpu.CompilerParams(
            collective_id=1, has_side_effects=True, vmem_limit_bytes=56 << 20
        ),
        cost_estimate=pl.CostEstimate(
            flops=0, bytes_accessed=sum(2 * a.size for a in arrays), transcendentals=0
        ),
        name="sum_all",
    )(*[a.reshape(chips, 2, 2, rows, a.shape[1]) for a in arrays])


def tie(*values):
    return lax.optimization_barrier(values)


def shares(total, count):
    return [total // count + (1 if i < total % count else 0) for i in range(count)]


def rows_of_four(own):
    pair = jnp.concatenate([own, swap(own, "fsdp")], 0)
    return jnp.concatenate([pair, swap(pair, "core")], 0)


def sum_of_four(partial):
    count = partial.shape[0] // 4
    low = partial[2 * count :].astype(BF16)
    pair = partial[: 2 * count] + swap(low, "core").astype(F32)
    low = pair[count:].astype(BF16)
    return pair[:count] + swap(low, "fsdp").astype(F32)


def body(
    tokens,
    per_layer,
    teacher,
    cont_lengths,
    w_query,
    w_kv,
    w_out,
    laurel_left,
    laurel_right,
    pl_gate,
    pl_proj,
    norm_gains,
    head_gains,
    ffn_weight,
):
    states = tokens[0].astype(F32)
    layer_in = per_layer[0].astype(F32)
    target = teacher[0].astype(F32)
    row_count = states.shape[0]
    chips = lax.axis_size("zy")
    seq_count = 2 * chips
    group_count = lax.axis_size("fsdp")
    shards = seq_count * group_count
    chip = lax.axis_index("zy")
    core = lax.axis_index("core")
    seq_index = chip * 2 + core
    group_index = lax.axis_index("fsdp")
    half_point = seq_count // 2
    prompt_len = half_point * row_count
    cont_shards = CONT_LEN // row_count
    cont_count = prompt_len // CONT_LEN
    is_cont = seq_index >= half_point
    rel_index = seq_index - half_point
    local_shard = jnp.where(is_cont, rel_index % cont_shards, 0)
    cont_index = jnp.where(is_cont, rel_index // cont_shards, 0)
    first_place = jnp.where(is_cont, prompt_len + local_shard * row_count, seq_index * row_count)
    row_range = jnp.arange(row_count, dtype=jnp.int32)
    places = first_place + row_range
    group_lengths = jnp.sum(
        jnp.where(
            jnp.arange(group_count, dtype=jnp.int32)[:, None] == group_index, cont_lengths, 0
        ),
        axis=0,
    )
    my_length = jnp.sum(
        jnp.where(jnp.arange(cont_count, dtype=jnp.int32) == cont_index, group_lengths, 0)
    )
    valid = jnp.logical_or(
        jnp.logical_not(is_cont), local_shard * row_count + row_range < my_length
    )
    weight_mask = valid.astype(F32)
    count = F32(group_count * prompt_len) + jnp.sum(cont_lengths).astype(F32)
    total_slots = float(row_count * seq_count * group_count)
    shard_rows = w_query.shape[0]
    key_cols = KV_HEADS * HEAD
    proj_cols = pl_proj.shape[0] * D // shard_rows
    misc_cols = RANK
    head_part = head_gains.reshape(-1, 1)
    misc = jnp.concatenate(
        [
            norm_gains.T,
            jnp.pad(head_part, ((0, shard_rows - head_part.shape[0]), (0, 0))),
            jnp.zeros((shard_rows, misc_cols - 7), BF16),
        ],
        1,
    )
    pack = jnp.concatenate(
        [
            w_query,
            w_kv,
            laurel_left,
            misc,
            pl_gate,
            pl_proj.reshape(shard_rows, proj_cols),
            w_out,
            laurel_right.T,
            jnp.zeros((shard_rows, 128 - RANK), BF16),
        ],
        1,
    )

    units = ffn_weight.shape[0]
    half = units // 2
    by_kind = ffn_weight.transpose(1, 0, 2)
    ups, downs = [by_kind[:, :half]], [by_kind[:, half:]]
    stage_steps = shares(chips - 1, 7)

    def pass_on(stage):
        for _ in range(stage_steps[stage]):
            ups.append(ring(ups[-1], 1))
            downs.append(ring(downs[-1], -1))

    def stage_end(values):
        (ups[-1], downs[-1]), values = tie((ups[-1], downs[-1]), values)
        return values

    pass_on(0)
    full = stage_end(gather_all(pack, chips))
    pass_on(1)
    at = 0
    pieces = []
    for width in (D, 2 * key_cols, RANK, misc_cols, PLD, proj_cols, D, RANK):
        pieces.append(full[:, at : at + width])
        at += width
    wq, wkv, lleft, misc_full, plg, plp, wo, lright = pieces
    plp = plp.reshape(PLD, D)
    lright = lright.T
    gains = misc_full[:, :6].T.astype(F32)
    head_n = head_gains.shape[1]
    head_gain = (
        misc_full[:, 6]
        .reshape(shards, shard_rows)[:, : 2 * head_n]
        .reshape(shards, 2, head_n)
        .transpose(1, 0, 2)
        .reshape(2, HEAD)
        .astype(F32)
    )

    normed = rms_norm(states, gains[0])
    normed_low = normed.astype(BF16)
    query_raw = full_dot(normed_low, wq)
    kv_raw = full_dot(normed_low, wkv)

    def prepare(q_input, k_input, v_input, q_gain, k_gain):
        q_heads = rotate(rms_norm(q_input.reshape(row_count, HEADS, HEAD), q_gain), places)
        k_heads = rotate(rms_norm(k_input.reshape(row_count, KV_HEADS, HEAD), k_gain), places)
        v_heads = plain_norm(v_input.reshape(row_count, KV_HEADS, HEAD))
        return (q_heads, k_heads, v_heads)

    (queries, keys_new, values_new), prepare_back = jax.vjp(
        prepare, query_raw, kv_raw[:, :key_cols], kv_raw[:, key_cols:], head_gain[0], head_gain[1]
    )
    query_low = queries.astype(BF16)
    kv_own = jnp.concatenate(
        [
            keys_new.reshape(row_count, key_cols).astype(BF16),
            values_new.reshape(row_count, key_cols).astype(BF16),
        ],
        1,
    )

    query_low, kv_own = stage_end((query_low, kv_own))
    pass_on(2)

    mid = chips // 2
    chain = [(i, i + 1) for i in range(mid - 1)] + [(mid - 1, mid + 1)]
    kv_before = jnp.where(
        chip == mid,
        lax.ppermute(kv_own, "zy", [(mid - 1, mid)]),
        lax.ppermute(kv_own, "zy", chain),
    )
    spans = []
    span = 2
    while span < mid:
        spans.append(span)
        span *= 2
    for span in spans:
        moved = lax.ppermute(
            kv_before, "zy", [(mid + i, mid + i + span) for i in range(min(span, mid - span))]
        )
        fresh = jnp.logical_and(chip >= mid + span, chip < mid + 2 * span)
        kv_before = jnp.where(fresh, moved, kv_before)
    kv_other = swap(jnp.where(core == 0, kv_own, kv_before), "core")
    keys_all = jnp.concatenate([kv_before, kv_other, kv_own], 0)
    keys_all = stage_end(keys_all)
    pass_on(3)
    key_len = keys_all.shape[0]
    key_places = first_place - 2 * row_count + jnp.arange(key_len, dtype=jnp.int32)
    visible = (
        (key_places[None, :] <= places[:, None])
        & (places[:, None] - key_places[None, :] < WINDOW)
        & (key_places[None, :] >= 0)
    )
    group_heads = HEADS // KV_HEADS
    query_grouped = query_low.reshape(row_count, KV_HEADS, group_heads, HEAD)
    key_heads = keys_all[:, :key_cols].reshape(key_len, KV_HEADS, HEAD)
    value_heads = keys_all[:, key_cols:].reshape(key_len, KV_HEADS, HEAD)

    def masked_scores():
        scores = jnp.einsum(
            "qgjd,kgd->gjqk", query_grouped, key_heads, preferred_element_type=F32
        )
        return jnp.where(visible, scores, -1e30)

    scores_fwd = masked_scores()
    top_score = jnp.max(scores_fwd, axis=-1, keepdims=True)
    expo = jnp.exp(scores_fwd - top_score)
    totals = jnp.sum(expo, axis=-1, keepdims=True)
    probs = expo / totals
    log_total = top_score + jnp.log(totals)
    probs_low = probs.astype(BF16)
    context = jnp.einsum("gjqk,kgd->qgjd", probs_low, value_heads, preferred_element_type=F32)
    context_low = context.reshape(row_count, HEADS * HEAD).astype(BF16)
    attn_raw = full_dot(context_low, wo)
    attn_out = rms_norm(attn_raw, gains[1])
    laurel_mid = full_dot(normed_low, lleft).astype(BF16)
    laurel_raw = full_dot(laurel_mid, lright)
    mixed = (states + attn_out + normed + rms_norm(laurel_raw, gains[2])) * INV_SQRT2
    ffn_in = rms_norm(mixed, gains[3]).astype(BF16)

    ffn_in = stage_end(ffn_in)
    pass_on(4)
    ffn_rows = stage_end(rows_of_four(ffn_in))
    gates, uppers, hiddens, part_weights, parts = [], [], [], [], []
    running = None

    def forward_part(running, first, last):
        weights = [
            jnp.concatenate([w[kind] for k in range(first, last) for w in (ups[k], downs[k])], 0)
            for kind in range(3)
        ]
        gate = right_dot(ffn_rows, weights[0])
        upper = right_dot(ffn_rows, weights[1])
        hidden = gated_product(gate, upper).astype(BF16)
        term = full_dot(hidden, weights[2])
        gates.append(gate)
        uppers.append(upper)
        hiddens.append(hidden)
        part_weights.append(weights)
        parts.append(range(first, last))
        return term if running is None else running + term

    here = len(ups)
    pass_on(5)
    cut_a = max(1, here * 2 // 3)
    running = stage_end(forward_part(None, 0, cut_a))
    here = len(ups)
    pass_on(6)
    running = forward_part(running, cut_a, here)
    if here < chips:
        running = stage_end(running)
        running = forward_part(running, here, chips)
    down_out = sum_of_four(running)
    after_ffn = mixed + rms_norm(down_out, gains[4])
    after_low = after_ffn.astype(BF16)
    pl_raw = full_dot(after_low, plg)
    pl_act = gelu_tanh(pl_raw)
    pl_mid = (pl_act * layer_in).astype(BF16)
    pl_out = full_dot(pl_mid, plp)
    result = after_ffn + rms_norm(pl_out, gains[5])
    errors = result - target
    squares = jnp.sum(weight_mask[:, None] * errors * errors)

    grad_out = weight_mask[:, None] * errors * (total_slots / count)
    unused, pl_norm_back = jax.vjp(rms_norm, pl_out, gains[5])
    grad_pl_out, grad_g5 = pl_norm_back(grad_out)
    grad_pl_low = grad_pl_out.astype(BF16)
    grad_plp = left_dot(pl_mid, grad_pl_low)
    grad_pl_mid = right_dot(grad_pl_low, plp)
    grad_layer_in = grad_pl_mid * pl_act
    unused, gelu_back = jax.vjp(gelu_tanh, pl_raw)
    grad_pl_raw = gelu_back(grad_pl_mid * layer_in)[0].astype(BF16)
    grad_plg = left_dot(after_low, grad_pl_raw)
    grad_after = grad_out + right_dot(grad_pl_raw, plg)
    unused, down_norm_back = jax.vjp(rms_norm, down_out, gains[4])
    grad_down, grad_g4 = down_norm_back(grad_after)
    grad_down_low = grad_down.astype(BF16)

    grad_down_rows = rows_of_four(grad_down_low)
    grad_gates, grad_uppers = [], []

    def backward_part(number):
        unused, act_back = jax.vjp(gated_product, gates[number], uppers[number])
        grad_gate, grad_upper = act_back(right_dot(grad_down_rows, part_weights[number][2]))
        return grad_gate.astype(BF16), grad_upper.astype(BF16)

    def unit_grads(k):
        for part, (gg, gu), hid in zip(parts, grad_parts, hiddens):
            if k in part:
                at = (k - part[0]) * units
                up_cut, down_cut = slice(at, at + half), slice(at + half, at + units)
                return (
                    left_dot(jnp.concatenate([gg[:, up_cut], gu[:, up_cut]], 1), ffn_rows),
                    left_dot(jnp.concatenate([gg[:, down_cut], gu[:, down_cut]], 1), ffn_rows),
                    left_dot(hid[:, at : at + units], grad_down_rows),
                )

    def add_terms(arrived, terms):
        halves = (terms[0], terms[2][:half], terms[1], terms[2][half:])
        if arrived is None:
            return halves
        return tuple(a.astype(F32) + t for a, t in zip(arrived, halves))

    order = list(range(1, chips)) + [0]
    ring_steps = shares(chips - 1, 7)
    done = 0
    sums = None

    def move(sums):
        low = [s.astype(BF16) for s in sums]
        return [ring(low[0], 1), ring(low[1], 1), ring(low[2], -1), ring(low[3], -1)]

    def beside(stage, work):
        nonlocal done, sums
        values = None
        for step in range(ring_steps[stage]):
            arrived = move(sums)
            done += 1
            terms = unit_grads(order[done])
            if step == 0:
                values = work()
            arrived, terms, values = tie(arrived, terms, values)
            sums = add_terms(arrived, terms)
        return work() if values is None else values

    grad_parts = [backward_part(0)]
    sums = add_terms(None, unit_grads(order[0]))

    def work():
        return [backward_part(number) for number in range(1, len(parts))]

    grad_parts += beside(0, work)

    def work():
        running = None
        for weights, (gg, gu) in zip(part_weights, grad_parts):
            term = full_dot(gg, weights[0]) + full_dot(gu, weights[1])
            running = term if running is None else running + term
        return running

    running = beside(1, work)
    grad_ffn_in = beside(2, lambda: sum_of_four(running))
    def work():
        unused, mix_norm_back = jax.vjp(rms_norm, mixed, gains[3])
        grad_mixed_norm, grad_g3 = mix_norm_back(grad_ffn_in)
        grad_scaled = (grad_after + grad_mixed_norm) * INV_SQRT2
        unused, laurel_norm_back = jax.vjp(rms_norm, laurel_raw, gains[2])
        grad_laurel, grad_g2 = laurel_norm_back(grad_scaled)
        grad_laurel_low = grad_laurel.astype(BF16)
        grad_lright_t = left_dot(grad_laurel_low, laurel_mid)
        grad_mid_low = right_dot(grad_laurel_low, lright).astype(BF16)
        grad_lleft = left_dot(normed_low, grad_mid_low)
        unused, attn_norm_back = jax.vjp(rms_norm, attn_raw, gains[1])
        grad_attn, grad_g1 = attn_norm_back(grad_scaled)
        grad_attn_low = grad_attn.astype(BF16)
        grad_wo = left_dot(context_low, grad_attn_low)
        grad_context = right_dot(grad_attn_low, wo).astype(BF16)
        return (
            grad_context,
            grad_scaled,
            grad_wo,
            grad_lleft,
            grad_lright_t,
            grad_mid_low,
            (grad_g1, grad_g2, grad_g3),
        )

    (
        grad_context,
        grad_scaled,
        grad_wo,
        grad_lleft,
        grad_lright_t,
        grad_mid_low,
        (grad_g1, grad_g2, grad_g3),
    ) = beside(3, work)
    grad_context = grad_context.reshape(row_count, KV_HEADS, group_heads, HEAD)

    def work():
        probs_again = jnp.exp(masked_scores() - log_total)
        grad_probs = jnp.einsum(
            "qgjd,kgd->gjqk", grad_context, value_heads, preferred_element_type=F32
        )
        grad_scores = (
            probs_again * (grad_probs - jnp.sum(probs_again * grad_probs, axis=-1, keepdims=True))
        ).astype(BF16)
        grad_queries = jnp.einsum("gjqk,kgd->qgjd", grad_scores, key_heads, preferred_element_type=F32)
        grad_keys = jnp.einsum(
            "gjqk,qgjd->kgd", grad_scores, query_grouped, preferred_element_type=F32
        )
        grad_values = jnp.einsum(
            "gjqk,qgjd->kgd", probs_again.astype(BF16), grad_context, preferred_element_type=F32
        )
        grad_kv = jnp.concatenate(
            [grad_keys.reshape(key_len, key_cols), grad_values.reshape(key_len, key_cols)], 1
        )
        return grad_queries, grad_kv

    grad_queries, grad_kv = beside(4, work)

    def work():
        grad_before = grad_kv[:row_count]
        grad_own = grad_kv[2 * row_count :]
        returned = swap(grad_kv[row_count : 2 * row_count].astype(BF16), "core").astype(F32)
        grad_own = grad_own + jnp.where(core == 0, returned, 0.0)
        grad_before = grad_before + jnp.where(core == 0, 0.0, returned)
        for span in reversed(spans):
            back = [(mid + i + span, mid + i) for i in range(min(span, mid - span))]
            grad_before = grad_before + lax.ppermute(grad_before.astype(BF16), "zy", back).astype(F32)
        before_low = grad_before.astype(BF16)
        grad_own = (
            grad_own
            + lax.ppermute(before_low, "zy", [(b, a) for a, b in chain]).astype(F32)
            + lax.ppermute(before_low, "zy", [(mid, mid - 1)]).astype(F32)
        )
        return grad_own

    grad_own = beside(5, work)
    def work():
        grad_query_raw, grad_key_raw, grad_value_raw, grad_hq, grad_hk = prepare_back(
            (
                grad_queries.reshape(row_count, HEADS, HEAD),
                grad_own[:, :key_cols].reshape(row_count, KV_HEADS, HEAD),
                grad_own[:, key_cols:].reshape(row_count, KV_HEADS, HEAD),
            )
        )
        grad_query_low = grad_query_raw.astype(BF16)
        grad_kv_low = jnp.concatenate([grad_key_raw, grad_value_raw], 1).astype(BF16)
        grad_wq = left_dot(normed_low, grad_query_low)
        grad_wkv = left_dot(normed_low, grad_kv_low)
        grad_normed = (
            grad_scaled
            + right_dot(grad_mid_low, lleft)
            + right_dot(grad_query_low, wq)
            + right_dot(grad_kv_low, wkv)
        )
        unused, input_norm_back = jax.vjp(rms_norm, states, gains[0])
        grad_states, grad_g0 = input_norm_back(grad_normed)
        grad_tokens = grad_scaled + grad_states
        return grad_tokens, grad_wq, grad_wkv, grad_g0, grad_hq, grad_hk

    grad_tokens, grad_wq, grad_wkv, grad_g0, grad_hq, grad_hk = beside(6, work)
    up_pair, up_down, down_pair, down_down = sums
    grad_ffn = jnp.stack(
        [
            jnp.concatenate([up_pair[:half], down_pair[:half]], 0),
            jnp.concatenate([up_pair[half:], down_pair[half:]], 0),
            jnp.concatenate([up_down, down_down], 0),
        ],
        1,
    )

    head_back = jnp.stack([grad_hq, grad_hk]).reshape(2, shards, head_n).transpose(1, 0, 2)
    head_back = head_back.reshape(shards, 2 * head_n)
    head_back = jnp.pad(head_back, ((0, 0), (0, shard_rows - 2 * head_n))).reshape(-1, 1)
    gains_back = jnp.stack([grad_g0, grad_g1, grad_g2, grad_g3, grad_g4, grad_g5], 1)
    misc_back = jnp.concatenate(
        [gains_back, head_back, jnp.zeros((D, misc_cols - 7), F32)], 1
    )
    rest_back = jnp.concatenate(
        [
            grad_lleft,
            misc_back,
            grad_plg,
            grad_plp.reshape(D, proj_cols),
            grad_lright_t,
            jnp.zeros((D, 128 - RANK), F32),
        ],
        1,
    )
    sums_wq, sums_wkv, sums_wo, sums_rest = sum_all(
        [g.astype(BF16) for g in (grad_wq, grad_wkv, grad_wo, rest_back)],
        (False, False, True, True),
        chips,
    )
    at = 0
    rest = []
    for width in (RANK, misc_cols, PLD, proj_cols, RANK):
        rest.append(sums_rest[:, at : at + width])
        at += width

    total = jnp.broadcast_to(squares, (8, 128))
    total = total + swap(total, "core")
    total = total + swap(total, "fsdp")
    span = 1
    while span < chips:
        total = total + lax.ppermute(total, "zy", [(i, i ^ span) for i in range(chips)])
        span *= 2
    match_loss = total[0, 0] / (2.0 * D * count)

    return (
        result[None],
        match_loss,
        grad_tokens[None],
        grad_layer_in[None],
        sums_wq,
        sums_wkv,
        sums_wo,
        rest[0],
        rest[4].T,
        rest[2],
        rest[3].reshape(pl_proj.shape),
        rest[1][:, :6].T,
        rest[1][: 2 * head_n, 6].reshape(2, head_n),
        grad_ffn,
    )


def solution(mesh):
    seq, fsdp = mesh.shape["seq"], mesh.shape["fsdp"]
    fine = Mesh(mesh.devices.reshape(seq // 2, 2, fsdp), ("zy", "core", "fsdp"))
    rows = P("fsdp", ("zy", "core"), None)
    split = ("zy", "core", "fsdp")
    weights = (
        P(split, None),
        P(split, None),
        P(split, None),
        P(split, None),
        P(None, split),
        P(split, None),
        P(split, None),
        P(None, split),
        P(None, split),
        P(split, None, None),
    )
    return jax.shard_map(
        body,
        mesh=fine,
        in_specs=(rows, rows, rows, P()) + weights,
        out_specs=(rows, P(), rows, rows) + weights,
        check_vma=False,
    )
```

time: 1390 us -> 1240 us (0.89)
  Pallas kernels: 0 us -> 238 us
  starting transfers between devices: 248 us -> 83 us
  waiting for transfers between devices: 478 us -> 320 us
  local copies, waits for them, and re-layouts: 208 us -> 159 us
    pallas_call x0 -> x2, Pallas kernels: none -> 238 us  [the longest x1 128 us: gather_all(): pl.pallas_call(functools.partial(gather_kernel, chips, streams), out_shap...]
    ppermute x112 -> x42, starting transfers between devices: 219 us -> 68.7 us  [ring(): return lax.ppermute(value, 'zy', ring_pairs(lax.axis_size('zy'), by))]
    ppermute x112 -> x42, waiting for transfers between devices: 326 us -> 193 us  [ring(): return lax.ppermute(value, 'zy', ring_pairs(lax.axis_size('zy'), by))]
    ppermute x16 -> x12, waiting for transfers between devices: 149 us -> 87 us  [swap(): return lax.ppermute(value, axis, [(0, 1), (1, 0)])]
    ppermute x3, waiting for transfers between devices: 0.01 us -> 30.7 us  [the longest x1 30.7 us: work(): lax.ppermute(before_low, 'zy', [(b, a) for a, b in chain]).astype(F32)]
    concatenate x24 -> x12, local copies, waits for them, and re-layouts: 55.4 us -> 26 us  [the longest x9 20.9 us: body(): jnp.concatenate([grad_lleft, misc_back, grad_plg, grad_plp.reshape(D, pro...]
    convert_element_type x6 -> x0, local copies, waits for them, and re-layouts: 23.8 us -> none  [the longest x2 15.9 us: scatter_sum(): blocks = mine + swap(other.astype(BF16), 'core').astype(F32)]
    convert_element_type x35 -> x23, other arithmetic: 31.1 us -> 44.7 us  [the longest x18 34.3 us: move(): low = [s.astype(BF16) for s in sums]]
  transfers between devices with their start and end apart: 139 -> 63, of which waited for: 82 -> 27; matrix products, arithmetic and copies ran while one was open for 32% -> 24% of each run, Pallas kernels for 0% -> 10%
where the time goes in v2:
time: 1240 us; the launch traced here: 1230 us
  waiting for transfers between devices  320 us (26%)
  matrix products  283 us (23%)
  Pallas kernels  238 us (19%)
  local copies, waits for them, and re-layouts  159 us (13%)
  other arithmetic  135 us (11%)
  starting transfers between devices  83 us (7%)
    ppermute x42, waiting for transfers between devices, ring(): return lax.ppermute(value, 'zy', ring_pairs(lax.axis_size('zy'), by))  193 us
    pallas_call x1, Pallas kernels, gather_all(): pl.pallas_call(functools.partial(gather_kernel, chips, streams), out_shap...  128 us
    pallas_call x1, Pallas kernels, sum_all(): pl.pallas_call(functools.partial(sum_kernel, chips, streams, (count, coun...  111 us
    dot_general x31, matrix products, left_dot(): lax.dot_general(left, right, (((0,), (0,)), ((), ())), preferred_element_...  96.4 us
    dot_general x16, matrix products, full_dot(): return jnp.dot(left, right, preferred_element_type=F32)  90.3 us
    ppermute x12, waiting for transfers between devices, swap(): return lax.ppermute(value, axis, [(0, 1), (1, 0)])  87 us
    dot_general x16, matrix products, right_dot(): lax.dot_general(left, right, (((1,), (1,)), ((), ())), preferred_element_...  74.6 us
    ppermute x42, starting transfers between devices, ring(): return lax.ppermute(value, 'zy', ring_pairs(lax.axis_size('zy'), by))  68.7 us
  transfers between devices with their start and end apart: 63, of which 27 were waited for; matrix products, arithmetic and copies ran while one was open for 24% of the time, Pallas kernels for 10%

profile of v2, /device:TPU:0, one launch (start us, length us, event | category | flops | bytes accessed | tf_op | source)
XLA Modules:
  0.0 1225.5 jit_solution(2585369460200863088)
XLA Ops:
  0.7 4.0 fusion.246
  11.2 127.6 %gather_all.1 = bf16[2048,5888]{1,0:T(8,128)(2,1)} custom-call(bf16[64,5888]{1,0:T(8,128)(2,1)} %concatenate.151.shard), custom_call_target="tpu_custom_call" | custom-call | bytes 48234496 | tf_op jit(solution)/shard_map/gather_all/pallas_call | solution.py:241
  142.9 8.4 slice_bitcast_fusion
  154.7 3.5 fusion.21
  163.2 12.4 %copy.217 = bf16[2048,2048]{1,0:T(8,128)(2,1)} copy(bf16[2048,2048]{0,1:T(8,128)(2,1)} %slice_bitcast_fusion) | data formatting | bytes 16777216 | tf_op jit(solution)/shard_map/dot_general | solution.py:57
  178.1 5.9 multiply_reduce_fusion.17
  185.4 27.3 %collective-permute-done.2 = bf16[3,128,2048]{2,1,0:T(8,128)(2,1)S(1)} collective-permute-done((bf16[3,128,2048]{2,1,0:T(8,128)(2,1)}, bf16[3,128,2048]{2,1,0:T(8,128)(2,1)S(1)}, u32[]{:S(2)}, u32[]{:S(2)}) %collective-permute-start.2) | collective-permute-done | bytes 1572896 | tf_op jit(solution)/shard_map/ppermute | solution.py:78
  222.8 6.6 collective-permute-done.7
  233.2 4.7 collective-permute-start.4
  243.1 27.1 %collective-permute-done.4 = bf16[3,128,2048]{2,1,0:T(8,128)(2,1)} collective-permute-done((bf16[3,128,2048]{2,1,0:T(8,128)(2,1)}, bf16[3,128,2048]{2,1,0:T(8,128)(2,1)}, u32[]{:S(2)}, u32[]{:S(2)}) %collective-permute-start.4) | collective-permute-done | bytes 1572896 | tf_op jit(solution)/shard_map/ppermute | solution.py:78
  281.8 6.8 collective-permute-start.11
  304.7 16.1 %collective-permute-done.10 = bf16[3,128,2048]{2,1,0:T(8,128)(2,1)} collective-permute-done((bf16[3,128,2048]{2,1,0:T(8,128)(2,1)}, bf16[3,128,2048]{2,1,0:T(8,128)(2,1)}, u32[]{:S(2)}, u32[]{:S(2)}) %collective-permute-start.10) | collective-permute-done | bytes 1572896 | tf_op jit(solution)/shard_map/ppermute | solution.py:78
  326.3 16.6 %collective-permute-done.14 = bf16[256,2048]{1,0:T(8,128)(2,1)S(1)} collective-permute-done((bf16[256,2048]{1,0:T(8,128)(2,1)S(1)}, bf16[256,2048]{1,0:T(8,128)(2,1)S(1)}, u32[]{:S(2)}, u32[]{:S(2)}) %collective-permute-start.14) | collective-permute-done | bytes 1048608 | tf_op jit(solution)/shard_map/ppermute | solution.py:82
  347.0 4.2 collective-permute-start.12
  357.2 28.6 %collective-permute-done.12 = bf16[3,128,2048]{2,1,0:T(8,128)(2,1)S(1)} collective-permute-done((bf16[3,128,2048]{2,1,0:T(8,128)(2,1)}, bf16[3,128,2048]{2,1,0:T(8,128)(2,1)S(1)}, u32[]{:S(2)}, u32[]{:S(2)}) %collective-permute-start.12) | collective-permute-done | bytes 1572896 | tf_op jit(solution)/shard_map/ppermute | solution.py:78
  385.8 10.2 collective-permute-done.13
  398.2 6.4 fusion.261
  404.6 10.6 multiply_convert_fusion.1
  416.5 9.0 fusion.262
  425.5 6.6 collective-permute-done.16
  442.0 5.5 multiply_convert_fusion.3
  448.6 5.7 fusion.264
  454.4 11.8 add.414
  477.5 4.6 fusion.89
  482.1 11.8 add.417
  496.4 4.1 collective-permute-done.20
  511.3 20.7 %collective-permute-done.21 = bf16[256,2048]{1,0:T(8,128)(2,1)} collective-permute-done((bf16[256,2048]{1,0:T(8,128)(2,1)}, bf16[256,2048]{1,0:T(8,128)(2,1)}, u32[]{:S(2)}, u32[]{:S(2)}) %collective-permute-start.21) | collective-permute-done | bytes 1048608 | tf_op jit(solution)/shard_map/ppermute | solution.py:82
  551.8 23.9 %collective-permute-done.27 = bf16[256,2048]{1,0:T(8,128)(2,1)S(1)} collective-permute-done((bf16[256,2048]{1,0:T(8,128)(2,1)S(1)}, bf16[256,2048]{1,0:T(8,128)(2,1)S(1)}, u32[]{:S(2)}, u32[]{:S(2)}) %collective-permute-start.27) | collective-permute-done | bytes 1048608 | tf_op jit(solution)/shard_map/ppermute | solution.py:82
  603.0 11.7 fusion.17
  614.8 9.0 fusion.265
  624.0 9.0 fusion.266
  657.7 4.3 fusion.104
  662.0 4.2 fusion.102
  666.2 4.2 fusion.100
  670.4 4.2 fusion.240
  674.6 4.3 fusion.96
  679.0 3.6 multiply_convert_fusion.5
  682.6 10.4 multiply_convert_fusion.2
  698.2 4.5 fusion.98
  702.8 5.6 fusion.267
  709.5 5.6 fusion.268
  716.6 4.5 fusion.90
  735.2 18.0 %add_add_fusion = f32[1024,2048]{1,0:T(8,128)} fusion(f32[1024,2048]{1,0:T(8,128)} %fusion.90, f32[1024,2048]{1,0:T(8,128)} %fusion.267, f32[1024,2048]{1,0:T(8,128)} %fusion.268, f32[1024,2048]{1,0:T(8,128)} %fusion.265, f32[1024,2048]{1,0:T(8,128)} %fusion.266, bf16[1024,256]{1,0:T(8,128)(2,1)S(1)} %get-tuple-element.144, ...), kind=kOutput, calls=%fused_computation | convolution fusion | flops 1086324736 | bytes 51904512 | tf_op jit(solution)/shard_map/dot_general | solution.py:57
  753.2 5.1 fusion.149
  758.3 5.0 fusion.145
  785.8 17.0 %collective-permute-done.42 = bf16[256,2048]{1,0:T(8,128)(2,1)S(1)} collective-permute-done((bf16[256,2048]{1,0:T(8,128)(2,1)S(1)}, bf16[256,2048]{1,0:T(8,128)(2,1)S(1)}, u32[]{:S(2)}, u32[]{:S(2)}) %collective-permute-start.42) | collective-permute-done | bytes 1048608 | tf_op jit(solution)/shard_map/ppermute | solution.py:82
  803.3 13.3 %collective-permute-done.38 = bf16[128,2048]{1,0:T(8,128)(2,1)S(1)} collective-permute-done((bf16[128,2048]{1,0:T(8,128)(2,1)S(1)}, bf16[128,2048]{1,0:T(8,128)(2,1)S(1)}, u32[]{:S(2)}, u32[]{:S(2)}) %collective-permute-start.38) | collective-permute-done | bytes 524320 | tf_op jit(solution)/shard_map/ppermute | solution.py:78
  820.0 4.6 multiply_reduce_fusion.5
  844.3 6.9 fusion.269
  851.2 19.7 %collective-permute-done.44 = bf16[128,2048]{1,0:T(8,128)(2,1)} collective-permute-done((bf16[128,2048]{1,0:T(8,128)(2,1)}, bf16[128,2048]{1,0:T(8,128)(2,1)}, u32[]{:S(2)}, u32[]{:S(2)}) %collective-permute-start.44) | collective-permute-done | bytes 524320 | tf_op jit(solution)/shard_map/ppermute | solution.py:78
  873.3 7.7 fusion.6
  881.0 5.4 fusion.23
  886.5 4.4 fusion.8
  924.2 4.0 convolution_bitcast_fusion
  928.2 12.6 %collective-permute-done.48 = bf16[128,2048]{1,0:T(8,128)(2,1)} collective-permute-done((bf16[128,2048]{1,0:T(8,128)(2,1)}, bf16[128,2048]{1,0:T(8,128)(2,1)}, u32[]{:S(2)}, u32[]{:S(2)}) %collective-permute-start.48) | collective-permute-done | bytes 524320 | tf_op jit(solution)/shard_map/ppermute | solution.py:78
  959.6 4.9 fusion.4
  964.5 30.7 %collective-permute-done.57 = bf16[256,1024]{1,0:T(8,128)(2,1)} collective-permute-done((bf16[256,1024]{1,0:T(8,128)(2,1)}, bf16[256,1024]{1,0:T(8,128)(2,1)}, u32[]{:S(2)}, u32[]{:S(2)}) %collective-permute-start.57) | collective-permute-done | bytes 524320 | tf_op jit(solution)/shard_map/ppermute | solution.py:915
  995.4 7.0 fusion.78
  1004.4 4.2 collective-permute-done.54
  1028.6 14.3 %collective-permute-start.61 = (bf16[256,2048]{1,0:T(8,128)(2,1)S(1)}, bf16[256,2048]{1,0:T(8,128)(2,1)}, u32[]{:S(2)}, u32[]{:S(2)}) collective-permute-start(bf16[256,2048]{1,0:T(8,128)(2,1)S(1)} %add_convert_fusion), channel_id=1, source_target_pairs={{0,4},{8,0},{16,8},{24,16},{28,24},{20,28},{12,20},{4,12},{1,5},{9... | collective-permute-start | bytes 3145736 | tf_op jit(solution)/shard_map/ppermute | solution.py:78
  1044.6 3.6 fusion.19
  1060.2 18.6 %collective-permute-done.60 = bf16[128,2048]{1,0:T(8,128)(2,1)S(1)} collective-permute-done((bf16[128,2048]{1,0:T(8,128)(2,1)S(1)}, bf16[128,2048]{1,0:T(8,128)(2,1)S(1)}, u32[]{:S(2)}, u32[]{:S(2)}) %collective-permute-start.60) | collective-permute-done | bytes 524320 | tf_op jit(solution)/shard_map/ppermute | solution.py:78
  1081.9 9.2 concatenate.198.refs_3_
  1091.1 110.5 %sum_all.1 = (f32[64,2048]{1,0:T(8,128)}, f32[64,1024]{1,0:T(8,128)}, f32[64,2048]{1,0:T(8,128)}, f32[64,768]{1,0:T(8,128)}) custom-call(bf16[8,2,2,64,2048]{4,3,2,1,0:T(8,128)(2,1)} %bitcast.355, bf16[8,2,2,64,1024]{4,3,2,1,0:T(8,128)(2,1)} %bitcast.369, bf16[8,2,2,64,2048]{4,3,2,1,0:T(8,128)(2,1)} %bitcast.354, ...), custom_call_target="tpu_custom_call" | custom-call | bytes 24117248 | tf_op jit(solution)/shard_map/sum_all/pallas_call | solution.py:483
  (796 shorter events, 376.2 us)
Async XLA Ops:
  4.8 134.4 %collective-permute-start = (bf16[3,128,2048]{2,1,0:T(8,128)(2,1)}, bf16[3,128,2048]{2,1,0:T(8,128)(2,1)}, u32[]{:S(2)}, u32[]{:S(2)}) collective-permute-start(bf16[3,128,2048]{2,1,0:T(8,128)(2,1)} %get-tuple-element.327), channel_id=1, source_target_pairs={{0,8},{8,16},{16,24},{24,28},{28,20},{20,12},{12,4},{4,0},{1,9},{9... | collective-permute-start | bytes 4718600 | tf_op jit(solution)/shard_map/ppermute | solution.py:78
  7.8 131.4 %collective-permute-start.1 = (bf16[3,128,2048]{2,1,0:T(8,128)(2,1)}, bf16[3,128,2048]{2,1,0:T(8,128)(2,1)S(1)}, u32[]{:S(2)}, u32[]{:S(2)}) collective-permute-start(bf16[3,128,2048]{2,1,0:T(8,128)(2,1)} %get-tuple-element.326), channel_id=1, source_target_pairs={{0,4},{8,0},{16,8},{24,16},{28,24},{20,28},{12,20},{4,12},{1,5},{9... | collective-permute-start | bytes 4718600 | tf_op jit(solution)/shard_map/ppermute | solution.py:78
  175.8 36.9 %collective-permute-start.2 = (bf16[3,128,2048]{2,1,0:T(8,128)(2,1)}, bf16[3,128,2048]{2,1,0:T(8,128)(2,1)S(1)}, u32[]{:S(2)}, u32[]{:S(2)}) collective-permute-start(bf16[3,128,2048]{2,1,0:T(8,128)(2,1)} %collective-permute-done), channel_id=1, source_target_pairs={{0,8},{8,16},{16,24},{24,28},{28,20},{20,12},{12,4},{4,0},{1,9},{9... | collective-permute-start | bytes 4718600 | tf_op jit(solution)/shard_map/ppermute | solution.py:78
  177.4 36.8 %collective-permute-start.3 = (bf16[3,128,2048]{2,1,0:T(8,128)(2,1)}, bf16[3,128,2048]{2,1,0:T(8,128)(2,1)S(1)}, u32[]{:S(2)}, u32[]{:S(2)}) collective-permute-start(bf16[3,128,2048]{2,1,0:T(8,128)(2,1)} %copy-done.83), channel_id=1, source_target_pairs={{0,4},{8,0},{16,8},{24,16},{28,24},{20,28},{12,20},{4,12},{1,5},{9... | collective-permute-start | bytes 4718600 | tf_op jit(solution)/shard_map/ppermute | solution.py:78
  215.4 6.6 collective-permute-start.6
  216.1 13.3 %collective-permute-start.7 = (bf16[256,1024]{1,0:T(8,128)(2,1)S(1)}, bf16[256,1024]{1,0:T(8,128)(2,1)}, u32[]{:S(2)}, u32[]{:S(2)}) collective-permute-start(bf16[256,1024]{1,0:T(8,128)(2,1)S(1)} %pad_maximum_fusion.17), channel_id=1, source_target_pairs={{0,4},{4,8},{8,12},{12,20},{1,5},{5,9},{9,13},{13,21},{2,6},{6,10}... | collective-permute-start | bytes 1572872 | tf_op jit(solution)/shard_map/ppermute | solution.py:672
  230.5 7.8 collective-permute-start.8
  233.2 36.9 %collective-permute-start.4 = (bf16[3,128,2048]{2,1,0:T(8,128)(2,1)}, bf16[3,128,2048]{2,1,0:T(8,128)(2,1)}, u32[]{:S(2)}, u32[]{:S(2)}) collective-permute-start(bf16[3,128,2048]{2,1,0:T(8,128)(2,1)} %copy-done.87), channel_id=1, source_target_pairs={{0,8},{8,16},{16,24},{24,28},{28,20},{20,12},{12,4},{4,0},{1,9},{9... | collective-permute-start | bytes 4718600 | tf_op jit(solution)/shard_map/ppermute | solution.py:78
  238.0 34.6 %collective-permute-start.5 = (bf16[3,128,2048]{2,1,0:T(8,128)(2,1)}, bf16[3,128,2048]{2,1,0:T(8,128)(2,1)}, u32[]{:S(2)}, u32[]{:S(2)}) collective-permute-start(bf16[3,128,2048]{2,1,0:T(8,128)(2,1)} %copy-done.85), channel_id=1, source_target_pairs={{0,4},{8,0},{16,8},{24,16},{28,24},{20,28},{12,20},{4,12},{1,5},{9... | collective-permute-start | bytes 4718600 | tf_op jit(solution)/shard_map/ppermute | solution.py:78
  238.4 4.5 collective-permute-start.9
  280.1 40.7 %collective-permute-start.10 = (bf16[3,128,2048]{2,1,0:T(8,128)(2,1)}, bf16[3,128,2048]{2,1,0:T(8,128)(2,1)}, u32[]{:S(2)}, u32[]{:S(2)}) collective-permute-start(bf16[3,128,2048]{2,1,0:T(8,128)(2,1)} %collective-permute-done.4), channel_id=1, source_target_pairs={{0,8},{8,16},{16,24},{24,28},{28,20},{20,12},{12,4},{4,0},{1,9},{9... | collective-permute-start | bytes 4718600 | tf_op jit(solution)/shard_map/ppermute | solution.py:78
  281.8 39.0 %collective-permute-start.11 = (bf16[3,128,2048]{2,1,0:T(8,128)(2,1)}, bf16[3,128,2048]{2,1,0:T(8,128)(2,1)}, u32[]{:S(2)}, u32[]{:S(2)}) collective-permute-start(bf16[3,128,2048]{2,1,0:T(8,128)(2,1)} %collective-permute-done.5), channel_id=1, source_target_pairs={{0,4},{8,0},{16,8},{24,16},{28,24},{20,28},{12,20},{4,12},{1,5},{9... | collective-permute-start | bytes 4718600 | tf_op jit(solution)/shard_map/ppermute | solution.py:78
  303.9 230.4 %copy-start.1 = (f32[256,2048]{1,0:T(8,128)}, f32[256,2048]{1,0:T(8,128)S(1)}, u32[]{:S(2)}) copy-start(f32[256,2048]{1,0:T(8,128)S(1)} %get-tuple-element.313) | copy-start | bytes 6291460
  320.8 22.1 %collective-permute-start.14 = (bf16[256,2048]{1,0:T(8,128)(2,1)S(1)}, bf16[256,2048]{1,0:T(8,128)(2,1)S(1)}, u32[]{:S(2)}, u32[]{:S(2)}) collective-permute-start(bf16[256,2048]{1,0:T(8,128)(2,1)S(1)} %multiply_convert_fusion.4), channel_id=1, source_target_pairs={{0,1},{1,0},{2,3},{3,2},{4,5},{5,4},{6,7},{7,6},{8,9},{9,8},{10,11... | collective-permute-start | bytes 3145736 | tf_op jit(solution)/shard_map/ppermute | solution.py:82
  343.2 13.7 %collective-permute-start.15 = (bf16[512,2048]{1,0:T(8,128)(2,1)S(1)}, bf16[512,2048]{1,0:T(8,128)(2,1)S(1)}, u32[]{:S(2)}, u32[]{:S(2)}) collective-permute-start(bf16[512,2048]{1,0:T(8,128)(2,1)S(1)} %pad_maximum_fusion.4), channel_id=1, source_target_pairs={{0,2},{2,0},{1,3},{3,1},{4,6},{6,4},{5,7},{7,5},{8,10},{10,8},{9,1... | collective-permute-start | bytes 6291464 | tf_op jit(solution)/shard_map/ppermute | solution.py:82
  347.0 38.8 %collective-permute-start.12 = (bf16[3,128,2048]{2,1,0:T(8,128)(2,1)}, bf16[3,128,2048]{2,1,0:T(8,128)(2,1)S(1)}, u32[]{:S(2)}, u32[]{:S(2)}) collective-permute-start(bf16[3,128,2048]{2,1,0:T(8,128)(2,1)} %collective-permute-done.10), channel_id=1, source_target_pairs={{0,8},{8,16},{16,24},{24,28},{28,20},{20,12},{12,4},{4,0},{1,9},{9... | collective-permute-start | bytes 4718600 | tf_op jit(solution)/shard_map/ppermute | solution.py:78
  351.2 44.8 %collective-permute-start.13 = (bf16[3,128,2048]{2,1,0:T(8,128)(2,1)}, bf16[3,128,2048]{2,1,0:T(8,128)(2,1)S(1)}, u32[]{:S(2)}, u32[]{:S(2)}) collective-permute-start(bf16[3,128,2048]{2,1,0:T(8,128)(2,1)} %collective-permute-done.11), channel_id=1, source_target_pairs={{0,4},{8,0},{16,8},{24,16},{28,24},{20,28},{12,20},{4,12},{1,5},{9... | collective-permute-start | bytes 4718600 | tf_op jit(solution)/shard_map/ppermute | solution.py:78
  396.0 36.1 %collective-permute-start.16 = (bf16[3,128,2048]{2,1,0:T(8,128)(2,1)S(1)}, bf16[3,128,2048]{2,1,0:T(8,128)(2,1)}, u32[]{:S(2)}, u32[]{:S(2)}) collective-permute-start(bf16[3,128,2048]{2,1,0:T(8,128)(2,1)S(1)} %collective-permute-done.12), channel_id=1, source_target_pairs={{0,8},{8,16},{16,24},{24,28},{28,20},{20,12},{12,4},{4,0},{1,9},{9... | collective-permute-start | bytes 4718600 | tf_op jit(solution)/shard_map/ppermute | solution.py:78
  397.7 35.7 %collective-permute-start.17 = (bf16[3,128,2048]{2,1,0:T(8,128)(2,1)S(1)}, bf16[3,128,2048]{2,1,0:T(8,128)(2,1)}, u32[]{:S(2)}, u32[]{:S(2)}) collective-permute-start(bf16[3,128,2048]{2,1,0:T(8,128)(2,1)S(1)} %collective-permute-done.13), channel_id=1, source_target_pairs={{0,4},{8,0},{16,8},{24,16},{28,24},{20,28},{12,20},{4,12},{1,5},{9... | collective-permute-start | bytes 4718600 | tf_op jit(solution)/shard_map/ppermute | solution.py:78
  433.4 34.8 %collective-permute-start.18 = (bf16[3,128,2048]{2,1,0:T(8,128)(2,1)}, bf16[3,128,2048]{2,1,0:T(8,128)(2,1)}, u32[]{:S(2)}, u32[]{:S(2)}) collective-permute-start(bf16[3,128,2048]{2,1,0:T(8,128)(2,1)} %collective-permute-done.16), channel_id=1, source_target_pairs={{0,8},{8,16},{16,24},{24,28},{28,20},{20,12},{12,4},{4,0},{1,9},{9... | collective-permute-start | bytes 4718600 | tf_op jit(solution)/shard_map/ppermute | solution.py:78
  434.8 34.5 %collective-permute-start.19 = (bf16[3,128,2048]{2,1,0:T(8,128)(2,1)}, bf16[3,128,2048]{2,1,0:T(8,128)(2,1)}, u32[]{:S(2)}, u32[]{:S(2)}) collective-permute-start(bf16[3,128,2048]{2,1,0:T(8,128)(2,1)} %collective-permute-done.17), channel_id=1, source_target_pairs={{0,4},{8,0},{16,8},{24,16},{28,24},{20,28},{12,20},{4,12},{1,5},{9... | collective-permute-start | bytes 4718600 | tf_op jit(solution)/shard_map/ppermute | solution.py:78
  496.4 4.2 collective-permute-start.20
  506.5 25.5 %collective-permute-start.21 = (bf16[256,2048]{1,0:T(8,128)(2,1)}, bf16[256,2048]{1,0:T(8,128)(2,1)}, u32[]{:S(2)}, u32[]{:S(2)}) collective-permute-start(bf16[256,2048]{1,0:T(8,128)(2,1)} %slice.873), channel_id=1, source_target_pairs={{0,1},{1,0},{2,3},{3,2},{4,5},{5,4},{6,7},{7,6},{8,9},{9,8},{10,11... | collective-permute-start | bytes 3145736 | tf_op jit(solution)/shard_map/ppermute | solution.py:82
  551.3 24.4 %collective-permute-start.27 = (bf16[256,2048]{1,0:T(8,128)(2,1)S(1)}, bf16[256,2048]{1,0:T(8,128)(2,1)S(1)}, u32[]{:S(2)}, u32[]{:S(2)}) collective-permute-start(bf16[256,2048]{1,0:T(8,128)(2,1)S(1)} %fusion.58), channel_id=1, source_target_pairs={{0,1},{1,0},{2,3},{3,2},{4,5},{5,4},{6,7},{7,6},{8,9},{9,8},{10,11... | collective-permute-start | bytes 3145736 | tf_op jit(solution)/shard_map/ppermute | solution.py:82
  577.4 25.6 %collective-permute-start.28 = (bf16[512,2048]{1,0:T(8,128)(2,1)}, bf16[512,2048]{1,0:T(8,128)(2,1)}, u32[]{:S(2)}, u32[]{:S(2)}) collective-permute-start(bf16[512,2048]{1,0:T(8,128)(2,1)} %pad_maximum_fusion.5), channel_id=1, source_target_pairs={{0,2},{2,0},{1,3},{3,1},{4,6},{6,4},{5,7},{7,5},{8,10},{10,8},{9,1... | collective-permute-start | bytes 6291464 | tf_op jit(solution)/shard_map/ppermute | solution.py:82
  578.6 3.3 collective-permute-start.22
  583.2 3.6 collective-permute-start.23
  588.1 3.6 collective-permute-start.24
  591.8 3.6 collective-permute-start.25
  595.4 6.5 collective-permute-start.26
  637.6 65.2 %collective-permute-start.31 = (bf16[256,2048]{1,0:T(8,128)(2,1)}, bf16[256,2048]{1,0:T(8,128)(2,1)S(1)}, u32[]{:S(2)}, u32[]{:S(2)}) collective-permute-start(bf16[256,2048]{1,0:T(8,128)(2,1)} %convolution_convert_fusion.2), channel_id=1, source_target_pairs={{0,4},{8,0},{16,8},{24,16},{28,24},{20,28},{12,20},{4,12},{1,5},{9... | collective-permute-start | bytes 3145736 | tf_op jit(solution)/shard_map/ppermute | solution.py:78
  641.2 61.6 %collective-permute-start.30 = (bf16[128,2048]{1,0:T(8,128)(2,1)S(1)}, bf16[128,2048]{1,0:T(8,128)(2,1)S(1)}, u32[]{:S(2)}, u32[]{:S(2)}) collective-permute-start(bf16[128,2048]{1,0:T(8,128)(2,1)S(1)} %get-tuple-element.429), channel_id=1, source_target_pairs={{0,8},{8,16},{16,24},{24,28},{28,20},{20,12},{12,4},{4,0},{1,9},{9... | collective-permute-start | bytes 1572872 | tf_op jit(solution)/shard_map/ppermute | solution.py:78
  642.7 60.1 %collective-permute-start.32 = (bf16[128,2048]{1,0:T(8,128)(2,1)S(1)}, bf16[128,2048]{1,0:T(8,128)(2,1)S(1)}, u32[]{:S(2)}, u32[]{:S(2)}) collective-permute-start(bf16[128,2048]{1,0:T(8,128)(2,1)S(1)} %get-tuple-element.428), channel_id=1, source_target_pairs={{0,4},{8,0},{16,8},{24,16},{28,24},{20,28},{12,20},{4,12},{1,5},{9... | collective-permute-start | bytes 1572872 | tf_op jit(solution)/shard_map/ppermute | solution.py:78
  645.5 57.2 %collective-permute-start.29 = (bf16[256,2048]{1,0:T(8,128)(2,1)}, bf16[256,2048]{1,0:T(8,128)(2,1)S(1)}, u32[]{:S(2)}, u32[]{:S(2)}) collective-permute-start(bf16[256,2048]{1,0:T(8,128)(2,1)} %convolution_convert_fusion.4), channel_id=1, source_target_pairs={{0,8},{8,16},{16,24},{24,28},{28,20},{20,12},{12,4},{4,0},{1,9},{9... | collective-permute-start | bytes 3145736 | tf_op jit(solution)/shard_map/ppermute | solution.py:78
  722.4 40.9 %collective-permute-start.35 = (bf16[256,2048]{1,0:T(8,128)(2,1)}, bf16[256,2048]{1,0:T(8,128)(2,1)}, u32[]{:S(2)}, u32[]{:S(2)}) collective-permute-start(bf16[256,2048]{1,0:T(8,128)(2,1)} %add_convert_fusion.10), channel_id=1, source_target_pairs={{0,4},{8,0},{16,8},{24,16},{28,24},{20,28},{12,20},{4,12},{1,5},{9... | collective-permute-start | bytes 3145736 | tf_op jit(solution)/shard_map/ppermute | solution.py:78
  724.2 39.1 %collective-permute-start.34 = (bf16[128,2048]{1,0:T(8,128)(2,1)}, bf16[128,2048]{1,0:T(8,128)(2,1)S(1)}, u32[]{:S(2)}, u32[]{:S(2)}) collective-permute-start(bf16[128,2048]{1,0:T(8,128)(2,1)} %get-tuple-element.367), channel_id=1, source_target_pairs={{0,8},{8,16},{16,24},{24,28},{28,20},{20,12},{12,4},{4,0},{1,9},{9... | collective-permute-start | bytes 1572872 | tf_op jit(solution)/shard_map/ppermute | solution.py:78
  725.7 37.6 %collective-permute-start.36 = (bf16[128,2048]{1,0:T(8,128)(2,1)}, bf16[128,2048]{1,0:T(8,128)(2,1)S(1)}, u32[]{:S(2)}, u32[]{:S(2)}) collective-permute-start(bf16[128,2048]{1,0:T(8,128)(2,1)} %get-tuple-element.366), channel_id=1, source_target_pairs={{0,4},{8,0},{16,8},{24,16},{28,24},{20,28},{12,20},{4,12},{1,5},{9... | collective-permute-start | bytes 1572872 | tf_op jit(solution)/shard_map/ppermute | solution.py:78
  727.5 35.8 %collective-permute-start.33 = (bf16[256,2048]{1,0:T(8,128)(2,1)}, bf16[256,2048]{1,0:T(8,128)(2,1)}, u32[]{:S(2)}, u32[]{:S(2)}) collective-permute-start(bf16[256,2048]{1,0:T(8,128)(2,1)} %add_convert_fusion.11), channel_id=1, source_target_pairs={{0,8},{8,16},{16,24},{24,28},{28,20},{20,12},{12,4},{4,0},{1,9},{9... | collective-permute-start | bytes 3145736 | tf_op jit(solution)/shard_map/ppermute | solution.py:78
  763.7 14.5 %collective-permute-start.41 = (bf16[512,2048]{1,0:T(8,128)(2,1)S(1)}, bf16[512,2048]{1,0:T(8,128)(2,1)S(1)}, u32[]{:S(2)}, u32[]{:S(2)}) collective-permute-start(bf16[512,2048]{1,0:T(8,128)(2,1)S(1)} %slice.870), channel_id=1, source_target_pairs={{0,2},{2,0},{1,3},{3,1},{4,6},{6,4},{5,7},{7,5},{8,10},{10,8},{9,1... | collective-permute-start | bytes 6291464 | tf_op jit(solution)/shard_map/ppermute | solution.py:82
  777.6 39.0 %collective-permute-start.39 = (bf16[256,2048]{1,0:T(8,128)(2,1)S(1)}, bf16[256,2048]{1,0:T(8,128)(2,1)S(1)}, u32[]{:S(2)}, u32[]{:S(2)}) collective-permute-start(bf16[256,2048]{1,0:T(8,128)(2,1)S(1)} %add_convert_fusion.8), channel_id=1, source_target_pairs={{0,4},{8,0},{16,8},{24,16},{28,24},{20,28},{12,20},{4,12},{1,5},{9... | collective-permute-start | bytes 3145736 | tf_op jit(solution)/shard_map/ppermute | solution.py:78
  779.3 23.6 %collective-permute-start.42 = (bf16[256,2048]{1,0:T(8,128)(2,1)S(1)}, bf16[256,2048]{1,0:T(8,128)(2,1)S(1)}, u32[]{:S(2)}, u32[]{:S(2)}) collective-permute-start(bf16[256,2048]{1,0:T(8,128)(2,1)S(1)} %slice.872), channel_id=1, source_target_pairs={{0,1},{1,0},{2,3},{3,2},{4,5},{5,4},{6,7},{7,6},{8,9},{9,8},{10,11... | collective-permute-start | bytes 3145736 | tf_op jit(solution)/shard_map/ppermute | solution.py:82
  781.8 34.8 %collective-permute-start.37 = (bf16[256,2048]{1,0:T(8,128)(2,1)S(1)}, bf16[256,2048]{1,0:T(8,128)(2,1)S(1)}, u32[]{:S(2)}, u32[]{:S(2)}) collective-permute-start(bf16[256,2048]{1,0:T(8,128)(2,1)S(1)} %add_convert_fusion.9), channel_id=1, source_target_pairs={{0,8},{8,16},{16,24},{24,28},{28,20},{20,12},{12,4},{4,0},{1,9},{9... | collective-permute-start | bytes 3145736 | tf_op jit(solution)/shard_map/ppermute | solution.py:78
  783.6 33.0 %collective-permute-start.38 = (bf16[128,2048]{1,0:T(8,128)(2,1)S(1)}, bf16[128,2048]{1,0:T(8,128)(2,1)S(1)}, u32[]{:S(2)}, u32[]{:S(2)}) collective-permute-start(bf16[128,2048]{1,0:T(8,128)(2,1)S(1)} %get-tuple-element.365), channel_id=1, source_target_pairs={{0,8},{8,16},{16,24},{24,28},{28,20},{20,12},{12,4},{4,0},{1,9},{9... | collective-permute-start | bytes 1572872 | tf_op jit(solution)/shard_map/ppermute | solution.py:78
  784.1 32.5 %collective-permute-start.40 = (bf16[128,2048]{1,0:T(8,128)(2,1)S(1)}, bf16[128,2048]{1,0:T(8,128)(2,1)S(1)}, u32[]{:S(2)}, u32[]{:S(2)}) collective-permute-start(bf16[128,2048]{1,0:T(8,128)(2,1)S(1)} %get-tuple-element.364), channel_id=1, source_target_pairs={{0,4},{8,0},{16,8},{24,16},{28,24},{20,28},{12,20},{4,12},{1,5},{9... | collective-permute-start | bytes 1572872 | tf_op jit(solution)/shard_map/ppermute | solution.py:78
  834.7 36.3 %collective-permute-start.45 = (bf16[256,2048]{1,0:T(8,128)(2,1)}, bf16[256,2048]{1,0:T(8,128)(2,1)}, u32[]{:S(2)}, u32[]{:S(2)}) collective-permute-start(bf16[256,2048]{1,0:T(8,128)(2,1)} %add_convert_fusion.6), channel_id=1, source_target_pairs={{0,4},{8,0},{16,8},{24,16},{28,24},{20,28},{12,20},{4,12},{1,5},{9... | collective-permute-start | bytes 3145736 | tf_op jit(solution)/shard_map/ppermute | solution.py:78
  836.8 34.2 %collective-permute-start.43 = (bf16[256,2048]{1,0:T(8,128)(2,1)}, bf16[256,2048]{1,0:T(8,128)(2,1)}, u32[]{:S(2)}, u32[]{:S(2)}) collective-permute-start(bf16[256,2048]{1,0:T(8,128)(2,1)} %add_convert_fusion.7), channel_id=1, source_target_pairs={{0,8},{8,16},{16,24},{24,28},{28,20},{20,12},{12,4},{4,0},{1,9},{9... | collective-permute-start | bytes 3145736 | tf_op jit(solution)/shard_map/ppermute | solution.py:78
  839.6 31.3 %collective-permute-start.44 = (bf16[128,2048]{1,0:T(8,128)(2,1)}, bf16[128,2048]{1,0:T(8,128)(2,1)}, u32[]{:S(2)}, u32[]{:S(2)}) collective-permute-start(bf16[128,2048]{1,0:T(8,128)(2,1)} %get-tuple-element.363), channel_id=1, source_target_pairs={{0,8},{8,16},{16,24},{24,28},{28,20},{20,12},{12,4},{4,0},{1,9},{9... | collective-permute-start | bytes 1572872 | tf_op jit(solution)/shard_map/ppermute | solution.py:78
  841.1 29.8 %collective-permute-start.46 = (bf16[128,2048]{1,0:T(8,128)(2,1)S(1)}, bf16[128,2048]{1,0:T(8,128)(2,1)}, u32[]{:S(2)}, u32[]{:S(2)}) collective-permute-start(bf16[128,2048]{1,0:T(8,128)(2,1)S(1)} %get-tuple-element.362), channel_id=1, source_target_pairs={{0,4},{8,0},{16,8},{24,16},{28,24},{20,28},{12,20},{4,12},{1,5},{9... | collective-permute-start | bytes 1572872 | tf_op jit(solution)/shard_map/ppermute | solution.py:78
  904.0 36.8 %collective-permute-start.49 = (bf16[256,2048]{1,0:T(8,128)(2,1)}, bf16[256,2048]{1,0:T(8,128)(2,1)}, u32[]{:S(2)}, u32[]{:S(2)}) collective-permute-start(bf16[256,2048]{1,0:T(8,128)(2,1)} %add_convert_fusion.4), channel_id=1, source_target_pairs={{0,4},{8,0},{16,8},{24,16},{28,24},{20,28},{12,20},{4,12},{1,5},{9... | collective-permute-start | bytes 3145736 | tf_op jit(solution)/shard_map/ppermute | solution.py:78
  908.1 32.7 %collective-permute-start.47 = (bf16[256,2048]{1,0:T(8,128)(2,1)}, bf16[256,2048]{1,0:T(8,128)(2,1)}, u32[]{:S(2)}, u32[]{:S(2)}) collective-permute-start(bf16[256,2048]{1,0:T(8,128)(2,1)} %add_convert_fusion.5), channel_id=1, source_target_pairs={{0,8},{8,16},{16,24},{24,28},{28,20},{20,12},{12,4},{4,0},{1,9},{9... | collective-permute-start | bytes 3145736 | tf_op jit(solution)/shard_map/ppermute | solution.py:78
  911.1 29.7 %collective-permute-start.48 = (bf16[128,2048]{1,0:T(8,128)(2,1)}, bf16[128,2048]{1,0:T(8,128)(2,1)}, u32[]{:S(2)}, u32[]{:S(2)}) collective-permute-start(bf16[128,2048]{1,0:T(8,128)(2,1)} %get-tuple-element.359), channel_id=1, source_target_pairs={{0,8},{8,16},{16,24},{24,28},{28,20},{20,12},{12,4},{4,0},{1,9},{9... | collective-permute-start | bytes 1572872 | tf_op jit(solution)/shard_map/ppermute | solution.py:78
  912.2 28.6 %collective-permute-start.50 = (bf16[128,2048]{1,0:T(8,128)(2,1)}, bf16[128,2048]{1,0:T(8,128)(2,1)}, u32[]{:S(2)}, u32[]{:S(2)}) collective-permute-start(bf16[128,2048]{1,0:T(8,128)(2,1)} %get-tuple-element.358), channel_id=1, source_target_pairs={{0,4},{8,0},{16,8},{24,16},{28,24},{20,28},{12,20},{4,12},{1,5},{9... | collective-permute-start | bytes 1572872 | tf_op jit(solution)/shard_map/ppermute | solution.py:78
  940.9 12.4 %collective-permute-start.55 = (bf16[256,1024]{1,0:T(8,128)(2,1)S(1)}, bf16[256,1024]{1,0:T(8,128)(2,1)S(1)}, u32[]{:S(2)}, u32[]{:S(2)}) collective-permute-start(bf16[256,1024]{1,0:T(8,128)(2,1)S(1)} %slice.874), channel_id=1, source_target_pairs={{0,2},{2,0},{1,3},{3,1},{4,6},{6,4},{5,7},{7,5},{8,10},{10,8},{9,1... | collective-permute-start | bytes 1572872 | tf_op jit(solution)/shard_map/ppermute | solution.py:82
  943.7 64.9 %collective-permute-start.53 = (bf16[256,2048]{1,0:T(8,128)(2,1)}, bf16[256,2048]{1,0:T(8,128)(2,1)}, u32[]{:S(2)}, u32[]{:S(2)}) collective-permute-start(bf16[256,2048]{1,0:T(8,128)(2,1)} %add_convert_fusion.2), channel_id=1, source_target_pairs={{0,4},{8,0},{16,8},{24,16},{28,24},{20,28},{12,20},{4,12},{1,5},{9... | collective-permute-start | bytes 3145736 | tf_op jit(solution)/shard_map/ppermute | solution.py:78
  947.2 57.2 %collective-permute-start.52 = (bf16[128,2048]{1,0:T(8,128)(2,1)}, bf16[128,2048]{1,0:T(8,128)(2,1)}, u32[]{:S(2)}, u32[]{:S(2)}) collective-permute-start(bf16[128,2048]{1,0:T(8,128)(2,1)} %get-tuple-element.357), channel_id=1, source_target_pairs={{0,8},{8,16},{16,24},{24,28},{28,20},{20,12},{12,4},{4,0},{1,9},{9... | collective-permute-start | bytes 1572872 | tf_op jit(solution)/shard_map/ppermute | solution.py:78
  951.1 57.5 %collective-permute-start.51 = (bf16[256,2048]{1,0:T(8,128)(2,1)}, bf16[256,2048]{1,0:T(8,128)(2,1)}, u32[]{:S(2)}, u32[]{:S(2)}) collective-permute-start(bf16[256,2048]{1,0:T(8,128)(2,1)} %add_convert_fusion.3), channel_id=1, source_target_pairs={{0,8},{8,16},{16,24},{24,28},{28,20},{20,12},{12,4},{4,0},{1,9},{9... | collective-permute-start | bytes 3145736 | tf_op jit(solution)/shard_map/ppermute | solution.py:78
  953.4 2.2 collective-permute-start.56
  956.7 38.4 %collective-permute-start.57 = (bf16[256,1024]{1,0:T(8,128)(2,1)}, bf16[256,1024]{1,0:T(8,128)(2,1)}, u32[]{:S(2)}, u32[]{:S(2)}) collective-permute-start(bf16[256,1024]{1,0:T(8,128)(2,1)} %add_convert_fusion.14), channel_id=1, source_target_pairs={{4,0},{8,4},{12,8},{20,12},{5,1},{9,5},{13,9},{21,13},{6,2},{10,6}... | collective-permute-start | bytes 1572872 | tf_op jit(solution)/shard_map/ppermute | solution.py:915
  958.0 44.4 %collective-permute-start.58 = (bf16[256,1024]{1,0:T(8,128)(2,1)}, bf16[256,1024]{1,0:T(8,128)(2,1)}, u32[]{:S(2)}, u32[]{:S(2)}) collective-permute-start(bf16[256,1024]{1,0:T(8,128)(2,1)} %add_convert_fusion.14), channel_id=1, source_target_pairs={{16,12},{17,13},{18,14},{19,15}} | collective-permute-start | bytes 1572872 | tf_op jit(solution)/shard_map/ppermute | solution.py:916
  995.2 13.4 %collective-permute-start.54 = (bf16[128,2048]{1,0:T(8,128)(2,1)}, bf16[128,2048]{1,0:T(8,128)(2,1)S(1)}, u32[]{:S(2)}, u32[]{:S(2)}) collective-permute-start(bf16[128,2048]{1,0:T(8,128)(2,1)} %get-tuple-element.356), channel_id=1, source_target_pairs={{0,4},{8,0},{16,8},{24,16},{28,24},{20,28},{12,20},{4,12},{1,5},{9... | collective-permute-start | bytes 1572872 | tf_op jit(solution)/shard_map/ppermute | solution.py:78
  1028.6 50.2 %collective-permute-start.61 = (bf16[256,2048]{1,0:T(8,128)(2,1)S(1)}, bf16[256,2048]{1,0:T(8,128)(2,1)}, u32[]{:S(2)}, u32[]{:S(2)}) collective-permute-start(bf16[256,2048]{1,0:T(8,128)(2,1)S(1)} %add_convert_fusion), channel_id=1, source_target_pairs={{0,4},{8,0},{16,8},{24,16},{28,24},{20,28},{12,20},{4,12},{1,5},{9... | collective-permute-start | bytes 3145736 | tf_op jit(solution)/shard_map/ppermute | solution.py:78
  1044.5 34.4 %collective-permute-start.59 = (bf16[256,2048]{1,0:T(8,128)(2,1)S(1)}, bf16[256,2048]{1,0:T(8,128)(2,1)}, u32[]{:S(2)}, u32[]{:S(2)}) collective-permute-start(bf16[256,2048]{1,0:T(8,128)(2,1)S(1)} %add_convert_fusion.1), channel_id=1, source_target_pairs={{0,8},{8,16},{16,24},{24,28},{28,20},{20,12},{12,4},{4,0},{1,9},{9... | collective-permute-start | bytes 3145736 | tf_op jit(solution)/shard_map/ppermute | solution.py:78
  1052.2 26.7 %collective-permute-start.60 = (bf16[128,2048]{1,0:T(8,128)(2,1)S(1)}, bf16[128,2048]{1,0:T(8,128)(2,1)S(1)}, u32[]{:S(2)}, u32[]{:S(2)}) collective-permute-start(bf16[128,2048]{1,0:T(8,128)(2,1)S(1)} %get-tuple-element.355), channel_id=1, source_target_pairs={{0,8},{8,16},{16,24},{24,28},{28,20},{20,12},{12,4},{4,0},{1,9},{9... | collective-permute-start | bytes 1572872 | tf_op jit(solution)/shard_map/ppermute | solution.py:78
  1052.2 26.6 %collective-permute-start.62 = (bf16[128,2048]{1,0:T(8,128)(2,1)S(1)}, bf16[128,2048]{1,0:T(8,128)(2,1)S(1)}, u32[]{:S(2)}, u32[]{:S(2)}) collective-permute-start(bf16[128,2048]{1,0:T(8,128)(2,1)S(1)} %get-tuple-element.354), channel_id=1, source_target_pairs={{0,4},{8,0},{16,8},{24,16},{28,24},{20,28},{12,20},{4,12},{1,5},{9... | collective-permute-start | bytes 1572872 | tf_op jit(solution)/shard_map/ppermute | solution.py:78
  (217 other events, 3100.0 us)

commit v3 on v2

--- a/solution.py
+++ b/solution.py
@@ -26,23 +26,6 @@
 
 def rms_norm(values, gain):
     return values * lax.rsqrt(jnp.mean(values * values, axis=-1, keepdims=True) + EPSILON) * gain
-
-
-def plain_norm(values):
-    return values * lax.rsqrt(jnp.mean(values * values, axis=-1, keepdims=True) + EPSILON)
-
-
-def rotate(values, places):
-    half_dim = values.shape[-1] // 2
-    freqs = jnp.exp(
-        jnp.arange(half_dim, dtype=F32) * (-2.0 * math.log(ROPE_BASE) / values.shape[-1])
-    )
-    angles = places.astype(F32)[:, None, None] * freqs
-    cosine = jnp.cos(angles)
-    sine = jnp.sin(angles)
-    first = values[..., :half_dim]
-    second = values[..., half_dim:]
-    return jnp.concatenate([first * cosine - second * sine, second * cosine + first * sine], -1)
 
 
 def gelu_tanh(values):
@@ -261,8 +244,9 @@
 
 
 def sum_kernel(chips, streams, counts, *refs):
-    arrays, outs, held, core_in, ring_in, x_in, sems = refs_of(counts, refs)
-    load_sem, core_send, core_recv, ring_send, ring_recv, x_send, x_recv = sems
+    arrays, (tile,), outs, (tile_out,), held, core_in, ring_in, x_in, tiles, sems = refs_of(counts, refs)
+    load_sem, core_send, core_recv, ring_send, ring_recv, x_send, x_recv, tile_send, tile_recv = sems
+    tile_pairs, tile_ring = tiles
     chip = lax.axis_index("zy")
     core = lax.axis_index("core")
     side = lax.axis_index("fsdp")
@@ -340,9 +324,24 @@
             core_copy(number, turn).start()
         return carry
 
+    def tile_copy(src, dst, number, peer):
+        return remote(src, dst, tile_send.at[number], tile_recv.at[number], peer)
+
+    def tile_turn(turn):
+        spot_ref = tile_ring.at[ring_chip(spot + 2 * chips - turn + 1, chips)]
+        return tile_copy(spot_ref, spot_ref, turn + 1, neighbour(1))
+
+    def tile_arrival(turn):
+        spot_ref = tile_ring.at[ring_chip(spot + 2 * chips - turn, chips)]
+        return tile_copy(spot_ref, spot_ref, turn + 1, neighbour(1))
+
+    tile_copy(tile, tile_pairs.at[0], 0, other_core).start()
     lax.fori_loop(1, 2, send_cores, 0)
     for load in loads:
         load.start()
+    tile_copy(tile, tile_pairs.at[0], 0, other_core).wait()
+    tile_pairs[1] = tile[...] + tile_pairs[0]
+    tile_copy(tile_pairs.at[1], tile_pairs.at[2], 1, other_side).start()
     lax.fori_loop(2, chips + 1, send_cores, 0)
     for load in loads:
         load.wait()
@@ -364,8 +363,18 @@
                 x_copy(number, turn).start()
 
     begin(1)
+    tile_copy(tile_pairs.at[1], tile_pairs.at[2], 1, other_side).wait()
+    tile_ring[chip] = tile_pairs[1] + tile_pairs[2]
 
     def round_trip(turn, carry):
+        @pl.when(turn > 1)
+        def _():
+            tile_arrival(turn - 1).wait_recv()
+
+        @pl.when(turn < chips)
+        def _():
+            tile_turn(turn).start()
+
         @pl.when(turn < chips)
         def _():
             begin(turn + 1)
@@ -426,6 +435,7 @@
     for number in numbers:
         if not streams[number][4]:
             x_copy(number, chips).start()
+    tile_out[...] = lax.fori_loop(1, chips, lambda i, total: total + tile_ring[i], tile_ring[0])
     for number in numbers:
         array = streams[number][0]
         if not streams[number][4]:
@@ -444,6 +454,10 @@
             def _(number=number):
                 ring_copy(number, turn).wait_send()
 
+        @pl.when(turn < chips)
+        def _():
+            tile_turn(turn).wait_send()
+
         return carry
 
     lax.fori_loop(1, chips + 1, drain, 0)
@@ -460,7 +474,7 @@
     return groups
 
 
-def sum_all(arrays, firsts, chips):
+def sum_all(arrays, firsts, tile, chips):
     rows = arrays[0].shape[0] // (4 * chips)
     streams = []
     for i, (array, first) in enumerate(zip(arrays, firsts)):
@@ -477,16 +491,19 @@
         + [vmem((chips, 2, rows, a.shape[1]), BF16) for a in arrays]
         + [vmem((chips - 1, 1 if first else 2, rows, width), BF16) for _, _, width, _, first in streams]
         + [vmem((chips if first else 1, rows, width), BF16) for _, _, width, _, first in streams]
+        + [vmem((3, 8, 128), F32), vmem((chips, 8, 128), F32)]
         + [dma((count,))]
         + [dma((number, chips)) for _ in range(6)]
+        + [dma((chips + 1,)) for _ in range(2)]
     )
     return pl.pallas_call(
         functools.partial(
-            sum_kernel, chips, streams, (count, count, count, count, number, number, 7)
+            sum_kernel, chips, streams, (count, 1, count, 1, count, count, number, number, 2, 9)
         ),
-        out_shape=[jax.ShapeDtypeStruct((rows, a.shape[1]), F32) for a in arrays],
-        in_specs=[pl.BlockSpec(memory_space=pl.ANY)] * count,
-        out_specs=[pl.BlockSpec(memory_space=pltpu.VMEM)] * count,
+        out_shape=[jax.ShapeDtypeStruct((rows, a.shape[1]), F32) for a in arrays]
+        + [jax.ShapeDtypeStruct((8, 128), F32)],
+        in_specs=[pl.BlockSpec(memory_space=pl.ANY)] * count + [pl.BlockSpec(memory_space=pltpu.VMEM)],
+        out_specs=[pl.BlockSpec(memory_space=pltpu.VMEM)] * (count + 1),
         scratch_shapes=scratch,
         compiler_params=pltpu.CompilerParams(
             collective_id=1, has_side_effects=True, vmem_limit_bytes=56 << 20
@@ -495,7 +512,522 @@
             flops=0, bytes_accessed=sum(2 * a.size for a in arrays), transcendentals=0
         ),
         name="sum_all",
-    )(*[a.reshape(chips, 2, 2, rows, a.shape[1]) for a in arrays])
+    )(*[a.reshape(chips, 2, 2, rows, a.shape[1]) for a in arrays], tile)
+
+
+LITTLE = pl.CostEstimate(flops=0, bytes_accessed=1024, transcendentals=0)
+VMEM_LIMIT = 56 << 20
+
+
+def whole(shape):
+    return pl.BlockSpec(shape, lambda *_: (0,) * len(shape))
+
+
+def piece(kernel, name, grid, in_specs, out_specs, out_shapes, scratch=()):
+    return pl.pallas_call(
+        kernel,
+        grid=grid,
+        in_specs=in_specs,
+        out_specs=out_specs,
+        out_shape=[jax.ShapeDtypeStruct(shape, dtype) for shape, dtype in out_shapes],
+        scratch_shapes=list(scratch),
+        compiler_params=pltpu.CompilerParams(vmem_limit_bytes=VMEM_LIMIT),
+        cost_estimate=LITTLE,
+        name=name,
+    )
+
+
+def inverse_rms(values):
+    return lax.rsqrt(jnp.mean(values * values, axis=-1, keepdims=True) + EPSILON)
+
+
+def norm_back(values, gain, grad):
+    scale = inverse_rms(values)
+    scaled = grad * gain
+    mean = jnp.mean(values * scaled, axis=-1, keepdims=True)
+    back = scale * scaled - values * (scale * scale * scale * mean)
+    return back, jnp.sum(grad * (values * scale), axis=0, keepdims=True)
+
+
+def qkv_kernel(tokens, gains, head_gain, cosine, sine, weight, low, raw, new):
+    at = pl.program_id(0)
+
+    @pl.when(at == 0)
+    def _():
+        states = tokens[...].astype(F32)
+        low[...] = (states * inverse_rms(states) * gains[0:1]).astype(BF16)
+
+    out = full_dot(low[...], weight[...])
+    raw[...] = out
+    plain = out * inverse_rms(out)
+    values = plain * jnp.where(at < HEADS, head_gain[0:1], head_gain[1:2])
+    half = HEAD // 2
+    first, second = values[:, :half], values[:, half:]
+    turned = jnp.concatenate(
+        [first * cosine[...] - second * sine[...], second * cosine[...] + first * sine[...]], 1
+    )
+    new[...] = jnp.where(at < HEADS + KV_HEADS, turned, plain).astype(BF16)
+
+
+def make_qkv(tokens, gains, head_gain, cosine, sine, full):
+    rows = tokens.shape[0]
+    heads = HEADS + 2 * KV_HEADS
+    return piece(
+        qkv_kernel,
+        "make_qkv",
+        (heads,),
+        [
+            whole((rows, D)),
+            whole(gains.shape),
+            whole((2, HEAD)),
+            whole(cosine.shape),
+            whole(sine.shape),
+            pl.BlockSpec((D, HEAD), lambda i: (0, HEADS + i)),
+        ],
+        [
+            whole((rows, D)),
+            pl.BlockSpec((rows, HEAD), lambda i: (0, i)),
+            pl.BlockSpec((rows, HEAD), lambda i: (0, i)),
+        ],
+        [((rows, D), BF16), ((rows, heads * HEAD), F32), ((rows, heads * HEAD), BF16)],
+    )(tokens, gains, head_gain, cosine, sine, full)
+
+
+def softmax_of(query, key, visible):
+    scores = jnp.where(visible > 0.0, right_dot(query, key), -1e30)
+    expo = jnp.exp(scores - jnp.max(scores, axis=-1, keepdims=True))
+    return expo / jnp.sum(expo, axis=-1, keepdims=True)
+
+
+def attend_kernel(
+    tokens, gains, low, query, key, value, visible, w_out, lleft, lright,
+    context, attn_raw, mixed, ffn_in, mid,
+):
+    at = pl.program_id(0)
+    probs = softmax_of(query[...], key[...], visible[...]).astype(BF16)
+    here = full_dot(probs, value[...]).astype(BF16)
+    context[...] = here
+    term = full_dot(here, w_out[...])
+
+    @pl.when(at == 0)
+    def _():
+        attn_raw[...] = term
+
+    @pl.when(at > 0)
+    def _():
+        attn_raw[...] += term
+
+    @pl.when(at == HEADS - 1)
+    def _():
+        states = tokens[...].astype(F32)
+        raw = attn_raw[...]
+        total = states + raw * inverse_rms(raw) * gains[1:2]
+        total = total + states * inverse_rms(states) * gains[0:1]
+        mid[...] = full_dot(low[...], lleft[...]).astype(BF16)
+        laurel = right_dot(mid[...], lright[...])
+        total = (total + laurel * inverse_rms(laurel) * gains[2:3]) * INV_SQRT2
+        mixed[...] = total
+        ffn_in[...] = (total * inverse_rms(total) * gains[3:4]).astype(BF16)
+
+
+def attend(tokens, gains, low, qkv, keys_all, visible, full):
+    rows = tokens.shape[0]
+    seen = keys_all.shape[0]
+    group = HEADS // KV_HEADS
+    side = 128
+    left_at, right_at = full.shape[1] // side - 2, full.shape[1] // side - 1
+    return piece(
+        attend_kernel,
+        "attend",
+        (HEADS,),
+        [
+            whole((rows, D)),
+            whole(gains.shape),
+            whole((rows, D)),
+            pl.BlockSpec((rows, HEAD), lambda i: (0, i)),
+            pl.BlockSpec((seen, HEAD), lambda i: (0, i // group)),
+            pl.BlockSpec((seen, HEAD), lambda i: (0, KV_HEADS + i // group)),
+            whole((rows, seen)),
+            pl.BlockSpec((HEAD, D), lambda i: (i, 0)),
+            pl.BlockSpec((D, side), lambda i: (0, left_at)),
+            pl.BlockSpec((D, side), lambda i: (0, right_at)),
+        ],
+        [
+            pl.BlockSpec((rows, HEAD), lambda i: (0, i)),
+            whole((rows, D)),
+            whole((rows, D)),
+            whole((rows, D)),
+            whole((rows, side)),
+        ],
+        [
+            ((rows, HEADS * HEAD), BF16),
+            ((rows, D), F32),
+            ((rows, D), F32),
+            ((rows, D), BF16),
+            ((rows, side), BF16),
+        ],
+    )(tokens, gains, low, qkv, keys_all, keys_all, visible, full, full, full)
+
+
+def load_weights(weights, held, sems):
+    copies, at = [], 0
+    for number, ref in enumerate(weights):
+        count = ref.shape[1]
+        copies.append(pltpu.make_async_copy(ref, held.at[:, pl.ds(at, count)], sems.at[number]))
+        at += count
+    return copies
+
+
+UNIT_BLOCK = 256
+
+
+def ffn_forward_kernel(count, add, *refs):
+    weights, refs = refs[:count], refs[count:]
+    if add:
+        before, refs = refs[0], refs[1:]
+    rows, total, gate, upper, hidden, held, sems = refs
+    copies = load_weights(weights, held, sems)
+
+    @pl.when(pl.program_id(0) == 0)
+    def _():
+        for copy in copies:
+            copy.start()
+        for copy in copies:
+            copy.wait()
+
+    here = rows[...]
+    running = before[...] if add else None
+    for first in range(0, held.shape[1], UNIT_BLOCK):
+        cut = slice(first, first + UNIT_BLOCK)
+        gate_in = right_dot(here, held[0, cut])
+        upper_in = right_dot(here, held[1, cut])
+        low = gated_product(gate_in, upper_in).astype(BF16)
+        gate[:, cut] = gate_in
+        upper[:, cut] = upper_in
+        hidden[:, cut] = low
+        term = full_dot(low, held[2, cut])
+        running = term if running is None else running + term
+    total[...] = running
+
+
+def ffn_forward(rows, before, weights):
+    many, step = rows.shape[0], 256
+    units = sum(w.shape[1] for w in weights)
+    by_row = lambda width: pl.BlockSpec((step, width), lambda i: (i, 0))
+    add = before is not None
+    return piece(
+        functools.partial(ffn_forward_kernel, len(weights), add),
+        "ffn_forward",
+        (many // step,),
+        [pl.BlockSpec(memory_space=pl.ANY)] * len(weights) + [by_row(D)] * (1 + add),
+        [by_row(D), by_row(units), by_row(units), by_row(units)],
+        [((many, D), F32), ((many, units), F32), ((many, units), F32), ((many, units), BF16)],
+        [pltpu.VMEM((3, units, D), BF16), pltpu.SemaphoreType.DMA((len(weights),))],
+    )(*weights, *([before] if add else []), rows)
+
+
+def ffn_backward_kernel(count, widths, add, *refs):
+    weights, refs = refs[:count], refs[count:]
+    if add:
+        before, refs = refs[0], refs[1:]
+    number = len(widths)
+    rows, refs = refs[0], refs[1:]
+    gates, uppers, refs = refs[:number], refs[number : 2 * number], refs[2 * number :]
+    total, refs = refs[0], refs[1:]
+    grad_gates, grad_uppers, (held, sems) = refs[:number], refs[number : 2 * number], refs[2 * number :]
+    copies = load_weights(weights, held, sems)
+
+    @pl.when(pl.program_id(0) == 0)
+    def _():
+        for copy in copies:
+            copy.start()
+        for copy in copies:
+            copy.wait()
+
+    here = rows[...]
+    running = before[...] if add else None
+    at = 0
+    for gate, upper, grad_gate, grad_upper, width in zip(gates, uppers, grad_gates, grad_uppers, widths):
+        for first in range(0, width, UNIT_BLOCK):
+            cut = slice(first, first + UNIT_BLOCK)
+            held_cut = slice(at + first, at + first + UNIT_BLOCK)
+            unused, act_back = jax.vjp(gated_product, gate[:, cut], upper[:, cut])
+            back_gate, back_upper = act_back(right_dot(here, held[2, held_cut]))
+            low_gate, low_upper = back_gate.astype(BF16), back_upper.astype(BF16)
+            grad_gate[:, cut] = low_gate
+            grad_upper[:, cut] = low_upper
+            term = full_dot(low_gate, held[0, held_cut]) + full_dot(low_upper, held[1, held_cut])
+            running = term if running is None else running + term
+        at += width
+    total[...] = running
+
+
+def ffn_backward(rows, before, weights, gates, uppers):
+    many, step = rows.shape[0], 256
+    widths = tuple(gate.shape[1] for gate in gates)
+    by_row = lambda width: pl.BlockSpec((step, width), lambda i: (i, 0))
+    add = before is not None
+    blocks = [by_row(width) for width in widths]
+    lows = [((many, width), BF16) for width in widths]
+    total, *grads = piece(
+        functools.partial(ffn_backward_kernel, len(weights), widths, add),
+        "ffn_backward",
+        (many // step,),
+        [pl.BlockSpec(memory_space=pl.ANY)] * len(weights) + [by_row(D)] * (1 + add) + blocks * 2,
+        [by_row(D)] + blocks * 2,
+        [((many, D), F32)] + lows * 2,
+        [pltpu.VMEM((3, sum(widths), D), BF16), pltpu.SemaphoreType.DMA((len(weights),))],
+    )(*weights, *([before] if add else []), rows, *gates, *uppers)
+    return total, list(zip(grads[: len(widths)], grads[len(widths) :]))
+
+
+def unit_grads_kernel(grad_gate, grad_upper, hidden, rows, down_rows, out):
+    out[0] = left_dot(grad_gate[...], rows[...])
+    out[1] = left_dot(grad_upper[...], rows[...])
+    out[2] = left_dot(hidden[...], down_rows[...])
+
+
+def unit_grads_of(at, units, grad_gate, grad_upper, hidden, rows, down_rows):
+    if units % 128:
+        cut = slice(at * units, (at + 1) * units)
+        return jnp.stack(
+            [
+                left_dot(grad_gate[:, cut], rows),
+                left_dot(grad_upper[:, cut], rows),
+                left_dot(hidden[:, cut], down_rows),
+            ]
+        )
+    many, width = rows.shape[0], 512
+    narrow = pl.BlockSpec((many, units), lambda i: (0, at))
+    wide = pl.BlockSpec((many, width), lambda i: (0, i))
+    return piece(
+        unit_grads_kernel,
+        "unit_grads",
+        (D // width,),
+        [narrow, narrow, narrow, wide, wide],
+        [pl.BlockSpec((3, units, width), lambda i: (0, 0, i))],
+        [((3, units, D), F32)],
+    )(grad_gate, grad_upper, hidden, rows, down_rows)[0]
+
+
+def attend_back_kernel(
+    gains, grad_in, grad_after, mixed, attn_raw, mid, low, lleft, lright, w_out, context, query, key, value, visible,
+    grad_mixed, grad_mid, grad_gains, grad_left, grad_right, grad_w_out, grad_query, grad_key, grad_value,
+    grad_attn,
+):
+    at = pl.program_id(0)
+
+    @pl.when(at == 0)
+    def _():
+        back, gain_3 = norm_back(mixed[...], gains[3:4], grad_in[...])
+        total = (grad_after[...] + back) * INV_SQRT2
+        grad_mixed[...] = total
+        back, gain_2 = norm_back(right_dot(mid[...], lright[...]), gains[2:3], total)
+        back_low = back.astype(BF16)
+        grad_right[...] = left_dot(back_low, mid[...])
+        mid_low = full_dot(back_low, lright[...]).astype(BF16)
+        grad_mid[...] = mid_low
+        grad_left[...] = left_dot(low[...], mid_low)
+        back, gain_1 = norm_back(attn_raw[...], gains[1:2], total)
+        grad_attn[...] = back.astype(BF16)
+        grad_gains[...] = jnp.concatenate(
+            [gain_1, gain_2, gain_3, jnp.zeros((5, D), F32)], 0
+        )
+
+    grad_context = right_dot(grad_attn[...], w_out[...]).astype(BF16)
+    grad_w_out[...] = left_dot(context[...], grad_attn[...]).astype(BF16)
+    probs = softmax_of(query[...], key[...], visible[...])
+    grad_probs = right_dot(grad_context, value[...])
+    inner = jnp.sum(probs * grad_probs, axis=-1, keepdims=True)
+    grad_scores = (probs * (grad_probs - inner)).astype(BF16)
+    grad_query[...] = full_dot(grad_scores, key[...])
+    key_term = left_dot(grad_scores, query[...])
+    value_term = left_dot(probs.astype(BF16), grad_context)
+    group = HEADS // KV_HEADS
+
+    @pl.when(lax.rem(at, group) == 0)
+    def _():
+        grad_key[...] = key_term
+        grad_value[...] = value_term
+
+    @pl.when(lax.rem(at, group) > 0)
+    def _():
+        grad_key[...] += key_term
+        grad_value[...] += value_term
+
+
+def attend_back(gains, grad_in, grad_after, mixed, attn_raw, mid, low, full, context, qkv, keys_all, visible):
+    rows = low.shape[0]
+    seen = keys_all.shape[0]
+    group = HEADS // KV_HEADS
+    side = 128
+    left_at, right_at = full.shape[1] // side - 2, full.shape[1] // side - 1
+    head = pl.BlockSpec((rows, HEAD), lambda i: (0, i))
+    once = lambda shape: pl.BlockSpec(shape, lambda i: (0, 0), pipeline_mode=pl.Buffered(1))
+    return piece(
+        attend_back_kernel,
+        "attend_back",
+        (HEADS,),
+        [
+            whole(gains.shape),
+            once((rows, D)),
+            once((rows, D)),
+            once((rows, D)),
+            once((rows, D)),
+            whole((rows, side)),
+            whole((rows, D)),
+            pl.BlockSpec((D, side), lambda i: (0, left_at)),
+            pl.BlockSpec((D, side), lambda i: (0, right_at)),
+            pl.BlockSpec((HEAD, D), lambda i: (i, 0)),
+            head,
+            head,
+            pl.BlockSpec((seen, HEAD), lambda i: (0, i // group)),
+            pl.BlockSpec((seen, HEAD), lambda i: (0, KV_HEADS + i // group)),
+            whole((rows, seen)),
+        ],
+        [
+            whole((rows, D)),
+            whole((rows, side)),
+            whole((8, D)),
+            whole((D, side)),
+            whole((D, side)),
+            pl.BlockSpec((HEAD, D), lambda i: (i, 0)),
+            head,
+            pl.BlockSpec((seen, HEAD), lambda i: (0, i // group)),
+            pl.BlockSpec((seen, HEAD), lambda i: (0, i // group)),
+        ],
+        [
+            ((rows, D), F32),
+            ((rows, side), BF16),
+            ((8, D), F32),
+            ((D, side), F32),
+            ((D, side), F32),
+            ((HEADS * HEAD, D), BF16),
+            ((rows, HEADS * HEAD), F32),
+            ((seen, KV_HEADS * HEAD), F32),
+            ((seen, KV_HEADS * HEAD), F32),
+        ],
+        [pltpu.VMEM((rows, D), BF16)],
+    )(
+        gains, grad_in, grad_after, mixed, attn_raw, mid, low, full, full, full, context, qkv, keys_all, keys_all,
+        visible,
+    )
+
+
+def turn_back(grad, cosine, sine):
+    half = HEAD // 2
+    first, second = grad[:, :half], grad[:, half:]
+    return jnp.concatenate([first * cosine + second * sine, second * cosine - first * sine], 1)
+
+
+def query_back_kernel(grad_query, raw, cosine, sine, head_gain, low, weight, grad_w, grad_low, grad_head):
+    at = pl.program_id(0)
+    turned = turn_back(grad_query[...], cosine[...], sine[...])
+    back, gain = norm_back(raw[...], head_gain[0:1], turned)
+    back_low = back.astype(BF16)
+    grad_w[...] = left_dot(low[...], back_low).astype(BF16)
+    term = right_dot(back_low, weight[...])
+
+    @pl.when(at == 0)
+    def _():
+        grad_low[...] = term
+        grad_head[...] = gain
+
+    @pl.when(at > 0)
+    def _():
+        grad_low[...] += term
+        grad_head[...] += gain
+
+
+def query_back(grad_query, raw, cosine, sine, head_gain, low, full):
+    rows = low.shape[0]
+    head = pl.BlockSpec((rows, HEAD), lambda i: (0, i))
+    return piece(
+        query_back_kernel,
+        "query_back",
+        (HEADS,),
+        [
+            head,
+            head,
+            whole(cosine.shape),
+            whole(sine.shape),
+            whole((2, HEAD)),
+            whole((rows, D)),
+            pl.BlockSpec((D, HEAD), lambda i: (0, HEADS + i)),
+        ],
+        [pl.BlockSpec((D, HEAD), lambda i: (0, i)), whole((rows, D)), whole((1, HEAD))],
+        [((D, HEADS * HEAD), BF16), ((rows, D), F32), ((1, HEAD), F32)],
+    )(grad_query, raw, cosine, sine, head_gain, low, full)
+
+
+def key_back_kernel(
+    grad_kv, raw, cosine, sine, head_gain, low, weight, before, grad_mixed, grad_mid, lleft, tokens, gains,
+    grad_w, grad_tokens, grad_head, grad_gain, total,
+):
+    at = pl.program_id(0)
+    is_key = at < KV_HEADS
+    grad = grad_kv[...]
+    turned = jnp.where(is_key, turn_back(grad, cosine[...], sine[...]), grad)
+    back, gain = norm_back(raw[...], jnp.where(is_key, head_gain[1:2], 1.0), turned)
+    back_low = back.astype(BF16)
+    grad_w[...] = left_dot(low[...], back_low).astype(BF16)
+    term = right_dot(back_low, weight[...])
+
+    @pl.when(at == 0)
+    def _():
+        total[...] = before[...] + term
+        grad_head[...] = gain
+
+    @pl.when(at > 0)
+    def _():
+        total[...] += term
+        grad_head[...] += jnp.where(is_key, gain, 0.0)
+
+    @pl.when(at == 2 * KV_HEADS - 1)
+    def _():
+        grad_normed = total[...] + grad_mixed[...] + right_dot(grad_mid[...], lleft[...])
+        back, gain_0 = norm_back(tokens[...].astype(F32), gains[0:1], grad_normed)
+        grad_tokens[...] = grad_mixed[...] + back
+        grad_gain[...] = gain_0
+
+
+def key_back(grad_kv, raw, cosine, sine, head_gain, low, full, before, grad_mixed, grad_mid, tokens, gains):
+    rows = low.shape[0]
+    side = 128
+    left_at = full.shape[1] // side - 2
+    return piece(
+        key_back_kernel,
+        "key_back",
+        (2 * KV_HEADS,),
+        [
+            pl.BlockSpec((rows, HEAD), lambda i: (0, i)),
+            pl.BlockSpec((rows, HEAD), lambda i: (0, HEADS + i)),
+            whole(cosine.shape),
+            whole(sine.shape),
+            whole((2, HEAD)),
+            whole((rows, D)),
+            pl.BlockSpec((D, HEAD), lambda i: (0, 2 * HEADS + i)),
+            whole((rows, D)),
+            whole((rows, D)),
+            whole((rows, side)),
+            pl.BlockSpec((D, side), lambda i: (0, left_at)),
+            whole((rows, D)),
+            whole(gains.shape),
+        ],
+        [
+            pl.BlockSpec((D, HEAD), lambda i: (0, i)),
+            whole((rows, D)),
+            whole((1, HEAD)),
+            whole((1, D)),
+        ],
+        [
+            ((D, 2 * KV_HEADS * HEAD), BF16),
+            ((rows, D), F32),
+            ((1, HEAD), F32),
+            ((1, D), F32),
+        ],
+        [pltpu.VMEM((rows, D), F32)],
+    )(grad_kv, raw, cosine, sine, head_gain, low, full, before, grad_mixed, grad_mid, full, tokens, gains)
 
 
 def tie(*values):
@@ -506,9 +1038,16 @@
     return [total // count + (1 if i < total % count else 0) for i in range(count)]
 
 
+def pair_of_rows(own):
+    return jnp.concatenate([own, swap(own, "fsdp")], 0)
+
+
+def both_pairs(pair):
+    return jnp.concatenate([pair, swap(pair, "core")], 0)
+
+
 def rows_of_four(own):
-    pair = jnp.concatenate([own, swap(own, "fsdp")], 0)
-    return jnp.concatenate([pair, swap(pair, "core")], 0)
+    return both_pairs(pair_of_rows(own))
 
 
 def sum_of_four(partial):
@@ -535,10 +1074,9 @@
     head_gains,
     ffn_weight,
 ):
-    states = tokens[0].astype(F32)
     layer_in = per_layer[0].astype(F32)
     target = teacher[0].astype(F32)
-    row_count = states.shape[0]
+    row_count = tokens.shape[1]
     chips = lax.axis_size("zy")
     seq_count = 2 * chips
     group_count = lax.axis_size("fsdp")
@@ -588,13 +1126,13 @@
     )
     pack = jnp.concatenate(
         [
+            w_out,
             w_query,
             w_kv,
+            pl_gate,
+            pl_proj.reshape(shard_rows, proj_cols),
             laurel_left,
             misc,
-            pl_gate,
-            pl_proj.reshape(shard_rows, proj_cols),
-            w_out,
             laurel_right.T,
             jnp.zeros((shard_rows, 128 - RANK), BF16),
         ],
@@ -617,17 +1155,14 @@
         return values
 
     pass_on(0)
-    full = stage_end(gather_all(pack, chips))
+    full = gather_all(pack, chips)
+    at = 2 * D + 2 * key_cols
+    plg = full[:, at : at + PLD]
+    plp = full[:, at + PLD : at + PLD + proj_cols].reshape(PLD, D)
+    at += PLD + proj_cols + RANK
+    misc_full = stage_end(full[:, at : at + misc_cols])
     pass_on(1)
-    at = 0
-    pieces = []
-    for width in (D, 2 * key_cols, RANK, misc_cols, PLD, proj_cols, D, RANK):
-        pieces.append(full[:, at : at + width])
-        at += width
-    wq, wkv, lleft, misc_full, plg, plp, wo, lright = pieces
-    plp = plp.reshape(PLD, D)
-    lright = lright.T
-    gains = misc_full[:, :6].T.astype(F32)
+    gains = jnp.pad(misc_full[:, :6].T.astype(F32), ((0, 2), (0, 0)))
     head_n = head_gains.shape[1]
     head_gain = (
         misc_full[:, 6]
@@ -637,32 +1172,13 @@
         .reshape(2, HEAD)
         .astype(F32)
     )
-
-    normed = rms_norm(states, gains[0])
-    normed_low = normed.astype(BF16)
-    query_raw = full_dot(normed_low, wq)
-    kv_raw = full_dot(normed_low, wkv)
-
-    def prepare(q_input, k_input, v_input, q_gain, k_gain):
-        q_heads = rotate(rms_norm(q_input.reshape(row_count, HEADS, HEAD), q_gain), places)
-        k_heads = rotate(rms_norm(k_input.reshape(row_count, KV_HEADS, HEAD), k_gain), places)
-        v_heads = plain_norm(v_input.reshape(row_count, KV_HEADS, HEAD))
-        return (q_heads, k_heads, v_heads)
-
-    (queries, keys_new, values_new), prepare_back = jax.vjp(
-        prepare, query_raw, kv_raw[:, :key_cols], kv_raw[:, key_cols:], head_gain[0], head_gain[1]
-    )
-    query_low = queries.astype(BF16)
-    kv_own = jnp.concatenate(
-        [
-            keys_new.reshape(row_count, key_cols).astype(BF16),
-            values_new.reshape(row_count, key_cols).astype(BF16),
-        ],
-        1,
-    )
-
-    query_low, kv_own = stage_end((query_low, kv_own))
-    pass_on(2)
+    freqs = jnp.exp(
+        jnp.arange(HEAD // 2, dtype=F32) * (-2.0 * math.log(ROPE_BASE) / HEAD)
+    )
+    angles = places.astype(F32)[:, None] * freqs
+    cosine, sine = jnp.cos(angles), jnp.sin(angles)
+    normed_low, qkv_raw, qkv = make_qkv(tokens[0], gains, head_gain, cosine, sine, full)
+    kv_own = qkv[:, D:]
 
     mid = chips // 2
     chain = [(i, i + 1) for i in range(mid - 1)] + [(mid - 1, mid + 1)]
@@ -685,72 +1201,44 @@
     kv_other = swap(jnp.where(core == 0, kv_own, kv_before), "core")
     keys_all = jnp.concatenate([kv_before, kv_other, kv_own], 0)
     keys_all = stage_end(keys_all)
-    pass_on(3)
+    pass_on(2)
     key_len = keys_all.shape[0]
     key_places = first_place - 2 * row_count + jnp.arange(key_len, dtype=jnp.int32)
     visible = (
         (key_places[None, :] <= places[:, None])
         & (places[:, None] - key_places[None, :] < WINDOW)
         & (key_places[None, :] >= 0)
-    )
-    group_heads = HEADS // KV_HEADS
-    query_grouped = query_low.reshape(row_count, KV_HEADS, group_heads, HEAD)
-    key_heads = keys_all[:, :key_cols].reshape(key_len, KV_HEADS, HEAD)
-    value_heads = keys_all[:, key_cols:].reshape(key_len, KV_HEADS, HEAD)
-
-    def masked_scores():
-        scores = jnp.einsum(
-            "qgjd,kgd->gjqk", query_grouped, key_heads, preferred_element_type=F32
-        )
-        return jnp.where(visible, scores, -1e30)
-
-    scores_fwd = masked_scores()
-    top_score = jnp.max(scores_fwd, axis=-1, keepdims=True)
-    expo = jnp.exp(scores_fwd - top_score)
-    totals = jnp.sum(expo, axis=-1, keepdims=True)
-    probs = expo / totals
-    log_total = top_score + jnp.log(totals)
-    probs_low = probs.astype(BF16)
-    context = jnp.einsum("gjqk,kgd->qgjd", probs_low, value_heads, preferred_element_type=F32)
-    context_low = context.reshape(row_count, HEADS * HEAD).astype(BF16)
-    attn_raw = full_dot(context_low, wo)
-    attn_out = rms_norm(attn_raw, gains[1])
-    laurel_mid = full_dot(normed_low, lleft).astype(BF16)
-    laurel_raw = full_dot(laurel_mid, lright)
-    mixed = (states + attn_out + normed + rms_norm(laurel_raw, gains[2])) * INV_SQRT2
-    ffn_in = rms_norm(mixed, gains[3]).astype(BF16)
-
-    ffn_in = stage_end(ffn_in)
-    pass_on(4)
-    ffn_rows = stage_end(rows_of_four(ffn_in))
+    ).astype(F32)
+    context_low, attn_raw, mixed, ffn_in, laurel_mid = attend(
+        tokens[0], gains, normed_low, qkv, keys_all, visible, full
+    )
+
+    pair = stage_end(pair_of_rows(ffn_in))
+    here = len(ups)
+    pass_on(3)
+    ffn_rows = both_pairs(pair)
     gates, uppers, hiddens, part_weights, parts = [], [], [], [], []
-    running = None
 
     def forward_part(running, first, last):
-        weights = [
-            jnp.concatenate([w[kind] for k in range(first, last) for w in (ups[k], downs[k])], 0)
-            for kind in range(3)
-        ]
-        gate = right_dot(ffn_rows, weights[0])
-        upper = right_dot(ffn_rows, weights[1])
-        hidden = gated_product(gate, upper).astype(BF16)
-        term = full_dot(hidden, weights[2])
+        weights = [w for k in range(first, last) for w in (ups[k], downs[k])]
+        running, gate, upper, hidden = ffn_forward(ffn_rows, running, weights)
         gates.append(gate)
         uppers.append(upper)
         hiddens.append(hidden)
         part_weights.append(weights)
         parts.append(range(first, last))
-        return term if running is None else running + term
-
-    here = len(ups)
+        return running
+
+    running = stage_end(forward_part(None, 0, here))
+    pass_on(4)
+    stage_end(())
+    then = len(ups)
     pass_on(5)
-    cut_a = max(1, here * 2 // 3)
-    running = stage_end(forward_part(None, 0, cut_a))
+    running = stage_end(forward_part(running, here, then))
     here = len(ups)
     pass_on(6)
-    running = forward_part(running, cut_a, here)
+    running = stage_end(forward_part(running, then, here))
     if here < chips:
-        running = stage_end(running)
         running = forward_part(running, here, chips)
     down_out = sum_of_four(running)
     after_ffn = mixed + rms_norm(down_out, gains[4])
@@ -779,128 +1267,73 @@
     grad_down_low = grad_down.astype(BF16)
 
     grad_down_rows = rows_of_four(grad_down_low)
-    grad_gates, grad_uppers = [], []
-
-    def backward_part(number):
-        unused, act_back = jax.vjp(gated_product, gates[number], uppers[number])
-        grad_gate, grad_upper = act_back(right_dot(grad_down_rows, part_weights[number][2]))
-        return grad_gate.astype(BF16), grad_upper.astype(BF16)
+    grad_parts = []
+
+    def backward_part(first, last, running):
+        return ffn_backward(
+            grad_down_rows,
+            running,
+            [w for weights in part_weights[first:last] for w in weights],
+            gates[first:last],
+            uppers[first:last],
+        )
 
     def unit_grads(k):
         for part, (gg, gu), hid in zip(parts, grad_parts, hiddens):
             if k in part:
-                at = (k - part[0]) * units
-                up_cut, down_cut = slice(at, at + half), slice(at + half, at + units)
-                return (
-                    left_dot(jnp.concatenate([gg[:, up_cut], gu[:, up_cut]], 1), ffn_rows),
-                    left_dot(jnp.concatenate([gg[:, down_cut], gu[:, down_cut]], 1), ffn_rows),
-                    left_dot(hid[:, at : at + units], grad_down_rows),
-                )
-
-    def add_terms(arrived, terms):
-        halves = (terms[0], terms[2][:half], terms[1], terms[2][half:])
-        if arrived is None:
-            return halves
-        return tuple(a.astype(F32) + t for a, t in zip(arrived, halves))
+                return unit_grads_of(k - part[0], units, gg, gu, hid, ffn_rows, grad_down_rows)
 
     order = list(range(1, chips)) + [0]
     ring_steps = shares(chips - 1, 7)
     done = 0
-    sums = None
-
-    def move(sums):
-        low = [s.astype(BF16) for s in sums]
-        return [ring(low[0], 1), ring(low[1], 1), ring(low[2], -1), ring(low[3], -1)]
 
     def beside(stage, work):
-        nonlocal done, sums
+        nonlocal done, up_sum, down_sum
         values = None
         for step in range(ring_steps[stage]):
-            arrived = move(sums)
+            up_in = ring(up_sum.astype(BF16), 1)
+            down_in = ring(down_sum.astype(BF16), -1)
+            if step == 0:
+                values = work()
             done += 1
             terms = unit_grads(order[done])
-            if step == 0:
-                values = work()
-            arrived, terms, values = tie(arrived, terms, values)
-            sums = add_terms(arrived, terms)
+            (up_in, down_in), terms, values = tie((up_in, down_in), terms, values)
+            up_sum = up_in.astype(F32) + terms[:, :half]
+            down_sum = down_in.astype(F32) + terms[:, half:]
         return work() if values is None else values
 
-    grad_parts = [backward_part(0)]
-    sums = add_terms(None, unit_grads(order[0]))
+    running, grads = backward_part(0, 1, None)
+    grad_parts += grads
+    terms = unit_grads(order[0])
+    up_sum, down_sum = terms[:, :half], terms[:, half:]
 
     def work():
-        return [backward_part(number) for number in range(1, len(parts))]
-
-    grad_parts += beside(0, work)
-
-    def work():
-        running = None
-        for weights, (gg, gu) in zip(part_weights, grad_parts):
-            term = full_dot(gg, weights[0]) + full_dot(gu, weights[1])
-            running = term if running is None else running + term
-        return running
-
-    running = beside(1, work)
-    grad_ffn_in = beside(2, lambda: sum_of_four(running))
-    def work():
-        unused, mix_norm_back = jax.vjp(rms_norm, mixed, gains[3])
-        grad_mixed_norm, grad_g3 = mix_norm_back(grad_ffn_in)
-        grad_scaled = (grad_after + grad_mixed_norm) * INV_SQRT2
-        unused, laurel_norm_back = jax.vjp(rms_norm, laurel_raw, gains[2])
-        grad_laurel, grad_g2 = laurel_norm_back(grad_scaled)
-        grad_laurel_low = grad_laurel.astype(BF16)
-        grad_lright_t = left_dot(grad_laurel_low, laurel_mid)
-        grad_mid_low = right_dot(grad_laurel_low, lright).astype(BF16)
-        grad_lleft = left_dot(normed_low, grad_mid_low)
-        unused, attn_norm_back = jax.vjp(rms_norm, attn_raw, gains[1])
-        grad_attn, grad_g1 = attn_norm_back(grad_scaled)
-        grad_attn_low = grad_attn.astype(BF16)
-        grad_wo = left_dot(context_low, grad_attn_low)
-        grad_context = right_dot(grad_attn_low, wo).astype(BF16)
-        return (
-            grad_context,
-            grad_scaled,
-            grad_wo,
-            grad_lleft,
-            grad_lright_t,
-            grad_mid_low,
-            (grad_g1, grad_g2, grad_g3),
-        )
-
+        total, grads = backward_part(1, len(parts), running)
+        grad_parts.extend(grads)
+        return total
+
+    running = beside(0, work)
+    grad_ffn_in = beside(1, lambda: sum_of_four(running))
     (
-        grad_context,
         grad_scaled,
-        grad_wo,
+        grad_mid_low,
+        grad_mid_gains,
         grad_lleft,
         grad_lright_t,
-        grad_mid_low,
-        (grad_g1, grad_g2, grad_g3),
-    ) = beside(3, work)
-    grad_context = grad_context.reshape(row_count, KV_HEADS, group_heads, HEAD)
+        grad_wo,
+        grad_queries,
+        grad_keys,
+        grad_values,
+    ) = beside(
+        2,
+        lambda: attend_back(
+            gains, grad_ffn_in, grad_after, mixed, attn_raw, laurel_mid, normed_low, full, context_low, qkv, keys_all,
+            visible,
+        ),
+    )
 
     def work():
-        probs_again = jnp.exp(masked_scores() - log_total)
-        grad_probs = jnp.einsum(
-            "qgjd,kgd->gjqk", grad_context, value_heads, preferred_element_type=F32
-        )
-        grad_scores = (
-            probs_again * (grad_probs - jnp.sum(probs_again * grad_probs, axis=-1, keepdims=True))
-        ).astype(BF16)
-        grad_queries = jnp.einsum("gjqk,kgd->qgjd", grad_scores, key_heads, preferred_element_type=F32)
-        grad_keys = jnp.einsum(
-            "gjqk,qgjd->kgd", grad_scores, query_grouped, preferred_element_type=F32
-        )
-        grad_values = jnp.einsum(
-            "gjqk,qgjd->kgd", probs_again.astype(BF16), grad_context, preferred_element_type=F32
-        )
-        grad_kv = jnp.concatenate(
-            [grad_keys.reshape(key_len, key_cols), grad_values.reshape(key_len, key_cols)], 1
-        )
-        return grad_queries, grad_kv
-
-    grad_queries, grad_kv = beside(4, work)
-
-    def work():
+        grad_kv = jnp.concatenate([grad_keys, grad_values], 1)
         grad_before = grad_kv[:row_count]
         grad_own = grad_kv[2 * row_count :]
         returned = swap(grad_kv[row_count : 2 * row_count].astype(BF16), "core").astype(F32)
@@ -915,79 +1348,50 @@
             + lax.ppermute(before_low, "zy", [(b, a) for a, b in chain]).astype(F32)
             + lax.ppermute(before_low, "zy", [(mid, mid - 1)]).astype(F32)
         )
-        return grad_own
-
-    grad_own = beside(5, work)
+        return grad_own, query_back(grad_queries, qkv_raw, cosine, sine, head_gain, normed_low, full)
+
+    grad_own, (grad_wq, grad_normed, grad_hq) = beside(3, work)
+    grad_wkv, grad_tokens, grad_hk, grad_g0 = beside(
+        4,
+        lambda: key_back(
+            grad_own, qkv_raw, cosine, sine, head_gain, normed_low, full, grad_normed, grad_scaled, grad_mid_low,
+            tokens[0], gains,
+        ),
+    )
     def work():
-        grad_query_raw, grad_key_raw, grad_value_raw, grad_hq, grad_hk = prepare_back(
-            (
-                grad_queries.reshape(row_count, HEADS, HEAD),
-                grad_own[:, :key_cols].reshape(row_count, KV_HEADS, HEAD),
-                grad_own[:, key_cols:].reshape(row_count, KV_HEADS, HEAD),
-            )
+        head_back = jnp.concatenate([grad_hq, grad_hk], 0).reshape(2, shards, head_n).transpose(1, 0, 2)
+        head_back = head_back.reshape(shards, 2 * head_n)
+        head_back = jnp.pad(head_back, ((0, 0), (0, shard_rows - 2 * head_n))).reshape(1, D)
+        misc_back = jnp.concatenate(
+            [grad_g0, grad_mid_gains[:3], grad_g4[None], grad_g5[None], head_back, jnp.zeros((1, D), F32)], 0
         )
-        grad_query_low = grad_query_raw.astype(BF16)
-        grad_kv_low = jnp.concatenate([grad_key_raw, grad_value_raw], 1).astype(BF16)
-        grad_wq = left_dot(normed_low, grad_query_low)
-        grad_wkv = left_dot(normed_low, grad_kv_low)
-        grad_normed = (
-            grad_scaled
-            + right_dot(grad_mid_low, lleft)
-            + right_dot(grad_query_low, wq)
-            + right_dot(grad_kv_low, wkv)
+        return jnp.concatenate(
+            [
+                grad_plg.astype(BF16),
+                grad_plp.astype(BF16).reshape(D, proj_cols),
+                grad_lleft[:, :RANK].astype(BF16),
+                jnp.pad(misc_back.T, ((0, 0), (0, misc_cols - 8))).astype(BF16),
+                grad_lright_t.astype(BF16),
+            ],
+            1,
         )
-        unused, input_norm_back = jax.vjp(rms_norm, states, gains[0])
-        grad_states, grad_g0 = input_norm_back(grad_normed)
-        grad_tokens = grad_scaled + grad_states
-        return grad_tokens, grad_wq, grad_wkv, grad_g0, grad_hq, grad_hk
-
-    grad_tokens, grad_wq, grad_wkv, grad_g0, grad_hq, grad_hk = beside(6, work)
-    up_pair, up_down, down_pair, down_down = sums
-    grad_ffn = jnp.stack(
-        [
-            jnp.concatenate([up_pair[:half], down_pair[:half]], 0),
-            jnp.concatenate([up_pair[half:], down_pair[half:]], 0),
-            jnp.concatenate([up_down, down_down], 0),
-        ],
-        1,
-    )
-
-    head_back = jnp.stack([grad_hq, grad_hk]).reshape(2, shards, head_n).transpose(1, 0, 2)
-    head_back = head_back.reshape(shards, 2 * head_n)
-    head_back = jnp.pad(head_back, ((0, 0), (0, shard_rows - 2 * head_n))).reshape(-1, 1)
-    gains_back = jnp.stack([grad_g0, grad_g1, grad_g2, grad_g3, grad_g4, grad_g5], 1)
-    misc_back = jnp.concatenate(
-        [gains_back, head_back, jnp.zeros((D, misc_cols - 7), F32)], 1
-    )
-    rest_back = jnp.concatenate(
-        [
-            grad_lleft,
-            misc_back,
-            grad_plg,
-            grad_plp.reshape(D, proj_cols),
-            grad_lright_t,
-            jnp.zeros((D, 128 - RANK), F32),
-        ],
-        1,
-    )
-    sums_wq, sums_wkv, sums_wo, sums_rest = sum_all(
-        [g.astype(BF16) for g in (grad_wq, grad_wkv, grad_wo, rest_back)],
+
+    rest_back = beside(5, work)
+    beside(6, lambda: ())
+    grad_ffn = jnp.concatenate([up_sum, down_sum], 1).transpose(1, 0, 2)
+
+    sums_wq, sums_wkv, sums_wo, sums_rest, total = sum_all(
+        [grad_wq, grad_wkv, grad_wo, rest_back],
         (False, False, True, True),
+        jnp.broadcast_to(squares, (8, 128)),
         chips,
     )
     at = 0
     rest = []
-    for width in (RANK, misc_cols, PLD, proj_cols, RANK):
+    for width in (PLD, proj_cols, RANK, misc_cols, RANK):
         rest.append(sums_rest[:, at : at + width])
         at += width
 
-    total = jnp.broadcast_to(squares, (8, 128))
-    total = total + swap(total, "core")
-    total = total + swap(total, "fsdp")
-    span = 1
-    while span < chips:
-        total = total + lax.ppermute(total, "zy", [(i, i ^ span) for i in range(chips)])
-        span *= 2
     match_loss = total[0, 0] / (2.0 * D * count)
 
     return (
@@ -998,12 +1402,12 @@
         sums_wq,
         sums_wkv,
         sums_wo,
+        rest[2],
+        rest[4].T,
         rest[0],
-        rest[4].T,
-        rest[2],
-        rest[3].reshape(pl_proj.shape),
-        rest[1][:, :6].T,
-        rest[1][: 2 * head_n, 6].reshape(2, head_n),
+        rest[1].reshape(pl_proj.shape),
+        rest[3][:, :6].T,
+        rest[3][: 2 * head_n, 6].reshape(2, head_n),
         grad_ffn,
     )
 

time: 1240 us -> 1010 us (0.81)
  Pallas kernels: 238 us -> 525 us
  matrix products: 283 us -> 8.08 us
  local copies, waits for them, and re-layouts: 159 us -> 67 us
  other arithmetic: 135 us -> 72.8 us
  waiting for transfers between devices: 320 us -> 271 us
  starting transfers between devices: 83 us -> 54.7 us
    pallas_call x1 -> x20, Pallas kernels: 111 us -> 403 us  [the longest x1 116 us: sum_all(): pl.pallas_call(functools.partial(sum_kernel, chips, streams, (count, 1, c...]
    dot_general x31 -> x2, matrix products: 96.4 us -> 1.97 us  [left_dot(): lax.dot_general(left, right, (((0,), (0,)), ((), ())), preferred_element_...]
    dot_general x16 -> x2, matrix products: 90.3 us -> 2.32 us  [full_dot(): return jnp.dot(left, right, preferred_element_type=F32)]
    dot_general x16 -> x2, matrix products: 74.6 us -> 3.79 us  [right_dot(): lax.dot_general(left, right, (((1,), (1,)), ((), ())), preferred_element_...]
    ppermute x42 -> x28, waiting for transfers between devices: 193 us -> 147 us  [ring(): return lax.ppermute(value, 'zy', ring_pairs(lax.axis_size('zy'), by))]
    unnamed x459 -> x102, local copies, waits for them, and re-layouts: 51.2 us -> 20 us
    add x12 -> x1, other arithmetic: 32.8 us -> 4.65 us  [beside(): up_sum = up_in.astype(F32) + terms[:, :half]]
    ppermute x42 -> x28, starting transfers between devices: 68.7 us -> 42.3 us  [ring(): return lax.ppermute(value, 'zy', ring_pairs(lax.axis_size('zy'), by))]
  transfers between devices with their start and end apart: 63 -> 44, of which waited for: 27 -> 26; matrix products, arithmetic and copies ran while one was open for 24% -> 6% of each run, Pallas kernels for 10% -> 46%
where the time goes in v3:
time: 1010 us; the launch traced here: 1000 us
  Pallas kernels  525 us (52%)
  waiting for transfers between devices  271 us (27%)
  other arithmetic  72.8 us (7%)
  local copies, waits for them, and re-layouts  67 us (7%)
  starting transfers between devices  54.7 us (5%)
    ppermute x28, waiting for transfers between devices, ring(): return lax.ppermute(value, 'zy', ring_pairs(lax.axis_size('zy'), by))  147 us
    pallas_call x1, Pallas kernels, gather_all(): pl.pallas_call(functools.partial(gather_kernel, chips, streams), out_shap...  122 us
    pallas_call x1, Pallas kernels, sum_all(): pl.pallas_call(functools.partial(sum_kernel, chips, streams, (count, 1, c...  116 us
    ppermute x10, waiting for transfers between devices, swap(): return lax.ppermute(value, axis, [(0, 1), (1, 0)])  95.7 us
    pallas_call x8, Pallas kernels, unit_grads_of(): piece(unit_grads_kernel, 'unit_grads', (D // width,), [narrow, narrow, na...  71.4 us
    pallas_call x2, Pallas kernels, ffn_backward(): piece(functools.partial(ffn_backward_kernel, len(weights), widths, add),...  65.4 us
    pallas_call x4, Pallas kernels, ffn_forward(): piece(functools.partial(ffn_forward_kernel, len(weights), add), 'ffn_forw...  63.6 us
    ppermute x28, starting transfers between devices, ring(): return lax.ppermute(value, 'zy', ring_pairs(lax.axis_size('zy'), by))  42.3 us
  transfers between devices with their start and end apart: 44, of which 26 were waited for; matrix products, arithmetic and copies ran while one was open for 6% of the time, Pallas kernels for 46%

profile of v3, /device:TPU:0, one launch (start us, length us, event | category | flops | bytes accessed | tf_op | source)
XLA Modules:
  0.0 1002.8 jit_solution(5914513829330598808)
XLA Ops:
  2.9 3.1 collective-permute-start
  14.7 122.0 %gather_all.1.weight.w_out.lleft.lright = bf16[2048,5888]{1,0:T(8,128)(2,1)} custom-call(bf16[64,5888]{1,0:T(8,128)(2,1)} %concatenate.36.shard), custom_call_target="tpu_custom_call" | custom-call | bytes 48234496 | tf_op jit(solution)/shard_map/gather_all/pallas_call | solution.py:224
  142.9 13.5 %make_qkv.1 = (bf16[256,2048]{1,0:T(8,128)(2,1)}, f32[256,3072]{1,0:T(8,128)}, bf16[256,3072]{1,0:T(8,128)(2,1)}) custom-call(bf16[256,2048]{1,0:T(8,128)(2,1)} %bitcast.57, f32[8,2048]{1,0:T(8,128)} %pad.19.gains, f32[2,256]{1,0:T(2,128)} %reshape.165.head_gain, f32[256,128]{1,0:T(8,128)} %get-tuple-element.311.cosine, f32[256,128]{1,0:T(8,128)} %get-tuple-element.310.sine, ...), custom_call_target="tpu_custom_call" | custom-call | bytes 1024 | tf_op jit(solution)/shard_map/make_qkv/pallas_call | solution.py:575
  159.8 4.2 collective-permute-start.5
  164.0 3.6 collective-permute-start.2
  167.6 8.2 collective-permute-done.5
  179.1 2.3 broadcast_select_fusion
  183.6 2.7 pad_maximum_fusion.3.key.value
  186.3 15.3 %collective-permute-done.2.refs_4_ = bf16[3,128,2048]{2,1,0:T(8,128)(2,1)S(1)} collective-permute-done((bf16[3,128,2048]{2,1,0:T(8,128)(2,1)}, bf16[3,128,2048]{2,1,0:T(8,128)(2,1)S(1)}, u32[]{:S(2)}, u32[]{:S(2)}) %collective-permute-start.2) | collective-permute-done | bytes 1572896 | tf_op jit(solution)/shard_map/ppermute | solution.py:61
  201.5 7.4 collective-permute-done.3.refs_5_
  208.9 2.4 collective-permute-start.9
  212.4 19.5 %attend.1 = (bf16[256,2048]{1,0:T(8,128)(2,1)}, f32[256,2048]{1,0:T(8,128)}, f32[256,2048]{1,0:T(8,128)}, bf16[256,2048]{1,0:T(8,128)(2,1)}, bf16[256,128]{1,0:T(8,128)(2,1)}) custom-call(bf16[256,2048]{1,0:T(8,128)(2,1)} %bitcast.58, f32[8,2048]{1,0:T(8,128)} %pad.19.gains, bf16[256,2048]{1,0:T(8,128)(2,1)} %get-tuple-element.131.low, ...), custom_call_target="tpu_custom_call" | custom-call | bytes 1024 | tf_op jit(solution)/shard_map/attend/pallas_call | solution.py:639
  232.5 24.0 %collective-permute-done.10 = bf16[256,2048]{1,0:T(8,128)(2,1)S(1)} collective-permute-done((bf16[256,2048]{1,0:T(8,128)(2,1)}, bf16[256,2048]{1,0:T(8,128)(2,1)S(1)}, u32[]{:S(2)}, u32[]{:S(2)}) %collective-permute-start.10) | collective-permute-done | bytes 1048608 | tf_op jit(solution)/shard_map/ppermute | solution.py:65
  258.1 8.3 collective-permute-start.11
  266.4 2.7 collective-permute-start.12
  271.4 23.3 %ffn_forward.4 = (f32[1024,2048]{1,0:T(8,128)}, f32[1024,1024]{1,0:T(8,128)}, f32[1024,1024]{1,0:T(8,128)}, bf16[1024,1024]{1,0:T(8,128)(2,1)}) custom-call(bf16[3,128,2048]{2,1,0:T(8,128)(2,1)} %copy-done.7, bf16[3,128,2048]{2,1,0:T(8,128)(2,1)} %copy-done.6, bf16[3,128,2048]{2,1,0:T(8,128)(2,1)} %collective-permute-done.refs_2_, ...), custom_call_target="tpu_custom_call" | custom-call | bytes 1024 | tf_op jit(solution)/shard_map/ffn_forward/pallas_call | solution.py:718
  294.7 9.2 collective-permute-done.11.refs_0_
  304.1 3.4 collective-permute-start.14
  307.5 33.5 %collective-permute-done.14.refs_2_ = bf16[3,128,2048]{2,1,0:T(8,128)(2,1)S(1)} collective-permute-done((bf16[3,128,2048]{2,1,0:T(8,128)(2,1)S(1)}, bf16[3,128,2048]{2,1,0:T(8,128)(2,1)S(1)}, u32[]{:S(2)}, u32[]{:S(2)}) %collective-permute-start.14) | collective-permute-done | bytes 1572896 | tf_op jit(solution)/shard_map/ppermute | solution.py:61
  345.2 15.5 %ffn_forward.5 = (f32[1024,2048]{1,0:T(8,128)}, f32[1024,512]{1,0:T(8,128)}, f32[1024,512]{1,0:T(8,128)}, bf16[1024,512]{1,0:T(8,128)(2,1)}) custom-call(bf16[3,128,2048]{2,1,0:T(8,128)(2,1)} %copy-done.10, bf16[3,128,2048]{2,1,0:T(8,128)(2,1)} %copy-done.11, bf16[3,128,2048]{2,1,0:T(8,128)(2,1)} %copy-done.12, bf16[3,128,2048]{2,1,0:T(8,128)(2,1)} %copy-done.13, ...), custom_call_target="tpu_custom_call" | custom-call | bytes 1024 | tf_op jit(solution)/shard_map/ffn_forward/pallas_call | solution.py:718
  360.7 17.3 %collective-permute-done.16.refs_0_.refs_4_ = bf16[3,128,2048]{2,1,0:T(8,128)(2,1)} collective-permute-done((bf16[3,128,2048]{2,1,0:T(8,128)(2,1)S(1)}, bf16[3,128,2048]{2,1,0:T(8,128)(2,1)}, u32[]{:S(2)}, u32[]{:S(2)}) %collective-permute-start.16) | collective-permute-done | bytes 1572896 | tf_op jit(solution)/shard_map/ppermute | solution.py:61
  381.4 12.4 %ffn_forward.6 = (f32[1024,2048]{1,0:T(8,128)}, f32[1024,256]{1,0:T(8,128)}, f32[1024,256]{1,0:T(8,128)}, bf16[1024,256]{1,0:T(8,128)(2,1)}) custom-call(bf16[3,128,2048]{2,1,0:T(8,128)(2,1)} %collective-permute-done.16.refs_0_.refs_4_, bf16[3,128,2048]{2,1,0:T(8,128)(2,1)} %collective-permute-done.17.refs_1_.refs_5_, ...), custom_call_target="tpu_custom_call" | custom-call | bytes 1024 | tf_op jit(solution)/shard_map/ffn_forward/pallas_call | solution.py:718
  393.8 18.5 %collective-permute-done.18.refs_0_.refs_6_ = bf16[3,128,2048]{2,1,0:T(8,128)(2,1)S(1)} collective-permute-done((bf16[3,128,2048]{2,1,0:T(8,128)(2,1)}, bf16[3,128,2048]{2,1,0:T(8,128)(2,1)S(1)}, u32[]{:S(2)}, u32[]{:S(2)}) %collective-permute-start.18) | collective-permute-done | bytes 1572896 | tf_op jit(solution)/shard_map/ppermute | solution.py:61
  415.4 12.4 %ffn_forward.7 = (f32[1024,2048]{1,0:T(8,128)}, f32[1024,256]{1,0:T(8,128)}, f32[1024,256]{1,0:T(8,128)}, bf16[1024,256]{1,0:T(8,128)(2,1)}) custom-call(bf16[3,128,2048]{2,1,0:T(8,128)(2,1)} %copy-done.16, bf16[3,128,2048]{2,1,0:T(8,128)(2,1)} %copy-done.17, f32[1024,2048]{1,0:T(8,128)} %get-tuple-element.156.refs_2_, bf16[1024,2048]{1,0:T(8,128)(2,1)} %copy-done), custom_call_target="tpu_custom_call" | custom-call | bytes 1024 | tf_op jit(solution)/shard_map/ffn_forward/pallas_call | solution.py:718
  427.9 2.5 slice.274
  430.4 4.1 collective-permute-done.20
  434.6 2.8 convert_add_fusion.1
  444.5 20.2 %collective-permute-done.21 = bf16[256,2048]{1,0:T(8,128)(2,1)S(1)} collective-permute-done((bf16[256,2048]{1,0:T(8,128)(2,1)S(1)}, bf16[256,2048]{1,0:T(8,128)(2,1)S(1)}, u32[]{:S(2)}, u32[]{:S(2)}) %collective-permute-start.21) | collective-permute-done | bytes 1048608 | tf_op jit(solution)/shard_map/ppermute | solution.py:65
  477.5 2.5 multiply_reduce_fusion.1
  481.9 23.8 %collective-permute-done.22 = bf16[256,2048]{1,0:T(8,128)(2,1)S(1)} collective-permute-done((bf16[256,2048]{1,0:T(8,128)(2,1)S(1)}, bf16[256,2048]{1,0:T(8,128)(2,1)S(1)}, u32[]{:S(2)}, u32[]{:S(2)}) %collective-permute-start.22) | collective-permute-done | bytes 1048608 | tf_op jit(solution)/shard_map/ppermute | solution.py:65
  506.1 4.1 collective-permute-done.23
  510.2 2.3 pad_maximum_fusion.refs_8_.down_rows.refs_9_
  512.5 32.1 %ffn_backward.2 = (f32[1024,2048]{1,0:T(8,128)}, bf16[1024,1024]{1,0:T(8,128)(2,1)}, bf16[1024,1024]{1,0:T(8,128)(2,1)}) custom-call(bf16[3,128,2048]{2,1,0:T(8,128)(2,1)} %copy-done.7, bf16[3,128,2048]{2,1,0:T(8,128)(2,1)} %copy-done.6, bf16[3,128,2048]{2,1,0:T(8,128)(2,1)} %collective-permute-done.refs_2_, ...), custom_call_target="tpu_custom_call" | custom-call | bytes 1024 | tf_op jit(solution)/shard_map/ffn_backward/pallas_call | solution.py:772
  544.6 8.8 unit_grads.8
  553.4 3.3 convert.63
  560.6 9.0 unit_grads.9
  569.6 33.3 %ffn_backward.3 = (f32[1024,2048]{1,0:T(8,128)}, bf16[1024,512]{1,0:T(8,128)(2,1)}, bf16[1024,256]{1,0:T(8,128)(2,1)}, bf16[1024,256]{1,0:T(8,128)(2,1)}, bf16[1...) custom-call(bf16[3,128,2048]{2,1,0:T(8,128)(2,1)} %copy-done.10, ...), custom_call_target="tpu_custom_call" | custom-call | bytes 1024 | tf_op jit(solution)/shard_map/ffn_backward/pallas_call | solution.py:772
  603.0 3.7 slice.273
  606.8 4.1 collective-permute-done.28
  610.9 3.2 convert_add_fusion
  615.9 2.9 add_convert_fusion.10
  620.8 8.8 unit_grads.10
  629.6 11.1 %collective-permute-done.29 = bf16[256,2048]{1,0:T(8,128)(2,1)S(1)} collective-permute-done((bf16[256,2048]{1,0:T(8,128)(2,1)}, bf16[256,2048]{1,0:T(8,128)(2,1)S(1)}, u32[]{:S(2)}, u32[]{:S(2)}) %collective-permute-start.29) | collective-permute-done | bytes 1048608 | tf_op jit(solution)/shard_map/ppermute | solution.py:65
  642.5 13.1 %collective-permute-done.26 = bf16[3,128,2048]{2,1,0:T(8,128)(2,1)} collective-permute-done((bf16[3,128,2048]{2,1,0:T(8,128)(2,1)}, bf16[3,128,2048]{2,1,0:T(8,128)(2,1)}, u32[]{:S(2)}, u32[]{:S(2)}) %collective-permute-start.26) | collective-permute-done | bytes 1572896 | tf_op jit(solution)/shard_map/ppermute | solution.py:61
  656.1 6.5 add_convert_fusion.8
  664.6 9.0 unit_grads.11
  673.7 27.7 %attend_back.1 = (f32[256,2048]{1,0:T(8,128)}, bf16[256,128]{1,0:T(8,128)(2,1)}, f32[8,2048]{1,0:T(8,128)}, f32[2048,128]{1,0:T(8,128)}, f32[2048,128]{1,0:T(8,1...) custom-call(f32[8,2048]{1,0:T(8,128)} %pad.19.gains, ...), custom_call_target="tpu_custom_call" | custom-call | bytes 1024 | tf_op jit(solution)/shard_map/attend_back/pallas_call | solution.py:867
  709.5 2.9 add_convert_fusion.6
  716.7 9.3 unit_grads.12
  725.9 14.4 %query_back.1 = (bf16[2048,2048]{1,0:T(8,128)(2,1)}, f32[256,2048]{1,0:T(8,128)}, f32[1,256]{1,0:T(1,128)}) custom-call(f32[256,2048]{1,0:T(8,128)} %get-tuple-element.199.grad_query, f32[256,3072]{1,0:T(8,128)} %get-tuple-element.200.raw, f32[256,128]{1,0:T(8,128)} %get-tuple-element.311.cosine, f32[256,128]{1,0:T(8,128)} %get-tuple-element.310.sine, ...), custom_call_target="tpu_custom_call" | custom-call | bytes 1024 | tf_op jit(solution)/shard_map/query_back/pallas_call | solution.py:945
  740.3 20.0 %collective-permute-done.36 = bf16[256,1024]{1,0:T(8,128)(2,1)S(1)} collective-permute-done((bf16[256,1024]{1,0:T(8,128)(2,1)S(1)}, bf16[256,1024]{1,0:T(8,128)(2,1)S(1)}, u32[]{:S(2)}, u32[]{:S(2)}) %collective-permute-start.36) | collective-permute-done | bytes 524320 | tf_op jit(solution)/shard_map/ppermute | solution.py:1348
  761.6 6.1 add_convert_fusion.4
  769.8 8.8 unit_grads.13
  778.6 11.8 %key_back.1 = (bf16[2048,1024]{1,0:T(8,128)(2,1)}, f32[256,2048]{1,0:T(8,128)}, f32[1,256]{1,0:T(1,128)}, f32[1,2048]{1,0:T(1,128)}) custom-call(f32[256,1024]{1,0:T(8,128)} %fusion.6.grad_kv, f32[256,3072]{1,0:T(8,128)} %get-tuple-element.200.raw, f32[256,128]{1,0:T(8,128)} %get-tuple-element.311.cosine, f32[256,128]{1,0:T(8,128)} %get-tuple-element.310.sine, ...), custom_call_target="tpu_custom_call" | custom-call | bytes 1024 | tf_op jit(solution)/shard_map/key_back/pallas_call | solution.py:998
  790.4 13.1 %collective-permute-done.38 = bf16[3,128,2048]{2,1,0:T(8,128)(2,1)S(1)} collective-permute-done((bf16[3,128,2048]{2,1,0:T(8,128)(2,1)}, bf16[3,128,2048]{2,1,0:T(8,128)(2,1)S(1)}, u32[]{:S(2)}, u32[]{:S(2)}) %collective-permute-start.38) | collective-permute-done | bytes 1572896 | tf_op jit(solution)/shard_map/ppermute | solution.py:61
  803.5 6.2 add_convert_fusion.2
  817.8 8.9 unit_grads.14
  830.9 13.9 %collective-permute-done.40 = bf16[3,128,2048]{2,1,0:T(8,128)(2,1)} collective-permute-done((bf16[3,128,2048]{2,1,0:T(8,128)(2,1)}, bf16[3,128,2048]{2,1,0:T(8,128)(2,1)}, u32[]{:S(2)}, u32[]{:S(2)}) %collective-permute-start.40) | collective-permute-done | bytes 1572896 | tf_op jit(solution)/shard_map/ppermute | solution.py:61
  845.1 4.8 add_convert_fusion
  852.0 8.8 unit_grads.15
  860.8 4.6 copy.49
  866.7 115.5 %sum_all.1 = (f32[64,2048]{1,0:T(8,128)}, f32[64,1024]{1,0:T(8,128)}, f32[64,2048]{1,0:T(8,128)}, f32[64,768]{1,0:T(8,128)}, f32[8,128]{1,0:T(8,128)}) custom-call(bf16[8,2,2,64,2048]{4,3,2,1,0:T(8,128)(2,1)} %bitcast.61, bf16[8,2,2,64,1024]{4,3,2,1,0:T(8,128)(2,1)} %bitcast.62, bf16[8,2,2,64,2048]{4,3,2,1,0:T(8,128)(2,1)} %bitcast.60, ...), custom_call_target="tpu_custom_call" | custom-call | bytes 24117248 | tf_op jit(solution)/shard_map/sum_all/pallas_call | solution.py:499
  991.4 4.6 slice_add_fusion.1
  996.0 3.1 maximum_bitcast_fusion
  (253 shorter events, 118.0 us)
Async XLA Ops:
  0.6 6.7 copy-start.41
  0.7 12.1 %copy-start.35 = (bf16[64,2048]{1,0:T(8,128)(2,1)S(1)}, bf16[64,2048]{1,0:T(8,128)(2,1)}, u32[]{:S(2)}) copy-start(bf16[64,2048]{1,0:T(8,128)(2,1)} %param.20) | copy-start | bytes 786436
  0.7 12.1 %copy-start.36 = (bf16[64,1024]{1,0:T(8,128)(2,1)S(1)}, bf16[64,1024]{1,0:T(8,128)(2,1)}, u32[]{:S(2)}) copy-start(bf16[64,1024]{1,0:T(8,128)(2,1)} %param.19) | copy-start | bytes 393220
  2.8 133.9 %copy-start.6 = (bf16[3,128,2048]{2,1,0:T(8,128)(2,1)}, bf16[3,128,2048]{2,1,0:T(8,128)(2,1)S(1)}, u32[]{:S(2)}) copy-start(bf16[3,128,2048]{2,1,0:T(8,128)(2,1)S(1)} %get-tuple-element.300.refs_1_) | copy-start | bytes 4718596
  2.8 133.9 %copy-start.7 = (bf16[3,128,2048]{2,1,0:T(8,128)(2,1)}, bf16[3,128,2048]{2,1,0:T(8,128)(2,1)S(1)}, u32[]{:S(2)}) copy-start(bf16[3,128,2048]{2,1,0:T(8,128)(2,1)S(1)} %get-tuple-element.301.refs_0_) | copy-start | bytes 4718596
  2.9 138.5 %collective-permute-start = (bf16[3,128,2048]{2,1,0:T(8,128)(2,1)S(1)}, bf16[3,128,2048]{2,1,0:T(8,128)(2,1)}, u32[]{:S(2)}, u32[]{:S(2)}) collective-permute-start(bf16[3,128,2048]{2,1,0:T(8,128)(2,1)S(1)} %get-tuple-element.301.refs_0_), channel_id=1, source_target_pairs={{0,8},{8,16},{16,24},{24,28},{28,20},{20,12},{12,4},{4,0},{1,9},{9... | collective-permute-start | bytes 4718600 | tf_op jit(solution)/shard_map/ppermute | solution.py:61
  5.9 135.4 %collective-permute-start.1 = (bf16[3,128,2048]{2,1,0:T(8,128)(2,1)S(1)}, bf16[3,128,2048]{2,1,0:T(8,128)(2,1)}, u32[]{:S(2)}, u32[]{:S(2)}) collective-permute-start(bf16[3,128,2048]{2,1,0:T(8,128)(2,1)S(1)} %get-tuple-element.300.refs_1_), channel_id=1, source_target_pairs={{0,4},{8,0},{16,8},{24,16},{28,24},{20,28},{12,20},{4,12},{1,5},{9... | collective-permute-start | bytes 4718600 | tf_op jit(solution)/shard_map/ppermute | solution.py:61
  158.3 9.3 collective-permute-start.4
  159.8 16.0 %collective-permute-start.5 = (bf16[256,1024]{1,0:T(8,128)(2,1)}, bf16[256,1024]{1,0:T(8,128)(2,1)}, u32[]{:S(2)}, u32[]{:S(2)}) collective-permute-start(bf16[256,1024]{1,0:T(8,128)(2,1)} %slice.163), channel_id=1, source_target_pairs={{0,4},{4,8},{8,12},{12,20},{1,5},{5,9},{9,13},{13,21},{2,6},{6,10}... | collective-permute-start | bytes 1572872 | tf_op jit(solution)/shard_map/ppermute | solution.py:1188
  164.0 37.6 %collective-permute-start.2 = (bf16[3,128,2048]{2,1,0:T(8,128)(2,1)}, bf16[3,128,2048]{2,1,0:T(8,128)(2,1)S(1)}, u32[]{:S(2)}, u32[]{:S(2)}) collective-permute-start(bf16[3,128,2048]{2,1,0:T(8,128)(2,1)} %collective-permute-done.refs_2_), channel_id=1, source_target_pairs={{0,8},{8,16},{16,24},{24,28},{28,20},{20,12},{12,4},{4,0},{1,9},{9... | collective-permute-start | bytes 4718600 | tf_op jit(solution)/shard_map/ppermute | solution.py:61
  167.6 41.3 %collective-permute-start.3 = (bf16[3,128,2048]{2,1,0:T(8,128)(2,1)}, bf16[3,128,2048]{2,1,0:T(8,128)(2,1)S(1)}, u32[]{:S(2)}, u32[]{:S(2)}) collective-permute-start(bf16[3,128,2048]{2,1,0:T(8,128)(2,1)} %collective-permute-done.1.refs_3_), channel_id=1, source_target_pairs={{0,4},{8,0},{16,8},{24,16},{28,24},{20,28},{12,20},{4,12},{1,5},{9... | collective-permute-start | bytes 4718600 | tf_op jit(solution)/shard_map/ppermute | solution.py:61
  177.7 1.4 collective-permute-start.6
  181.4 2.3 collective-permute-start.7
  201.5 30.4 %copy-start.14 = (bf16[3,128,2048]{2,1,0:T(8,128)(2,1)}, bf16[3,128,2048]{2,1,0:T(8,128)(2,1)S(1)}, u32[]{:S(2)}) copy-start(bf16[3,128,2048]{2,1,0:T(8,128)(2,1)S(1)} %collective-permute-done.2.refs_4_) | copy-start | bytes 4718596
  208.9 23.0 %copy-start.15 = (bf16[3,128,2048]{2,1,0:T(8,128)(2,1)}, bf16[3,128,2048]{2,1,0:T(8,128)(2,1)S(1)}, u32[]{:S(2)}) copy-start(bf16[3,128,2048]{2,1,0:T(8,128)(2,1)S(1)} %collective-permute-done.3.refs_5_) | copy-start | bytes 4718596
  208.9 49.1 %collective-permute-start.8 = (bf16[3,128,2048]{2,1,0:T(8,128)(2,1)S(1)}, bf16[3,128,2048]{2,1,0:T(8,128)(2,1)}, u32[]{:S(2)}, u32[]{:S(2)}) collective-permute-start(bf16[3,128,2048]{2,1,0:T(8,128)(2,1)S(1)} %collective-permute-done.2.refs_4_), channel_id=1, source_target_pairs={{0,8},{8,16},{16,24},{24,28},{28,20},{20,12},{12,4},{4,0},{1,9},{9... | collective-permute-start | bytes 4718600 | tf_op jit(solution)/shard_map/ppermute | solution.py:61
  208.9 49.1 %collective-permute-start.9 = (bf16[3,128,2048]{2,1,0:T(8,128)(2,1)S(1)}, bf16[3,128,2048]{2,1,0:T(8,128)(2,1)}, u32[]{:S(2)}, u32[]{:S(2)}) collective-permute-start(bf16[3,128,2048]{2,1,0:T(8,128)(2,1)S(1)} %collective-permute-done.3.refs_5_), channel_id=1, source_target_pairs={{0,4},{8,0},{16,8},{24,16},{28,24},{20,28},{12,20},{4,12},{1,5},{9... | collective-permute-start | bytes 4718600 | tf_op jit(solution)/shard_map/ppermute | solution.py:61
  231.9 24.6 %collective-permute-start.10 = (bf16[256,2048]{1,0:T(8,128)(2,1)}, bf16[256,2048]{1,0:T(8,128)(2,1)S(1)}, u32[]{:S(2)}, u32[]{:S(2)}) collective-permute-start(bf16[256,2048]{1,0:T(8,128)(2,1)} %get-tuple-element.139), channel_id=1, source_target_pairs={{0,1},{1,0},{2,3},{3,2},{4,5},{5,4},{6,7},{7,6},{8,9},{9,8},{10,11... | collective-permute-start | bytes 3145736 | tf_op jit(solution)/shard_map/ppermute | solution.py:65
  258.0 11.3 %collective-permute-start.13 = (bf16[512,2048]{1,0:T(8,128)(2,1)S(1)}, bf16[512,2048]{1,0:T(8,128)(2,1)S(1)}, u32[]{:S(2)}, u32[]{:S(2)}) collective-permute-start(bf16[512,2048]{1,0:T(8,128)(2,1)S(1)} %pad_maximum_fusion.1), channel_id=1, source_target_pairs={{0,2},{2,0},{1,3},{3,1},{4,6},{6,4},{5,7},{7,5},{8,10},{10,8},{9,1... | collective-permute-start | bytes 6291464 | tf_op jit(solution)/shard_map/ppermute | solution.py:65
  258.1 45.8 %collective-permute-start.11 = (bf16[3,128,2048]{2,1,0:T(8,128)(2,1)}, bf16[3,128,2048]{2,1,0:T(8,128)(2,1)S(1)}, u32[]{:S(2)}, u32[]{:S(2)}) collective-permute-start(bf16[3,128,2048]{2,1,0:T(8,128)(2,1)} %collective-permute-done.8.refs_6_), channel_id=1, source_target_pairs={{0,8},{8,16},{16,24},{24,28},{28,20},{20,12},{12,4},{4,0},{1,9},{9... | collective-permute-start | bytes 4718600 | tf_op jit(solution)/shard_map/ppermute | solution.py:61
  266.4 37.7 %collective-permute-start.12 = (bf16[3,128,2048]{2,1,0:T(8,128)(2,1)}, bf16[3,128,2048]{2,1,0:T(8,128)(2,1)S(1)}, u32[]{:S(2)}, u32[]{:S(2)}) collective-permute-start(bf16[3,128,2048]{2,1,0:T(8,128)(2,1)} %collective-permute-done.9.refs_7_), channel_id=1, source_target_pairs={{0,4},{8,0},{16,8},{24,16},{28,24},{20,28},{12,20},{4,12},{1,5},{9... | collective-permute-start | bytes 4718600 | tf_op jit(solution)/shard_map/ppermute | solution.py:61
  303.9 41.3 %copy-start.10 = (bf16[3,128,2048]{2,1,0:T(8,128)(2,1)}, bf16[3,128,2048]{2,1,0:T(8,128)(2,1)S(1)}, u32[]{:S(2)}) copy-start(bf16[3,128,2048]{2,1,0:T(8,128)(2,1)S(1)} %collective-permute-done.11.refs_0_) | copy-start | bytes 4718596
  304.1 41.1 %copy-start.11 = (bf16[3,128,2048]{2,1,0:T(8,128)(2,1)}, bf16[3,128,2048]{2,1,0:T(8,128)(2,1)S(1)}, u32[]{:S(2)}) copy-start(bf16[3,128,2048]{2,1,0:T(8,128)(2,1)S(1)} %collective-permute-done.12.refs_1_) | copy-start | bytes 4718596
  304.1 36.9 %collective-permute-start.14 = (bf16[3,128,2048]{2,1,0:T(8,128)(2,1)S(1)}, bf16[3,128,2048]{2,1,0:T(8,128)(2,1)S(1)}, u32[]{:S(2)}, u32[]{:S(2)}) collective-permute-start(bf16[3,128,2048]{2,1,0:T(8,128)(2,1)S(1)} %collective-permute-done.11.refs_0_), channel_id=1, source_target_pairs={{0,8},{8,16},{16,24},{24,28},{28,20},{20,12},{12,4},{4,0},{1,9},{9... | collective-permute-start | bytes 4718600 | tf_op jit(solution)/shard_map/ppermute | solution.py:61
  307.5 35.7 %collective-permute-start.15 = (bf16[3,128,2048]{2,1,0:T(8,128)(2,1)S(1)}, bf16[3,128,2048]{2,1,0:T(8,128)(2,1)S(1)}, u32[]{:S(2)}, u32[]{:S(2)}) collective-permute-start(bf16[3,128,2048]{2,1,0:T(8,128)(2,1)S(1)} %collective-permute-done.12.refs_1_), channel_id=1, source_target_pairs={{0,4},{8,0},{16,8},{24,16},{28,24},{20,28},{12,20},{4,12},{1,5},{9... | collective-permute-start | bytes 4718600 | tf_op jit(solution)/shard_map/ppermute | solution.py:61
  343.2 34.9 %collective-permute-start.16 = (bf16[3,128,2048]{2,1,0:T(8,128)(2,1)S(1)}, bf16[3,128,2048]{2,1,0:T(8,128)(2,1)}, u32[]{:S(2)}, u32[]{:S(2)}) collective-permute-start(bf16[3,128,2048]{2,1,0:T(8,128)(2,1)S(1)} %collective-permute-done.14.refs_2_), channel_id=1, source_target_pairs={{0,8},{8,16},{16,24},{24,28},{28,20},{20,12},{12,4},{4,0},{1,9},{9... | collective-permute-start | bytes 4718600 | tf_op jit(solution)/shard_map/ppermute | solution.py:61
  344.6 34.3 %collective-permute-start.17 = (bf16[3,128,2048]{2,1,0:T(8,128)(2,1)S(1)}, bf16[3,128,2048]{2,1,0:T(8,128)(2,1)}, u32[]{:S(2)}, u32[]{:S(2)}) collective-permute-start(bf16[3,128,2048]{2,1,0:T(8,128)(2,1)S(1)} %collective-permute-done.15.refs_3_), channel_id=1, source_target_pairs={{0,4},{8,0},{16,8},{24,16},{28,24},{20,28},{12,20},{4,12},{1,5},{9... | collective-permute-start | bytes 4718600 | tf_op jit(solution)/shard_map/ppermute | solution.py:61
  378.8 33.4 %collective-permute-start.18 = (bf16[3,128,2048]{2,1,0:T(8,128)(2,1)}, bf16[3,128,2048]{2,1,0:T(8,128)(2,1)S(1)}, u32[]{:S(2)}, u32[]{:S(2)}) collective-permute-start(bf16[3,128,2048]{2,1,0:T(8,128)(2,1)} %collective-permute-done.16.refs_0_.refs_4_), channel_id=1, source_target_pairs={{0,8},{8,16},{16,24},{24,28},{28,20},{20,12},{12,4},{4,0},{1,9},{9... | collective-permute-start | bytes 4718600 | tf_op jit(solution)/shard_map/ppermute | solution.py:61
  380.6 33.7 %collective-permute-start.19 = (bf16[3,128,2048]{2,1,0:T(8,128)(2,1)}, bf16[3,128,2048]{2,1,0:T(8,128)(2,1)S(1)}, u32[]{:S(2)}, u32[]{:S(2)}) collective-permute-start(bf16[3,128,2048]{2,1,0:T(8,128)(2,1)} %collective-permute-done.17.refs_1_.refs_5_), channel_id=1, source_target_pairs={{0,4},{8,0},{16,8},{24,16},{28,24},{20,28},{12,20},{4,12},{1,5},{9... | collective-permute-start | bytes 4718600 | tf_op jit(solution)/shard_map/ppermute | solution.py:61
  430.4 4.2 collective-permute-start.20
  439.5 25.3 %collective-permute-start.21 = (bf16[256,2048]{1,0:T(8,128)(2,1)S(1)}, bf16[256,2048]{1,0:T(8,128)(2,1)S(1)}, u32[]{:S(2)}, u32[]{:S(2)}) collective-permute-start(bf16[256,2048]{1,0:T(8,128)(2,1)S(1)} %slice.276), channel_id=1, source_target_pairs={{0,1},{1,0},{2,3},{3,2},{4,5},{5,4},{6,7},{7,6},{8,9},{9,8},{10,11... | collective-permute-start | bytes 3145736 | tf_op jit(solution)/shard_map/ppermute | solution.py:65
  443.2 23.5 %copy-start.9 = (f32[256,2048]{1,0:T(8,128)S(1)}, f32[256,2048]{1,0:T(8,128)}, u32[]{:S(2)}) copy-start(f32[256,2048]{1,0:T(8,128)} %get-tuple-element.136.mixed) | copy-start | bytes 6291460
  474.9 5.2 copy-start.18
  481.4 24.4 %collective-permute-start.22 = (bf16[256,2048]{1,0:T(8,128)(2,1)S(1)}, bf16[256,2048]{1,0:T(8,128)(2,1)S(1)}, u32[]{:S(2)}, u32[]{:S(2)}) collective-permute-start(bf16[256,2048]{1,0:T(8,128)(2,1)S(1)} %fusion.3), channel_id=1, source_target_pairs={{0,1},{1,0},{2,3},{3,2},{4,5},{5,4},{6,7},{7,6},{8,9},{9,8},{10,11... | collective-permute-start | bytes 3145736 | tf_op jit(solution)/shard_map/ppermute | solution.py:65
  506.0 4.2 collective-permute-start.23
  558.6 44.4 %collective-permute-start.24 = (bf16[3,128,2048]{2,1,0:T(8,128)(2,1)}, bf16[3,128,2048]{2,1,0:T(8,128)(2,1)S(1)}, u32[]{:S(2)}, u32[]{:S(2)}) collective-permute-start(bf16[3,128,2048]{2,1,0:T(8,128)(2,1)} %get-tuple-element.299), channel_id=1, source_target_pairs={{0,8},{8,16},{16,24},{24,28},{28,20},{20,12},{12,4},{4,0},{1,9},{9... | collective-permute-start | bytes 4718600 | tf_op jit(solution)/shard_map/ppermute | solution.py:61
  559.4 43.6 %collective-permute-start.25 = (bf16[3,128,2048]{2,1,0:T(8,128)(2,1)}, bf16[3,128,2048]{2,1,0:T(8,128)(2,1)S(1)}, u32[]{:S(2)}, u32[]{:S(2)}) collective-permute-start(bf16[3,128,2048]{2,1,0:T(8,128)(2,1)} %get-tuple-element.298), channel_id=1, source_target_pairs={{0,4},{8,0},{16,8},{24,16},{28,24},{20,28},{12,20},{4,12},{1,5},{9... | collective-permute-start | bytes 4718600 | tf_op jit(solution)/shard_map/ppermute | solution.py:61
  603.0 12.9 %slice-start.1 = ((s8[6291456]{0:T(1024)(128)(4,1)}), s8[4194304]{0:T(1024)(128)(4,1)S(1)}, s32[]{:S(2)}) async-start(s8[6291456]{0:T(1024)(128)(4,1)} %bitcast.53), calls=%async_computation.1 | async-start | bytes 8388608
  606.7 9.2 slice-start.2
  606.7 4.2 collective-permute-start.28
  610.9 4.9 copy-start.26
  615.3 25.4 %collective-permute-start.29 = (bf16[256,2048]{1,0:T(8,128)(2,1)}, bf16[256,2048]{1,0:T(8,128)(2,1)S(1)}, u32[]{:S(2)}, u32[]{:S(2)}) collective-permute-start(bf16[256,2048]{1,0:T(8,128)(2,1)} %slice.275), channel_id=1, source_target_pairs={{0,1},{1,0},{2,3},{3,2},{4,5},{5,4},{6,7},{7,6},{8,9},{9,8},{10,11... | collective-permute-start | bytes 3145736 | tf_op jit(solution)/shard_map/ppermute | solution.py:65
  618.8 36.8 %collective-permute-start.26 = (bf16[3,128,2048]{2,1,0:T(8,128)(2,1)}, bf16[3,128,2048]{2,1,0:T(8,128)(2,1)}, u32[]{:S(2)}, u32[]{:S(2)}) collective-permute-start(bf16[3,128,2048]{2,1,0:T(8,128)(2,1)} %get-tuple-element.297), channel_id=1, source_target_pairs={{0,8},{8,16},{16,24},{24,28},{28,20},{20,12},{12,4},{4,0},{1,9},{9... | collective-permute-start | bytes 4718600 | tf_op jit(solution)/shard_map/ppermute | solution.py:61
  619.6 36.5 %collective-permute-start.27 = (bf16[3,128,2048]{2,1,0:T(8,128)(2,1)}, bf16[3,128,2048]{2,1,0:T(8,128)(2,1)}, u32[]{:S(2)}, u32[]{:S(2)}) collective-permute-start(bf16[3,128,2048]{2,1,0:T(8,128)(2,1)} %get-tuple-element.296), channel_id=1, source_target_pairs={{0,4},{8,0},{16,8},{24,16},{28,24},{20,28},{12,20},{4,12},{1,5},{9... | collective-permute-start | bytes 4718600 | tf_op jit(solution)/shard_map/ppermute | solution.py:61
  662.6 38.8 %collective-permute-start.30 = (bf16[3,128,2048]{2,1,0:T(8,128)(2,1)}, bf16[3,128,2048]{2,1,0:T(8,128)(2,1)S(1)}, u32[]{:S(2)}, u32[]{:S(2)}) collective-permute-start(bf16[3,128,2048]{2,1,0:T(8,128)(2,1)} %get-tuple-element.295), channel_id=1, source_target_pairs={{0,8},{8,16},{16,24},{24,28},{28,20},{20,12},{12,4},{4,0},{1,9},{9... | collective-permute-start | bytes 4718600 | tf_op jit(solution)/shard_map/ppermute | solution.py:61
  663.5 37.9 %collective-permute-start.31 = (bf16[3,128,2048]{2,1,0:T(8,128)(2,1)}, bf16[3,128,2048]{2,1,0:T(8,128)(2,1)S(1)}, u32[]{:S(2)}, u32[]{:S(2)}) collective-permute-start(bf16[3,128,2048]{2,1,0:T(8,128)(2,1)} %get-tuple-element.294), channel_id=1, source_target_pairs={{0,4},{8,0},{16,8},{24,16},{28,24},{20,28},{12,20},{4,12},{1,5},{9... | collective-permute-start | bytes 4718600 | tf_op jit(solution)/shard_map/ppermute | solution.py:61
  703.1 6.4 copy-start.24
  703.1 6.4 copy-start.28
  704.8 4.7 copy-start.3
  706.6 2.0 collective-permute-start.34
  708.8 5.7 collective-permute-start.35
  712.4 49.2 %collective-permute-start.32 = (bf16[3,128,2048]{2,1,0:T(8,128)(2,1)}, bf16[3,128,2048]{2,1,0:T(8,128)(2,1)}, u32[]{:S(2)}, u32[]{:S(2)}) collective-permute-start(bf16[3,128,2048]{2,1,0:T(8,128)(2,1)} %get-tuple-element.293), channel_id=1, source_target_pairs={{0,8},{8,16},{16,24},{24,28},{28,20},{20,12},{12,4},{4,0},{1,9},{9... | collective-permute-start | bytes 4718600 | tf_op jit(solution)/shard_map/ppermute | solution.py:61
  713.3 48.3 %collective-permute-start.33 = (bf16[3,128,2048]{2,1,0:T(8,128)(2,1)}, bf16[3,128,2048]{2,1,0:T(8,128)(2,1)}, u32[]{:S(2)}, u32[]{:S(2)}) collective-permute-start(bf16[3,128,2048]{2,1,0:T(8,128)(2,1)} %get-tuple-element.292), channel_id=1, source_target_pairs={{0,4},{8,0},{16,8},{24,16},{28,24},{20,28},{12,20},{4,12},{1,5},{9... | collective-permute-start | bytes 4718600 | tf_op jit(solution)/shard_map/ppermute | solution.py:61
  714.7 45.6 %collective-permute-start.36 = (bf16[256,1024]{1,0:T(8,128)(2,1)S(1)}, bf16[256,1024]{1,0:T(8,128)(2,1)S(1)}, u32[]{:S(2)}, u32[]{:S(2)}) collective-permute-start(bf16[256,1024]{1,0:T(8,128)(2,1)S(1)} %add_convert_fusion.12), channel_id=1, source_target_pairs={{4,0},{8,4},{12,8},{20,12},{5,1},{9,5},{13,9},{21,13},{6,2},{10,6}... | collective-permute-start | bytes 1572872 | tf_op jit(solution)/shard_map/ppermute | solution.py:1348
  716.0 44.3 %collective-permute-start.37 = (bf16[256,1024]{1,0:T(8,128)(2,1)S(1)}, bf16[256,1024]{1,0:T(8,128)(2,1)S(1)}, u32[]{:S(2)}, u32[]{:S(2)}) collective-permute-start(bf16[256,1024]{1,0:T(8,128)(2,1)S(1)} %add_convert_fusion.12), channel_id=1, source_target_pairs={{16,12},{17,13},{18,14},{19,15}} | collective-permute-start | bytes 1572872 | tf_op jit(solution)/shard_map/ppermute | solution.py:1349
  767.7 35.8 %collective-permute-start.38 = (bf16[3,128,2048]{2,1,0:T(8,128)(2,1)}, bf16[3,128,2048]{2,1,0:T(8,128)(2,1)S(1)}, u32[]{:S(2)}, u32[]{:S(2)}) collective-permute-start(bf16[3,128,2048]{2,1,0:T(8,128)(2,1)} %get-tuple-element.291), channel_id=1, source_target_pairs={{0,8},{8,16},{16,24},{24,28},{28,20},{20,12},{12,4},{4,0},{1,9},{9... | collective-permute-start | bytes 4718600 | tf_op jit(solution)/shard_map/ppermute | solution.py:61
  767.8 35.7 %collective-permute-start.39 = (bf16[3,128,2048]{2,1,0:T(8,128)(2,1)S(1)}, bf16[3,128,2048]{2,1,0:T(8,128)(2,1)}, u32[]{:S(2)}, u32[]{:S(2)}) collective-permute-start(bf16[3,128,2048]{2,1,0:T(8,128)(2,1)S(1)} %get-tuple-element.290), channel_id=1, source_target_pairs={{0,4},{8,0},{16,8},{24,16},{28,24},{20,28},{12,20},{4,12},{1,5},{9... | collective-permute-start | bytes 4718600 | tf_op jit(solution)/shard_map/ppermute | solution.py:61
  803.5 8.2 copy-start.19
  809.7 35.1 %collective-permute-start.40 = (bf16[3,128,2048]{2,1,0:T(8,128)(2,1)}, bf16[3,128,2048]{2,1,0:T(8,128)(2,1)}, u32[]{:S(2)}, u32[]{:S(2)}) collective-permute-start(bf16[3,128,2048]{2,1,0:T(8,128)(2,1)} %get-tuple-element.289), channel_id=1, source_target_pairs={{0,8},{8,16},{16,24},{24,28},{28,20},{20,12},{12,4},{4,0},{1,9},{9... | collective-permute-start | bytes 4718600 | tf_op jit(solution)/shard_map/ppermute | solution.py:61
  811.0 34.1 %collective-permute-start.41 = (bf16[3,128,2048]{2,1,0:T(8,128)(2,1)}, bf16[3,128,2048]{2,1,0:T(8,128)(2,1)}, u32[]{:S(2)}, u32[]{:S(2)}) collective-permute-start(bf16[3,128,2048]{2,1,0:T(8,128)(2,1)} %get-tuple-element.288), channel_id=1, source_target_pairs={{0,4},{8,0},{16,8},{24,16},{28,24},{20,28},{12,20},{4,12},{1,5},{9... | collective-permute-start | bytes 4718600 | tf_op jit(solution)/shard_map/ppermute | solution.py:61
  817.7 9.8 copy-start.33
  849.9 141.4 %collective-permute-start.42 = (bf16[3,128,2048]{2,1,0:T(8,128)(2,1)S(1)}, bf16[3,128,2048]{2,1,0:T(8,128)(2,1)}, u32[]{:S(2)}, u32[]{:S(2)}) collective-permute-start(bf16[3,128,2048]{2,1,0:T(8,128)(2,1)S(1)} %get-tuple-element.287), channel_id=1, source_target_pairs={{0,8},{8,16},{16,24},{24,28},{28,20},{20,12},{12,4},{4,0},{1,9},{9... | collective-permute-start | bytes 4718600 | tf_op jit(solution)/shard_map/ppermute | solution.py:61
  850.8 140.6 %collective-permute-start.43 = (bf16[3,128,2048]{2,1,0:T(8,128)(2,1)S(1)}, bf16[3,128,2048]{2,1,0:T(8,128)(2,1)}, u32[]{:S(2)}, u32[]{:S(2)}) collective-permute-start(bf16[3,128,2048]{2,1,0:T(8,128)(2,1)S(1)} %get-tuple-element.286), channel_id=1, source_target_pairs={{0,4},{8,0},{16,8},{24,16},{28,24},{20,28},{12,20},{4,12},{1,5},{9... | collective-permute-start | bytes 4718600 | tf_op jit(solution)/shard_map/ppermute | solution.py:61
  996.0 4.6 copy-start.30
  (25 other events, 53.0 us)

commit v4 on v3

--- a/solution.py
+++ b/solution.py
@@ -244,9 +244,9 @@
 
 
 def sum_kernel(chips, streams, counts, *refs):
-    arrays, (tile,), outs, (tile_out,), held, core_in, ring_in, x_in, tiles, sems = refs_of(counts, refs)
-    load_sem, core_send, core_recv, ring_send, ring_recv, x_send, x_recv, tile_send, tile_recv = sems
-    tile_pairs, tile_ring = tiles
+    arrays, (tile, up_sum, down_sum, terms), outs, (tile_out, units_out), held, core_in, ring_in, x_in, tiles, sems = refs_of(counts, refs)
+    load_sem, core_send, core_recv, ring_send, ring_recv, x_send, x_recv, tile_send, tile_recv, hop_send, hop_recv = sems
+    tile_pairs, tile_ring, up_in, down_in = tiles
     chip = lax.axis_index("zy")
     core = lax.axis_index("core")
     side = lax.axis_index("fsdp")
@@ -324,6 +324,18 @@
             core_copy(number, turn).start()
         return carry
 
+    half = up_in.shape[1]
+
+    def hop_copy(way, kind):
+        src, dst = ((up_sum, up_in), (down_sum, down_in))[way]
+        return remote(src.at[kind], dst.at[kind], hop_send.at[way, kind], hop_recv.at[way, kind], neighbour(1 - 2 * way))
+
+    def hop_done(kind):
+        for way, arrived in enumerate((up_in, down_in)):
+            rows_here = pl.ds(way * half, half)
+            hop_copy(way, kind).wait()
+            units_out[kind, rows_here] = terms[kind, rows_here].astype(F32) + arrived[kind].astype(F32)
+
     def tile_copy(src, dst, number, peer):
         return remote(src, dst, tile_send.at[number], tile_recv.at[number], peer)
 
@@ -374,6 +386,17 @@
         @pl.when(turn < chips)
         def _():
             tile_turn(turn).start()
+
+        for kind in range(3):
+
+            @pl.when(turn == 1 + kind)
+            def _(kind=kind):
+                for way in range(2):
+                    hop_copy(way, kind).start()
+
+            @pl.when(turn == 5 + kind)
+            def _(kind=kind):
+                hop_done(kind)
 
         @pl.when(turn < chips)
         def _():
@@ -474,7 +497,7 @@
     return groups
 
 
-def sum_all(arrays, firsts, tile, chips):
+def sum_all(arrays, firsts, tile, up_sum, down_sum, terms, chips):
     rows = arrays[0].shape[0] // (4 * chips)
     streams = []
     for i, (array, first) in enumerate(zip(arrays, firsts)):
@@ -492,27 +515,32 @@
         + [vmem((chips - 1, 1 if first else 2, rows, width), BF16) for _, _, width, _, first in streams]
         + [vmem((chips if first else 1, rows, width), BF16) for _, _, width, _, first in streams]
         + [vmem((3, 8, 128), F32), vmem((chips, 8, 128), F32)]
+        + [vmem(up_sum.shape, BF16), vmem(down_sum.shape, BF16)]
         + [dma((count,))]
         + [dma((number, chips)) for _ in range(6)]
         + [dma((chips + 1,)) for _ in range(2)]
+        + [dma((2, 3)) for _ in range(2)]
     )
     return pl.pallas_call(
         functools.partial(
-            sum_kernel, chips, streams, (count, 1, count, 1, count, count, number, number, 2, 9)
+            sum_kernel, chips, streams, (count, 4, count, 2, count, count, number, number, 4, 11)
         ),
         out_shape=[jax.ShapeDtypeStruct((rows, a.shape[1]), F32) for a in arrays]
-        + [jax.ShapeDtypeStruct((8, 128), F32)],
-        in_specs=[pl.BlockSpec(memory_space=pl.ANY)] * count + [pl.BlockSpec(memory_space=pltpu.VMEM)],
-        out_specs=[pl.BlockSpec(memory_space=pltpu.VMEM)] * (count + 1),
+        + [jax.ShapeDtypeStruct((8, 128), F32), jax.ShapeDtypeStruct(terms.shape, F32)],
+        in_specs=[pl.BlockSpec(memory_space=pl.ANY)] * count
+        + [pl.BlockSpec(memory_space=pltpu.VMEM)]
+        + [pl.BlockSpec(memory_space=pl.ANY)] * 2
+        + [pl.BlockSpec(memory_space=pltpu.VMEM)],
+        out_specs=[pl.BlockSpec(memory_space=pltpu.VMEM)] * (count + 2),
         scratch_shapes=scratch,
         compiler_params=pltpu.CompilerParams(
-            collective_id=1, has_side_effects=True, vmem_limit_bytes=56 << 20
+            collective_id=1, has_side_effects=True, vmem_limit_bytes=58 << 20
         ),
         cost_estimate=pl.CostEstimate(
             flops=0, bytes_accessed=sum(2 * a.size for a in arrays), transcendentals=0
         ),
         name="sum_all",
-    )(*[a.reshape(chips, 2, 2, rows, a.shape[1]) for a in arrays], tile)
+    )(*[a.reshape(chips, 2, 2, rows, a.shape[1]) for a in arrays], tile, up_sum, down_sum, terms)
 
 
 LITTLE = pl.CostEstimate(flops=0, bytes_accessed=1024, transcendentals=0)
@@ -675,18 +703,6 @@
         count = ref.shape[1]
         copies.append(pltpu.make_async_copy(ref, held.at[:, pl.ds(at, count)], sems.at[number]))
         at += count
-    return copies
-
-
-UNIT_BLOCK = 256
-
-
-def ffn_forward_kernel(count, add, *refs):
-    weights, refs = refs[:count], refs[count:]
-    if add:
-        before, refs = refs[0], refs[1:]
-    rows, total, gate, upper, hidden, held, sems = refs
-    copies = load_weights(weights, held, sems)
 
     @pl.when(pl.program_id(0) == 0)
     def _():
@@ -695,110 +711,146 @@
         for copy in copies:
             copy.wait()
 
+
+ROW_BLOCK = 256
+UNIT_BLOCK = 512
+
+
+def unit_blocks(steps, units):
+    many = max(1, UNIT_BLOCK // units)
+    return [range(first, min(first + many, steps)) for first in range(0, steps, many)]
+
+
+def ffn_forward_kernel(steps, add, last, *refs):
+    weights, refs = refs[: 2 * steps], refs[2 * steps :]
+    if add:
+        before, refs = refs[0], refs[1:]
+    rows, total, refs = refs[0], refs[1], refs[2:]
+    if last:
+        low_total, refs = refs[0], refs[1:]
+    gates, uppers, hiddens, (held, sems) = refs_of((steps, steps, steps, 2), refs)
+    load_weights(weights, held, sems)
+    units = held.shape[1] // steps
     here = rows[...]
     running = before[...] if add else None
-    for first in range(0, held.shape[1], UNIT_BLOCK):
-        cut = slice(first, first + UNIT_BLOCK)
+    for block in unit_blocks(steps, units):
+        cut = slice(block[0] * units, (block[-1] + 1) * units)
         gate_in = right_dot(here, held[0, cut])
         upper_in = right_dot(here, held[1, cut])
         low = gated_product(gate_in, upper_in).astype(BF16)
-        gate[:, cut] = gate_in
-        upper[:, cut] = upper_in
-        hidden[:, cut] = low
+        for i, step in enumerate(block):
+            own = slice(i * units, (i + 1) * units)
+            gates[step][...] = gate_in[:, own]
+            uppers[step][...] = upper_in[:, own]
+            hiddens[step][...] = low[:, own]
         term = full_dot(low, held[2, cut])
         running = term if running is None else running + term
-    total[...] = running
-
-
-def ffn_forward(rows, before, weights):
-    many, step = rows.shape[0], 256
-    units = sum(w.shape[1] for w in weights)
-    by_row = lambda width: pl.BlockSpec((step, width), lambda i: (i, 0))
+    write_sum(running, total, low_total if last else None)
+
+
+def write_sum(running, total, low_total):
+    if low_total is None:
+        total[...] = running
+        return
+    half = pl.num_programs(0) // 2
+
+    @pl.when(pl.program_id(0) < half)
+    def _():
+        low_total[...] = running.astype(BF16)
+
+    @pl.when(pl.program_id(0) >= half)
+    def _():
+        total[...] = running
+
+
+def sum_specs(many, last):
+    blocks = many // ROW_BLOCK
+    half = blocks // 2
+    if not last:
+        return (lambda i: i), [pl.BlockSpec((ROW_BLOCK, D), lambda i: (i, 0))], [((many, D), F32)]
+    specs = [
+        pl.BlockSpec((ROW_BLOCK, D), lambda i: (jnp.maximum(i - half, 0), 0)),
+        pl.BlockSpec((ROW_BLOCK, D), lambda i: (jnp.minimum(i, half - 1), 0)),
+    ]
+    return (lambda i: lax.rem(i + half, blocks)), specs, [((many // 2, D), F32), ((many // 2, D), BF16)]
+
+
+def ffn_forward(rows, before, weights, last):
+    many = rows.shape[0]
+    steps, units = len(weights) // 2, 2 * weights[0].shape[1]
+    at, sums, sum_shapes = sum_specs(many, last)
+    by_row = lambda width: pl.BlockSpec((ROW_BLOCK, width), lambda i: (at(i), 0))
     add = before is not None
-    return piece(
-        functools.partial(ffn_forward_kernel, len(weights), add),
+    outs = piece(
+        functools.partial(ffn_forward_kernel, steps, add, last),
         "ffn_forward",
-        (many // step,),
+        (many // ROW_BLOCK,),
         [pl.BlockSpec(memory_space=pl.ANY)] * len(weights) + [by_row(D)] * (1 + add),
-        [by_row(D), by_row(units), by_row(units), by_row(units)],
-        [((many, D), F32), ((many, units), F32), ((many, units), F32), ((many, units), BF16)],
-        [pltpu.VMEM((3, units, D), BF16), pltpu.SemaphoreType.DMA((len(weights),))],
+        sums + [by_row(units)] * (3 * steps),
+        sum_shapes + [((many, units), F32)] * (2 * steps) + [((many, units), BF16)] * steps,
+        [pltpu.VMEM((3, steps * units, D), BF16), pltpu.SemaphoreType.DMA((len(weights),))],
     )(*weights, *([before] if add else []), rows)
-
-
-def ffn_backward_kernel(count, widths, add, *refs):
-    weights, refs = refs[:count], refs[count:]
+    return refs_of((len(sums), steps, steps, steps), outs)
+
+
+def ffn_backward_kernel(steps, add, last, *refs):
+    weights, refs = refs[: 2 * steps], refs[2 * steps :]
     if add:
         before, refs = refs[0], refs[1:]
-    number = len(widths)
-    rows, refs = refs[0], refs[1:]
-    gates, uppers, refs = refs[:number], refs[number : 2 * number], refs[2 * number :]
-    total, refs = refs[0], refs[1:]
-    grad_gates, grad_uppers, (held, sems) = refs[:number], refs[number : 2 * number], refs[2 * number :]
-    copies = load_weights(weights, held, sems)
-
-    @pl.when(pl.program_id(0) == 0)
-    def _():
-        for copy in copies:
-            copy.start()
-        for copy in copies:
-            copy.wait()
-
+    (rows,), gates, uppers, totals, grad_gates, grad_uppers, (held, sems) = refs_of(
+        (1, steps, steps, 1 + last, steps, steps, 2), refs
+    )
+    load_weights(weights, held, sems)
+    units = held.shape[1] // steps
     here = rows[...]
     running = before[...] if add else None
-    at = 0
-    for gate, upper, grad_gate, grad_upper, width in zip(gates, uppers, grad_gates, grad_uppers, widths):
-        for first in range(0, width, UNIT_BLOCK):
-            cut = slice(first, first + UNIT_BLOCK)
-            held_cut = slice(at + first, at + first + UNIT_BLOCK)
-            unused, act_back = jax.vjp(gated_product, gate[:, cut], upper[:, cut])
-            back_gate, back_upper = act_back(right_dot(here, held[2, held_cut]))
-            low_gate, low_upper = back_gate.astype(BF16), back_upper.astype(BF16)
-            grad_gate[:, cut] = low_gate
-            grad_upper[:, cut] = low_upper
-            term = full_dot(low_gate, held[0, held_cut]) + full_dot(low_upper, held[1, held_cut])
-            running = term if running is None else running + term
-        at += width
-    total[...] = running
-
-
-def ffn_backward(rows, before, weights, gates, uppers):
-    many, step = rows.shape[0], 256
-    widths = tuple(gate.shape[1] for gate in gates)
-    by_row = lambda width: pl.BlockSpec((step, width), lambda i: (i, 0))
+    for block in unit_blocks(steps, units):
+        cut = slice(block[0] * units, (block[-1] + 1) * units)
+        grad_hidden = right_dot(here, held[2, cut])
+        low_gates, low_uppers = [], []
+        for i, step in enumerate(block):
+            unused, act_back = jax.vjp(gated_product, gates[step][...], uppers[step][...])
+            back_gate, back_upper = act_back(grad_hidden[:, i * units : (i + 1) * units])
+            low_gates.append(back_gate.astype(BF16))
+            low_uppers.append(back_upper.astype(BF16))
+            grad_gates[step][...] = low_gates[-1]
+            grad_uppers[step][...] = low_uppers[-1]
+        term = full_dot(jnp.concatenate(low_gates, 1), held[0, cut])
+        term = term + full_dot(jnp.concatenate(low_uppers, 1), held[1, cut])
+        running = term if running is None else running + term
+    write_sum(running, totals[0], totals[1] if last else None)
+
+
+def ffn_backward(rows, before, weights, gates, uppers, last):
+    many = rows.shape[0]
+    steps, units = len(gates), gates[0].shape[1]
+    at, sums, sum_shapes = sum_specs(many, last)
+    by_row = lambda width: pl.BlockSpec((ROW_BLOCK, width), lambda i: (at(i), 0))
     add = before is not None
-    blocks = [by_row(width) for width in widths]
-    lows = [((many, width), BF16) for width in widths]
-    total, *grads = piece(
-        functools.partial(ffn_backward_kernel, len(weights), widths, add),
+    outs = piece(
+        functools.partial(ffn_backward_kernel, steps, add, last),
         "ffn_backward",
-        (many // step,),
-        [pl.BlockSpec(memory_space=pl.ANY)] * len(weights) + [by_row(D)] * (1 + add) + blocks * 2,
-        [by_row(D)] + blocks * 2,
-        [((many, D), F32)] + lows * 2,
-        [pltpu.VMEM((3, sum(widths), D), BF16), pltpu.SemaphoreType.DMA((len(weights),))],
+        (many // ROW_BLOCK,),
+        [pl.BlockSpec(memory_space=pl.ANY)] * len(weights)
+        + [by_row(D)] * (1 + add)
+        + [by_row(units)] * (2 * steps),
+        sums + [by_row(units)] * (2 * steps),
+        sum_shapes + [((many, units), BF16)] * (2 * steps),
+        [pltpu.VMEM((3, steps * units, D), BF16), pltpu.SemaphoreType.DMA((len(weights),))],
     )(*weights, *([before] if add else []), rows, *gates, *uppers)
-    return total, list(zip(grads[: len(widths)], grads[len(widths) :]))
+    return refs_of((len(sums), steps, steps), outs)
 
 
 def unit_grads_kernel(grad_gate, grad_upper, hidden, rows, down_rows, out):
-    out[0] = left_dot(grad_gate[...], rows[...])
-    out[1] = left_dot(grad_upper[...], rows[...])
-    out[2] = left_dot(hidden[...], down_rows[...])
-
-
-def unit_grads_of(at, units, grad_gate, grad_upper, hidden, rows, down_rows):
-    if units % 128:
-        cut = slice(at * units, (at + 1) * units)
-        return jnp.stack(
-            [
-                left_dot(grad_gate[:, cut], rows),
-                left_dot(grad_upper[:, cut], rows),
-                left_dot(hidden[:, cut], down_rows),
-            ]
-        )
-    many, width = rows.shape[0], 512
-    narrow = pl.BlockSpec((many, units), lambda i: (0, at))
+    out[0] = left_dot(grad_gate[...], rows[...]).astype(BF16)
+    out[1] = left_dot(grad_upper[...], rows[...]).astype(BF16)
+    out[2] = left_dot(hidden[...], down_rows[...]).astype(BF16)
+
+
+def unit_grads_of(grad_gate, grad_upper, hidden, rows, down_rows):
+    many, units = hidden.shape
+    width = 1024
+    narrow = whole((many, units))
     wide = pl.BlockSpec((many, width), lambda i: (0, i))
     return piece(
         unit_grads_kernel,
@@ -806,7 +858,7 @@
         (D // width,),
         [narrow, narrow, narrow, wide, wide],
         [pl.BlockSpec((3, units, width), lambda i: (0, 0, i))],
-        [((3, units, D), F32)],
+        [((3, units, D), BF16)],
     )(grad_gate, grad_upper, hidden, rows, down_rows)[0]
 
 
@@ -1038,24 +1090,144 @@
     return [total // count + (1 if i < total % count else 0) for i in range(count)]
 
 
-def pair_of_rows(own):
-    return jnp.concatenate([own, swap(own, "fsdp")], 0)
-
-
-def both_pairs(pair):
-    return jnp.concatenate([pair, swap(pair, "core")], 0)
-
-
-def rows_of_four(own):
-    return both_pairs(pair_of_rows(own))
-
-
-def sum_of_four(partial):
-    count = partial.shape[0] // 4
-    low = partial[2 * count :].astype(BF16)
-    pair = partial[: 2 * count] + swap(low, "core").astype(F32)
-    low = pair[count:].astype(BF16)
-    return pair[:count] + swap(low, "fsdp").astype(F32)
+def greet(peers):
+    barrier = pltpu.get_barrier_semaphore()
+    for peer in peers:
+        pl.semaphore_signal(barrier, inc=1, device_id=peer, device_id_type=MESH)
+    pl.semaphore_wait(barrier, len(peers))
+
+
+def partners():
+    return {"core": 1 - lax.axis_index("core")}, {"fsdp": 1 - lax.axis_index("fsdp")}
+
+
+CUTS = 4
+
+
+def spread_kernel(own, rows, x_send, x_recv, near_send, near_recv, far_send, far_recv, own_sem):
+    count = own.shape[0]
+    cut = count // CUTS
+    other_core, other_side = partners()
+    greet((other_core, other_side))
+
+    def copy(src, block, at, send, recv, peer):
+        return pltpu.make_async_remote_copy(
+            src_ref=src,
+            dst_ref=rows.at[pl.ds(block * count + at * cut, cut)],
+            send_sem=send.at[at],
+            recv_sem=recv.at[at],
+            device_id=peer,
+            device_id_type=MESH,
+        )
+
+    mine = [own.at[pl.ds(at * cut, cut)] for at in range(CUTS)]
+    came = [rows.at[pl.ds(count + at * cut, cut)] for at in range(CUTS)]
+    across = [copy(mine[at], 1, at, x_send, x_recv, other_side) for at in range(CUTS)]
+    near = [copy(mine[at], 2, at, near_send, near_recv, other_core) for at in range(CUTS)]
+    far = [copy(came[at], 3, at, far_send, far_recv, other_core) for at in range(CUTS)]
+    for one in across + near:
+        one.start()
+    keep = pltpu.make_async_copy(own, rows.at[pl.ds(0, count)], own_sem)
+    keep.start()
+    for at in range(CUTS):
+        across[at].wait_recv()
+        far[at].start()
+    for one in near + far:
+        one.wait()
+    for one in across:
+        one.wait_send()
+    keep.wait()
+
+
+def rows_of_four(own, number):
+    count = own.shape[0]
+    dma = pltpu.SemaphoreType.DMA
+    return pl.pallas_call(
+        spread_kernel,
+        out_shape=jax.ShapeDtypeStruct((4 * count, D), BF16),
+        in_specs=[pl.BlockSpec(memory_space=pl.ANY)],
+        out_specs=pl.BlockSpec(memory_space=pl.ANY),
+        scratch_shapes=[dma((CUTS,)) for _ in range(6)] + [dma],
+        compiler_params=pltpu.CompilerParams(collective_id=number, has_side_effects=True),
+        cost_estimate=LITTLE,
+        name="spread_rows",
+    )(own)
+
+
+def gather_sum_kernel(own, low, out, core_in, pair_low, x_in, core_send, core_recv, x_send, x_recv):
+    count = out.shape[0]
+    cut = count // CUTS
+    other_core, other_side = partners()
+    greet((other_core, other_side))
+
+    def core_copy(block, at):
+        here = pl.ds(block * count + at * cut, cut)
+        number = block * CUTS + at
+        return pltpu.make_async_remote_copy(
+            src_ref=low.at[here],
+            dst_ref=core_in.at[here],
+            send_sem=core_send.at[number],
+            recv_sem=core_recv.at[number],
+            device_id=other_core,
+            device_id_type=MESH,
+        )
+
+    def x_copy(at):
+        here = pl.ds(at * cut, cut)
+        return pltpu.make_async_remote_copy(
+            src_ref=pair_low.at[here],
+            dst_ref=x_in.at[here],
+            send_sem=x_send.at[at],
+            recv_sem=x_recv.at[at],
+            device_id=other_side,
+            device_id_type=MESH,
+        )
+
+    for block in (1, 0):
+        for at in range(CUTS):
+            core_copy(block, at).start()
+    for at in range(CUTS):
+        there = pl.ds(count + at * cut, cut)
+        core_copy(1, at).wait_recv()
+        pair_low[pl.ds(at * cut, cut)] = (own[there] + core_in[there].astype(F32)).astype(BF16)
+        x_copy(at).start()
+    for at in range(CUTS):
+        here = pl.ds(at * cut, cut)
+        core_copy(0, at).wait_recv()
+        out[here] = own[here] + core_in[here].astype(F32)
+    for at in range(CUTS):
+        here = pl.ds(at * cut, cut)
+        x_copy(at).wait_recv()
+        out[here] += x_in[here].astype(F32)
+    for at in range(CUTS):
+        x_copy(at).wait_send()
+        for block in (0, 1):
+            core_copy(block, at).wait_send()
+
+
+def sum_of_four(own, low, number):
+    count = own.shape[0] // 2
+    dma = pltpu.SemaphoreType.DMA
+    return pl.pallas_call(
+        gather_sum_kernel,
+        out_shape=jax.ShapeDtypeStruct((count, D), F32),
+        in_specs=[pl.BlockSpec(memory_space=pltpu.VMEM), pl.BlockSpec(memory_space=pl.ANY)],
+        out_specs=pl.BlockSpec(memory_space=pltpu.VMEM),
+        scratch_shapes=[
+            pltpu.VMEM((2 * count, D), BF16),
+            pltpu.VMEM((count, D), BF16),
+            pltpu.VMEM((count, D), BF16),
+            dma((2 * CUTS,)),
+            dma((2 * CUTS,)),
+            dma((CUTS,)),
+            dma((CUTS,)),
+        ],
+        compiler_params=pltpu.CompilerParams(
+            collective_id=number, has_side_effects=True, vmem_limit_bytes=VMEM_LIMIT
+        ),
+        cost_estimate=LITTLE,
+        name="gather_sum",
+    )(own, low)
 
 
 def body(
@@ -1178,7 +1350,9 @@
     angles = places.astype(F32)[:, None] * freqs
     cosine, sine = jnp.cos(angles), jnp.sin(angles)
     normed_low, qkv_raw, qkv = make_qkv(tokens[0], gains, head_gain, cosine, sine, full)
+    qkv = stage_end(qkv)
     kv_own = qkv[:, D:]
+    pass_on(2)
 
     mid = chips // 2
     chain = [(i, i + 1) for i in range(mid - 1)] + [(mid - 1, mid + 1)]
@@ -1201,7 +1375,7 @@
     kv_other = swap(jnp.where(core == 0, kv_own, kv_before), "core")
     keys_all = jnp.concatenate([kv_before, kv_other, kv_own], 0)
     keys_all = stage_end(keys_all)
-    pass_on(2)
+    pass_on(3)
     key_len = keys_all.shape[0]
     key_places = first_place - 2 * row_count + jnp.arange(key_len, dtype=jnp.int32)
     visible = (
@@ -1213,34 +1387,29 @@
         tokens[0], gains, normed_low, qkv, keys_all, visible, full
     )
 
-    pair = stage_end(pair_of_rows(ffn_in))
+    ffn_in = stage_end(ffn_in)
+    pass_on(4)
+    ffn_rows = stage_end(rows_of_four(ffn_in, 2))
     here = len(ups)
-    pass_on(3)
-    ffn_rows = both_pairs(pair)
-    gates, uppers, hiddens, part_weights, parts = [], [], [], [], []
-
-    def forward_part(running, first, last):
-        weights = [w for k in range(first, last) for w in (ups[k], downs[k])]
-        running, gate, upper, hidden = ffn_forward(ffn_rows, running, weights)
-        gates.append(gate)
-        uppers.append(upper)
-        hiddens.append(hidden)
-        part_weights.append(weights)
-        parts.append(range(first, last))
-        return running
+    pass_on(5)
+    gates, uppers, hiddens = [], [], []
+
+    def weights_of(steps):
+        return [w for k in steps for w in (ups[k], downs[k])]
+
+    def forward_part(running, first, end, last=False):
+        sums, gate, upper, hidden = ffn_forward(ffn_rows, running, weights_of(range(first, end)), last)
+        gates.extend(gate)
+        uppers.extend(upper)
+        hiddens.extend(hidden)
+        return sums if last else sums[0]
 
     running = stage_end(forward_part(None, 0, here))
-    pass_on(4)
-    stage_end(())
     then = len(ups)
-    pass_on(5)
+    pass_on(6)
     running = stage_end(forward_part(running, here, then))
-    here = len(ups)
-    pass_on(6)
-    running = stage_end(forward_part(running, then, here))
-    if here < chips:
-        running = forward_part(running, here, chips)
-    down_out = sum_of_four(running)
+    own_sum, low_sum = forward_part(running, then, chips, True)
+    down_out = sum_of_four(own_sum, low_sum, 3)
     after_ffn = mixed + rms_norm(down_out, gains[4])
     after_low = after_ffn.astype(BF16)
     pl_raw = full_dot(after_low, plg)
@@ -1266,54 +1435,49 @@
     grad_down, grad_g4 = down_norm_back(grad_after)
     grad_down_low = grad_down.astype(BF16)
 
-    grad_down_rows = rows_of_four(grad_down_low)
-    grad_parts = []
-
-    def backward_part(first, last, running):
-        return ffn_backward(
-            grad_down_rows,
-            running,
-            [w for weights in part_weights[first:last] for w in weights],
-            gates[first:last],
-            uppers[first:last],
+    grad_down_rows = rows_of_four(grad_down_low, 4)
+    grad_gates, grad_uppers = [None] * chips, [None] * chips
+
+    def backward_part(steps, running, last=False):
+        sums, grad_gate, grad_upper = ffn_backward(
+            grad_down_rows, running, weights_of(steps), [gates[k] for k in steps], [uppers[k] for k in steps], last
         )
+        for k, gg, gu in zip(steps, grad_gate, grad_upper):
+            grad_gates[k], grad_uppers[k] = gg, gu
+        return sums if last else sums[0]
 
     def unit_grads(k):
-        for part, (gg, gu), hid in zip(parts, grad_parts, hiddens):
-            if k in part:
-                return unit_grads_of(k - part[0], units, gg, gu, hid, ffn_rows, grad_down_rows)
+        return unit_grads_of(grad_gates[k], grad_uppers[k], hiddens[k], ffn_rows, grad_down_rows)
 
     order = list(range(1, chips)) + [0]
-    ring_steps = shares(chips - 1, 7)
+    ring_steps = shares(chips - 2, 6)
     done = 0
 
     def beside(stage, work):
         nonlocal done, up_sum, down_sum
         values = None
         for step in range(ring_steps[stage]):
-            up_in = ring(up_sum.astype(BF16), 1)
-            down_in = ring(down_sum.astype(BF16), -1)
+            up_in = ring(up_sum, 1)
+            down_in = ring(down_sum, -1)
             if step == 0:
                 values = work()
             done += 1
             terms = unit_grads(order[done])
             (up_in, down_in), terms, values = tie((up_in, down_in), terms, values)
-            up_sum = up_in.astype(F32) + terms[:, :half]
-            down_sum = down_in.astype(F32) + terms[:, half:]
+            up_sum = (up_in.astype(F32) + terms[:, :half].astype(F32)).astype(BF16)
+            down_sum = (down_in.astype(F32) + terms[:, half:].astype(F32)).astype(BF16)
         return work() if values is None else values
 
-    running, grads = backward_part(0, 1, None)
-    grad_parts += grads
+    first = ring_steps[0]
+    then = first + 1 + ring_steps[0] + ring_steps[1]
+    running = backward_part(order[:first], None)
     terms = unit_grads(order[0])
     up_sum, down_sum = terms[:, :half], terms[:, half:]
-
-    def work():
-        total, grads = backward_part(1, len(parts), running)
-        grad_parts.extend(grads)
-        return total
-
-    running = beside(0, work)
-    grad_ffn_in = beside(1, lambda: sum_of_four(running))
+    running = beside(0, lambda: backward_part(order[first:then], running))
+    own_sum, low_sum = beside(1, lambda: backward_part(order[then:], running, True))
+    grad_ffn_in = beside(
+        2, lambda: sum_of_four(own_sum, low_sum, 5)
+    )
     (
         grad_scaled,
         grad_mid_low,
@@ -1325,7 +1489,7 @@
         grad_keys,
         grad_values,
     ) = beside(
-        2,
+        3,
         lambda: attend_back(
             gains, grad_ffn_in, grad_after, mixed, attn_raw, laurel_mid, normed_low, full, context_low, qkv, keys_all,
             visible,
@@ -1350,22 +1514,19 @@
         )
         return grad_own, query_back(grad_queries, qkv_raw, cosine, sine, head_gain, normed_low, full)
 
-    grad_own, (grad_wq, grad_normed, grad_hq) = beside(3, work)
-    grad_wkv, grad_tokens, grad_hk, grad_g0 = beside(
-        4,
-        lambda: key_back(
+    grad_own, (grad_wq, grad_normed, grad_hq) = beside(4, work)
+    def work():
+        grad_wkv, grad_tokens, grad_hk, grad_g0 = key_back(
             grad_own, qkv_raw, cosine, sine, head_gain, normed_low, full, grad_normed, grad_scaled, grad_mid_low,
             tokens[0], gains,
-        ),
-    )
-    def work():
+        )
         head_back = jnp.concatenate([grad_hq, grad_hk], 0).reshape(2, shards, head_n).transpose(1, 0, 2)
         head_back = head_back.reshape(shards, 2 * head_n)
         head_back = jnp.pad(head_back, ((0, 0), (0, shard_rows - 2 * head_n))).reshape(1, D)
         misc_back = jnp.concatenate(
             [grad_g0, grad_mid_gains[:3], grad_g4[None], grad_g5[None], head_back, jnp.zeros((1, D), F32)], 0
         )
-        return jnp.concatenate(
+        return grad_wkv, grad_tokens, jnp.concatenate(
             [
                 grad_plg.astype(BF16),
                 grad_plp.astype(BF16).reshape(D, proj_cols),
@@ -1376,16 +1537,17 @@
             1,
         )
 
-    rest_back = beside(5, work)
-    beside(6, lambda: ())
-    grad_ffn = jnp.concatenate([up_sum, down_sum], 1).transpose(1, 0, 2)
-
-    sums_wq, sums_wkv, sums_wo, sums_rest, total = sum_all(
+    grad_wkv, grad_tokens, rest_back = beside(5, work)
+    sums_wq, sums_wkv, sums_wo, sums_rest, total, grad_units = sum_all(
         [grad_wq, grad_wkv, grad_wo, rest_back],
-        (False, False, True, True),
+        (True, True, True, False),
         jnp.broadcast_to(squares, (8, 128)),
+        up_sum,
+        down_sum,
+        unit_grads(0),
         chips,
     )
+    grad_ffn = grad_units.transpose(1, 0, 2)
     at = 0
     rest = []
     for width in (PLD, proj_cols, RANK, misc_cols, RANK):

time: 1010 us -> 960 us (0.950)
  waiting for transfers between devices: 271 us -> 125 us
  Pallas kernels: 525 us -> 662 us
  other arithmetic: 72.8 us -> 48.8 us
  starting transfers between devices: 54.7 us -> 40.8 us
    pallas_call x7 -> x11, Pallas kernels: 245 us -> 380 us  [the longest x1 133 us: sum_all(): pl.pallas_call(functools.partial(sum_kernel, chips, streams, (count, 4, c...]
    ppermute x10 -> x2, waiting for transfers between devices: 95.7 us -> 3.79 us  [swap(): return lax.ppermute(value, axis, [(0, 1), (1, 0)])]
    ppermute x28 -> x26, waiting for transfers between devices: 147 us -> 90.5 us  [ring(): return lax.ppermute(value, 'zy', ring_pairs(lax.axis_size('zy'), by))]
    add x4 -> x0, other arithmetic: 12.4 us -> none  [the longest x2 6 us: sum_of_four(): pair = partial[:2 * count] + swap(low, 'core').astype(F32)]
    ppermute x28 -> x26, starting transfers between devices: 42.3 us -> 30.9 us  [ring(): return lax.ppermute(value, 'zy', ring_pairs(lax.axis_size('zy'), by))]
    unnamed x102 -> x80, local copies, waits for them, and re-layouts: 20 us -> 22.5 us
  transfers between devices with their start and end apart: 44 -> 34, of which waited for: 26 -> 18; matrix products, arithmetic and copies ran while one was open for 6% -> 5% of each run, Pallas kernels for 46% -> 44%
where the time goes in v4:
time: 960 us; the launch traced here: 951 us
  Pallas kernels  662 us (69%)
  waiting for transfers between devices  125 us (13%)
  local copies, waits for them, and re-layouts  62.1 us (6%)
  other arithmetic  48.8 us (5%)
  starting transfers between devices  40.8 us (4%)
    pallas_call x1, Pallas kernels, sum_all(): pl.pallas_call(functools.partial(sum_kernel, chips, streams, (count, 4, c...  133 us
    pallas_call x1, Pallas kernels, gather_all(): pl.pallas_call(functools.partial(gather_kernel, chips, streams), out_shap...  123 us
    ppermute x26, waiting for transfers between devices, ring(): return lax.ppermute(value, 'zy', ring_pairs(lax.axis_size('zy'), by))  90.5 us
    pallas_call x8, Pallas kernels, unit_grads_of(): piece(unit_grads_kernel, 'unit_grads', (D // width,), [narrow, narrow, na...  72.1 us
    pallas_call x2, Pallas kernels, rows_of_four(): pl.pallas_call(spread_kernel, out_shape=jax.ShapeDtypeStruct((4 * count,...  69.1 us
    pallas_call x3, Pallas kernels, ffn_backward(): piece(functools.partial(ffn_backward_kernel, steps, add, last), 'ffn_back...  61.8 us
    pallas_call x2, Pallas kernels, sum_of_four(): pl.pallas_call(gather_sum_kernel, out_shape=jax.ShapeDtypeStruct((count,...  60.1 us
    pallas_call x3, Pallas kernels, ffn_forward(): piece(functools.partial(ffn_forward_kernel, steps, add, last), 'ffn_forwa...  55.8 us
  transfers between devices with their start and end apart: 34, of which 18 were waited for; matrix products, arithmetic and copies ran while one was open for 5% of the time, Pallas kernels for 44%

profile of v4, /device:TPU:0, one launch (start us, length us, event | category | flops | bytes accessed | tf_op | source)
XLA Modules:
  0.0 950.6 jit_solution(2152153848343300011)
XLA Ops:
  0.7 2.2 fusion.33
  2.9 3.0 collective-permute-start.1
  12.8 2.0 concatenate.20.shard
  14.8 122.9 %gather_all.1.weight.w_out.lleft.lright = bf16[2048,5888]{1,0:T(8,128)(2,1)} custom-call(bf16[64,5888]{1,0:T(8,128)(2,1)} %concatenate.20.shard), custom_call_target="tpu_custom_call" | custom-call | bytes 48234496 | tf_op jit(solution)/shard_map/gather_all/pallas_call | solution.py:224
  137.7 2.0 slice.123
  146.0 13.5 %make_qkv.1 = (bf16[256,2048]{1,0:T(8,128)(2,1)}, f32[256,3072]{1,0:T(8,128)}, bf16[256,3072]{1,0:T(8,128)(2,1)}) custom-call(bf16[256,2048]{1,0:T(8,128)(2,1)} %bitcast.54, f32[8,2048]{1,0:T(8,128)} %pad.19.gains, f32[2,256]{1,0:T(2,128)} %reshape.165.head_gain, f32[256,128]{1,0:T(8,128)} %get-tuple-element.351.cosine, f32[256,128]{1,0:T(8,128)} %get-tuple-element.350.sine, ...), custom_call_target="tpu_custom_call" | custom-call | bytes 1024 | tf_op jit(solution)/shard_map/make_qkv/pallas_call | solution.py:603
  159.5 18.5 %collective-permute-done.2.refs_4_.refs_0_ = bf16[3,128,2048]{2,1,0:T(8,128)(2,1)S(1)} collective-permute-done((bf16[3,128,2048]{2,1,0:T(8,128)(2,1)}, bf16[3,128,2048]{2,1,0:T(8,128)(2,1)S(1)}, u32[]{:S(2)}, u32[]{:S(2)}) %collective-permute-start.2) | collective-permute-done | bytes 1572896 | tf_op jit(solution)/shard_map/ppermute | solution.py:61
  178.2 2.3 slice.127
  180.4 4.2 collective-permute-start.7
  188.1 8.4 collective-permute-done.7
  196.5 1.9 broadcast_select_fusion.1
  201.3 1.9 collective-permute-done.9
  203.2 2.3 pad_maximum_fusion.key.value
  205.5 16.2 %collective-permute-done.4.refs_6_.refs_2_ = bf16[3,128,2048]{2,1,0:T(8,128)(2,1)} collective-permute-done((bf16[3,128,2048]{2,1,0:T(8,128)(2,1)S(1)}, bf16[3,128,2048]{2,1,0:T(8,128)(2,1)}, u32[]{:S(2)}, u32[]{:S(2)}) %collective-permute-start.4) | collective-permute-done | bytes 1572896 | tf_op jit(solution)/shard_map/ppermute | solution.py:61
  221.6 6.9 collective-permute-done.5.refs_7_.refs_3_
  228.5 2.6 collective-permute-start.11
  232.2 19.5 %attend.1 = (bf16[256,2048]{1,0:T(8,128)(2,1)}, f32[256,2048]{1,0:T(8,128)}, f32[256,2048]{1,0:T(8,128)}, bf16[256,2048]{1,0:T(8,128)(2,1)}, bf16[256,128]{1,0:T(8,128)(2,1)}) custom-call(bf16[256,2048]{1,0:T(8,128)(2,1)} %bitcast.55, f32[8,2048]{1,0:T(8,128)} %pad.19.gains, bf16[256,2048]{1,0:T(8,128)(2,1)} %get-tuple-element.152.low, ...), custom_call_target="tpu_custom_call" | custom-call | bytes 1024 | tf_op jit(solution)/shard_map/attend/pallas_call | solution.py:667
  251.7 12.6 %collective-permute-done.10.refs_8_.refs_4_ = bf16[3,128,2048]{2,1,0:T(8,128)(2,1)S(1)} collective-permute-done((bf16[3,128,2048]{2,1,0:T(8,128)(2,1)}, bf16[3,128,2048]{2,1,0:T(8,128)(2,1)S(1)}, u32[]{:S(2)}, u32[]{:S(2)}) %collective-permute-start.10) | collective-permute-done | bytes 1572896 | tf_op jit(solution)/shard_map/ppermute | solution.py:61
  264.3 8.4 collective-permute-done.11.refs_9_.refs_5_
  273.9 2.5 collective-permute-start.12
  276.3 2.1 collective-permute-start.13
  278.5 33.6 %spread_rows.2.refs_12_.refs_3_.rows = bf16[1024,2048]{1,0:T(8,128)(2,1)} custom-call(bf16[256,2048]{1,0:T(8,128)(2,1)} %get-tuple-element.166.own), custom_call_target="tpu_custom_call" | custom-call | bytes 1024 | tf_op jit(solution)/shard_map/spread_rows/pallas_call | solution.py:1145
  315.5 31.0 %ffn_forward.3 = (f32[1024,2048]{1,0:T(8,128)}, f32[1024,256]{1,0:T(8,128)}, f32[1024,256]{1,0:T(8,128)}, f32[1024,256]{1,0:T(8,128)}, f32[1024,256]{1,0:T(8,128...) custom-call(bf16[3,128,2048]{2,1,0:T(8,128)(2,1)} %copy-done.4, ...), custom_call_target="tpu_custom_call" | custom-call | bytes 1024 | tf_op jit(solution)/shard_map/ffn_forward/pallas_call | solution.py:784
  346.5 2.9 collective-permute-done.14.refs_0_.refs_2_
  350.2 2.0 collective-permute-start.16
  356.2 12.4 %ffn_forward.4 = (f32[1024,2048]{1,0:T(8,128)}, f32[1024,256]{1,0:T(8,128)}, f32[1024,256]{1,0:T(8,128)}, bf16[1024,256]{1,0:T(8,128)(2,1)}) custom-call(bf16[3,128,2048]{2,1,0:T(8,128)(2,1)} %collective-permute-done.14.refs_0_.refs_2_, bf16[3,128,2048]{2,1,0:T(8,128)(2,1)} %collective-permute-done.15.refs_1_.refs_3_, ...), custom_call_target="tpu_custom_call" | custom-call | bytes 1024 | tf_op jit(solution)/shard_map/ffn_forward/pallas_call | solution.py:784
  368.6 17.1 %collective-permute-done.16.refs_0_.refs_4_ = bf16[3,128,2048]{2,1,0:T(8,128)(2,1)S(1)} collective-permute-done((bf16[3,128,2048]{2,1,0:T(8,128)(2,1)}, bf16[3,128,2048]{2,1,0:T(8,128)(2,1)S(1)}, u32[]{:S(2)}, u32[]{:S(2)}) %collective-permute-start.16) | collective-permute-done | bytes 1572896 | tf_op jit(solution)/shard_map/ppermute | solution.py:61
  386.9 12.4 %ffn_forward.5 = (f32[512,2048]{1,0:T(8,128)}, bf16[512,2048]{1,0:T(8,128)(2,1)}, f32[1024,256]{1,0:T(8,128)}, f32[1024,256]{1,0:T(8,128)}, bf16[1024,256]{1,0:T(8,128)(2,1)}) custom-call(bf16[3,128,2048]{2,1,0:T(8,128)(2,1)} %copy-done.18, bf16[3,128,2048]{2,1,0:T(8,128)(2,1)} %collective-permute-done.17.refs_1_.refs_5_, ...), custom_call_target="tpu_custom_call" | custom-call | bytes 1024 | tf_op jit(solution)/shard_map/ffn_forward/pallas_call | solution.py:784
  399.3 29.0 %gather_sum.2 = f32[256,2048]{1,0:T(8,128)} custom-call(f32[512,2048]{1,0:T(8,128)} %get-tuple-element.178.own, bf16[512,2048]{1,0:T(8,128)(2,1)} %get-tuple-element.179.low), custom_call_target="tpu_custom_call" | custom-call | bytes 1024 | tf_op jit(solution)/shard_map/gather_sum/pallas_call | solution.py:1211
  428.3 2.0 multiply_reduce_fusion.5
  433.9 2.1 multiply_reduce_fusion
  438.1 2.4 multiply_reduce_fusion.1
  443.2 35.5 %spread_rows.3.refs_2_.down_rows.refs_7_.refs_9_ = bf16[1024,2048]{1,0:T(8,128)(2,1)} custom-call(bf16[256,2048]{1,0:T(8,128)(2,1)} %fusion.3.own), custom_call_target="tpu_custom_call" | custom-call | bytes 1024 | tf_op jit(solution)/shard_map/spread_rows/pallas_call | solution.py:1145
  478.6 12.1 %ffn_backward.3 = (f32[1024,2048]{1,0:T(8,128)}, bf16[1024,256]{1,0:T(8,128)(2,1)}, bf16[1024,256]{1,0:T(8,128)(2,1)}) custom-call(bf16[3,128,2048]{2,1,0:T(8,128)(2,1)} %collective-permute-done.refs_2_.refs_0_, bf16[3,128,2048]{2,1,0:T(8,128)(2,1)} %collective-permute-done.1.refs_3_.refs_1_, ...), custom_call_target="tpu_custom_call" | custom-call | bytes 1024 | tf_op jit(solution)/shard_map/ffn_backward/pallas_call | solution.py:830
  490.8 18.9 %unit_grads.8 = bf16[3,256,2048]{2,1,0:T(8,128)(2,1)} custom-call(bf16[1024,256]{1,0:T(8,128)(2,1)} %get-tuple-element.182.grad_gate, bf16[1024,256]{1,0:T(8,128)(2,1)} %get-tuple-element.183.grad_upper, bf16[1024,256]{1,0:T(8,128)(2,1)} %get-tuple-element.184.hidden, bf16[1024,2048]{1,0:T(8,128)(2,1)} %spread_rows.2.refs_12_.refs_3_.rows, ...), custom_call_target="tpu_custom_call" | custom-call | bytes 1024 | tf_op jit(solution)/shard_map/unit_grads/pallas_call | solution.py:855
  509.7 3.5 fusion.32
  515.2 22.4 %ffn_backward.4 = (f32[1024,2048]{1,0:T(8,128)}, bf16[1024,256]{1,0:T(8,128)(2,1)}, bf16[1024,256]{1,0:T(8,128)(2,1)}, bf16[1024,256]{1,0:T(8,128)(2,1)}, bf16[1...) custom-call(bf16[3,128,2048]{2,1,0:T(8,128)(2,1)} %copy-done.14, ...), custom_call_target="tpu_custom_call" | custom-call | bytes 1024 | tf_op jit(solution)/shard_map/ffn_backward/pallas_call | solution.py:830
  537.6 7.5 unit_grads.9
  545.1 4.1 collective-permute-done.19
  550.1 4.6 add_convert_fusion.10
  556.8 7.5 unit_grads.10
  564.3 27.3 %ffn_backward.5 = (f32[512,2048]{1,0:T(8,128)}, bf16[512,2048]{1,0:T(8,128)(2,1)}, bf16[1024,256]{1,0:T(8,128)(2,1)}, bf16[1024,256]{1,0:T(8,128)(2,1)}, bf16[10...) custom-call(bf16[3,128,2048]{2,1,0:T(8,128)(2,1)} %copy-done.13, ...), custom_call_target="tpu_custom_call" | custom-call | bytes 1024 | tf_op jit(solution)/shard_map/ffn_backward/pallas_call | solution.py:830
  591.6 4.7 add_convert_fusion.8
  598.3 7.5 unit_grads.11
  605.8 31.1 %gather_sum.3.grad_in = f32[256,2048]{1,0:T(8,128)} custom-call(f32[512,2048]{1,0:T(8,128)} %get-tuple-element.219.own, bf16[512,2048]{1,0:T(8,128)(2,1)} %get-tuple-element.220.low), custom_call_target="tpu_custom_call" | custom-call | bytes 1024 | tf_op jit(solution)/shard_map/gather_sum/pallas_call | solution.py:1211
  636.9 4.7 add_convert_fusion.6
  643.6 7.9 unit_grads.12
  651.5 27.7 %attend_back.1 = (f32[256,2048]{1,0:T(8,128)}, bf16[256,128]{1,0:T(8,128)(2,1)}, f32[8,2048]{1,0:T(8,128)}, f32[2048,128]{1,0:T(8,128)}, f32[2048,128]{1,0:T(8,1...) custom-call(f32[8,2048]{1,0:T(8,128)} %pad.19.gains, ...), custom_call_target="tpu_custom_call" | custom-call | bytes 1024 | tf_op jit(solution)/shard_map/attend_back/pallas_call | solution.py:919
  681.4 1.9 collective-permute-done.28
  684.3 3.0 add_convert_fusion.4
  692.4 7.6 unit_grads.13
  700.0 14.4 %query_back.1 = (bf16[2048,2048]{1,0:T(8,128)(2,1)}, f32[256,2048]{1,0:T(8,128)}, f32[1,256]{1,0:T(1,128)}) custom-call(f32[256,2048]{1,0:T(8,128)} %get-tuple-element.248.grad_query, f32[256,3072]{1,0:T(8,128)} %get-tuple-element.249.raw, f32[256,128]{1,0:T(8,128)} %get-tuple-element.351.cosine, f32[256,128]{1,0:T(8,128)} %get-tuple-element.350.sine, ...), custom_call_target="tpu_custom_call" | custom-call | bytes 1024 | tf_op jit(solution)/shard_map/query_back/pallas_call | solution.py:997
  714.4 22.3 %collective-permute-done.30 = bf16[256,1024]{1,0:T(8,128)(2,1)} collective-permute-done((bf16[256,1024]{1,0:T(8,128)(2,1)}, bf16[256,1024]{1,0:T(8,128)(2,1)}, u32[]{:S(2)}, u32[]{:S(2)}) %collective-permute-start.30) | collective-permute-done | bytes 524320 | tf_op jit(solution)/shard_map/ppermute | solution.py:1512
  736.7 2.7 fusion.6.grad_kv
  739.4 5.0 add_convert_fusion.2
  744.5 1.9 collective-permute-start.32
  752.6 7.5 unit_grads.14
  760.1 7.7 unit_grads.15.refs_7_
  770.0 11.8 %key_back.1 = (bf16[2048,1024]{1,0:T(8,128)(2,1)}, f32[256,2048]{1,0:T(8,128)}, f32[1,256]{1,0:T(1,128)}, f32[1,2048]{1,0:T(1,128)}) custom-call(f32[256,1024]{1,0:T(8,128)} %fusion.6.grad_kv, f32[256,3072]{1,0:T(8,128)} %get-tuple-element.249.raw, f32[256,128]{1,0:T(8,128)} %get-tuple-element.351.cosine, f32[256,128]{1,0:T(8,128)} %get-tuple-element.350.sine, ...), custom_call_target="tpu_custom_call" | custom-call | bytes 1024 | tf_op jit(solution)/shard_map/key_back/pallas_call | solution.py:1050
  785.2 4.8 copy.49
  790.1 4.9 add_convert_fusion
  796.3 133.2 %sum_all.1 = (f32[64,2048]{1,0:T(8,128)}, f32[64,1024]{1,0:T(8,128)}, f32[64,2048]{1,0:T(8,128)}, f32[64,768]{1,0:T(8,128)}, f32[8,128]{1,0:T(8,128)}, /*index=5*/f32[3,256,2048]{2,1,0:T(8,128)}) custom-call(bf16[8,2,2,64,2048]{4,3,2,1,0:T(8,128)(2,1)} %bitcast.58, bf16[8,2,2,64,1024]{4,3,2,1,0:T(8,128)(2,1)} %bitcast.60, ...), custom_call_target="tpu_custom_call" | custom-call | bytes 24117248 | tf_op jit(solution)/shard_map/sum_all/pallas_call | solution.py:524
  938.6 1.9 copy.64
  943.0 6.3 copy.67
  (200 shorter events, 80.1 us)
Async XLA Ops:
  0.6 5.4 copy-start.32
  0.7 12.1 %copy-start.28 = (bf16[64,2048]{1,0:T(8,128)(2,1)S(1)}, bf16[64,2048]{1,0:T(8,128)(2,1)}, u32[]{:S(2)}) copy-start(bf16[64,2048]{1,0:T(8,128)(2,1)} %param.20) | copy-start | bytes 786436
  0.7 12.1 %copy-start.29 = (bf16[64,1024]{1,0:T(8,128)(2,1)S(1)}, bf16[64,1024]{1,0:T(8,128)(2,1)}, u32[]{:S(2)}) copy-start(bf16[64,1024]{1,0:T(8,128)(2,1)} %param.19) | copy-start | bytes 393220
  2.8 134.9 %copy-start.3 = (bf16[3,128,2048]{2,1,0:T(8,128)(2,1)}, bf16[3,128,2048]{2,1,0:T(8,128)(2,1)S(1)}, u32[]{:S(2)}) copy-start(bf16[3,128,2048]{2,1,0:T(8,128)(2,1)S(1)} %get-tuple-element.340.refs_1_.refs_7_) | copy-start | bytes 4718596
  2.8 134.9 %copy-start.4 = (bf16[3,128,2048]{2,1,0:T(8,128)(2,1)}, bf16[3,128,2048]{2,1,0:T(8,128)(2,1)S(1)}, u32[]{:S(2)}) copy-start(bf16[3,128,2048]{2,1,0:T(8,128)(2,1)S(1)} %get-tuple-element.341.refs_0_.refs_6_) | copy-start | bytes 4718596
  2.9 138.1 %collective-permute-start.1 = (bf16[3,128,2048]{2,1,0:T(8,128)(2,1)S(1)}, bf16[3,128,2048]{2,1,0:T(8,128)(2,1)}, u32[]{:S(2)}, u32[]{:S(2)}) collective-permute-start(bf16[3,128,2048]{2,1,0:T(8,128)(2,1)S(1)} %get-tuple-element.340.refs_1_.refs_7_), channel_id=1, source_target_pairs={{0,4},{8,0},{16,8},{24,16},{28,24},{20,28},{12,20},{4,12},{1,5},{9... | collective-permute-start | bytes 4718600 | tf_op jit(solution)/shard_map/ppermute | solution.py:61
  5.9 135.1 %collective-permute-start = (bf16[3,128,2048]{2,1,0:T(8,128)(2,1)S(1)}, bf16[3,128,2048]{2,1,0:T(8,128)(2,1)}, u32[]{:S(2)}, u32[]{:S(2)}) collective-permute-start(bf16[3,128,2048]{2,1,0:T(8,128)(2,1)S(1)} %get-tuple-element.341.refs_0_.refs_6_), channel_id=1, source_target_pairs={{0,8},{8,16},{16,24},{24,28},{28,20},{20,12},{12,4},{4,0},{1,9},{9... | collective-permute-start | bytes 4718600 | tf_op jit(solution)/shard_map/ppermute | solution.py:61
  141.0 36.9 %collective-permute-start.2 = (bf16[3,128,2048]{2,1,0:T(8,128)(2,1)}, bf16[3,128,2048]{2,1,0:T(8,128)(2,1)S(1)}, u32[]{:S(2)}, u32[]{:S(2)}) collective-permute-start(bf16[3,128,2048]{2,1,0:T(8,128)(2,1)} %collective-permute-done.refs_2_.refs_0_), channel_id=1, source_target_pairs={{0,8},{8,16},{16,24},{24,28},{28,20},{20,12},{12,4},{4,0},{1,9},{9... | collective-permute-start | bytes 4718600 | tf_op jit(solution)/shard_map/ppermute | solution.py:61
  141.6 36.6 %collective-permute-start.3 = (bf16[3,128,2048]{2,1,0:T(8,128)(2,1)}, bf16[3,128,2048]{2,1,0:T(8,128)(2,1)S(1)}, u32[]{:S(2)}, u32[]{:S(2)}) collective-permute-start(bf16[3,128,2048]{2,1,0:T(8,128)(2,1)} %collective-permute-done.1.refs_3_.refs_1_), channel_id=1, source_target_pairs={{0,4},{8,0},{16,8},{24,16},{28,24},{20,28},{12,20},{4,12},{1,5},{9... | collective-permute-start | bytes 4718600 | tf_op jit(solution)/shard_map/ppermute | solution.py:61
  177.9 23.2 %copy-start.14 = (bf16[3,128,2048]{2,1,0:T(8,128)(2,1)}, bf16[3,128,2048]{2,1,0:T(8,128)(2,1)S(1)}, u32[]{:S(2)}) copy-start(bf16[3,128,2048]{2,1,0:T(8,128)(2,1)S(1)} %collective-permute-done.2.refs_4_.refs_0_) | copy-start | bytes 4718596
  178.2 23.0 %copy-start.15 = (bf16[3,128,2048]{2,1,0:T(8,128)(2,1)}, bf16[3,128,2048]{2,1,0:T(8,128)(2,1)S(1)}, u32[]{:S(2)}) copy-start(bf16[3,128,2048]{2,1,0:T(8,128)(2,1)S(1)} %collective-permute-done.3.refs_5_.refs_1_) | copy-start | bytes 4718596
  180.4 16.1 %collective-permute-start.7 = (bf16[256,1024]{1,0:T(8,128)(2,1)}, bf16[256,1024]{1,0:T(8,128)(2,1)}, u32[]{:S(2)}, u32[]{:S(2)}) collective-permute-start(bf16[256,1024]{1,0:T(8,128)(2,1)} %slice.127), channel_id=1, source_target_pairs={{0,4},{4,8},{8,12},{12,20},{1,5},{5,9},{9,13},{13,21},{2,6},{6,10}... | collective-permute-start | bytes 1572872 | tf_op jit(solution)/shard_map/ppermute | solution.py:1362
  184.6 11.9 %collective-permute-start.6 = (bf16[256,1024]{1,0:T(8,128)(2,1)}, bf16[256,1024]{1,0:T(8,128)(2,1)}, u32[]{:S(2)}, u32[]{:S(2)}) collective-permute-start(bf16[256,1024]{1,0:T(8,128)(2,1)} %slice.127), channel_id=1, source_target_pairs={{12,16},{13,17},{14,18},{15,19}} | collective-permute-start | bytes 1572872 | tf_op jit(solution)/shard_map/ppermute | solution.py:1361
  186.1 35.5 %collective-permute-start.4 = (bf16[3,128,2048]{2,1,0:T(8,128)(2,1)S(1)}, bf16[3,128,2048]{2,1,0:T(8,128)(2,1)}, u32[]{:S(2)}, u32[]{:S(2)}) collective-permute-start(bf16[3,128,2048]{2,1,0:T(8,128)(2,1)S(1)} %collective-permute-done.2.refs_4_.refs_0_), channel_id=1, source_target_pairs={{0,8},{8,16},{16,24},{24,28},{28,20},{20,12},{12,4},{4,0},{1,9},{9... | collective-permute-start | bytes 4718600 | tf_op jit(solution)/shard_map/ppermute | solution.py:61
  186.9 41.6 %collective-permute-start.5 = (bf16[3,128,2048]{2,1,0:T(8,128)(2,1)S(1)}, bf16[3,128,2048]{2,1,0:T(8,128)(2,1)}, u32[]{:S(2)}, u32[]{:S(2)}) collective-permute-start(bf16[3,128,2048]{2,1,0:T(8,128)(2,1)S(1)} %collective-permute-done.3.refs_5_.refs_1_), channel_id=1, source_target_pairs={{0,4},{8,0},{16,8},{24,16},{28,24},{20,28},{12,20},{4,12},{1,5},{9... | collective-permute-start | bytes 4718600 | tf_op jit(solution)/shard_map/ppermute | solution.py:61
  198.4 1.5 collective-permute-start.8
  201.2 2.0 collective-permute-start.9
  228.5 35.8 %collective-permute-start.10 = (bf16[3,128,2048]{2,1,0:T(8,128)(2,1)}, bf16[3,128,2048]{2,1,0:T(8,128)(2,1)S(1)}, u32[]{:S(2)}, u32[]{:S(2)}) collective-permute-start(bf16[3,128,2048]{2,1,0:T(8,128)(2,1)} %collective-permute-done.4.refs_6_.refs_2_), channel_id=1, source_target_pairs={{0,8},{8,16},{16,24},{24,28},{28,20},{20,12},{12,4},{4,0},{1,9},{9... | collective-permute-start | bytes 4718600 | tf_op jit(solution)/shard_map/ppermute | solution.py:61
  228.5 44.2 %collective-permute-start.11 = (bf16[3,128,2048]{2,1,0:T(8,128)(2,1)}, bf16[3,128,2048]{2,1,0:T(8,128)(2,1)S(1)}, u32[]{:S(2)}, u32[]{:S(2)}) collective-permute-start(bf16[3,128,2048]{2,1,0:T(8,128)(2,1)} %collective-permute-done.5.refs_7_.refs_3_), channel_id=1, source_target_pairs={{0,4},{8,0},{16,8},{24,16},{28,24},{20,28},{12,20},{4,12},{1,5},{9... | collective-permute-start | bytes 4718600 | tf_op jit(solution)/shard_map/ppermute | solution.py:61
  264.3 8.4 copy-start.16
  273.9 38.3 %collective-permute-start.12 = (bf16[3,128,2048]{2,1,0:T(8,128)(2,1)}, bf16[3,128,2048]{2,1,0:T(8,128)(2,1)S(1)}, u32[]{:S(2)}, u32[]{:S(2)}) collective-permute-start(bf16[3,128,2048]{2,1,0:T(8,128)(2,1)} %copy-done.16), channel_id=1, source_target_pairs={{0,8},{8,16},{16,24},{24,28},{28,20},{20,12},{12,4},{4,0},{1,9},{9... | collective-permute-start | bytes 4718600 | tf_op jit(solution)/shard_map/ppermute | solution.py:61
  276.3 36.9 %collective-permute-start.13 = (bf16[3,128,2048]{2,1,0:T(8,128)(2,1)}, bf16[3,128,2048]{2,1,0:T(8,128)(2,1)}, u32[]{:S(2)}, u32[]{:S(2)}) collective-permute-start(bf16[3,128,2048]{2,1,0:T(8,128)(2,1)} %copy-done.17), channel_id=1, source_target_pairs={{0,4},{8,0},{16,8},{24,16},{28,24},{20,28},{12,20},{4,12},{1,5},{9... | collective-permute-start | bytes 4718600 | tf_op jit(solution)/shard_map/ppermute | solution.py:61
  312.1 3.3 copy-start.13
  313.2 36.2 %collective-permute-start.14 = (bf16[3,128,2048]{2,1,0:T(8,128)(2,1)S(1)}, bf16[3,128,2048]{2,1,0:T(8,128)(2,1)}, u32[]{:S(2)}, u32[]{:S(2)}) collective-permute-start(bf16[3,128,2048]{2,1,0:T(8,128)(2,1)S(1)} %collective-permute-done.12.refs_10_.refs_0_), channel_id=1, source_target_pairs={{0,8},{8,16},{16,24},{24,28},{28,20},{20,12},{12,4},{4,0},{1,9},{9... | collective-permute-start | bytes 4718600 | tf_op jit(solution)/shard_map/ppermute | solution.py:61
  314.9 35.2 %collective-permute-start.15 = (bf16[3,128,2048]{2,1,0:T(8,128)(2,1)}, bf16[3,128,2048]{2,1,0:T(8,128)(2,1)}, u32[]{:S(2)}, u32[]{:S(2)}) collective-permute-start(bf16[3,128,2048]{2,1,0:T(8,128)(2,1)} %collective-permute-done.13.refs_11_.refs_1_), channel_id=1, source_target_pairs={{0,4},{8,0},{16,8},{24,16},{28,24},{20,28},{12,20},{4,12},{1,5},{9... | collective-permute-start | bytes 4718600 | tf_op jit(solution)/shard_map/ppermute | solution.py:61
  346.5 5.7 copy-start.30
  346.5 7.0 slice-start
  350.2 35.5 %collective-permute-start.16 = (bf16[3,128,2048]{2,1,0:T(8,128)(2,1)}, bf16[3,128,2048]{2,1,0:T(8,128)(2,1)S(1)}, u32[]{:S(2)}, u32[]{:S(2)}) collective-permute-start(bf16[3,128,2048]{2,1,0:T(8,128)(2,1)} %collective-permute-done.14.refs_0_.refs_2_), channel_id=1, source_target_pairs={{0,8},{8,16},{16,24},{24,28},{28,20},{20,12},{12,4},{4,0},{1,9},{9... | collective-permute-start | bytes 4718600 | tf_op jit(solution)/shard_map/ppermute | solution.py:61
  352.2 34.4 %collective-permute-start.17 = (bf16[3,128,2048]{2,1,0:T(8,128)(2,1)}, bf16[3,128,2048]{2,1,0:T(8,128)(2,1)}, u32[]{:S(2)}, u32[]{:S(2)}) collective-permute-start(bf16[3,128,2048]{2,1,0:T(8,128)(2,1)} %collective-permute-done.15.refs_1_.refs_3_), channel_id=1, source_target_pairs={{0,4},{8,0},{16,8},{24,16},{28,24},{20,28},{12,20},{4,12},{1,5},{9... | collective-permute-start | bytes 4718600 | tf_op jit(solution)/shard_map/ppermute | solution.py:61
  399.3 31.0 %copy-start.12 = (f32[256,2048]{1,0:T(8,128)S(1)}, f32[256,2048]{1,0:T(8,128)}, u32[]{:S(2)}) copy-start(f32[256,2048]{1,0:T(8,128)} %get-tuple-element.160.mixed) | copy-start | bytes 6291460
  428.3 2.2 copy-start
  430.9 1.8 copy-start.21
  430.9 1.8 copy-start.25
  436.0 2.0 copy-start.1
  436.8 3.7 copy-start.19
  440.4 1.3 copy-start.2
  513.2 36.0 %collective-permute-start.19 = (bf16[3,128,2048]{2,1,0:T(8,128)(2,1)}, bf16[3,128,2048]{2,1,0:T(8,128)(2,1)S(1)}, u32[]{:S(2)}, u32[]{:S(2)}) collective-permute-start(bf16[3,128,2048]{2,1,0:T(8,128)(2,1)} %get-tuple-element.338), channel_id=1, source_target_pairs={{0,4},{8,0},{16,8},{24,16},{28,24},{20,28},{12,20},{4,12},{1,5},{9... | collective-permute-start | bytes 4718600 | tf_op jit(solution)/shard_map/ppermute | solution.py:61
  514.9 35.2 %collective-permute-start.18 = (bf16[3,128,2048]{2,1,0:T(8,128)(2,1)S(1)}, bf16[3,128,2048]{2,1,0:T(8,128)(2,1)S(1)}, u32[]{:S(2)}, u32[]{:S(2)}) collective-permute-start(bf16[3,128,2048]{2,1,0:T(8,128)(2,1)S(1)} %get-tuple-element.339), channel_id=1, source_target_pairs={{0,8},{8,16},{16,24},{24,28},{28,20},{20,12},{12,4},{4,0},{1,9},{9... | collective-permute-start | bytes 4718600 | tf_op jit(solution)/shard_map/ppermute | solution.py:61
  554.8 36.8 %collective-permute-start.21 = (bf16[3,128,2048]{2,1,0:T(8,128)(2,1)}, bf16[3,128,2048]{2,1,0:T(8,128)(2,1)}, u32[]{:S(2)}, u32[]{:S(2)}) collective-permute-start(bf16[3,128,2048]{2,1,0:T(8,128)(2,1)} %get-tuple-element.336), channel_id=1, source_target_pairs={{0,4},{8,0},{16,8},{24,16},{28,24},{20,28},{12,20},{4,12},{1,5},{9... | collective-permute-start | bytes 4718600 | tf_op jit(solution)/shard_map/ppermute | solution.py:61
  556.5 35.1 %collective-permute-start.20 = (bf16[3,128,2048]{2,1,0:T(8,128)(2,1)S(1)}, bf16[3,128,2048]{2,1,0:T(8,128)(2,1)}, u32[]{:S(2)}, u32[]{:S(2)}) collective-permute-start(bf16[3,128,2048]{2,1,0:T(8,128)(2,1)S(1)} %get-tuple-element.337), channel_id=1, source_target_pairs={{0,8},{8,16},{16,24},{24,28},{28,20},{20,12},{12,4},{4,0},{1,9},{9... | collective-permute-start | bytes 4718600 | tf_op jit(solution)/shard_map/ppermute | solution.py:61
  564.3 27.3 %copy-start.7 = (bf16[3,256,2048]{2,1,0:T(8,128)(2,1)S(1)}, bf16[3,256,2048]{2,1,0:T(8,128)(2,1)}, u32[]{:S(2)}) copy-start(bf16[3,256,2048]{2,1,0:T(8,128)(2,1)} %unit_grads.10) | copy-start | bytes 9437188
  596.3 40.6 %collective-permute-start.23 = (bf16[3,128,2048]{2,1,0:T(8,128)(2,1)}, bf16[3,128,2048]{2,1,0:T(8,128)(2,1)}, u32[]{:S(2)}, u32[]{:S(2)}) collective-permute-start(bf16[3,128,2048]{2,1,0:T(8,128)(2,1)} %get-tuple-element.334), channel_id=1, source_target_pairs={{0,4},{8,0},{16,8},{24,16},{28,24},{20,28},{12,20},{4,12},{1,5},{9... | collective-permute-start | bytes 4718600 | tf_op jit(solution)/shard_map/ppermute | solution.py:61
  598.0 38.9 %collective-permute-start.22 = (bf16[3,128,2048]{2,1,0:T(8,128)(2,1)S(1)}, bf16[3,128,2048]{2,1,0:T(8,128)(2,1)}, u32[]{:S(2)}, u32[]{:S(2)}) collective-permute-start(bf16[3,128,2048]{2,1,0:T(8,128)(2,1)S(1)} %get-tuple-element.335), channel_id=1, source_target_pairs={{0,8},{8,16},{16,24},{24,28},{28,20},{20,12},{12,4},{4,0},{1,9},{9... | collective-permute-start | bytes 4718600 | tf_op jit(solution)/shard_map/ppermute | solution.py:61
  605.8 31.1 %copy-start.9 = (bf16[3,256,2048]{2,1,0:T(8,128)(2,1)S(1)}, bf16[3,256,2048]{2,1,0:T(8,128)(2,1)}, u32[]{:S(2)}) copy-start(bf16[3,256,2048]{2,1,0:T(8,128)(2,1)} %unit_grads.11) | copy-start | bytes 9437188
  641.6 37.6 %collective-permute-start.25 = (bf16[3,128,2048]{2,1,0:T(8,128)(2,1)}, bf16[3,128,2048]{2,1,0:T(8,128)(2,1)S(1)}, u32[]{:S(2)}, u32[]{:S(2)}) collective-permute-start(bf16[3,128,2048]{2,1,0:T(8,128)(2,1)} %get-tuple-element.332), channel_id=1, source_target_pairs={{0,4},{8,0},{16,8},{24,16},{28,24},{20,28},{12,20},{4,12},{1,5},{9... | collective-permute-start | bytes 4718600 | tf_op jit(solution)/shard_map/ppermute | solution.py:61
  643.4 36.0 %collective-permute-start.24 = (bf16[3,128,2048]{2,1,0:T(8,128)(2,1)S(1)}, bf16[3,128,2048]{2,1,0:T(8,128)(2,1)S(1)}, u32[]{:S(2)}, u32[]{:S(2)}) collective-permute-start(bf16[3,128,2048]{2,1,0:T(8,128)(2,1)S(1)} %get-tuple-element.333), channel_id=1, source_target_pairs={{0,8},{8,16},{16,24},{24,28},{28,20},{20,12},{12,4},{4,0},{1,9},{9... | collective-permute-start | bytes 4718600 | tf_op jit(solution)/shard_map/ppermute | solution.py:61
  679.2 1.9 copy-start.22
  681.2 8.1 copy-start.11
  681.2 3.0 copy-start.6
  681.3 2.0 collective-permute-start.28
  683.5 5.9 collective-permute-start.29
  687.3 52.0 %collective-permute-start.27 = (bf16[3,128,2048]{2,1,0:T(8,128)(2,1)}, bf16[3,128,2048]{2,1,0:T(8,128)(2,1)}, u32[]{:S(2)}, u32[]{:S(2)}) collective-permute-start(bf16[3,128,2048]{2,1,0:T(8,128)(2,1)} %get-tuple-element.330), channel_id=1, source_target_pairs={{0,4},{8,0},{16,8},{24,16},{28,24},{20,28},{12,20},{4,12},{1,5},{9... | collective-permute-start | bytes 4718600 | tf_op jit(solution)/shard_map/ppermute | solution.py:61
  689.1 50.3 %collective-permute-start.26 = (bf16[3,128,2048]{2,1,0:T(8,128)(2,1)}, bf16[3,128,2048]{2,1,0:T(8,128)(2,1)}, u32[]{:S(2)}, u32[]{:S(2)}) collective-permute-start(bf16[3,128,2048]{2,1,0:T(8,128)(2,1)} %get-tuple-element.331), channel_id=1, source_target_pairs={{0,8},{8,16},{16,24},{24,28},{28,20},{20,12},{12,4},{4,0},{1,9},{9... | collective-permute-start | bytes 4718600 | tf_op jit(solution)/shard_map/ppermute | solution.py:61
  690.4 24.0 %collective-permute-start.31 = (bf16[256,1024]{1,0:T(8,128)(2,1)}, bf16[256,1024]{1,0:T(8,128)(2,1)S(1)}, u32[]{:S(2)}, u32[]{:S(2)}) collective-permute-start(bf16[256,1024]{1,0:T(8,128)(2,1)} %add_convert_fusion.12), channel_id=1, source_target_pairs={{16,12},{17,13},{18,14},{19,15}} | collective-permute-start | bytes 1572872 | tf_op jit(solution)/shard_map/ppermute | solution.py:1513
  691.1 45.6 %collective-permute-start.30 = (bf16[256,1024]{1,0:T(8,128)(2,1)}, bf16[256,1024]{1,0:T(8,128)(2,1)}, u32[]{:S(2)}, u32[]{:S(2)}) collective-permute-start(bf16[256,1024]{1,0:T(8,128)(2,1)} %add_convert_fusion.12), channel_id=1, source_target_pairs={{4,0},{8,4},{12,8},{20,12},{5,1},{9,5},{13,9},{21,13},{6,2},{10,6}... | collective-permute-start | bytes 1572872 | tf_op jit(solution)/shard_map/ppermute | solution.py:1512
  714.3 25.0 %copy-start.8 = (bf16[3,256,2048]{2,1,0:T(8,128)(2,1)S(1)}, bf16[3,256,2048]{2,1,0:T(8,128)(2,1)}, u32[]{:S(2)}) copy-start(bf16[3,256,2048]{2,1,0:T(8,128)(2,1)} %unit_grads.13) | copy-start | bytes 9437188
  739.4 7.1 copy-start.20
  739.4 7.1 copy-start.26
  744.4 40.8 %collective-permute-start.33 = (bf16[3,128,2048]{2,1,0:T(8,128)(2,1)}, bf16[3,128,2048]{2,1,0:T(8,128)(2,1)}, u32[]{:S(2)}, u32[]{:S(2)}) collective-permute-start(bf16[3,128,2048]{2,1,0:T(8,128)(2,1)} %get-tuple-element.328), channel_id=1, source_target_pairs={{0,4},{8,0},{16,8},{24,16},{28,24},{20,28},{12,20},{4,12},{1,5},{9... | collective-permute-start | bytes 4718600 | tf_op jit(solution)/shard_map/ppermute | solution.py:61
  744.5 40.7 %collective-permute-start.32 = (bf16[3,128,2048]{2,1,0:T(8,128)(2,1)}, bf16[3,128,2048]{2,1,0:T(8,128)(2,1)}, u32[]{:S(2)}, u32[]{:S(2)}) collective-permute-start(bf16[3,128,2048]{2,1,0:T(8,128)(2,1)} %get-tuple-element.329), channel_id=1, source_target_pairs={{0,8},{8,16},{16,24},{24,28},{28,20},{20,12},{12,4},{4,0},{1,9},{9... | collective-permute-start | bytes 4718600 | tf_op jit(solution)/shard_map/ppermute | solution.py:61
  760.1 8.6 copy-start.27
  770.0 12.5 %copy-start.31 = (f32[1,256]{1,0:T(1,128)S(1)}, f32[1,256]{1,0:T(1,128)}, u32[]{:S(2)}) copy-start(f32[1,256]{1,0:T(1,128)} %get-tuple-element.269) | copy-start | bytes 3076
  785.2 4.8 copy-start.5
  929.4 12.7 %copy-start.24 = (f32[64,2048]{1,0:T(8,128)S(1)}, f32[64,2048]{1,0:T(8,128)}, u32[]{:S(2)}) copy-start(f32[64,2048]{1,0:T(8,128)} %get-tuple-element.375) | copy-start | bytes 1572868
  (4 other events, 4.9 us)

commit v5 on v4

--- a/solution.py
+++ b/solution.py
@@ -244,9 +244,9 @@
 
 
 def sum_kernel(chips, streams, counts, *refs):
-    arrays, (tile, up_sum, down_sum, terms), outs, (tile_out, units_out), held, core_in, ring_in, x_in, tiles, sems = refs_of(counts, refs)
+    arrays, (tile, up_sum, down_sum), outs, (tile_out, up_in, down_in), held, core_in, ring_in, x_in, tiles, sems = refs_of(counts, refs)
     load_sem, core_send, core_recv, ring_send, ring_recv, x_send, x_recv, tile_send, tile_recv, hop_send, hop_recv = sems
-    tile_pairs, tile_ring, up_in, down_in = tiles
+    tile_pairs, tile_ring = tiles
     chip = lax.axis_index("zy")
     core = lax.axis_index("core")
     side = lax.axis_index("fsdp")
@@ -324,17 +324,9 @@
             core_copy(number, turn).start()
         return carry
 
-    half = up_in.shape[1]
-
     def hop_copy(way, kind):
         src, dst = ((up_sum, up_in), (down_sum, down_in))[way]
         return remote(src.at[kind], dst.at[kind], hop_send.at[way, kind], hop_recv.at[way, kind], neighbour(1 - 2 * way))
-
-    def hop_done(kind):
-        for way, arrived in enumerate((up_in, down_in)):
-            rows_here = pl.ds(way * half, half)
-            hop_copy(way, kind).wait()
-            units_out[kind, rows_here] = terms[kind, rows_here].astype(F32) + arrived[kind].astype(F32)
 
     def tile_copy(src, dst, number, peer):
         return remote(src, dst, tile_send.at[number], tile_recv.at[number], peer)
@@ -393,10 +385,6 @@
             def _(kind=kind):
                 for way in range(2):
                     hop_copy(way, kind).start()
-
-            @pl.when(turn == 5 + kind)
-            def _(kind=kind):
-                hop_done(kind)
 
         @pl.when(turn < chips)
         def _():
@@ -467,6 +455,10 @@
                 F32
             ) + x_in[number][0].astype(F32)
 
+    for kind in range(3):
+        for way in range(2):
+            hop_copy(way, kind).wait()
+
     def drain(turn, carry):
         for number in numbers:
             core_copy(number, turn).wait_send()
@@ -497,7 +489,7 @@
     return groups
 
 
-def sum_all(arrays, firsts, tile, up_sum, down_sum, terms, chips):
+def sum_all(arrays, firsts, tile, up_sum, down_sum, chips):
     rows = arrays[0].shape[0] // (4 * chips)
     streams = []
     for i, (array, first) in enumerate(zip(arrays, firsts)):
@@ -515,7 +507,6 @@
         + [vmem((chips - 1, 1 if first else 2, rows, width), BF16) for _, _, width, _, first in streams]
         + [vmem((chips if first else 1, rows, width), BF16) for _, _, width, _, first in streams]
         + [vmem((3, 8, 128), F32), vmem((chips, 8, 128), F32)]
-        + [vmem(up_sum.shape, BF16), vmem(down_sum.shape, BF16)]
         + [dma((count,))]
         + [dma((number, chips)) for _ in range(6)]
         + [dma((chips + 1,)) for _ in range(2)]
@@ -523,15 +514,15 @@
     )
     return pl.pallas_call(
         functools.partial(
-            sum_kernel, chips, streams, (count, 4, count, 2, count, count, number, number, 4, 11)
+            sum_kernel, chips, streams, (count, 3, count, 3, count, count, number, number, 2, 11)
         ),
         out_shape=[jax.ShapeDtypeStruct((rows, a.shape[1]), F32) for a in arrays]
-        + [jax.ShapeDtypeStruct((8, 128), F32), jax.ShapeDtypeStruct(terms.shape, F32)],
+        + [jax.ShapeDtypeStruct((8, 128), F32)]
+        + [jax.ShapeDtypeStruct(up_sum.shape, BF16)] * 2,
         in_specs=[pl.BlockSpec(memory_space=pl.ANY)] * count
         + [pl.BlockSpec(memory_space=pltpu.VMEM)]
-        + [pl.BlockSpec(memory_space=pl.ANY)] * 2
-        + [pl.BlockSpec(memory_space=pltpu.VMEM)],
-        out_specs=[pl.BlockSpec(memory_space=pltpu.VMEM)] * (count + 2),
+        + [pl.BlockSpec(memory_space=pl.ANY)] * 2,
+        out_specs=[pl.BlockSpec(memory_space=pltpu.VMEM)] * (count + 1) + [pl.BlockSpec(memory_space=pl.ANY)] * 2,
         scratch_shapes=scratch,
         compiler_params=pltpu.CompilerParams(
             collective_id=1, has_side_effects=True, vmem_limit_bytes=58 << 20
@@ -540,7 +531,7 @@
             flops=0, bytes_accessed=sum(2 * a.size for a in arrays), transcendentals=0
         ),
         name="sum_all",
-    )(*[a.reshape(chips, 2, 2, rows, a.shape[1]) for a in arrays], tile, up_sum, down_sum, terms)
+    )(*[a.reshape(chips, 2, 2, rows, a.shape[1]) for a in arrays], tile, up_sum, down_sum)
 
 
 LITTLE = pl.CostEstimate(flops=0, bytes_accessed=1024, transcendentals=0)
@@ -841,10 +832,13 @@
     return refs_of((len(sums), steps, steps), outs)
 
 
-def unit_grads_kernel(grad_gate, grad_upper, hidden, rows, down_rows, out):
-    out[0] = left_dot(grad_gate[...], rows[...]).astype(BF16)
-    out[1] = left_dot(grad_upper[...], rows[...]).astype(BF16)
-    out[2] = left_dot(hidden[...], down_rows[...]).astype(BF16)
+def unit_grads_kernel(grad_gate, grad_upper, hidden, rows, down_rows, up_out, down_out):
+    half = up_out.shape[1]
+    pairs = ((grad_gate, rows), (grad_upper, rows), (hidden, down_rows))
+    for kind, (left, right) in enumerate(pairs):
+        out = left_dot(left[...], right[...]).astype(BF16)
+        up_out[kind] = out[:half]
+        down_out[kind] = out[half:]
 
 
 def unit_grads_of(grad_gate, grad_upper, hidden, rows, down_rows):
@@ -852,14 +846,15 @@
     width = 1024
     narrow = whole((many, units))
     wide = pl.BlockSpec((many, width), lambda i: (0, i))
+    part = pl.BlockSpec((3, units // 2, width), lambda i: (0, 0, i))
     return piece(
         unit_grads_kernel,
         "unit_grads",
         (D // width,),
         [narrow, narrow, narrow, wide, wide],
-        [pl.BlockSpec((3, units, width), lambda i: (0, 0, i))],
-        [((3, units, D), BF16)],
-    )(grad_gate, grad_upper, hidden, rows, down_rows)[0]
+        [part, part],
+        [((3, units // 2, D), BF16)] * 2,
+    )(grad_gate, grad_upper, hidden, rows, down_rows)
 
 
 def attend_back_kernel(
@@ -1101,7 +1096,8 @@
     return {"core": 1 - lax.axis_index("core")}, {"fsdp": 1 - lax.axis_index("fsdp")}
 
 
-CUTS = 4
+CUTS = 8
+FLYING = 2
 
 
 def spread_kernel(own, rows, x_send, x_recv, near_send, near_recv, far_send, far_recv, own_sem):
@@ -1125,17 +1121,18 @@
     across = [copy(mine[at], 1, at, x_send, x_recv, other_side) for at in range(CUTS)]
     near = [copy(mine[at], 2, at, near_send, near_recv, other_core) for at in range(CUTS)]
     far = [copy(came[at], 3, at, far_send, far_recv, other_core) for at in range(CUTS)]
-    for one in across + near:
+    for one in across[:FLYING] + near:
         one.start()
     keep = pltpu.make_async_copy(own, rows.at[pl.ds(0, count)], own_sem)
     keep.start()
     for at in range(CUTS):
+        across[at].wait_send()
+        if at + FLYING < CUTS:
+            across[at + FLYING].start()
         across[at].wait_recv()
         far[at].start()
     for one in near + far:
         one.wait()
-    for one in across:
-        one.wait_send()
     keep.wait()
 
 
@@ -1145,7 +1142,7 @@
     return pl.pallas_call(
         spread_kernel,
         out_shape=jax.ShapeDtypeStruct((4 * count, D), BF16),
-        in_specs=[pl.BlockSpec(memory_space=pl.ANY)],
+        in_specs=[pl.BlockSpec(memory_space=pltpu.VMEM)],
         out_specs=pl.BlockSpec(memory_space=pl.ANY),
         scratch_shapes=[dma((CUTS,)) for _ in range(6)] + [dma],
         compiler_params=pltpu.CompilerParams(collective_id=number, has_side_effects=True),
@@ -1154,7 +1151,31 @@
     )(own)
 
 
-def gather_sum_kernel(own, low, out, core_in, pair_low, x_in, core_send, core_recv, x_send, x_recv):
+def gather_sum_kernel(steps, *refs):
+    if steps:
+        (own, low, rows, down_rows), sides, (out,), grads, more, held, sems = refs_of(
+            (4, 3 * steps, 1, 2 * steps, 4 + 4, 3, 3), refs
+        )
+        core_in, pair_low, x_in, parts, *copy_sems = more
+        core_send, core_recv, x_send, x_recv = copy_sems
+        rows_in, down_in, more_out = held
+        loads_sem, parts_sem, grads_sem = sems
+        parts_out = more_out
+
+        def store(step, way):
+            return pltpu.make_async_copy(parts_out.at[step, way], grads[2 * step + way], grads_sem.at[step, way])
+
+        loads = [
+            pltpu.make_async_copy(rows, rows_in, loads_sem.at[0]),
+            pltpu.make_async_copy(down_rows, down_in, loads_sem.at[1]),
+        ]
+        part_loads = [
+            pltpu.make_async_copy(side, parts.at[number], parts_sem.at[number]) for number, side in enumerate(sides)
+        ]
+        for load in loads + part_loads:
+            load.start()
+    else:
+        own, low, out, core_in, pair_low, x_in, core_send, core_recv, x_send, x_recv = refs
     count = out.shape[0]
     cut = count // CUTS
     other_core, other_side = partners()
@@ -1183,51 +1204,82 @@
             device_id_type=MESH,
         )
 
-    for block in (1, 0):
-        for at in range(CUTS):
-            core_copy(block, at).start()
+    pieces = [(block, at) for block in (1, 0) for at in range(CUTS)]
+
+    def next_piece(number):
+        core_copy(*pieces[number]).wait_send()
+        if number + FLYING < len(pieces):
+            core_copy(*pieces[number + FLYING]).start()
+
+    for one in pieces[:FLYING]:
+        core_copy(*one).start()
     for at in range(CUTS):
         there = pl.ds(count + at * cut, cut)
+        next_piece(at)
         core_copy(1, at).wait_recv()
         pair_low[pl.ds(at * cut, cut)] = (own[there] + core_in[there].astype(F32)).astype(BF16)
         x_copy(at).start()
     for at in range(CUTS):
         here = pl.ds(at * cut, cut)
+        next_piece(CUTS + at)
         core_copy(0, at).wait_recv()
         out[here] = own[here] + core_in[here].astype(F32)
+    if steps:
+        for load in loads:
+            load.wait()
+        half = grads[0].shape[1]
+        width = D // 2
+        for step in range(steps):
+            for kind in range(3):
+                number = 3 * step + kind
+                part_loads[number].wait()
+                left, right = parts[number], down_in if kind == 2 else rows_in
+                for first in range(0, D, width):
+                    cols = slice(first, first + width)
+                    term = left_dot(left, right[:, cols]).astype(BF16)
+                    parts_out[step, 0, kind, :, cols] = term[:half]
+                    parts_out[step, 1, kind, :, cols] = term[half:]
+            for way in range(2):
+                store(step, way).start()
     for at in range(CUTS):
         here = pl.ds(at * cut, cut)
         x_copy(at).wait_recv()
         out[here] += x_in[here].astype(F32)
     for at in range(CUTS):
         x_copy(at).wait_send()
-        for block in (0, 1):
-            core_copy(block, at).wait_send()
-
-
-def sum_of_four(own, low, number):
+    for step in range(steps):
+        for way in range(2):
+            store(step, way).wait()
+
+
+def sum_of_four(own, low, number, units=(), rows=None, down_rows=None):
     count = own.shape[0] // 2
+    steps = len(units)
     dma = pltpu.SemaphoreType.DMA
-    return pl.pallas_call(
-        gather_sum_kernel,
-        out_shape=jax.ShapeDtypeStruct((count, D), F32),
-        in_specs=[pl.BlockSpec(memory_space=pltpu.VMEM), pl.BlockSpec(memory_space=pl.ANY)],
-        out_specs=pl.BlockSpec(memory_space=pltpu.VMEM),
-        scratch_shapes=[
-            pltpu.VMEM((2 * count, D), BF16),
-            pltpu.VMEM((count, D), BF16),
-            pltpu.VMEM((count, D), BF16),
-            dma((2 * CUTS,)),
-            dma((2 * CUTS,)),
-            dma((CUTS,)),
-            dma((CUTS,)),
-        ],
+    vmem, anywhere = pltpu.VMEM, pl.BlockSpec(memory_space=pl.ANY)
+    scratch = [vmem((2 * count, D), BF16), vmem((count, D), BF16), vmem((count, D), BF16)]
+    copy_sems = [dma((2 * CUTS,)), dma((2 * CUTS,)), dma((CUTS,)), dma((CUTS,))]
+    operands, shapes = [], []
+    if steps:
+        many, width = units[0][0].shape
+        operands = [rows, down_rows] + [side for sides in units for side in sides]
+        shapes = [jax.ShapeDtypeStruct((3, width // 2, D), BF16)] * (2 * steps)
+        scratch += [vmem((3 * steps, many, width), BF16)]
+        copy_sems += [vmem((many, D), BF16), vmem((many, D), BF16), vmem((steps, 2, 3, width // 2, D), BF16)]
+        copy_sems += [dma((2,)), dma((3 * steps,)), dma((steps, 2))]
+    total, *grads = pl.pallas_call(
+        functools.partial(gather_sum_kernel, steps),
+        out_shape=[jax.ShapeDtypeStruct((count, D), F32)] + shapes,
+        in_specs=[pl.BlockSpec(memory_space=pltpu.VMEM), anywhere] + [anywhere] * len(operands),
+        out_specs=[pl.BlockSpec(memory_space=pltpu.VMEM)] + [anywhere] * len(shapes),
+        scratch_shapes=scratch + copy_sems,
         compiler_params=pltpu.CompilerParams(
             collective_id=number, has_side_effects=True, vmem_limit_bytes=VMEM_LIMIT
         ),
         cost_estimate=LITTLE,
         name="gather_sum",
-    )(own, low)
+    )(own, low, *operands)
+    return total, [(grads[2 * i], grads[2 * i + 1]) for i in range(steps)]
 
 
 def body(
@@ -1409,7 +1461,7 @@
     pass_on(6)
     running = stage_end(forward_part(running, here, then))
     own_sum, low_sum = forward_part(running, then, chips, True)
-    down_out = sum_of_four(own_sum, low_sum, 3)
+    down_out, unused = sum_of_four(own_sum, low_sum, 3)
     after_ffn = mixed + rms_norm(down_out, gains[4])
     after_low = after_ffn.astype(BF16)
     pl_raw = full_dot(after_low, plg)
@@ -1446,7 +1498,11 @@
             grad_gates[k], grad_uppers[k] = gg, gu
         return sums if last else sums[0]
 
+    ready = {}
+
     def unit_grads(k):
+        if k in ready:
+            return ready[k]
         return unit_grads_of(grad_gates[k], grad_uppers[k], hiddens[k], ffn_rows, grad_down_rows)
 
     order = list(range(1, chips)) + [0]
@@ -1464,20 +1520,31 @@
             done += 1
             terms = unit_grads(order[done])
             (up_in, down_in), terms, values = tie((up_in, down_in), terms, values)
-            up_sum = (up_in.astype(F32) + terms[:, :half].astype(F32)).astype(BF16)
-            down_sum = (down_in.astype(F32) + terms[:, half:].astype(F32)).astype(BF16)
+            up_sum = (up_in.astype(F32) + terms[0].astype(F32)).astype(BF16)
+            down_sum = (down_in.astype(F32) + terms[1].astype(F32)).astype(BF16)
         return work() if values is None else values
 
     first = ring_steps[0]
     then = first + 1 + ring_steps[0] + ring_steps[1]
     running = backward_part(order[:first], None)
-    terms = unit_grads(order[0])
-    up_sum, down_sum = terms[:, :half], terms[:, half:]
+    up_sum, down_sum = unit_grads(order[0])
     running = beside(0, lambda: backward_part(order[first:then], running))
     own_sum, low_sum = beside(1, lambda: backward_part(order[then:], running, True))
-    grad_ffn_in = beside(
-        2, lambda: sum_of_four(own_sum, low_sum, 5)
-    )
+
+    def work():
+        steps = order[done + ring_steps[2] :] if units % 128 == 0 else []
+        total, grads = sum_of_four(
+            own_sum,
+            low_sum,
+            5,
+            [(grad_gates[k], grad_uppers[k], hiddens[k]) for k in steps],
+            ffn_rows,
+            grad_down_rows,
+        )
+        ready.update(zip(steps, grads))
+        return total
+
+    grad_ffn_in = beside(2, work)
     (
         grad_scaled,
         grad_mid_low,
@@ -1537,17 +1604,22 @@
             1,
         )
 
-    grad_wkv, grad_tokens, rest_back = beside(5, work)
-    sums_wq, sums_wkv, sums_wo, sums_rest, total, grad_units = sum_all(
+    last_terms, (grad_wkv, grad_tokens, rest_back) = beside(5, lambda: (unit_grads(0), work()))
+    sums_wq, sums_wkv, sums_wo, sums_rest, total, up_in, down_in = sum_all(
         [grad_wq, grad_wkv, grad_wo, rest_back],
         (True, True, True, False),
         jnp.broadcast_to(squares, (8, 128)),
         up_sum,
         down_sum,
-        unit_grads(0),
         chips,
     )
-    grad_ffn = grad_units.transpose(1, 0, 2)
+    grad_ffn = jnp.concatenate(
+        [
+            (arrived.astype(F32) + term.astype(F32)).transpose(1, 0, 2)
+            for arrived, term in zip((up_in, down_in), last_terms)
+        ],
+        0,
+    )
     at = 0
     rest = []
     for width in (PLD, proj_cols, RANK, misc_cols, RANK):

time: 960 us -> 943 us (0.982)
  Pallas kernels: 662 us -> 604 us
  waiting for transfers between devices: 125 us -> 160 us
  starting transfers between devices: 40.8 us -> 51.5 us
  local copies, waits for them, and re-layouts: 62.1 us -> 51.9 us
  other arithmetic: 48.8 us -> 58.8 us
    pallas_call x8 -> x3, Pallas kernels: 72.1 us -> 22.9 us  [unit_grads_of(): piece(unit_grads_kernel, 'unit_grads', (D // width,), [narrow, narrow, na...]
    ppermute x26, waiting for transfers between devices: 90.5 us -> 121 us  [ring(): return lax.ppermute(value, 'zy', ring_pairs(lax.axis_size('zy'), by))]
    pallas_call x2, Pallas kernels: 69.1 us -> 55.4 us  [rows_of_four(): pl.pallas_call(spread_kernel, out_shape=jax.ShapeDtypeStruct((4 * count,...]
    ppermute x26, starting transfers between devices: 30.9 us -> 41.4 us  [ring(): return lax.ppermute(value, 'zy', ring_pairs(lax.axis_size('zy'), by))]
    unnamed x80 -> x95, local copies, waits for them, and re-layouts: 22.5 us -> 16.1 us
    convert_element_type x6 -> x12, other arithmetic: 27 us -> 30.7 us  [the longest x6 17.1 us: beside(): down_sum = (down_in.astype(F32) + terms[1].astype(F32)).astype(BF16)]
  transfers between devices with their start and end apart: 34 -> 34, of which waited for: 18 -> 21; matrix products, arithmetic and copies ran while one was open for 5% -> 6% of each run, Pallas kernels for 44% -> 41%
where the time goes in v5:
time: 943 us; the launch traced here: 939 us
  Pallas kernels  604 us (64%)
  waiting for transfers between devices  160 us (17%)
  other arithmetic  58.8 us (6%)
  local copies, waits for them, and re-layouts  51.9 us (6%)
  starting transfers between devices  51.5 us (5%)
    pallas_call x1, Pallas kernels, sum_all(): pl.pallas_call(functools.partial(sum_kernel, chips, streams, (count, 3, c...  132 us
    pallas_call x1, Pallas kernels, gather_all(): pl.pallas_call(functools.partial(gather_kernel, chips, streams), out_shap...  123 us
    ppermute x26, waiting for transfers between devices, ring(): return lax.ppermute(value, 'zy', ring_pairs(lax.axis_size('zy'), by))  121 us
    pallas_call x2, Pallas kernels, sum_of_four(): pl.pallas_call(functools.partial(gather_sum_kernel, steps), out_shape=[ja...  67.5 us
    pallas_call x3, Pallas kernels, ffn_backward(): piece(functools.partial(ffn_backward_kernel, steps, add, last), 'ffn_back...  61.7 us
    pallas_call x3, Pallas kernels, ffn_forward(): piece(functools.partial(ffn_forward_kernel, steps, add, last), 'ffn_forwa...  55.8 us
    pallas_call x2, Pallas kernels, rows_of_four(): pl.pallas_call(spread_kernel, out_shape=jax.ShapeDtypeStruct((4 * count,...  55.4 us
    ppermute x26, starting transfers between devices, ring(): return lax.ppermute(value, 'zy', ring_pairs(lax.axis_size('zy'), by))  41.4 us
  transfers between devices with their start and end apart: 34, of which 21 were waited for; matrix products, arithmetic and copies ran while one was open for 6% of the time, Pallas kernels for 41%

profile of v5, /device:TPU:0, one launch (start us, length us, event | category | flops | bytes accessed | tf_op | source)
XLA Modules:
  0.0 938.6 jit_solution(14773614019430962472)
XLA Ops:
  0.7 2.2 fusion.32
  2.9 3.0 collective-permute-start.1
  12.8 2.0 concatenate.23.shard
  14.8 122.9 %gather_all.1.weight.w_out.lleft.lright = bf16[2048,5888]{1,0:T(8,128)(2,1)} custom-call(bf16[64,5888]{1,0:T(8,128)(2,1)} %concatenate.23.shard), custom_call_target="tpu_custom_call" | custom-call | bytes 48234496 | tf_op jit(solution)/shard_map/gather_all/pallas_call | solution.py:224
  137.7 2.0 slice.81
  146.0 13.5 %make_qkv.1 = (bf16[256,2048]{1,0:T(8,128)(2,1)}, f32[256,3072]{1,0:T(8,128)}, bf16[256,3072]{1,0:T(8,128)(2,1)}) custom-call(bf16[256,2048]{1,0:T(8,128)(2,1)} %bitcast.57, f32[8,2048]{1,0:T(8,128)} %pad.19.gains, f32[2,256]{1,0:T(2,128)} %reshape.165.head_gain, f32[256,128]{1,0:T(8,128)} %get-tuple-element.389.cosine, f32[256,128]{1,0:T(8,128)} %get-tuple-element.388.sine, ...), custom_call_target="tpu_custom_call" | custom-call | bytes 1024 | tf_op jit(solution)/shard_map/make_qkv/pallas_call | solution.py:594
  159.4 18.5 %collective-permute-done.2.refs_4_.refs_0_ = bf16[3,128,2048]{2,1,0:T(8,128)(2,1)S(1)} collective-permute-done((bf16[3,128,2048]{2,1,0:T(8,128)(2,1)}, bf16[3,128,2048]{2,1,0:T(8,128)(2,1)S(1)}, u32[]{:S(2)}, u32[]{:S(2)}) %collective-permute-start.2) | collective-permute-done | bytes 1572896 | tf_op jit(solution)/shard_map/ppermute | solution.py:61
  178.2 2.3 slice.85
  180.4 4.2 collective-permute-start.7
  188.1 8.4 collective-permute-done.7
  196.5 1.9 broadcast_select_fusion.1
  201.3 1.9 collective-permute-done.9
  203.2 2.3 pad_maximum_fusion.1.key.value
  205.5 16.1 %collective-permute-done.4.refs_6_.refs_2_ = bf16[3,128,2048]{2,1,0:T(8,128)(2,1)} collective-permute-done((bf16[3,128,2048]{2,1,0:T(8,128)(2,1)S(1)}, bf16[3,128,2048]{2,1,0:T(8,128)(2,1)}, u32[]{:S(2)}, u32[]{:S(2)}) %collective-permute-start.4) | collective-permute-done | bytes 1572896 | tf_op jit(solution)/shard_map/ppermute | solution.py:61
  221.6 6.9 collective-permute-done.5.refs_7_.refs_3_
  228.5 2.6 collective-permute-start.11
  232.2 19.5 %attend.1 = (bf16[256,2048]{1,0:T(8,128)(2,1)}, f32[256,2048]{1,0:T(8,128)}, f32[256,2048]{1,0:T(8,128)}, bf16[256,2048]{1,0:T(8,128)(2,1)}, bf16[256,128]{1,0:T(8,128)(2,1)}) custom-call(bf16[256,2048]{1,0:T(8,128)(2,1)} %bitcast.58, f32[8,2048]{1,0:T(8,128)} %pad.19.gains, bf16[256,2048]{1,0:T(8,128)(2,1)} %get-tuple-element.178.low, ...), custom_call_target="tpu_custom_call" | custom-call | bytes 1024 | tf_op jit(solution)/shard_map/attend/pallas_call | solution.py:658
  251.7 12.6 %collective-permute-done.10.refs_8_.refs_4_ = bf16[3,128,2048]{2,1,0:T(8,128)(2,1)S(1)} collective-permute-done((bf16[3,128,2048]{2,1,0:T(8,128)(2,1)}, bf16[3,128,2048]{2,1,0:T(8,128)(2,1)S(1)}, u32[]{:S(2)}, u32[]{:S(2)}) %collective-permute-start.10) | collective-permute-done | bytes 1572896 | tf_op jit(solution)/shard_map/ppermute | solution.py:61
  264.3 8.4 collective-permute-done.11.refs_9_.refs_5_
  273.9 2.5 collective-permute-start.12
  276.3 2.1 collective-permute-start.13
  278.4 27.5 %spread_rows.2.refs_12_.refs_3_.rows.refs_2_ = bf16[1024,2048]{1,0:T(8,128)(2,1)} custom-call(bf16[256,2048]{1,0:T(8,128)(2,1)} %get-tuple-element.192.own), custom_call_target="tpu_custom_call" | custom-call | bytes 1024 | tf_op jit(solution)/shard_map/spread_rows/pallas_call | solution.py:1142
  305.9 5.1 collective-permute-done.12.refs_10_.refs_0_
  311.0 2.2 collective-permute-done.13.refs_11_.refs_1_
  314.9 11.0 %collective-permute-start.15 = (bf16[3,128,2048]{2,1,0:T(8,128)(2,1)}, bf16[3,128,2048]{2,1,0:T(8,128)(2,1)}, u32[]{:S(2)}, u32[]{:S(2)}) collective-permute-start(bf16[3,128,2048]{2,1,0:T(8,128)(2,1)} %collective-permute-done.13.refs_11_.refs_1_), channel_id=1, source_target_pairs={{0,4},{8,0},{16,8},{24,16},{28,24},{20,28},{12,20},{4,12},{1,5},{9... | collective-permute-start | bytes 4718600 | tf_op jit(solution)/shard_map/ppermute | solution.py:61
  325.9 31.0 %ffn_forward.3 = (f32[1024,2048]{1,0:T(8,128)}, f32[1024,256]{1,0:T(8,128)}, f32[1024,256]{1,0:T(8,128)}, f32[1024,256]{1,0:T(8,128)}, f32[1024,256]{1,0:T(8,128...) custom-call(bf16[3,128,2048]{2,1,0:T(8,128)(2,1)} %copy-done.4, ...), custom_call_target="tpu_custom_call" | custom-call | bytes 1024 | tf_op jit(solution)/shard_map/ffn_forward/pallas_call | solution.py:775
  356.9 3.2 collective-permute-done.15.refs_1_.refs_3_
  366.2 12.4 %ffn_forward.4 = (f32[1024,2048]{1,0:T(8,128)}, f32[1024,256]{1,0:T(8,128)}, f32[1024,256]{1,0:T(8,128)}, bf16[1024,256]{1,0:T(8,128)(2,1)}) custom-call(bf16[3,128,2048]{2,1,0:T(8,128)(2,1)} %collective-permute-done.14.refs_0_.refs_2_, bf16[3,128,2048]{2,1,0:T(8,128)(2,1)} %collective-permute-done.15.refs_1_.refs_3_, ...), custom_call_target="tpu_custom_call" | custom-call | bytes 1024 | tf_op jit(solution)/shard_map/ffn_forward/pallas_call | solution.py:775
  378.6 14.4 %collective-permute-done.16.refs_0_.refs_4_ = bf16[3,128,2048]{2,1,0:T(8,128)(2,1)S(1)} collective-permute-done((bf16[3,128,2048]{2,1,0:T(8,128)(2,1)}, bf16[3,128,2048]{2,1,0:T(8,128)(2,1)S(1)}, u32[]{:S(2)}, u32[]{:S(2)}) %collective-permute-start.16) | collective-permute-done | bytes 1572896 | tf_op jit(solution)/shard_map/ppermute | solution.py:61
  394.1 12.4 %ffn_forward.5 = (f32[512,2048]{1,0:T(8,128)}, bf16[512,2048]{1,0:T(8,128)(2,1)}, f32[1024,256]{1,0:T(8,128)}, f32[1024,256]{1,0:T(8,128)}, bf16[1024,256]{1,0:T(8,128)(2,1)}) custom-call(bf16[3,128,2048]{2,1,0:T(8,128)(2,1)} %copy-done.13, bf16[3,128,2048]{2,1,0:T(8,128)(2,1)} %collective-permute-done.17.refs_1_.refs_5_, ...), custom_call_target="tpu_custom_call" | custom-call | bytes 1024 | tf_op jit(solution)/shard_map/ffn_forward/pallas_call | solution.py:775
  406.5 31.1 %gather_sum.2 = f32[256,2048]{1,0:T(8,128)} custom-call(f32[512,2048]{1,0:T(8,128)} %get-tuple-element.204.refs_0_, bf16[512,2048]{1,0:T(8,128)(2,1)} %get-tuple-element.205.refs_1_), custom_call_target="tpu_custom_call" | custom-call | bytes 1024 | tf_op jit(solution)/shard_map/gather_sum/pallas_call | solution.py:1270
  437.6 2.0 multiply_reduce_fusion.5
  443.2 2.1 multiply_reduce_fusion
  447.4 2.4 multiply_reduce_fusion.1
  452.5 27.9 %spread_rows.3.refs_2_.down_rows.refs_7_.refs_9_.refs_3_ = bf16[1024,2048]{1,0:T(8,128)(2,1)} custom-call(bf16[256,2048]{1,0:T(8,128)(2,1)} %fusion.3.own), custom_call_target="tpu_custom_call" | custom-call | bytes 1024 | tf_op jit(solution)/shard_map/spread_rows/pallas_call | solution.py:1142
  480.4 12.1 %ffn_backward.3 = (f32[1024,2048]{1,0:T(8,128)}, bf16[1024,256]{1,0:T(8,128)(2,1)}, bf16[1024,256]{1,0:T(8,128)(2,1)}) custom-call(bf16[3,128,2048]{2,1,0:T(8,128)(2,1)} %collective-permute-done.refs_2_.refs_0_, bf16[3,128,2048]{2,1,0:T(8,128)(2,1)} %collective-permute-done.1.refs_3_.refs_1_, ...), custom_call_target="tpu_custom_call" | custom-call | bytes 1024 | tf_op jit(solution)/shard_map/ffn_backward/pallas_call | solution.py:821
  492.6 7.9 unit_grads.3
  502.5 22.4 %ffn_backward.4 = (f32[1024,2048]{1,0:T(8,128)}, bf16[1024,256]{1,0:T(8,128)(2,1)}, bf16[1024,256]{1,0:T(8,128)(2,1)}, bf16[1024,256]{1,0:T(8,128)(2,1)}, bf16[1...) custom-call(bf16[3,128,2048]{2,1,0:T(8,128)(2,1)} %copy-done.9, ...), custom_call_target="tpu_custom_call" | custom-call | bytes 1024 | tf_op jit(solution)/shard_map/ffn_backward/pallas_call | solution.py:821
  524.9 7.5 unit_grads.4
  532.4 4.9 collective-permute-done.18
  537.8 2.2 add_convert_fusion.10
  543.8 7.5 unit_grads.5
  551.3 27.1 %ffn_backward.5 = (f32[512,2048]{1,0:T(8,128)}, bf16[512,2048]{1,0:T(8,128)(2,1)}, bf16[1024,256]{1,0:T(8,128)(2,1)}, bf16[1024,256]{1,0:T(8,128)(2,1)}, bf16[10...) custom-call(bf16[3,128,2048]{2,1,0:T(8,128)(2,1)} %copy-done.8, ...), custom_call_target="tpu_custom_call" | custom-call | bytes 1024 | tf_op jit(solution)/shard_map/ffn_backward/pallas_call | solution.py:821
  578.6 3.4 add_convert_fusion.8
  586.0 36.4 %gather_sum.3 = (f32[256,2048]{1,0:T(8,128)}, bf16[3,128,2048]{2,1,0:T(8,128)(2,1)}, bf16[3,128,2048]{2,1,0:T(8,128)(2,1)}, bf16[3,128,2048]{2,1,0:T(8,128)(2,1)...) custom-call(f32[512,2048]{1,0:T(8,128)} %get-tuple-element.250.refs_, ...), custom_call_target="tpu_custom_call" | custom-call | bytes 1024 | tf_op jit(solution)/shard_map/gather_sum/pallas_call | solution.py:1270
  622.4 3.3 add_convert_fusion.6
  629.5 27.6 %attend_back.1 = (f32[256,2048]{1,0:T(8,128)}, bf16[256,128]{1,0:T(8,128)(2,1)}, f32[8,2048]{1,0:T(8,128)}, f32[2048,128]{1,0:T(8,128)}, f32[2048,128]{1,0:T(8,1...) custom-call(f32[8,2048]{1,0:T(8,128)} %pad.19.gains, ...), custom_call_target="tpu_custom_call" | custom-call | bytes 1024 | tf_op jit(solution)/shard_map/attend_back/pallas_call | solution.py:914
  657.2 5.4 collective-permute-done.25
  662.6 2.9 collective-permute-done.24
  678.8 14.4 %query_back.1 = (bf16[2048,2048]{1,0:T(8,128)(2,1)}, f32[256,2048]{1,0:T(8,128)}, f32[1,256]{1,0:T(1,128)}) custom-call(f32[256,2048]{1,0:T(8,128)} %get-tuple-element.297.grad_query, f32[256,3072]{1,0:T(8,128)} %get-tuple-element.298.raw, f32[256,128]{1,0:T(8,128)} %get-tuple-element.389.cosine, f32[256,128]{1,0:T(8,128)} %get-tuple-element.388.sine, ...), custom_call_target="tpu_custom_call" | custom-call | bytes 1024 | tf_op jit(solution)/shard_map/query_back/pallas_call | solution.py:992
  693.2 28.3 %collective-permute-done.30 = bf16[256,1024]{1,0:T(8,128)(2,1)} collective-permute-done((bf16[256,1024]{1,0:T(8,128)(2,1)}, bf16[256,1024]{1,0:T(8,128)(2,1)}, u32[]{:S(2)}, u32[]{:S(2)}) %collective-permute-start.30) | collective-permute-done | bytes 524320 | tf_op jit(solution)/shard_map/ppermute | solution.py:1579
  721.5 2.7 fusion.6.grad_kv
  724.2 3.3 add_convert_fusion.2
  727.5 3.3 add_convert_fusion.3
  730.8 1.9 collective-permute-start.32
  740.9 11.8 %key_back.1 = (bf16[2048,1024]{1,0:T(8,128)(2,1)}, f32[256,2048]{1,0:T(8,128)}, f32[1,256]{1,0:T(1,128)}, f32[1,2048]{1,0:T(1,128)}) custom-call(f32[256,1024]{1,0:T(8,128)} %fusion.6.grad_kv, f32[256,3072]{1,0:T(8,128)} %get-tuple-element.298.raw, f32[256,128]{1,0:T(8,128)} %get-tuple-element.389.cosine, f32[256,128]{1,0:T(8,128)} %get-tuple-element.388.sine, ...), custom_call_target="tpu_custom_call" | custom-call | bytes 1024 | tf_op jit(solution)/shard_map/key_back/pallas_call | solution.py:1045
  756.1 6.0 collective-permute-done.33
  762.1 13.4 %collective-permute-done.32 = bf16[3,128,2048]{2,1,0:T(8,128)(2,1)} collective-permute-done((bf16[3,128,2048]{2,1,0:T(8,128)(2,1)}, bf16[3,128,2048]{2,1,0:T(8,128)(2,1)}, u32[]{:S(2)}, u32[]{:S(2)}) %collective-permute-start.32) | collective-permute-done | bytes 1572896 | tf_op jit(solution)/shard_map/ppermute | solution.py:61
  775.5 4.8 copy.49
  780.3 3.3 add_convert_fusion.1.refs_5_
  783.5 3.2 add_convert_fusion.refs_6_
  787.9 131.6 %sum_all.1 = (f32[64,2048]{1,0:T(8,128)}, f32[64,1024]{1,0:T(8,128)}, f32[64,2048]{1,0:T(8,128)}, f32[64,768]{1,0:T(8,128)}, f32[8,128]{1,0:T(8,128)}, /*index=5...) custom-call(bf16[8,2,2,64,2048]{4,3,2,1,0:T(8,128)(2,1)} %bitcast.61, bf16[8,2,2,64,1024]{4,3,2,1,0:T(8,128)(2,1)} %bitcast.62, ...), custom_call_target="tpu_custom_call" | custom-call | bytes 24117248 | tf_op jit(solution)/shard_map/sum_all/pallas_call | solution.py:515
  928.7 3.1 add_bitcast_fusion
  931.8 3.1 pad_maximum_fusion
  (217 shorter events, 89.5 us)
Async XLA Ops:
  0.6 5.4 copy-start.40
  0.7 12.1 %copy-start.36 = (bf16[64,2048]{1,0:T(8,128)(2,1)S(1)}, bf16[64,2048]{1,0:T(8,128)(2,1)}, u32[]{:S(2)}) copy-start(bf16[64,2048]{1,0:T(8,128)(2,1)} %param.20) | copy-start | bytes 786436
  0.7 12.1 %copy-start.37 = (bf16[64,1024]{1,0:T(8,128)(2,1)S(1)}, bf16[64,1024]{1,0:T(8,128)(2,1)}, u32[]{:S(2)}) copy-start(bf16[64,1024]{1,0:T(8,128)(2,1)} %param.19) | copy-start | bytes 393220
  2.8 134.9 %copy-start.3 = (bf16[3,128,2048]{2,1,0:T(8,128)(2,1)}, bf16[3,128,2048]{2,1,0:T(8,128)(2,1)S(1)}, u32[]{:S(2)}) copy-start(bf16[3,128,2048]{2,1,0:T(8,128)(2,1)S(1)} %get-tuple-element.378.refs_1_.refs_7_) | copy-start | bytes 4718596
  2.8 134.9 %copy-start.4 = (bf16[3,128,2048]{2,1,0:T(8,128)(2,1)}, bf16[3,128,2048]{2,1,0:T(8,128)(2,1)S(1)}, u32[]{:S(2)}) copy-start(bf16[3,128,2048]{2,1,0:T(8,128)(2,1)S(1)} %get-tuple-element.379.refs_0_.refs_6_) | copy-start | bytes 4718596
  2.9 138.1 %collective-permute-start.1 = (bf16[3,128,2048]{2,1,0:T(8,128)(2,1)S(1)}, bf16[3,128,2048]{2,1,0:T(8,128)(2,1)}, u32[]{:S(2)}, u32[]{:S(2)}) collective-permute-start(bf16[3,128,2048]{2,1,0:T(8,128)(2,1)S(1)} %get-tuple-element.378.refs_1_.refs_7_), channel_id=1, source_target_pairs={{0,4},{8,0},{16,8},{24,16},{28,24},{20,28},{12,20},{4,12},{1,5},{9... | collective-permute-start | bytes 4718600 | tf_op jit(solution)/shard_map/ppermute | solution.py:61
  5.9 135.1 %collective-permute-start = (bf16[3,128,2048]{2,1,0:T(8,128)(2,1)S(1)}, bf16[3,128,2048]{2,1,0:T(8,128)(2,1)}, u32[]{:S(2)}, u32[]{:S(2)}) collective-permute-start(bf16[3,128,2048]{2,1,0:T(8,128)(2,1)S(1)} %get-tuple-element.379.refs_0_.refs_6_), channel_id=1, source_target_pairs={{0,8},{8,16},{16,24},{24,28},{28,20},{20,12},{12,4},{4,0},{1,9},{9... | collective-permute-start | bytes 4718600 | tf_op jit(solution)/shard_map/ppermute | solution.py:61
  141.0 36.9 %collective-permute-start.2 = (bf16[3,128,2048]{2,1,0:T(8,128)(2,1)}, bf16[3,128,2048]{2,1,0:T(8,128)(2,1)S(1)}, u32[]{:S(2)}, u32[]{:S(2)}) collective-permute-start(bf16[3,128,2048]{2,1,0:T(8,128)(2,1)} %collective-permute-done.refs_2_.refs_0_), channel_id=1, source_target_pairs={{0,8},{8,16},{16,24},{24,28},{28,20},{20,12},{12,4},{4,0},{1,9},{9... | collective-permute-start | bytes 4718600 | tf_op jit(solution)/shard_map/ppermute | solution.py:61
  141.6 36.6 %collective-permute-start.3 = (bf16[3,128,2048]{2,1,0:T(8,128)(2,1)}, bf16[3,128,2048]{2,1,0:T(8,128)(2,1)S(1)}, u32[]{:S(2)}, u32[]{:S(2)}) collective-permute-start(bf16[3,128,2048]{2,1,0:T(8,128)(2,1)} %collective-permute-done.1.refs_3_.refs_1_), channel_id=1, source_target_pairs={{0,4},{8,0},{16,8},{24,16},{28,24},{20,28},{12,20},{4,12},{1,5},{9... | collective-permute-start | bytes 4718600 | tf_op jit(solution)/shard_map/ppermute | solution.py:61
  177.9 23.2 %copy-start.9 = (bf16[3,128,2048]{2,1,0:T(8,128)(2,1)}, bf16[3,128,2048]{2,1,0:T(8,128)(2,1)S(1)}, u32[]{:S(2)}) copy-start(bf16[3,128,2048]{2,1,0:T(8,128)(2,1)S(1)} %collective-permute-done.2.refs_4_.refs_0_) | copy-start | bytes 4718596
  178.2 23.0 %copy-start.10 = (bf16[3,128,2048]{2,1,0:T(8,128)(2,1)}, bf16[3,128,2048]{2,1,0:T(8,128)(2,1)S(1)}, u32[]{:S(2)}) copy-start(bf16[3,128,2048]{2,1,0:T(8,128)(2,1)S(1)} %collective-permute-done.3.refs_5_.refs_1_) | copy-start | bytes 4718596
  180.4 16.1 %collective-permute-start.7 = (bf16[256,1024]{1,0:T(8,128)(2,1)}, bf16[256,1024]{1,0:T(8,128)(2,1)}, u32[]{:S(2)}, u32[]{:S(2)}) collective-permute-start(bf16[256,1024]{1,0:T(8,128)(2,1)} %slice.85), channel_id=1, source_target_pairs={{0,4},{4,8},{8,12},{12,20},{1,5},{5,9},{9,13},{13,21},{2,6},{6,10}... | collective-permute-start | bytes 1572872 | tf_op jit(solution)/shard_map/ppermute | solution.py:1414
  184.6 11.9 %collective-permute-start.6 = (bf16[256,1024]{1,0:T(8,128)(2,1)}, bf16[256,1024]{1,0:T(8,128)(2,1)}, u32[]{:S(2)}, u32[]{:S(2)}) collective-permute-start(bf16[256,1024]{1,0:T(8,128)(2,1)} %slice.85), channel_id=1, source_target_pairs={{12,16},{13,17},{14,18},{15,19}} | collective-permute-start | bytes 1572872 | tf_op jit(solution)/shard_map/ppermute | solution.py:1413
  186.1 35.5 %collective-permute-start.4 = (bf16[3,128,2048]{2,1,0:T(8,128)(2,1)S(1)}, bf16[3,128,2048]{2,1,0:T(8,128)(2,1)}, u32[]{:S(2)}, u32[]{:S(2)}) collective-permute-start(bf16[3,128,2048]{2,1,0:T(8,128)(2,1)S(1)} %collective-permute-done.2.refs_4_.refs_0_), channel_id=1, source_target_pairs={{0,8},{8,16},{16,24},{24,28},{28,20},{20,12},{12,4},{4,0},{1,9},{9... | collective-permute-start | bytes 4718600 | tf_op jit(solution)/shard_map/ppermute | solution.py:61
  186.9 41.6 %collective-permute-start.5 = (bf16[3,128,2048]{2,1,0:T(8,128)(2,1)S(1)}, bf16[3,128,2048]{2,1,0:T(8,128)(2,1)}, u32[]{:S(2)}, u32[]{:S(2)}) collective-permute-start(bf16[3,128,2048]{2,1,0:T(8,128)(2,1)S(1)} %collective-permute-done.3.refs_5_.refs_1_), channel_id=1, source_target_pairs={{0,4},{8,0},{16,8},{24,16},{28,24},{20,28},{12,20},{4,12},{1,5},{9... | collective-permute-start | bytes 4718600 | tf_op jit(solution)/shard_map/ppermute | solution.py:61
  198.4 1.5 collective-permute-start.8
  201.2 2.0 collective-permute-start.9
  228.5 35.8 %collective-permute-start.10 = (bf16[3,128,2048]{2,1,0:T(8,128)(2,1)}, bf16[3,128,2048]{2,1,0:T(8,128)(2,1)S(1)}, u32[]{:S(2)}, u32[]{:S(2)}) collective-permute-start(bf16[3,128,2048]{2,1,0:T(8,128)(2,1)} %collective-permute-done.4.refs_6_.refs_2_), channel_id=1, source_target_pairs={{0,8},{8,16},{16,24},{24,28},{28,20},{20,12},{12,4},{4,0},{1,9},{9... | collective-permute-start | bytes 4718600 | tf_op jit(solution)/shard_map/ppermute | solution.py:61
  228.5 44.2 %collective-permute-start.11 = (bf16[3,128,2048]{2,1,0:T(8,128)(2,1)}, bf16[3,128,2048]{2,1,0:T(8,128)(2,1)S(1)}, u32[]{:S(2)}, u32[]{:S(2)}) collective-permute-start(bf16[3,128,2048]{2,1,0:T(8,128)(2,1)} %collective-permute-done.5.refs_7_.refs_3_), channel_id=1, source_target_pairs={{0,4},{8,0},{16,8},{24,16},{28,24},{20,28},{12,20},{4,12},{1,5},{9... | collective-permute-start | bytes 4718600 | tf_op jit(solution)/shard_map/ppermute | solution.py:61
  264.3 8.4 copy-start.11
  273.9 37.2 %collective-permute-start.12 = (bf16[3,128,2048]{2,1,0:T(8,128)(2,1)}, bf16[3,128,2048]{2,1,0:T(8,128)(2,1)S(1)}, u32[]{:S(2)}, u32[]{:S(2)}) collective-permute-start(bf16[3,128,2048]{2,1,0:T(8,128)(2,1)} %copy-done.11), channel_id=1, source_target_pairs={{0,8},{8,16},{16,24},{24,28},{28,20},{20,12},{12,4},{4,0},{1,9},{9... | collective-permute-start | bytes 4718600 | tf_op jit(solution)/shard_map/ppermute | solution.py:61
  276.3 36.9 %collective-permute-start.13 = (bf16[3,128,2048]{2,1,0:T(8,128)(2,1)}, bf16[3,128,2048]{2,1,0:T(8,128)(2,1)}, u32[]{:S(2)}, u32[]{:S(2)}) collective-permute-start(bf16[3,128,2048]{2,1,0:T(8,128)(2,1)} %copy-done.12), channel_id=1, source_target_pairs={{0,4},{8,0},{16,8},{24,16},{28,24},{20,28},{12,20},{4,12},{1,5},{9... | collective-permute-start | bytes 4718600 | tf_op jit(solution)/shard_map/ppermute | solution.py:61
  311.0 14.9 %copy-start.8 = (bf16[3,128,2048]{2,1,0:T(8,128)(2,1)}, bf16[3,128,2048]{2,1,0:T(8,128)(2,1)S(1)}, u32[]{:S(2)}) copy-start(bf16[3,128,2048]{2,1,0:T(8,128)(2,1)S(1)} %collective-permute-done.12.refs_10_.refs_0_) | copy-start | bytes 4718596
  313.2 43.7 %collective-permute-start.14 = (bf16[3,128,2048]{2,1,0:T(8,128)(2,1)S(1)}, bf16[3,128,2048]{2,1,0:T(8,128)(2,1)}, u32[]{:S(2)}, u32[]{:S(2)}) collective-permute-start(bf16[3,128,2048]{2,1,0:T(8,128)(2,1)S(1)} %collective-permute-done.12.refs_10_.refs_0_), channel_id=1, source_target_pairs={{0,8},{8,16},{16,24},{24,28},{28,20},{20,12},{12,4},{4,0},{1,9},{9... | collective-permute-start | bytes 4718600 | tf_op jit(solution)/shard_map/ppermute | solution.py:61
  314.9 45.2 %collective-permute-start.15 = (bf16[3,128,2048]{2,1,0:T(8,128)(2,1)}, bf16[3,128,2048]{2,1,0:T(8,128)(2,1)}, u32[]{:S(2)}, u32[]{:S(2)}) collective-permute-start(bf16[3,128,2048]{2,1,0:T(8,128)(2,1)} %collective-permute-done.13.refs_11_.refs_1_), channel_id=1, source_target_pairs={{0,4},{8,0},{16,8},{24,16},{28,24},{20,28},{12,20},{4,12},{1,5},{9... | collective-permute-start | bytes 4718600 | tf_op jit(solution)/shard_map/ppermute | solution.py:61
  356.9 5.3 copy-start.38
  356.9 6.6 slice-start
  360.1 32.8 %collective-permute-start.16 = (bf16[3,128,2048]{2,1,0:T(8,128)(2,1)}, bf16[3,128,2048]{2,1,0:T(8,128)(2,1)S(1)}, u32[]{:S(2)}, u32[]{:S(2)}) collective-permute-start(bf16[3,128,2048]{2,1,0:T(8,128)(2,1)} %collective-permute-done.14.refs_0_.refs_2_), channel_id=1, source_target_pairs={{0,8},{8,16},{16,24},{24,28},{28,20},{20,12},{12,4},{4,0},{1,9},{9... | collective-permute-start | bytes 4718600 | tf_op jit(solution)/shard_map/ppermute | solution.py:61
  360.7 32.8 %collective-permute-start.17 = (bf16[3,128,2048]{2,1,0:T(8,128)(2,1)}, bf16[3,128,2048]{2,1,0:T(8,128)(2,1)}, u32[]{:S(2)}, u32[]{:S(2)}) collective-permute-start(bf16[3,128,2048]{2,1,0:T(8,128)(2,1)} %collective-permute-done.15.refs_1_.refs_3_), channel_id=1, source_target_pairs={{0,4},{8,0},{16,8},{24,16},{28,24},{20,28},{12,20},{4,12},{1,5},{9... | collective-permute-start | bytes 4718600 | tf_op jit(solution)/shard_map/ppermute | solution.py:61
  406.5 33.1 %copy-start.7 = (f32[256,2048]{1,0:T(8,128)S(1)}, f32[256,2048]{1,0:T(8,128)}, u32[]{:S(2)}) copy-start(f32[256,2048]{1,0:T(8,128)} %get-tuple-element.186.mixed) | copy-start | bytes 6291460
  446.1 3.6 copy-start.14
  500.5 36.9 %collective-permute-start.18 = (bf16[3,128,2048]{2,1,0:T(8,128)(2,1)}, bf16[3,128,2048]{2,1,0:T(8,128)(2,1)S(1)}, u32[]{:S(2)}, u32[]{:S(2)}) collective-permute-start(bf16[3,128,2048]{2,1,0:T(8,128)(2,1)} %get-tuple-element.211), channel_id=1, source_target_pairs={{0,8},{8,16},{16,24},{24,28},{28,20},{20,12},{12,4},{4,0},{1,9},{9... | collective-permute-start | bytes 4718600 | tf_op jit(solution)/shard_map/ppermute | solution.py:61
  501.2 36.6 %collective-permute-start.19 = (bf16[3,128,2048]{2,1,0:T(8,128)(2,1)}, bf16[3,128,2048]{2,1,0:T(8,128)(2,1)S(1)}, u32[]{:S(2)}, u32[]{:S(2)}) collective-permute-start(bf16[3,128,2048]{2,1,0:T(8,128)(2,1)} %get-tuple-element.212), channel_id=1, source_target_pairs={{0,4},{8,0},{16,8},{24,16},{28,24},{20,28},{12,20},{4,12},{1,5},{9... | collective-permute-start | bytes 4718600 | tf_op jit(solution)/shard_map/ppermute | solution.py:61
  537.8 3.6 copy-start.28
  540.0 38.4 %collective-permute-start.21 = (bf16[3,128,2048]{2,1,0:T(8,128)(2,1)S(1)}, bf16[3,128,2048]{2,1,0:T(8,128)(2,1)S(1)}, u32[]{:S(2)}, u32[]{:S(2)}) collective-permute-start(bf16[3,128,2048]{2,1,0:T(8,128)(2,1)S(1)} %add_convert_fusion.10), channel_id=1, source_target_pairs={{0,4},{8,0},{16,8},{24,16},{28,24},{20,28},{12,20},{4,12},{1,5},{9... | collective-permute-start | bytes 4718600 | tf_op jit(solution)/shard_map/ppermute | solution.py:61
  543.1 35.5 %collective-permute-start.20 = (bf16[3,128,2048]{2,1,0:T(8,128)(2,1)}, bf16[3,128,2048]{2,1,0:T(8,128)(2,1)S(1)}, u32[]{:S(2)}, u32[]{:S(2)}) collective-permute-start(bf16[3,128,2048]{2,1,0:T(8,128)(2,1)} %add_convert_fusion.11), channel_id=1, source_target_pairs={{0,8},{8,16},{16,24},{24,28},{28,20},{20,12},{12,4},{4,0},{1,9},{9... | collective-permute-start | bytes 4718600 | tf_op jit(solution)/shard_map/ppermute | solution.py:61
  578.6 4.8 copy-start.26
  582.0 40.4 %collective-permute-start.23 = (bf16[3,128,2048]{2,1,0:T(8,128)(2,1)}, bf16[3,128,2048]{2,1,0:T(8,128)(2,1)S(1)}, u32[]{:S(2)}, u32[]{:S(2)}) collective-permute-start(bf16[3,128,2048]{2,1,0:T(8,128)(2,1)} %add_convert_fusion.8), channel_id=1, source_target_pairs={{0,4},{8,0},{16,8},{24,16},{28,24},{20,28},{12,20},{4,12},{1,5},{9... | collective-permute-start | bytes 4718600 | tf_op jit(solution)/shard_map/ppermute | solution.py:61
  585.2 37.2 %collective-permute-start.22 = (bf16[3,128,2048]{2,1,0:T(8,128)(2,1)}, bf16[3,128,2048]{2,1,0:T(8,128)(2,1)S(1)}, u32[]{:S(2)}, u32[]{:S(2)}) collective-permute-start(bf16[3,128,2048]{2,1,0:T(8,128)(2,1)} %add_convert_fusion.9), channel_id=1, source_target_pairs={{0,8},{8,16},{16,24},{24,28},{28,20},{20,12},{12,4},{4,0},{1,9},{9... | collective-permute-start | bytes 4718600 | tf_op jit(solution)/shard_map/ppermute | solution.py:61
  622.4 4.7 copy-start.27
  625.8 36.8 %collective-permute-start.25 = (bf16[3,128,2048]{2,1,0:T(8,128)(2,1)}, bf16[3,128,2048]{2,1,0:T(8,128)(2,1)S(1)}, u32[]{:S(2)}, u32[]{:S(2)}) collective-permute-start(bf16[3,128,2048]{2,1,0:T(8,128)(2,1)} %add_convert_fusion.6), channel_id=1, source_target_pairs={{0,4},{8,0},{16,8},{24,16},{28,24},{20,28},{12,20},{4,12},{1,5},{9... | collective-permute-start | bytes 4718600 | tf_op jit(solution)/shard_map/ppermute | solution.py:61
  628.9 36.5 %collective-permute-start.24 = (bf16[3,128,2048]{2,1,0:T(8,128)(2,1)}, bf16[3,128,2048]{2,1,0:T(8,128)(2,1)S(1)}, u32[]{:S(2)}, u32[]{:S(2)}) collective-permute-start(bf16[3,128,2048]{2,1,0:T(8,128)(2,1)} %add_convert_fusion.7), channel_id=1, source_target_pairs={{0,8},{8,16},{16,24},{24,28},{28,20},{20,12},{12,4},{4,0},{1,9},{9... | collective-permute-start | bytes 4718600 | tf_op jit(solution)/shard_map/ppermute | solution.py:61
  657.2 9.8 %copy-start.19 = (f32[768,512]{1,0:T(8,128)S(1)}, f32[768,512]{1,0:T(8,128)}, u32[]{:S(2)}) copy-start(f32[768,512]{1,0:T(8,128)} %get-tuple-element.296) | copy-start | bytes 4718596
  667.1 8.5 copy-start.6
  667.2 4.9 collective-permute-start.28
  670.9 53.3 %collective-permute-start.27 = (bf16[3,128,2048]{2,1,0:T(8,128)(2,1)}, bf16[3,128,2048]{2,1,0:T(8,128)(2,1)}, u32[]{:S(2)}, u32[]{:S(2)}) collective-permute-start(bf16[3,128,2048]{2,1,0:T(8,128)(2,1)} %add_convert_fusion.4), channel_id=1, source_target_pairs={{0,4},{8,0},{16,8},{24,16},{28,24},{20,28},{12,20},{4,12},{1,5},{9... | collective-permute-start | bytes 4718600 | tf_op jit(solution)/shard_map/ppermute | solution.py:61
  672.3 3.3 collective-permute-start.29
  674.8 49.4 %collective-permute-start.26 = (bf16[3,128,2048]{2,1,0:T(8,128)(2,1)}, bf16[3,128,2048]{2,1,0:T(8,128)(2,1)}, u32[]{:S(2)}, u32[]{:S(2)}) collective-permute-start(bf16[3,128,2048]{2,1,0:T(8,128)(2,1)} %add_convert_fusion.5), channel_id=1, source_target_pairs={{0,8},{8,16},{16,24},{24,28},{28,20},{20,12},{12,4},{4,0},{1,9},{9... | collective-permute-start | bytes 4718600 | tf_op jit(solution)/shard_map/ppermute | solution.py:61
  676.7 16.5 %collective-permute-start.31 = (bf16[256,1024]{1,0:T(8,128)(2,1)}, bf16[256,1024]{1,0:T(8,128)(2,1)S(1)}, u32[]{:S(2)}, u32[]{:S(2)}) collective-permute-start(bf16[256,1024]{1,0:T(8,128)(2,1)} %add_convert_fusion.12), channel_id=1, source_target_pairs={{16,12},{17,13},{18,14},{19,15}} | collective-permute-start | bytes 1572872 | tf_op jit(solution)/shard_map/ppermute | solution.py:1580
  677.4 44.2 %collective-permute-start.30 = (bf16[256,1024]{1,0:T(8,128)(2,1)}, bf16[256,1024]{1,0:T(8,128)(2,1)}, u32[]{:S(2)}, u32[]{:S(2)}) collective-permute-start(bf16[256,1024]{1,0:T(8,128)(2,1)} %add_convert_fusion.12), channel_id=1, source_target_pairs={{4,0},{8,4},{12,8},{20,12},{5,1},{9,5},{13,9},{21,13},{6,2},{10,6}... | collective-permute-start | bytes 1572872 | tf_op jit(solution)/shard_map/ppermute | solution.py:1579
  693.2 31.0 %copy-start.23 = (bf16[3,128,2048]{2,1,0:T(8,128)(2,1)S(1)}, bf16[3,128,2048]{2,1,0:T(8,128)(2,1)}, u32[]{:S(2)}) copy-start(bf16[3,128,2048]{2,1,0:T(8,128)(2,1)} %get-tuple-element.306) | copy-start | bytes 4718596
  724.2 3.3 copy-start.22
  727.5 5.2 copy-start.15
  727.5 5.2 copy-start.33
  727.5 34.6 %collective-permute-start.33 = (bf16[3,128,2048]{2,1,0:T(8,128)(2,1)}, bf16[3,128,2048]{2,1,0:T(8,128)(2,1)}, u32[]{:S(2)}, u32[]{:S(2)}) collective-permute-start(bf16[3,128,2048]{2,1,0:T(8,128)(2,1)} %add_convert_fusion.2), channel_id=1, source_target_pairs={{0,4},{8,0},{16,8},{24,16},{28,24},{20,28},{12,20},{4,12},{1,5},{9... | collective-permute-start | bytes 4718600 | tf_op jit(solution)/shard_map/ppermute | solution.py:61
  730.8 44.7 %collective-permute-start.32 = (bf16[3,128,2048]{2,1,0:T(8,128)(2,1)}, bf16[3,128,2048]{2,1,0:T(8,128)(2,1)}, u32[]{:S(2)}, u32[]{:S(2)}) collective-permute-start(bf16[3,128,2048]{2,1,0:T(8,128)(2,1)} %add_convert_fusion.3), channel_id=1, source_target_pairs={{0,8},{8,16},{16,24},{24,28},{28,20},{20,12},{12,4},{4,0},{1,9},{9... | collective-permute-start | bytes 4718600 | tf_op jit(solution)/shard_map/ppermute | solution.py:61
  736.1 3.5 copy-start.34
  740.9 12.5 %copy-start.39 = (f32[1,256]{1,0:T(1,128)S(1)}, f32[1,256]{1,0:T(1,128)}, u32[]{:S(2)}) copy-start(f32[1,256]{1,0:T(1,128)} %get-tuple-element.320) | copy-start | bytes 3076
  775.5 4.8 copy-start.21
  780.2 3.3 copy-start.20
  787.9 140.7 %copy-start.17 = (bf16[3,128,2048]{2,1,0:T(8,128)(2,1)S(1)}, bf16[3,128,2048]{2,1,0:T(8,128)(2,1)}, u32[]{:S(2)}) copy-start(bf16[3,128,2048]{2,1,0:T(8,128)(2,1)} %get-tuple-element.337) | copy-start | bytes 4718596
  787.9 140.7 %copy-start.18 = (bf16[3,128,2048]{2,1,0:T(8,128)(2,1)S(1)}, bf16[3,128,2048]{2,1,0:T(8,128)(2,1)}, u32[]{:S(2)}) copy-start(bf16[3,128,2048]{2,1,0:T(8,128)(2,1)} %get-tuple-element.339) | copy-start | bytes 4718596
  931.8 4.0 copy-start.35
  931.8 4.6 copy-start.30
  (12 other events, 21.4 us)

commit v6 on v5

--- a/solution.py
+++ b/solution.py
@@ -22,10 +22,6 @@
 ROPE_BASE = 10000.0
 BF16 = jnp.bfloat16
 F32 = jnp.float32
-
-
-def rms_norm(values, gain):
-    return values * lax.rsqrt(jnp.mean(values * values, axis=-1, keepdims=True) + EPSILON) * gain
 
 
 def gelu_tanh(values):
@@ -1282,6 +1278,191 @@
     return total, [(grads[2 * i], grads[2 * i + 1]) for i in range(steps)]
 
 
+PARTS = 4
+
+
+def middle_kernel(
+    own, low, mixed, layer_in, teacher, mask, scale, gains, gate_w, proj_w,
+    result, grad_after, grad_layer, rows, grad_gate_w, grad_proj_w, grad_gains, squares,
+    own_in, mixed_in, teacher_in, gate_in, proj_in, core_in, pair_low, x_in,
+    result_out, after_out, after_low, mid_low, grad_pl, grad_raw, grad_low,
+    loads, stores, core_send, core_recv, x_send, x_recv, y_send, y_recv, near_send, near_recv, far_send, far_recv,
+):
+    count = mixed.shape[0]
+    cut = count // PARTS
+    other_core, other_side = partners()
+
+    def load(number, src, dst):
+        return pltpu.make_async_copy(src, dst, loads.at[number])
+
+    incoming = [
+        load(0, own.at[pl.ds(count, count)], own_in.at[pl.ds(count, count)]),
+        load(1, own.at[pl.ds(0, count)], own_in.at[pl.ds(0, count)]),
+        load(2, mixed, mixed_in),
+        load(3, gate_w, gate_in),
+        load(4, proj_w, proj_in),
+        load(5, teacher, teacher_in),
+    ]
+    for one in incoming:
+        one.start()
+    greet((other_core, other_side))
+
+    def remote(src, dst, send, recv, peer):
+        return pltpu.make_async_remote_copy(
+            src_ref=src, dst_ref=dst, send_sem=send, recv_sem=recv, device_id=peer, device_id_type=MESH
+        )
+
+    def piece_of(at):
+        return pl.ds(at * cut, cut)
+
+    def core_copy(block, at):
+        here = pl.ds(block * count + at * cut, cut)
+        number = block * PARTS + at
+        return remote(low.at[here], core_in.at[here], core_send.at[number], core_recv.at[number], other_core)
+
+    def x_copy(at):
+        here = piece_of(at)
+        return remote(pair_low.at[here], x_in.at[here], x_send.at[at], x_recv.at[at], other_side)
+
+    def out_copy(src, block, at, send, recv, peer):
+        return remote(src, rows.at[pl.ds(block * count + at * cut, cut)], send.at[at], recv.at[at], peer)
+
+    def across(at):
+        return out_copy(grad_low.at[piece_of(at)], 1, at, y_send, y_recv, other_side)
+
+    def near(at):
+        return out_copy(grad_low.at[piece_of(at)], 2, at, near_send, near_recv, other_core)
+
+    def far(at):
+        return out_copy(rows.at[pl.ds(count + at * cut, cut)], 3, at, far_send, far_recv, other_core)
+
+    def kept(number, at):
+        here = piece_of(at)
+        src, dst = ((result_out, result), (after_out, grad_after), (grad_low, rows))[number]
+        return pltpu.make_async_copy(src.at[here], dst.at[here], stores.at[number, at])
+
+    for block in (1, 0):
+        for at in range(PARTS):
+            core_copy(block, at).start()
+    incoming[0].wait()
+    for at in range(PARTS):
+        there = pl.ds(count + at * cut, cut)
+        core_copy(1, at).wait_recv()
+        pair_low[piece_of(at)] = (own_in[there] + core_in[there].astype(F32)).astype(BF16)
+        x_copy(at).start()
+    for one in incoming[1:]:
+        one.wait()
+    gain_4, gain_5 = gains[4:5], gains[5:6]
+    total = jnp.zeros((), F32)
+    sum_4 = sum_5 = jnp.zeros((1, D), F32)
+    for at in range(PARTS):
+        here = piece_of(at)
+        core_copy(0, at).wait_recv()
+        x_copy(at).wait_recv()
+        down = own_in[here] + core_in[here].astype(F32) + x_in[here].astype(F32)
+        after = mixed_in[here] + down * inverse_rms(down) * gain_4
+        low_here = after.astype(BF16)
+        after_low[here] = low_here
+        raw = full_dot(low_here, gate_in[...])
+        act, act_back = jax.vjp(gelu_tanh, raw)
+        layer = layer_in[here].astype(F32)
+        mid = (act * layer).astype(BF16)
+        mid_low[here] = mid
+        out = full_dot(mid, proj_in[...])
+        done = after + out * inverse_rms(out) * gain_5
+        result_out[here] = done
+        kept(0, at).start()
+        errors = done - teacher_in[here].astype(F32)
+        masked = mask[here][:, 0:1] * errors
+        total += jnp.sum(masked * errors)
+        grad_out = masked * scale[0:1, 0:1]
+        back, term = norm_back(out, gain_5, grad_out)
+        sum_5 += term
+        back_low = back.astype(BF16)
+        grad_pl[here] = back_low
+        grad_mid = right_dot(back_low, proj_in[...])
+        grad_layer[here] = grad_mid * act
+        raw_low = act_back(grad_mid * layer)[0].astype(BF16)
+        grad_raw[here] = raw_low
+        grad_here = grad_out + right_dot(raw_low, gate_in[...])
+        after_out[here] = grad_here
+        kept(1, at).start()
+        back, term = norm_back(down, gain_4, grad_here)
+        sum_4 += term
+        grad_low[here] = back.astype(BF16)
+        across(at).start()
+        near(at).start()
+        kept(2, at).start()
+    grad_gains[...] = jnp.concatenate([sum_4, sum_5, jnp.zeros((6, D), F32)], 0)
+    squares[...] = jnp.broadcast_to(total, squares.shape)
+    for at in range(PARTS // 2):
+        across(at).wait_recv()
+        far(at).start()
+    grad_proj_w[...] = left_dot(mid_low[...], grad_pl[...]).astype(BF16)
+    grad_gate_w[...] = left_dot(after_low[...], grad_raw[...]).astype(BF16)
+    for at in range(PARTS // 2, PARTS):
+        across(at).wait_recv()
+        far(at).start()
+    for at in range(PARTS):
+        far(at).wait()
+        near(at).wait()
+        across(at).wait_send()
+        x_copy(at).wait_send()
+        for block in (0, 1):
+            core_copy(block, at).wait_send()
+        for number in range(3):
+            kept(number, at).wait()
+
+
+def middle(own, low, mixed, layer_in, teacher, mask, scale, gains, gate_w, proj_w):
+    count = mixed.shape[0]
+    dma, vmem = pltpu.SemaphoreType.DMA, pltpu.VMEM
+    anywhere, inside = pl.BlockSpec(memory_space=pl.ANY), pl.BlockSpec(memory_space=pltpu.VMEM)
+    shape = jax.ShapeDtypeStruct
+    return pl.pallas_call(
+        middle_kernel,
+        out_shape=[
+            shape((count, D), F32),
+            shape((count, D), F32),
+            shape((count, PLD), F32),
+            shape((4 * count, D), BF16),
+            shape((D, PLD), BF16),
+            shape((PLD, D), BF16),
+            shape((8, D), F32),
+            shape((8, 128), F32),
+        ],
+        in_specs=[anywhere, anywhere, anywhere, inside, anywhere, inside, inside, inside, anywhere, anywhere],
+        out_specs=[anywhere, anywhere, inside, anywhere, inside, inside, inside, inside],
+        scratch_shapes=[
+            vmem((2 * count, D), F32),
+            vmem((count, D), F32),
+            vmem((count, D), BF16),
+            vmem((D, PLD), BF16),
+            vmem((PLD, D), BF16),
+            vmem((2 * count, D), BF16),
+            vmem((count, D), BF16),
+            vmem((count, D), BF16),
+            vmem((count, D), F32),
+            vmem((count, D), F32),
+            vmem((count, D), BF16),
+            vmem((count, PLD), BF16),
+            vmem((count, D), BF16),
+            vmem((count, PLD), BF16),
+            vmem((count, D), BF16),
+            dma((6,)),
+            dma((3, PARTS)),
+            dma((2 * PARTS,)),
+            dma((2 * PARTS,)),
+        ]
+        + [dma((PARTS,)) for _ in range(8)],
+        compiler_params=pltpu.CompilerParams(
+            collective_id=3, has_side_effects=True, vmem_limit_bytes=VMEM_LIMIT
+        ),
+        cost_estimate=LITTLE,
+        name="middle",
+    )(own, low, mixed, layer_in, teacher, mask, scale, gains, gate_w, proj_w)
+
+
 def body(
     tokens,
     per_layer,
@@ -1298,8 +1479,6 @@
     head_gains,
     ffn_weight,
 ):
-    layer_in = per_layer[0].astype(F32)
-    target = teacher[0].astype(F32)
     row_count = tokens.shape[1]
     chips = lax.axis_size("zy")
     seq_count = 2 * chips
@@ -1461,33 +1640,18 @@
     pass_on(6)
     running = stage_end(forward_part(running, here, then))
     own_sum, low_sum = forward_part(running, then, chips, True)
-    down_out, unused = sum_of_four(own_sum, low_sum, 3)
-    after_ffn = mixed + rms_norm(down_out, gains[4])
-    after_low = after_ffn.astype(BF16)
-    pl_raw = full_dot(after_low, plg)
-    pl_act = gelu_tanh(pl_raw)
-    pl_mid = (pl_act * layer_in).astype(BF16)
-    pl_out = full_dot(pl_mid, plp)
-    result = after_ffn + rms_norm(pl_out, gains[5])
-    errors = result - target
-    squares = jnp.sum(weight_mask[:, None] * errors * errors)
-
-    grad_out = weight_mask[:, None] * errors * (total_slots / count)
-    unused, pl_norm_back = jax.vjp(rms_norm, pl_out, gains[5])
-    grad_pl_out, grad_g5 = pl_norm_back(grad_out)
-    grad_pl_low = grad_pl_out.astype(BF16)
-    grad_plp = left_dot(pl_mid, grad_pl_low)
-    grad_pl_mid = right_dot(grad_pl_low, plp)
-    grad_layer_in = grad_pl_mid * pl_act
-    unused, gelu_back = jax.vjp(gelu_tanh, pl_raw)
-    grad_pl_raw = gelu_back(grad_pl_mid * layer_in)[0].astype(BF16)
-    grad_plg = left_dot(after_low, grad_pl_raw)
-    grad_after = grad_out + right_dot(grad_pl_raw, plg)
-    unused, down_norm_back = jax.vjp(rms_norm, down_out, gains[4])
-    grad_down, grad_g4 = down_norm_back(grad_after)
-    grad_down_low = grad_down.astype(BF16)
-
-    grad_down_rows = rows_of_four(grad_down_low, 4)
+    result, grad_after, grad_layer_in, grad_down_rows, grad_plg, grad_plp, late_gains, squares = middle(
+        own_sum,
+        low_sum,
+        mixed,
+        per_layer[0],
+        teacher[0],
+        jnp.broadcast_to(weight_mask[:, None], (row_count, 128)),
+        jnp.broadcast_to(total_slots / count, (8, 128)),
+        gains,
+        plg,
+        plp,
+    )
     grad_gates, grad_uppers = [None] * chips, [None] * chips
 
     def backward_part(steps, running, last=False):
@@ -1591,12 +1755,12 @@
         head_back = head_back.reshape(shards, 2 * head_n)
         head_back = jnp.pad(head_back, ((0, 0), (0, shard_rows - 2 * head_n))).reshape(1, D)
         misc_back = jnp.concatenate(
-            [grad_g0, grad_mid_gains[:3], grad_g4[None], grad_g5[None], head_back, jnp.zeros((1, D), F32)], 0
+            [grad_g0, grad_mid_gains[:3], late_gains[:2], head_back, jnp.zeros((1, D), F32)], 0
         )
         return grad_wkv, grad_tokens, jnp.concatenate(
             [
-                grad_plg.astype(BF16),
-                grad_plp.astype(BF16).reshape(D, proj_cols),
+                grad_plg,
+                grad_plp.reshape(D, proj_cols),
                 grad_lleft[:, :RANK].astype(BF16),
                 jnp.pad(misc_back.T, ((0, 0), (0, misc_cols - 8))).astype(BF16),
                 grad_lright_t.astype(BF16),
@@ -1608,7 +1772,7 @@
     sums_wq, sums_wkv, sums_wo, sums_rest, total, up_in, down_in = sum_all(
         [grad_wq, grad_wkv, grad_wo, rest_back],
         (True, True, True, False),
-        jnp.broadcast_to(squares, (8, 128)),
+        squares,
         up_sum,
         down_sum,
         chips,

time: 943 us -> 911 us (0.966)
  other arithmetic: 58.8 us -> 43 us
    pallas_call x0 -> x1, Pallas kernels: none -> 53.1 us  [middle(): pl.pallas_call(middle_kernel, out_shape=[shape((count, D), F32), shape((c...]
    pallas_call x2 -> x1, Pallas kernels: 67.5 us -> 37.4 us  [sum_of_four(): pl.pallas_call(functools.partial(gather_sum_kernel, steps), out_shape=[ja...]
    pallas_call x2 -> x1, Pallas kernels: 55.4 us -> 27.5 us  [rows_of_four(): pl.pallas_call(spread_kernel, out_shape=jax.ShapeDtypeStruct((4 * count,...]
  transfers between devices with their start and end apart: 34 -> 34, of which waited for: 21 -> 20; matrix products, arithmetic and copies ran while one was open for 6% -> 6% of each run, Pallas kernels for 41% -> 42%
where the time goes in v6:
time: 911 us; the launch traced here: 906 us
  Pallas kernels  599 us (66%)
  waiting for transfers between devices  157 us (17%)
  local copies, waits for them, and re-layouts  52.3 us (6%)
  starting transfers between devices  50.9 us (6%)
  other arithmetic  43 us (5%)
    pallas_call x1, Pallas kernels, sum_all(): pl.pallas_call(functools.partial(sum_kernel, chips, streams, (count, 3, c...  131 us
    pallas_call x1, Pallas kernels, gather_all(): pl.pallas_call(functools.partial(gather_kernel, chips, streams), out_shap...  123 us
    ppermute x26, waiting for transfers between devices, ring(): return lax.ppermute(value, 'zy', ring_pairs(lax.axis_size('zy'), by))  117 us
    pallas_call x3, Pallas kernels, ffn_backward(): piece(functools.partial(ffn_backward_kernel, steps, add, last), 'ffn_back...  62.2 us
    pallas_call x3, Pallas kernels, ffn_forward(): piece(functools.partial(ffn_forward_kernel, steps, add, last), 'ffn_forwa...  55.7 us
    pallas_call x1, Pallas kernels, middle(): pl.pallas_call(middle_kernel, out_shape=[shape((count, D), F32), shape((c...  53.1 us
    ppermute x26, starting transfers between devices, ring(): return lax.ppermute(value, 'zy', ring_pairs(lax.axis_size('zy'), by))  40.7 us
    pallas_call x1, Pallas kernels, sum_of_four(): pl.pallas_call(functools.partial(gather_sum_kernel, steps), out_shape=[ja...  37.4 us
  transfers between devices with their start and end apart: 34, of which 20 were waited for; matrix products, arithmetic and copies ran while one was open for 6% of the time, Pallas kernels for 42%

profile of v6, /device:TPU:0, one launch (start us, length us, event | category | flops | bytes accessed | tf_op | source)
XLA Modules:
  0.0 906.2 jit_solution(7613790196602141568)
XLA Ops:
  0.7 2.2 fusion.12
  2.9 3.0 collective-permute-start.1
  12.8 2.0 concatenate.23.shard
  14.8 122.9 %gather_all.1.weight.w_out.lleft.lright = bf16[2048,5888]{1,0:T(8,128)(2,1)} custom-call(bf16[64,5888]{1,0:T(8,128)(2,1)} %concatenate.23.shard), custom_call_target="tpu_custom_call" | custom-call | bytes 48234496 | tf_op jit(solution)/shard_map/gather_all/pallas_call | solution.py:220
  137.7 2.0 slice.75
  141.6 1.5 collective-permute-start.3
  146.0 13.5 %make_qkv.1 = (bf16[256,2048]{1,0:T(8,128)(2,1)}, f32[256,3072]{1,0:T(8,128)}, bf16[256,3072]{1,0:T(8,128)(2,1)}) custom-call(bf16[256,2048]{1,0:T(8,128)(2,1)} %bitcast.34, f32[8,2048]{1,0:T(8,128)} %pad_convert_fusion.gains, f32[2,256]{1,0:T(2,128)} %reshape.117.head_gain, f32[256,128]{1,0:T(8,128)} %get-tuple-element.397.cosine, ...), custom_call_target="tpu_custom_call" | custom-call | bytes 1024 | tf_op jit(solution)/shard_map/make_qkv/pallas_call | solution.py:590
  159.4 18.5 %collective-permute-done.2.refs_4_.refs_0_ = bf16[3,128,2048]{2,1,0:T(8,128)(2,1)S(1)} collective-permute-done((bf16[3,128,2048]{2,1,0:T(8,128)(2,1)}, bf16[3,128,2048]{2,1,0:T(8,128)(2,1)S(1)}, u32[]{:S(2)}, u32[]{:S(2)}) %collective-permute-start.2) | collective-permute-done | bytes 1572896 | tf_op jit(solution)/shard_map/ppermute | solution.py:57
  178.2 2.3 slice.79
  180.4 4.2 collective-permute-start.7
  188.2 8.3 collective-permute-done.7
  196.5 1.9 broadcast_select_fusion.1
  201.3 1.9 collective-permute-done.9
  203.2 2.4 pad_maximum_fusion.1.key.value
  205.5 16.1 %collective-permute-done.4.refs_6_.refs_2_ = bf16[3,128,2048]{2,1,0:T(8,128)(2,1)} collective-permute-done((bf16[3,128,2048]{2,1,0:T(8,128)(2,1)S(1)}, bf16[3,128,2048]{2,1,0:T(8,128)(2,1)}, u32[]{:S(2)}, u32[]{:S(2)}) %collective-permute-start.4) | collective-permute-done | bytes 1572896 | tf_op jit(solution)/shard_map/ppermute | solution.py:57
  221.7 6.8 collective-permute-done.5.refs_7_.refs_3_
  228.5 2.6 collective-permute-start.11
  232.2 19.5 %attend.1 = (bf16[256,2048]{1,0:T(8,128)(2,1)}, f32[256,2048]{1,0:T(8,128)}, f32[256,2048]{1,0:T(8,128)}, bf16[256,2048]{1,0:T(8,128)(2,1)}, bf16[256,128]{1,0:T(8,128)(2,1)}) custom-call(bf16[256,2048]{1,0:T(8,128)(2,1)} %bitcast.35, f32[8,2048]{1,0:T(8,128)} %pad_convert_fusion.gains, bf16[256,2048]{1,0:T(8,128)(2,1)} %get-tuple-element.194.low, ...), custom_call_target="tpu_custom_call" | custom-call | bytes 1024 | tf_op jit(solution)/shard_map/attend/pallas_call | solution.py:654
  251.7 12.7 %collective-permute-done.10.refs_8_.refs_4_ = bf16[3,128,2048]{2,1,0:T(8,128)(2,1)} collective-permute-done((bf16[3,128,2048]{2,1,0:T(8,128)(2,1)}, bf16[3,128,2048]{2,1,0:T(8,128)(2,1)}, u32[]{:S(2)}, u32[]{:S(2)}) %collective-permute-start.10) | collective-permute-done | bytes 1572896 | tf_op jit(solution)/shard_map/ppermute | solution.py:57
  264.4 8.4 collective-permute-done.11.refs_9_.refs_5_
  273.9 2.5 collective-permute-start.12
  277.4 27.5 %spread_rows.1.refs_12_.refs_3_.rows.refs_2_ = bf16[1024,2048]{1,0:T(8,128)(2,1)} custom-call(bf16[256,2048]{1,0:T(8,128)(2,1)} %get-tuple-element.199.own), custom_call_target="tpu_custom_call" | custom-call | bytes 1024 | tf_op jit(solution)/shard_map/spread_rows/pallas_call | solution.py:1138
  304.9 5.1 collective-permute-done.12.refs_10_.refs_0_
  310.0 3.2 collective-permute-done.13.refs_11_.refs_1_
  313.2 1.7 collective-permute-start.14
  314.9 11.0 %collective-permute-start.15 = (bf16[3,128,2048]{2,1,0:T(8,128)(2,1)S(1)}, bf16[3,128,2048]{2,1,0:T(8,128)(2,1)}, u32[]{:S(2)}, u32[]{:S(2)}) collective-permute-start(bf16[3,128,2048]{2,1,0:T(8,128)(2,1)S(1)} %collective-permute-done.13.refs_11_.refs_1_), channel_id=1, source_target_pairs={{0,4},{8,0},{16,8},{24,16},{28,24},{20,28},{12,20},{4,12},{1,5},{9... | collective-permute-start | bytes 4718600 | tf_op jit(solution)/shard_map/ppermute | solution.py:57
  326.0 30.9 %ffn_forward.3 = (f32[1024,2048]{1,0:T(8,128)}, f32[1024,256]{1,0:T(8,128)}, f32[1024,256]{1,0:T(8,128)}, f32[1024,256]{1,0:T(8,128)}, f32[1024,256]{1,0:T(8,128...) custom-call(bf16[3,128,2048]{2,1,0:T(8,128)(2,1)} %copy-done.1, ...), custom_call_target="tpu_custom_call" | custom-call | bytes 1024 | tf_op jit(solution)/shard_map/ffn_forward/pallas_call | solution.py:771
  356.9 2.7 collective-permute-done.15.refs_1_.refs_3_
  363.0 3.0 fusion.11
  366.0 2.3 reshape.107.proj_w
  369.7 12.4 %ffn_forward.4 = (f32[1024,2048]{1,0:T(8,128)}, f32[1024,256]{1,0:T(8,128)}, f32[1024,256]{1,0:T(8,128)}, bf16[1024,256]{1,0:T(8,128)(2,1)}) custom-call(bf16[3,128,2048]{2,1,0:T(8,128)(2,1)} %collective-permute-done.14.refs_0_.refs_2_, bf16[3,128,2048]{2,1,0:T(8,128)(2,1)} %collective-permute-done.15.refs_1_.refs_3_, ...), custom_call_target="tpu_custom_call" | custom-call | bytes 1024 | tf_op jit(solution)/shard_map/ffn_forward/pallas_call | solution.py:771
  382.1 10.8 %collective-permute-done.16.refs_0_.refs_4_ = bf16[3,128,2048]{2,1,0:T(8,128)(2,1)S(1)} collective-permute-done((bf16[3,128,2048]{2,1,0:T(8,128)(2,1)}, bf16[3,128,2048]{2,1,0:T(8,128)(2,1)S(1)}, u32[]{:S(2)}, u32[]{:S(2)}) %collective-permute-start.16) | collective-permute-done | bytes 1572896 | tf_op jit(solution)/shard_map/ppermute | solution.py:57
  394.9 12.4 %ffn_forward.5 = (f32[512,2048]{1,0:T(8,128)}, bf16[512,2048]{1,0:T(8,128)(2,1)}, f32[1024,256]{1,0:T(8,128)}, f32[1024,256]{1,0:T(8,128)}, bf16[1024,256]{1,0:T(8,128)(2,1)}) custom-call(bf16[3,128,2048]{2,1,0:T(8,128)(2,1)} %copy-done.7, bf16[3,128,2048]{2,1,0:T(8,128)(2,1)} %copy-done.8, f32[1024,2048]{1,0:T(8,128)} %get-tuple-element.210.refs_2_, ...), custom_call_target="tpu_custom_call" | custom-call | bytes 1024 | tf_op jit(solution)/shard_map/ffn_forward/pallas_call | solution.py:771
  408.7 53.1 %middle.1 = (f32[256,2048]{1,0:T(8,128)}, f32[256,2048]{1,0:T(8,128)}, f32[256,256]{1,0:T(8,128)}, bf16[1024,2048]{1,0:T(8,128)(2,1)}, bf16[2048,256]{1,0:T(8,12...) custom-call(f32[512,2048]{1,0:T(8,128)} %get-tuple-element.211.own, ...), custom_call_target="tpu_custom_call" | custom-call | bytes 1024 | tf_op jit(solution)/shard_map/middle/pallas_call | solution.py:1422
  461.8 12.6 %ffn_backward.3 = (f32[1024,2048]{1,0:T(8,128)}, bf16[1024,256]{1,0:T(8,128)(2,1)}, bf16[1024,256]{1,0:T(8,128)(2,1)}) custom-call(bf16[3,128,2048]{2,1,0:T(8,128)(2,1)} %collective-permute-done.refs_2_.refs_0_, bf16[3,128,2048]{2,1,0:T(8,128)(2,1)} %collective-permute-done.1.refs_3_.refs_1_, ...), custom_call_target="tpu_custom_call" | custom-call | bytes 1024 | tf_op jit(solution)/shard_map/ffn_backward/pallas_call | solution.py:817
  474.4 7.5 unit_grads.3
  484.0 22.4 %ffn_backward.4 = (f32[1024,2048]{1,0:T(8,128)}, bf16[1024,256]{1,0:T(8,128)(2,1)}, bf16[1024,256]{1,0:T(8,128)(2,1)}, bf16[1024,256]{1,0:T(8,128)(2,1)}, bf16[1...) custom-call(bf16[3,128,2048]{2,1,0:T(8,128)(2,1)} %copy-done.4, ...), custom_call_target="tpu_custom_call" | custom-call | bytes 1024 | tf_op jit(solution)/shard_map/ffn_backward/pallas_call | solution.py:817
  506.4 7.5 unit_grads.4
  513.8 4.7 collective-permute-done.18
  519.1 2.2 add_convert_fusion.10
  524.1 7.5 unit_grads.5
  531.6 27.2 %ffn_backward.5 = (f32[512,2048]{1,0:T(8,128)}, bf16[512,2048]{1,0:T(8,128)(2,1)}, bf16[1024,256]{1,0:T(8,128)(2,1)}, bf16[1024,256]{1,0:T(8,128)(2,1)}, bf16[10...) custom-call(bf16[3,128,2048]{2,1,0:T(8,128)(2,1)} %copy-done.2, ...), custom_call_target="tpu_custom_call" | custom-call | bytes 1024 | tf_op jit(solution)/shard_map/ffn_backward/pallas_call | solution.py:817
  562.4 37.4 %gather_sum.1 = (f32[256,2048]{1,0:T(8,128)}, bf16[3,128,2048]{2,1,0:T(8,128)(2,1)}, bf16[3,128,2048]{2,1,0:T(8,128)(2,1)}, bf16[3,128,2048]{2,1,0:T(8,128)(2,1)...) custom-call(f32[512,2048]{1,0:T(8,128)} %get-tuple-element.260.refs_, ...), custom_call_target="tpu_custom_call" | custom-call | bytes 1024 | tf_op jit(solution)/shard_map/gather_sum/pallas_call | solution.py:1266
  599.8 3.3 add_convert_fusion.6
  605.9 27.6 %attend_back.1 = (f32[256,2048]{1,0:T(8,128)}, bf16[256,128]{1,0:T(8,128)(2,1)}, f32[8,2048]{1,0:T(8,128)}, f32[2048,128]{1,0:T(8,128)}, f32[2048,128]{1,0:T(8,1...) custom-call(f32[8,2048]{1,0:T(8,128)} %pad_convert_fusion.gains, ...), custom_call_target="tpu_custom_call" | custom-call | bytes 1024 | tf_op jit(solution)/shard_map/attend_back/pallas_call | solution.py:910
  633.5 6.5 collective-permute-done.25
  641.4 1.7 constant_dynamic-update-slice_fusion.1
  644.7 1.8 add_convert_fusion.4
  648.2 1.7 add_convert_fusion.5
  653.5 14.4 %query_back.1 = (bf16[2048,2048]{1,0:T(8,128)(2,1)}, f32[256,2048]{1,0:T(8,128)}, f32[1,256]{1,0:T(1,128)}) custom-call(f32[256,2048]{1,0:T(8,128)} %get-tuple-element.308.grad_query, f32[256,3072]{1,0:T(8,128)} %get-tuple-element.309.raw, f32[256,128]{1,0:T(8,128)} %get-tuple-element.397.cosine, f32[256,128]{1,0:T(8,128)} %get-tuple-element.396.sine, ...), custom_call_target="tpu_custom_call" | custom-call | bytes 1024 | tf_op jit(solution)/shard_map/query_back/pallas_call | solution.py:988
  667.9 29.1 %collective-permute-done.30 = bf16[256,1024]{1,0:T(8,128)(2,1)} collective-permute-done((bf16[256,1024]{1,0:T(8,128)(2,1)S(1)}, bf16[256,1024]{1,0:T(8,128)(2,1)}, u32[]{:S(2)}, u32[]{:S(2)}) %collective-permute-start.30) | collective-permute-done | bytes 524320 | tf_op jit(solution)/shard_map/ppermute | solution.py:1743
  697.0 2.3 fusion.2.grad_kv
  699.3 1.8 add_convert_fusion.2
  701.1 1.7 add_convert_fusion.3
  702.9 2.0 collective-permute-start.32
  708.6 11.8 %key_back.1 = (bf16[2048,1024]{1,0:T(8,128)(2,1)}, f32[256,2048]{1,0:T(8,128)}, f32[1,256]{1,0:T(1,128)}, f32[1,2048]{1,0:T(1,128)}) custom-call(f32[256,1024]{1,0:T(8,128)} %fusion.2.grad_kv, f32[256,3072]{1,0:T(8,128)} %get-tuple-element.309.raw, f32[256,128]{1,0:T(8,128)} %get-tuple-element.397.cosine, f32[256,128]{1,0:T(8,128)} %get-tuple-element.396.sine, ...), custom_call_target="tpu_custom_call" | custom-call | bytes 1024 | tf_op jit(solution)/shard_map/key_back/pallas_call | solution.py:1041
  722.6 5.4 concatenate.28
  728.1 7.9 collective-permute-done.33
  736.0 10.8 %collective-permute-done.32 = bf16[3,128,2048]{2,1,0:T(8,128)(2,1)} collective-permute-done((bf16[3,128,2048]{2,1,0:T(8,128)(2,1)}, bf16[3,128,2048]{2,1,0:T(8,128)(2,1)}, u32[]{:S(2)}, u32[]{:S(2)}) %collective-permute-start.32) | collective-permute-done | bytes 1572896 | tf_op jit(solution)/shard_map/ppermute | solution.py:57
  746.8 3.8 add_convert_fusion.1.refs_5_
  750.6 3.2 add_convert_fusion.refs_6_
  753.8 131.4 %sum_all.1 = (f32[64,2048]{1,0:T(8,128)}, f32[64,1024]{1,0:T(8,128)}, f32[64,2048]{1,0:T(8,128)}, f32[64,768]{1,0:T(8,128)}, f32[8,128]{1,0:T(8,128)}, /*index=5...) custom-call(bf16[8,2,2,64,2048]{4,3,2,1,0:T(8,128)(2,1)} %bitcast.38, bf16[8,2,2,64,1024]{4,3,2,1,0:T(8,128)(2,1)} %bitcast.39, ...), custom_call_target="tpu_custom_call" | custom-call | bytes 24117248 | tf_op jit(solution)/shard_map/sum_all/pallas_call | solution.py:511
  894.3 3.1 add_bitcast_fusion
  897.4 3.1 pad_maximum_fusion
  (180 shorter events, 67.3 us)
Async XLA Ops:
  0.6 5.4 copy-start.32
  0.7 12.1 %copy-start.28 = (bf16[64,2048]{1,0:T(8,128)(2,1)S(1)}, bf16[64,2048]{1,0:T(8,128)(2,1)}, u32[]{:S(2)}) copy-start(bf16[64,2048]{1,0:T(8,128)(2,1)} %param.20) | copy-start | bytes 786436
  0.7 12.1 %copy-start.29 = (bf16[64,1024]{1,0:T(8,128)(2,1)S(1)}, bf16[64,1024]{1,0:T(8,128)(2,1)}, u32[]{:S(2)}) copy-start(bf16[64,1024]{1,0:T(8,128)(2,1)} %param.19) | copy-start | bytes 393220
  2.8 134.9 %copy-start = (bf16[3,128,2048]{2,1,0:T(8,128)(2,1)}, bf16[3,128,2048]{2,1,0:T(8,128)(2,1)S(1)}, u32[]{:S(2)}) copy-start(bf16[3,128,2048]{2,1,0:T(8,128)(2,1)S(1)} %get-tuple-element.390.refs_1_.refs_7_) | copy-start | bytes 4718596
  2.8 134.9 %copy-start.1 = (bf16[3,128,2048]{2,1,0:T(8,128)(2,1)}, bf16[3,128,2048]{2,1,0:T(8,128)(2,1)S(1)}, u32[]{:S(2)}) copy-start(bf16[3,128,2048]{2,1,0:T(8,128)(2,1)S(1)} %get-tuple-element.391.refs_0_.refs_6_) | copy-start | bytes 4718596
  2.9 138.1 %collective-permute-start.1 = (bf16[3,128,2048]{2,1,0:T(8,128)(2,1)S(1)}, bf16[3,128,2048]{2,1,0:T(8,128)(2,1)}, u32[]{:S(2)}, u32[]{:S(2)}) collective-permute-start(bf16[3,128,2048]{2,1,0:T(8,128)(2,1)S(1)} %get-tuple-element.390.refs_1_.refs_7_), channel_id=1, source_target_pairs={{0,4},{8,0},{16,8},{24,16},{28,24},{20,28},{12,20},{4,12},{1,5},{9... | collective-permute-start | bytes 4718600 | tf_op jit(solution)/shard_map/ppermute | solution.py:57
  5.9 135.1 %collective-permute-start = (bf16[3,128,2048]{2,1,0:T(8,128)(2,1)S(1)}, bf16[3,128,2048]{2,1,0:T(8,128)(2,1)}, u32[]{:S(2)}, u32[]{:S(2)}) collective-permute-start(bf16[3,128,2048]{2,1,0:T(8,128)(2,1)S(1)} %get-tuple-element.391.refs_0_.refs_6_), channel_id=1, source_target_pairs={{0,8},{8,16},{16,24},{24,28},{28,20},{20,12},{12,4},{4,0},{1,9},{9... | collective-permute-start | bytes 4718600 | tf_op jit(solution)/shard_map/ppermute | solution.py:57
  141.0 36.9 %collective-permute-start.2 = (bf16[3,128,2048]{2,1,0:T(8,128)(2,1)}, bf16[3,128,2048]{2,1,0:T(8,128)(2,1)S(1)}, u32[]{:S(2)}, u32[]{:S(2)}) collective-permute-start(bf16[3,128,2048]{2,1,0:T(8,128)(2,1)} %collective-permute-done.refs_2_.refs_0_), channel_id=1, source_target_pairs={{0,8},{8,16},{16,24},{24,28},{28,20},{20,12},{12,4},{4,0},{1,9},{9... | collective-permute-start | bytes 4718600 | tf_op jit(solution)/shard_map/ppermute | solution.py:57
  141.6 36.6 %collective-permute-start.3 = (bf16[3,128,2048]{2,1,0:T(8,128)(2,1)}, bf16[3,128,2048]{2,1,0:T(8,128)(2,1)S(1)}, u32[]{:S(2)}, u32[]{:S(2)}) collective-permute-start(bf16[3,128,2048]{2,1,0:T(8,128)(2,1)} %collective-permute-done.1.refs_3_.refs_1_), channel_id=1, source_target_pairs={{0,4},{8,0},{16,8},{24,16},{28,24},{20,28},{12,20},{4,12},{1,5},{9... | collective-permute-start | bytes 4718600 | tf_op jit(solution)/shard_map/ppermute | solution.py:57
  177.9 23.2 %copy-start.4 = (bf16[3,128,2048]{2,1,0:T(8,128)(2,1)}, bf16[3,128,2048]{2,1,0:T(8,128)(2,1)S(1)}, u32[]{:S(2)}) copy-start(bf16[3,128,2048]{2,1,0:T(8,128)(2,1)S(1)} %collective-permute-done.2.refs_4_.refs_0_) | copy-start | bytes 4718596
  178.2 23.0 %copy-start.5 = (bf16[3,128,2048]{2,1,0:T(8,128)(2,1)}, bf16[3,128,2048]{2,1,0:T(8,128)(2,1)S(1)}, u32[]{:S(2)}) copy-start(bf16[3,128,2048]{2,1,0:T(8,128)(2,1)S(1)} %collective-permute-done.3.refs_5_.refs_1_) | copy-start | bytes 4718596
  180.4 16.1 %collective-permute-start.7 = (bf16[256,1024]{1,0:T(8,128)(2,1)}, bf16[256,1024]{1,0:T(8,128)(2,1)}, u32[]{:S(2)}, u32[]{:S(2)}) collective-permute-start(bf16[256,1024]{1,0:T(8,128)(2,1)} %slice.79), channel_id=1, source_target_pairs={{0,4},{4,8},{8,12},{12,20},{1,5},{5,9},{9,13},{13,21},{2,6},{6,10}... | collective-permute-start | bytes 1572872 | tf_op jit(solution)/shard_map/ppermute | solution.py:1593
  184.7 11.8 %collective-permute-start.6 = (bf16[256,1024]{1,0:T(8,128)(2,1)}, bf16[256,1024]{1,0:T(8,128)(2,1)}, u32[]{:S(2)}, u32[]{:S(2)}) collective-permute-start(bf16[256,1024]{1,0:T(8,128)(2,1)} %slice.79), channel_id=1, source_target_pairs={{12,16},{13,17},{14,18},{15,19}} | collective-permute-start | bytes 1572872 | tf_op jit(solution)/shard_map/ppermute | solution.py:1592
  186.1 35.5 %collective-permute-start.4 = (bf16[3,128,2048]{2,1,0:T(8,128)(2,1)S(1)}, bf16[3,128,2048]{2,1,0:T(8,128)(2,1)}, u32[]{:S(2)}, u32[]{:S(2)}) collective-permute-start(bf16[3,128,2048]{2,1,0:T(8,128)(2,1)S(1)} %collective-permute-done.2.refs_4_.refs_0_), channel_id=1, source_target_pairs={{0,8},{8,16},{16,24},{24,28},{28,20},{20,12},{12,4},{4,0},{1,9},{9... | collective-permute-start | bytes 4718600 | tf_op jit(solution)/shard_map/ppermute | solution.py:57
  186.9 41.6 %collective-permute-start.5 = (bf16[3,128,2048]{2,1,0:T(8,128)(2,1)S(1)}, bf16[3,128,2048]{2,1,0:T(8,128)(2,1)}, u32[]{:S(2)}, u32[]{:S(2)}) collective-permute-start(bf16[3,128,2048]{2,1,0:T(8,128)(2,1)S(1)} %collective-permute-done.3.refs_5_.refs_1_), channel_id=1, source_target_pairs={{0,4},{8,0},{16,8},{24,16},{28,24},{20,28},{12,20},{4,12},{1,5},{9... | collective-permute-start | bytes 4718600 | tf_op jit(solution)/shard_map/ppermute | solution.py:57
  198.4 1.5 collective-permute-start.8
  201.2 2.0 collective-permute-start.9
  228.5 35.9 %collective-permute-start.10 = (bf16[3,128,2048]{2,1,0:T(8,128)(2,1)}, bf16[3,128,2048]{2,1,0:T(8,128)(2,1)}, u32[]{:S(2)}, u32[]{:S(2)}) collective-permute-start(bf16[3,128,2048]{2,1,0:T(8,128)(2,1)} %collective-permute-done.4.refs_6_.refs_2_), channel_id=1, source_target_pairs={{0,8},{8,16},{16,24},{24,28},{28,20},{20,12},{12,4},{4,0},{1,9},{9... | collective-permute-start | bytes 4718600 | tf_op jit(solution)/shard_map/ppermute | solution.py:57
  228.5 44.3 %collective-permute-start.11 = (bf16[3,128,2048]{2,1,0:T(8,128)(2,1)}, bf16[3,128,2048]{2,1,0:T(8,128)(2,1)S(1)}, u32[]{:S(2)}, u32[]{:S(2)}) collective-permute-start(bf16[3,128,2048]{2,1,0:T(8,128)(2,1)} %collective-permute-done.5.refs_7_.refs_3_), channel_id=1, source_target_pairs={{0,4},{8,0},{16,8},{24,16},{28,24},{20,28},{12,20},{4,12},{1,5},{9... | collective-permute-start | bytes 4718600 | tf_op jit(solution)/shard_map/ppermute | solution.py:57
  273.9 36.0 %collective-permute-start.12 = (bf16[3,128,2048]{2,1,0:T(8,128)(2,1)}, bf16[3,128,2048]{2,1,0:T(8,128)(2,1)S(1)}, u32[]{:S(2)}, u32[]{:S(2)}) collective-permute-start(bf16[3,128,2048]{2,1,0:T(8,128)(2,1)} %collective-permute-done.10.refs_8_.refs_4_), channel_id=1, source_target_pairs={{0,8},{8,16},{16,24},{24,28},{28,20},{20,12},{12,4},{4,0},{1,9},{9... | collective-permute-start | bytes 4718600 | tf_op jit(solution)/shard_map/ppermute | solution.py:57
  276.4 36.7 %collective-permute-start.13 = (bf16[3,128,2048]{2,1,0:T(8,128)(2,1)}, bf16[3,128,2048]{2,1,0:T(8,128)(2,1)S(1)}, u32[]{:S(2)}, u32[]{:S(2)}) collective-permute-start(bf16[3,128,2048]{2,1,0:T(8,128)(2,1)} %copy-done.6), channel_id=1, source_target_pairs={{0,4},{8,0},{16,8},{24,16},{28,24},{20,28},{12,20},{4,12},{1,5},{9... | collective-permute-start | bytes 4718600 | tf_op jit(solution)/shard_map/ppermute | solution.py:57
  304.9 56.8 %copy-start.30 = (s32[2,4]{1,0:T(2,128)S(1)}, s32[2,4]{1,0:T(2,128)}, u32[]{:S(2)}) copy-start(s32[2,4]{1,0:T(2,128)} %param.17) | copy-start | bytes 100
  310.0 16.0 %copy-start.2 = (bf16[3,128,2048]{2,1,0:T(8,128)(2,1)}, bf16[3,128,2048]{2,1,0:T(8,128)(2,1)S(1)}, u32[]{:S(2)}) copy-start(bf16[3,128,2048]{2,1,0:T(8,128)(2,1)S(1)} %collective-permute-done.12.refs_10_.refs_0_) | copy-start | bytes 4718596
  313.2 12.8 %copy-start.3 = (bf16[3,128,2048]{2,1,0:T(8,128)(2,1)}, bf16[3,128,2048]{2,1,0:T(8,128)(2,1)S(1)}, u32[]{:S(2)}) copy-start(bf16[3,128,2048]{2,1,0:T(8,128)(2,1)S(1)} %collective-permute-done.13.refs_11_.refs_1_) | copy-start | bytes 4718596
  313.2 43.8 %collective-permute-start.14 = (bf16[3,128,2048]{2,1,0:T(8,128)(2,1)S(1)}, bf16[3,128,2048]{2,1,0:T(8,128)(2,1)}, u32[]{:S(2)}, u32[]{:S(2)}) collective-permute-start(bf16[3,128,2048]{2,1,0:T(8,128)(2,1)S(1)} %collective-permute-done.12.refs_10_.refs_0_), channel_id=1, source_target_pairs={{0,8},{8,16},{16,24},{24,28},{28,20},{20,12},{12,4},{4,0},{1,9},{9... | collective-permute-start | bytes 4718600 | tf_op jit(solution)/shard_map/ppermute | solution.py:57
  314.9 44.8 %collective-permute-start.15 = (bf16[3,128,2048]{2,1,0:T(8,128)(2,1)S(1)}, bf16[3,128,2048]{2,1,0:T(8,128)(2,1)}, u32[]{:S(2)}, u32[]{:S(2)}) collective-permute-start(bf16[3,128,2048]{2,1,0:T(8,128)(2,1)S(1)} %collective-permute-done.13.refs_11_.refs_1_), channel_id=1, source_target_pairs={{0,4},{8,0},{16,8},{24,16},{28,24},{20,28},{12,20},{4,12},{1,5},{9... | collective-permute-start | bytes 4718600 | tf_op jit(solution)/shard_map/ppermute | solution.py:57
  359.7 33.2 %collective-permute-start.16 = (bf16[3,128,2048]{2,1,0:T(8,128)(2,1)}, bf16[3,128,2048]{2,1,0:T(8,128)(2,1)S(1)}, u32[]{:S(2)}, u32[]{:S(2)}) collective-permute-start(bf16[3,128,2048]{2,1,0:T(8,128)(2,1)} %collective-permute-done.14.refs_0_.refs_2_), channel_id=1, source_target_pairs={{0,8},{8,16},{16,24},{24,28},{28,20},{20,12},{12,4},{4,0},{1,9},{9... | collective-permute-start | bytes 4718600 | tf_op jit(solution)/shard_map/ppermute | solution.py:57
  360.5 33.3 %collective-permute-start.17 = (bf16[3,128,2048]{2,1,0:T(8,128)(2,1)}, bf16[3,128,2048]{2,1,0:T(8,128)(2,1)S(1)}, u32[]{:S(2)}, u32[]{:S(2)}) collective-permute-start(bf16[3,128,2048]{2,1,0:T(8,128)(2,1)} %collective-permute-done.15.refs_1_.refs_3_), channel_id=1, source_target_pairs={{0,4},{8,0},{16,8},{24,16},{28,24},{20,28},{12,20},{4,12},{1,5},{9... | collective-permute-start | bytes 4718600 | tf_op jit(solution)/shard_map/ppermute | solution.py:57
  481.9 36.6 %collective-permute-start.18 = (bf16[3,128,2048]{2,1,0:T(8,128)(2,1)}, bf16[3,128,2048]{2,1,0:T(8,128)(2,1)S(1)}, u32[]{:S(2)}, u32[]{:S(2)}) collective-permute-start(bf16[3,128,2048]{2,1,0:T(8,128)(2,1)} %get-tuple-element.221), channel_id=1, source_target_pairs={{0,8},{8,16},{16,24},{24,28},{28,20},{20,12},{12,4},{4,0},{1,9},{9... | collective-permute-start | bytes 4718600 | tf_op jit(solution)/shard_map/ppermute | solution.py:57
  482.8 36.4 %collective-permute-start.19 = (bf16[3,128,2048]{2,1,0:T(8,128)(2,1)}, bf16[3,128,2048]{2,1,0:T(8,128)(2,1)S(1)}, u32[]{:S(2)}, u32[]{:S(2)}) collective-permute-start(bf16[3,128,2048]{2,1,0:T(8,128)(2,1)} %get-tuple-element.222), channel_id=1, source_target_pairs={{0,4},{8,0},{16,8},{24,16},{28,24},{20,28},{12,20},{4,12},{1,5},{9... | collective-permute-start | bytes 4718600 | tf_op jit(solution)/shard_map/ppermute | solution.py:57
  519.1 3.5 copy-start.21
  521.3 37.5 %collective-permute-start.21 = (bf16[3,128,2048]{2,1,0:T(8,128)(2,1)S(1)}, bf16[3,128,2048]{2,1,0:T(8,128)(2,1)S(1)}, u32[]{:S(2)}, u32[]{:S(2)}) collective-permute-start(bf16[3,128,2048]{2,1,0:T(8,128)(2,1)S(1)} %add_convert_fusion.10), channel_id=1, source_target_pairs={{0,4},{8,0},{16,8},{24,16},{28,24},{20,28},{12,20},{4,12},{1,5},{9... | collective-permute-start | bytes 4718600 | tf_op jit(solution)/shard_map/ppermute | solution.py:57
  523.2 35.6 %collective-permute-start.20 = (bf16[3,128,2048]{2,1,0:T(8,128)(2,1)S(1)}, bf16[3,128,2048]{2,1,0:T(8,128)(2,1)S(1)}, u32[]{:S(2)}, u32[]{:S(2)}) collective-permute-start(bf16[3,128,2048]{2,1,0:T(8,128)(2,1)S(1)} %add_convert_fusion.11), channel_id=1, source_target_pairs={{0,8},{8,16},{16,24},{24,28},{28,20},{20,12},{12,4},{4,0},{1,9},{9... | collective-permute-start | bytes 4718600 | tf_op jit(solution)/shard_map/ppermute | solution.py:57
  531.6 27.3 %copy-start.20 = (bf16[3,128,2048]{2,1,0:T(8,128)(2,1)S(1)}, bf16[3,128,2048]{2,1,0:T(8,128)(2,1)}, u32[]{:S(2)}) copy-start(bf16[3,128,2048]{2,1,0:T(8,128)(2,1)} %get-tuple-element.259) | copy-start | bytes 4718596
  558.8 1.9 copy-start.18
  559.5 40.3 %collective-permute-start.23 = (bf16[3,128,2048]{2,1,0:T(8,128)(2,1)S(1)}, bf16[3,128,2048]{2,1,0:T(8,128)(2,1)S(1)}, u32[]{:S(2)}, u32[]{:S(2)}) collective-permute-start(bf16[3,128,2048]{2,1,0:T(8,128)(2,1)S(1)} %add_convert_fusion.8), channel_id=1, source_target_pairs={{0,4},{8,0},{16,8},{24,16},{28,24},{20,28},{12,20},{4,12},{1,5},{9... | collective-permute-start | bytes 4718600 | tf_op jit(solution)/shard_map/ppermute | solution.py:57
  561.4 38.4 %collective-permute-start.22 = (bf16[3,128,2048]{2,1,0:T(8,128)(2,1)S(1)}, bf16[3,128,2048]{2,1,0:T(8,128)(2,1)S(1)}, u32[]{:S(2)}, u32[]{:S(2)}) collective-permute-start(bf16[3,128,2048]{2,1,0:T(8,128)(2,1)S(1)} %add_convert_fusion.9), channel_id=1, source_target_pairs={{0,8},{8,16},{16,24},{24,28},{28,20},{20,12},{12,4},{4,0},{1,9},{9... | collective-permute-start | bytes 4718600 | tf_op jit(solution)/shard_map/ppermute | solution.py:57
  599.8 4.6 copy-start.19
  603.2 36.8 %collective-permute-start.25 = (bf16[3,128,2048]{2,1,0:T(8,128)(2,1)}, bf16[3,128,2048]{2,1,0:T(8,128)(2,1)S(1)}, u32[]{:S(2)}, u32[]{:S(2)}) collective-permute-start(bf16[3,128,2048]{2,1,0:T(8,128)(2,1)} %add_convert_fusion.6), channel_id=1, source_target_pairs={{0,4},{8,0},{16,8},{24,16},{28,24},{20,28},{12,20},{4,12},{1,5},{9... | collective-permute-start | bytes 4718600 | tf_op jit(solution)/shard_map/ppermute | solution.py:57
  605.0 36.4 %collective-permute-start.24 = (bf16[3,128,2048]{2,1,0:T(8,128)(2,1)S(1)}, bf16[3,128,2048]{2,1,0:T(8,128)(2,1)S(1)}, u32[]{:S(2)}, u32[]{:S(2)}) collective-permute-start(bf16[3,128,2048]{2,1,0:T(8,128)(2,1)S(1)} %add_convert_fusion.7), channel_id=1, source_target_pairs={{0,8},{8,16},{16,24},{24,28},{28,20},{20,12},{12,4},{4,0},{1,9},{9... | collective-permute-start | bytes 4718600 | tf_op jit(solution)/shard_map/ppermute | solution.py:57
  641.4 1.9 copy-start.12
  643.3 1.4 copy-start.17
  643.5 3.9 collective-permute-start.28
  646.4 1.8 copy-start.16
  646.4 52.9 %collective-permute-start.27 = (bf16[3,128,2048]{2,1,0:T(8,128)(2,1)}, bf16[3,128,2048]{2,1,0:T(8,128)(2,1)S(1)}, u32[]{:S(2)}, u32[]{:S(2)}) collective-permute-start(bf16[3,128,2048]{2,1,0:T(8,128)(2,1)} %add_convert_fusion.4), channel_id=1, source_target_pairs={{0,4},{8,0},{16,8},{24,16},{28,24},{20,28},{12,20},{4,12},{1,5},{9... | collective-permute-start | bytes 4718600 | tf_op jit(solution)/shard_map/ppermute | solution.py:57
  647.5 3.6 collective-permute-start.29
  650.0 49.3 %collective-permute-start.26 = (bf16[3,128,2048]{2,1,0:T(8,128)(2,1)}, bf16[3,128,2048]{2,1,0:T(8,128)(2,1)S(1)}, u32[]{:S(2)}, u32[]{:S(2)}) collective-permute-start(bf16[3,128,2048]{2,1,0:T(8,128)(2,1)} %add_convert_fusion.5), channel_id=1, source_target_pairs={{0,8},{8,16},{16,24},{24,28},{28,20},{20,12},{12,4},{4,0},{1,9},{9... | collective-permute-start | bytes 4718600 | tf_op jit(solution)/shard_map/ppermute | solution.py:57
  651.3 16.6 %collective-permute-start.31 = (bf16[256,1024]{1,0:T(8,128)(2,1)S(1)}, bf16[256,1024]{1,0:T(8,128)(2,1)S(1)}, u32[]{:S(2)}, u32[]{:S(2)}) collective-permute-start(bf16[256,1024]{1,0:T(8,128)(2,1)S(1)} %add_convert_fusion.12), channel_id=1, source_target_pairs={{16,12},{17,13},{18,14},{19,15}} | collective-permute-start | bytes 1572872 | tf_op jit(solution)/shard_map/ppermute | solution.py:1744
  652.0 44.9 %collective-permute-start.30 = (bf16[256,1024]{1,0:T(8,128)(2,1)S(1)}, bf16[256,1024]{1,0:T(8,128)(2,1)}, u32[]{:S(2)}, u32[]{:S(2)}) collective-permute-start(bf16[256,1024]{1,0:T(8,128)(2,1)S(1)} %add_convert_fusion.12), channel_id=1, source_target_pairs={{4,0},{8,4},{12,8},{20,12},{5,1},{9,5},{13,9},{21,13},{6,2},{10,6}... | collective-permute-start | bytes 1572872 | tf_op jit(solution)/shard_map/ppermute | solution.py:1743
  667.9 31.4 %copy-start.15 = (bf16[3,128,2048]{2,1,0:T(8,128)(2,1)S(1)}, bf16[3,128,2048]{2,1,0:T(8,128)(2,1)}, u32[]{:S(2)}) copy-start(bf16[3,128,2048]{2,1,0:T(8,128)(2,1)} %get-tuple-element.317) | copy-start | bytes 4718596
  699.3 1.8 copy-start.14
  701.1 4.6 copy-start.23
  701.1 34.8 %collective-permute-start.33 = (bf16[3,128,2048]{2,1,0:T(8,128)(2,1)}, bf16[3,128,2048]{2,1,0:T(8,128)(2,1)}, u32[]{:S(2)}, u32[]{:S(2)}) collective-permute-start(bf16[3,128,2048]{2,1,0:T(8,128)(2,1)} %add_convert_fusion.2), channel_id=1, source_target_pairs={{0,4},{8,0},{16,8},{24,16},{28,24},{20,28},{12,20},{4,12},{1,5},{9... | collective-permute-start | bytes 4718600 | tf_op jit(solution)/shard_map/ppermute | solution.py:57
  702.9 43.9 %collective-permute-start.32 = (bf16[3,128,2048]{2,1,0:T(8,128)(2,1)}, bf16[3,128,2048]{2,1,0:T(8,128)(2,1)}, u32[]{:S(2)}, u32[]{:S(2)}) collective-permute-start(bf16[3,128,2048]{2,1,0:T(8,128)(2,1)} %add_convert_fusion.3), channel_id=1, source_target_pairs={{0,8},{8,16},{16,24},{24,28},{28,20},{20,12},{12,4},{4,0},{1,9},{9... | collective-permute-start | bytes 4718600 | tf_op jit(solution)/shard_map/ppermute | solution.py:57
  706.3 2.2 copy-start.22
  708.6 12.5 %copy-start.31 = (f32[1,256]{1,0:T(1,128)S(1)}, f32[1,256]{1,0:T(1,128)}, u32[]{:S(2)}) copy-start(f32[1,256]{1,0:T(1,128)} %get-tuple-element.334) | copy-start | bytes 3076
  746.8 3.8 copy-start.13
  753.8 140.5 %copy-start.10 = (bf16[3,128,2048]{2,1,0:T(8,128)(2,1)S(1)}, bf16[3,128,2048]{2,1,0:T(8,128)(2,1)}, u32[]{:S(2)}) copy-start(bf16[3,128,2048]{2,1,0:T(8,128)(2,1)} %get-tuple-element.353) | copy-start | bytes 4718596
  753.8 140.5 %copy-start.11 = (bf16[3,128,2048]{2,1,0:T(8,128)(2,1)S(1)}, bf16[3,128,2048]{2,1,0:T(8,128)(2,1)}, u32[]{:S(2)}) copy-start(bf16[3,128,2048]{2,1,0:T(8,128)(2,1)} %get-tuple-element.355) | copy-start | bytes 4718596
  897.4 3.1 copy-start.9
  900.5 1.3 copy-start.26
  900.5 2.0 copy-start.25
  901.9 1.5 copy-start.27
  901.9 2.2 copy-start.24
  (3 other events, 3.5 us)

commit v7 on v6

--- a/solution.py
+++ b/solution.py
@@ -489,10 +489,11 @@
     rows = arrays[0].shape[0] // (4 * chips)
     streams = []
     for i, (array, first) in enumerate(zip(arrays, firsts)):
-        width = array.shape[1]
-        left = width // 256 * 128
-        streams.append((i, 0, left, 1, first))
-        streams.append((i, left, width - left, -1, first))
+        for low, high, is_first in ((0, first, True), (first, array.shape[1], False)):
+            left = (high - low) // 256 * 128
+            if high > low:
+                streams.append((i, low, left, 1, is_first))
+                streams.append((i, low + left, high - low - left, -1, is_first))
     streams = tuple(sorted(streams, key=lambda stream: stream[4]))
     count, number = len(arrays), len(streams)
     dma = pltpu.SemaphoreType.DMA
@@ -1709,6 +1710,20 @@
         return total
 
     grad_ffn_in = beside(2, work)
+    def work():
+        *out, grad_keys, grad_values = attend_back(
+            gains, grad_ffn_in, grad_after, mixed, attn_raw, laurel_mid, normed_low, full, context_low, qkv, keys_all,
+            visible,
+        )
+        grad_kv = jnp.concatenate([grad_keys, grad_values], 1)
+        grad_before = grad_kv[:row_count]
+        grad_own = grad_kv[2 * row_count :]
+        returned = swap(grad_kv[row_count : 2 * row_count].astype(BF16), "core").astype(F32)
+        grad_own = grad_own + jnp.where(core == 0, returned, 0.0)
+        grad_before = grad_before + jnp.where(core == 0, 0.0, returned)
+        return out, grad_own, grad_before
+
+    out, grad_own, grad_before = beside(3, work)
     (
         grad_scaled,
         grad_mid_low,
@@ -1717,35 +1732,22 @@
         grad_lright_t,
         grad_wo,
         grad_queries,
-        grad_keys,
-        grad_values,
-    ) = beside(
-        3,
-        lambda: attend_back(
-            gains, grad_ffn_in, grad_after, mixed, attn_raw, laurel_mid, normed_low, full, context_low, qkv, keys_all,
-            visible,
-        ),
-    )
+    ) = out
 
     def work():
-        grad_kv = jnp.concatenate([grad_keys, grad_values], 1)
-        grad_before = grad_kv[:row_count]
-        grad_own = grad_kv[2 * row_count :]
-        returned = swap(grad_kv[row_count : 2 * row_count].astype(BF16), "core").astype(F32)
-        grad_own = grad_own + jnp.where(core == 0, returned, 0.0)
-        grad_before = grad_before + jnp.where(core == 0, 0.0, returned)
+        total = grad_before
         for span in reversed(spans):
             back = [(mid + i + span, mid + i) for i in range(min(span, mid - span))]
-            grad_before = grad_before + lax.ppermute(grad_before.astype(BF16), "zy", back).astype(F32)
-        before_low = grad_before.astype(BF16)
-        grad_own = (
+            total = total + lax.ppermute(total.astype(BF16), "zy", back).astype(F32)
+        before_low = total.astype(BF16)
+        return (
             grad_own
             + lax.ppermute(before_low, "zy", [(b, a) for a, b in chain]).astype(F32)
             + lax.ppermute(before_low, "zy", [(mid, mid - 1)]).astype(F32)
-        )
-        return grad_own, query_back(grad_queries, qkv_raw, cosine, sine, head_gain, normed_low, full)
+        ), query_back(grad_queries, qkv_raw, cosine, sine, head_gain, normed_low, full)
 
     grad_own, (grad_wq, grad_normed, grad_hq) = beside(4, work)
+
     def work():
         grad_wkv, grad_tokens, grad_hk, grad_g0 = key_back(
             grad_own, qkv_raw, cosine, sine, head_gain, normed_low, full, grad_normed, grad_scaled, grad_mid_low,
@@ -1771,7 +1773,7 @@
     last_terms, (grad_wkv, grad_tokens, rest_back) = beside(5, lambda: (unit_grads(0), work()))
     sums_wq, sums_wkv, sums_wo, sums_rest, total, up_in, down_in = sum_all(
         [grad_wq, grad_wkv, grad_wo, rest_back],
-        (True, True, True, False),
+        (D, 2 * key_cols, D - 512, 0),
         squares,
         up_sum,
         down_sum,

time: 911 us -> 886 us (0.973)
  waiting for transfers between devices: 157 us -> 145 us
    ppermute x26, waiting for transfers between devices: 117 us -> 105 us  [ring(): return lax.ppermute(value, 'zy', ring_pairs(lax.axis_size('zy'), by))]
  transfers between devices with their start and end apart: 34 -> 34, of which waited for: 20 -> 21; matrix products, arithmetic and copies ran while one was open for 6% -> 6% of each run, Pallas kernels for 42% -> 43%
where the time goes in v7:
time: 886 us; the launch traced here: 882 us
  Pallas kernels  591 us (67%)
  waiting for transfers between devices  145 us (16%)
  starting transfers between devices  51.9 us (6%)
  local copies, waits for them, and re-layouts  51.3 us (6%)
  other arithmetic  39.7 us (4%)
    pallas_call x1, Pallas kernels, gather_all(): pl.pallas_call(functools.partial(gather_kernel, chips, streams), out_shap...  123 us
    pallas_call x1, Pallas kernels, sum_all(): pl.pallas_call(functools.partial(sum_kernel, chips, streams, (count, 3, c...  123 us
    ppermute x26, waiting for transfers between devices, ring(): return lax.ppermute(value, 'zy', ring_pairs(lax.axis_size('zy'), by))  105 us
    pallas_call x3, Pallas kernels, ffn_backward(): piece(functools.partial(ffn_backward_kernel, steps, add, last), 'ffn_back...  62.2 us
    pallas_call x3, Pallas kernels, ffn_forward(): piece(functools.partial(ffn_forward_kernel, steps, add, last), 'ffn_forwa...  55.8 us
    pallas_call x1, Pallas kernels, middle(): pl.pallas_call(middle_kernel, out_shape=[shape((count, D), F32), shape((c...  53.2 us
    ppermute x26, starting transfers between devices, ring(): return lax.ppermute(value, 'zy', ring_pairs(lax.axis_size('zy'), by))  40.9 us
    pallas_call x1, Pallas kernels, sum_of_four(): pl.pallas_call(functools.partial(gather_sum_kernel, steps), out_shape=[ja...  37.4 us
  transfers between devices with their start and end apart: 34, of which 21 were waited for; matrix products, arithmetic and copies ran while one was open for 6% of the time, Pallas kernels for 43%

profile of v7, /device:TPU:0, one launch (start us, length us, event | category | flops | bytes accessed | tf_op | source)
XLA Modules:
  0.0 882.4 jit_solution(8182555675899326329)
XLA Ops:
  0.7 2.2 fusion.9
  2.9 3.0 collective-permute-start.1
  12.8 2.0 concatenate.23.shard
  14.8 122.9 %gather_all.1.weight.w_out.lleft.lright = bf16[2048,5888]{1,0:T(8,128)(2,1)} custom-call(bf16[64,5888]{1,0:T(8,128)(2,1)} %concatenate.23.shard), custom_call_target="tpu_custom_call" | custom-call | bytes 48234496 | tf_op jit(solution)/shard_map/gather_all/pallas_call | solution.py:220
  137.7 2.0 slice.75
  141.6 1.5 collective-permute-start.3
  146.0 13.5 %make_qkv.1 = (bf16[256,2048]{1,0:T(8,128)(2,1)}, f32[256,3072]{1,0:T(8,128)}, bf16[256,3072]{1,0:T(8,128)(2,1)}) custom-call(bf16[256,2048]{1,0:T(8,128)(2,1)} %bitcast.34, f32[8,2048]{1,0:T(8,128)} %pad_convert_fusion.gains, f32[2,256]{1,0:T(2,128)} %reshape.117.head_gain, f32[256,128]{1,0:T(8,128)} %get-tuple-element.399.cosine, ...), custom_call_target="tpu_custom_call" | custom-call | bytes 1024 | tf_op jit(solution)/shard_map/make_qkv/pallas_call | solution.py:591
  159.5 18.5 %collective-permute-done.2.refs_4_.refs_0_ = bf16[3,128,2048]{2,1,0:T(8,128)(2,1)S(1)} collective-permute-done((bf16[3,128,2048]{2,1,0:T(8,128)(2,1)}, bf16[3,128,2048]{2,1,0:T(8,128)(2,1)S(1)}, u32[]{:S(2)}, u32[]{:S(2)}) %collective-permute-start.2) | collective-permute-done | bytes 1572896 | tf_op jit(solution)/shard_map/ppermute | solution.py:57
  178.2 2.3 slice.79
  180.4 4.2 collective-permute-start.7
  188.2 8.4 collective-permute-done.7
  196.5 1.9 broadcast_select_fusion.1
  201.3 1.9 collective-permute-done.9
  203.2 2.4 pad_maximum_fusion.1.key.value
  205.6 16.1 %collective-permute-done.4.refs_6_.refs_2_ = bf16[3,128,2048]{2,1,0:T(8,128)(2,1)} collective-permute-done((bf16[3,128,2048]{2,1,0:T(8,128)(2,1)S(1)}, bf16[3,128,2048]{2,1,0:T(8,128)(2,1)}, u32[]{:S(2)}, u32[]{:S(2)}) %collective-permute-start.4) | collective-permute-done | bytes 1572896 | tf_op jit(solution)/shard_map/ppermute | solution.py:57
  221.6 6.8 collective-permute-done.5.refs_7_.refs_3_
  228.5 2.6 collective-permute-start.11
  232.2 19.5 %attend.1 = (bf16[256,2048]{1,0:T(8,128)(2,1)}, f32[256,2048]{1,0:T(8,128)}, f32[256,2048]{1,0:T(8,128)}, bf16[256,2048]{1,0:T(8,128)(2,1)}, bf16[256,128]{1,0:T(8,128)(2,1)}) custom-call(bf16[256,2048]{1,0:T(8,128)(2,1)} %bitcast.35, f32[8,2048]{1,0:T(8,128)} %pad_convert_fusion.gains, bf16[256,2048]{1,0:T(8,128)(2,1)} %get-tuple-element.194.low, ...), custom_call_target="tpu_custom_call" | custom-call | bytes 1024 | tf_op jit(solution)/shard_map/attend/pallas_call | solution.py:655
  251.7 12.7 %collective-permute-done.10.refs_8_.refs_4_ = bf16[3,128,2048]{2,1,0:T(8,128)(2,1)} collective-permute-done((bf16[3,128,2048]{2,1,0:T(8,128)(2,1)}, bf16[3,128,2048]{2,1,0:T(8,128)(2,1)}, u32[]{:S(2)}, u32[]{:S(2)}) %collective-permute-start.10) | collective-permute-done | bytes 1572896 | tf_op jit(solution)/shard_map/ppermute | solution.py:57
  264.4 8.4 collective-permute-done.11.refs_9_.refs_5_
  274.0 2.5 collective-permute-start.12
  277.4 27.5 %spread_rows.1.refs_12_.refs_3_.rows.refs_2_ = bf16[1024,2048]{1,0:T(8,128)(2,1)} custom-call(bf16[256,2048]{1,0:T(8,128)(2,1)} %get-tuple-element.199.own), custom_call_target="tpu_custom_call" | custom-call | bytes 1024 | tf_op jit(solution)/shard_map/spread_rows/pallas_call | solution.py:1139
  304.9 5.1 collective-permute-done.12.refs_10_.refs_0_
  310.0 3.2 collective-permute-done.13.refs_11_.refs_1_
  313.2 1.7 collective-permute-start.14
  314.9 11.0 %collective-permute-start.15 = (bf16[3,128,2048]{2,1,0:T(8,128)(2,1)S(1)}, bf16[3,128,2048]{2,1,0:T(8,128)(2,1)}, u32[]{:S(2)}, u32[]{:S(2)}) collective-permute-start(bf16[3,128,2048]{2,1,0:T(8,128)(2,1)S(1)} %collective-permute-done.13.refs_11_.refs_1_), channel_id=1, source_target_pairs={{0,4},{8,0},{16,8},{24,16},{28,24},{20,28},{12,20},{4,12},{1,5},{9... | collective-permute-start | bytes 4718600 | tf_op jit(solution)/shard_map/ppermute | solution.py:57
  326.0 31.0 %ffn_forward.3 = (f32[1024,2048]{1,0:T(8,128)}, f32[1024,256]{1,0:T(8,128)}, f32[1024,256]{1,0:T(8,128)}, f32[1024,256]{1,0:T(8,128)}, f32[1024,256]{1,0:T(8,128...) custom-call(bf16[3,128,2048]{2,1,0:T(8,128)(2,1)} %copy-done.1, ...), custom_call_target="tpu_custom_call" | custom-call | bytes 1024 | tf_op jit(solution)/shard_map/ffn_forward/pallas_call | solution.py:772
  357.0 2.7 collective-permute-done.15.refs_1_.refs_3_
  363.0 3.0 fusion.8
  366.0 2.3 reshape.107.proj_w
  369.7 12.4 %ffn_forward.4 = (f32[1024,2048]{1,0:T(8,128)}, f32[1024,256]{1,0:T(8,128)}, f32[1024,256]{1,0:T(8,128)}, bf16[1024,256]{1,0:T(8,128)(2,1)}) custom-call(bf16[3,128,2048]{2,1,0:T(8,128)(2,1)} %collective-permute-done.14.refs_0_.refs_2_, bf16[3,128,2048]{2,1,0:T(8,128)(2,1)} %collective-permute-done.15.refs_1_.refs_3_, ...), custom_call_target="tpu_custom_call" | custom-call | bytes 1024 | tf_op jit(solution)/shard_map/ffn_forward/pallas_call | solution.py:772
  382.1 10.8 %collective-permute-done.16.refs_0_.refs_4_ = bf16[3,128,2048]{2,1,0:T(8,128)(2,1)S(1)} collective-permute-done((bf16[3,128,2048]{2,1,0:T(8,128)(2,1)}, bf16[3,128,2048]{2,1,0:T(8,128)(2,1)S(1)}, u32[]{:S(2)}, u32[]{:S(2)}) %collective-permute-start.16) | collective-permute-done | bytes 1572896 | tf_op jit(solution)/shard_map/ppermute | solution.py:57
  395.0 12.4 %ffn_forward.5 = (f32[512,2048]{1,0:T(8,128)}, bf16[512,2048]{1,0:T(8,128)(2,1)}, f32[1024,256]{1,0:T(8,128)}, f32[1024,256]{1,0:T(8,128)}, bf16[1024,256]{1,0:T(8,128)(2,1)}) custom-call(bf16[3,128,2048]{2,1,0:T(8,128)(2,1)} %copy-done.7, bf16[3,128,2048]{2,1,0:T(8,128)(2,1)} %copy-done.8, f32[1024,2048]{1,0:T(8,128)} %get-tuple-element.210.refs_2_, ...), custom_call_target="tpu_custom_call" | custom-call | bytes 1024 | tf_op jit(solution)/shard_map/ffn_forward/pallas_call | solution.py:772
  408.8 53.2 %middle.1 = (f32[256,2048]{1,0:T(8,128)}, f32[256,2048]{1,0:T(8,128)}, f32[256,256]{1,0:T(8,128)}, bf16[1024,2048]{1,0:T(8,128)(2,1)}, bf16[2048,256]{1,0:T(8,12...) custom-call(f32[512,2048]{1,0:T(8,128)} %get-tuple-element.211.own, ...), custom_call_target="tpu_custom_call" | custom-call | bytes 1024 | tf_op jit(solution)/shard_map/middle/pallas_call | solution.py:1423
  461.9 12.6 %ffn_backward.3 = (f32[1024,2048]{1,0:T(8,128)}, bf16[1024,256]{1,0:T(8,128)(2,1)}, bf16[1024,256]{1,0:T(8,128)(2,1)}) custom-call(bf16[3,128,2048]{2,1,0:T(8,128)(2,1)} %collective-permute-done.refs_2_.refs_0_, bf16[3,128,2048]{2,1,0:T(8,128)(2,1)} %collective-permute-done.1.refs_3_.refs_1_, ...), custom_call_target="tpu_custom_call" | custom-call | bytes 1024 | tf_op jit(solution)/shard_map/ffn_backward/pallas_call | solution.py:818
  474.5 7.5 unit_grads.3
  484.0 22.4 %ffn_backward.4 = (f32[1024,2048]{1,0:T(8,128)}, bf16[1024,256]{1,0:T(8,128)(2,1)}, bf16[1024,256]{1,0:T(8,128)(2,1)}, bf16[1024,256]{1,0:T(8,128)(2,1)}, bf16[1...) custom-call(bf16[3,128,2048]{2,1,0:T(8,128)(2,1)} %copy-done.4, ...), custom_call_target="tpu_custom_call" | custom-call | bytes 1024 | tf_op jit(solution)/shard_map/ffn_backward/pallas_call | solution.py:818
  506.4 7.5 unit_grads.4
  513.9 4.7 collective-permute-done.18
  519.2 2.2 add_convert_fusion.10
  524.1 7.4 unit_grads.5
  531.6 27.2 %ffn_backward.5 = (f32[512,2048]{1,0:T(8,128)}, bf16[512,2048]{1,0:T(8,128)(2,1)}, bf16[1024,256]{1,0:T(8,128)(2,1)}, bf16[1024,256]{1,0:T(8,128)(2,1)}, bf16[10...) custom-call(bf16[3,128,2048]{2,1,0:T(8,128)(2,1)} %copy-done.2, ...), custom_call_target="tpu_custom_call" | custom-call | bytes 1024 | tf_op jit(solution)/shard_map/ffn_backward/pallas_call | solution.py:818
  562.4 37.4 %gather_sum.1 = (f32[256,2048]{1,0:T(8,128)}, bf16[3,128,2048]{2,1,0:T(8,128)(2,1)}, bf16[3,128,2048]{2,1,0:T(8,128)(2,1)}, bf16[3,128,2048]{2,1,0:T(8,128)(2,1)...) custom-call(f32[512,2048]{1,0:T(8,128)} %get-tuple-element.260.refs_, ...), custom_call_target="tpu_custom_call" | custom-call | bytes 1024 | tf_op jit(solution)/shard_map/gather_sum/pallas_call | solution.py:1267
  599.9 2.2 add_convert_fusion.6
  604.8 27.6 %attend_back.1 = (f32[256,2048]{1,0:T(8,128)}, bf16[256,128]{1,0:T(8,128)(2,1)}, f32[8,2048]{1,0:T(8,128)}, f32[2048,128]{1,0:T(8,128)}, f32[2048,128]{1,0:T(8,1...) custom-call(f32[8,2048]{1,0:T(8,128)} %pad_convert_fusion.gains, ...), custom_call_target="tpu_custom_call" | custom-call | bytes 1024 | tf_op jit(solution)/shard_map/attend_back/pallas_call | solution.py:911
  632.4 1.7 constant_dynamic-update-slice_fusion.1
  634.6 1.9 collective-permute-done.26
  636.8 1.9 collective-permute-done.25
  638.7 1.6 collective-permute-done.24
  647.7 14.4 %query_back.1 = (bf16[2048,2048]{1,0:T(8,128)(2,1)}, f32[256,2048]{1,0:T(8,128)}, f32[1,256]{1,0:T(1,128)}) custom-call(f32[256,2048]{1,0:T(8,128)} %get-tuple-element.308.grad_query, f32[256,3072]{1,0:T(8,128)} %get-tuple-element.309.raw, f32[256,128]{1,0:T(8,128)} %get-tuple-element.399.cosine, f32[256,128]{1,0:T(8,128)} %get-tuple-element.398.sine, ...), custom_call_target="tpu_custom_call" | custom-call | bytes 1024 | tf_op jit(solution)/shard_map/query_back/pallas_call | solution.py:989
  662.1 27.9 %collective-permute-done.30 = bf16[256,1024]{1,0:T(8,128)(2,1)} collective-permute-done((bf16[256,1024]{1,0:T(8,128)(2,1)S(1)}, bf16[256,1024]{1,0:T(8,128)(2,1)}, u32[]{:S(2)}, u32[]{:S(2)}) %collective-permute-start.30) | collective-permute-done | bytes 524320 | tf_op jit(solution)/shard_map/ppermute | solution.py:1745
  690.0 2.4 convert_add_fusion.grad_kv
  692.5 1.8 add_convert_fusion.2
  694.4 1.7 add_convert_fusion.3
  696.1 1.9 collective-permute-start.32
  701.7 11.9 %key_back.1 = (bf16[2048,1024]{1,0:T(8,128)(2,1)}, f32[256,2048]{1,0:T(8,128)}, f32[1,256]{1,0:T(1,128)}, f32[1,2048]{1,0:T(1,128)}) custom-call(f32[256,1024]{1,0:T(8,128)} %convert_add_fusion.grad_kv, f32[256,3072]{1,0:T(8,128)} %get-tuple-element.309.raw, f32[256,128]{1,0:T(8,128)} %get-tuple-element.399.cosine, f32[256,128]{1,0:T(8,128)} %get-tuple-element.398.sine, ...), custom_call_target="tpu_custom_call" | custom-call | bytes 1024 | tf_op jit(solution)/shard_map/key_back/pallas_call | solution.py:1042
  715.8 5.4 concatenate.28
  721.2 7.6 collective-permute-done.33
  728.8 2.9 collective-permute-done.32
  731.7 3.8 add_convert_fusion.1.refs_5_
  735.5 3.2 add_convert_fusion.refs_6_
  738.7 122.6 %sum_all.1 = (f32[64,2048]{1,0:T(8,128)}, f32[64,1024]{1,0:T(8,128)}, f32[64,2048]{1,0:T(8,128)}, f32[64,768]{1,0:T(8,128)}, f32[8,128]{1,0:T(8,128)}, /*index=5...) custom-call(bf16[8,2,2,64,2048]{4,3,2,1,0:T(8,128)(2,1)} %bitcast.38, bf16[8,2,2,64,1024]{4,3,2,1,0:T(8,128)(2,1)} %bitcast.39, ...), custom_call_target="tpu_custom_call" | custom-call | bytes 24117248 | tf_op jit(solution)/shard_map/sum_all/pallas_call | solution.py:512
  870.5 3.1 add_bitcast_fusion
  873.6 3.1 pad_maximum_fusion
  (181 shorter events, 67.4 us)
Async XLA Ops:
  0.6 5.4 copy-start.32
  0.7 12.1 %copy-start.28 = (bf16[64,2048]{1,0:T(8,128)(2,1)S(1)}, bf16[64,2048]{1,0:T(8,128)(2,1)}, u32[]{:S(2)}) copy-start(bf16[64,2048]{1,0:T(8,128)(2,1)} %param.20) | copy-start | bytes 786436
  0.7 12.1 %copy-start.29 = (bf16[64,1024]{1,0:T(8,128)(2,1)S(1)}, bf16[64,1024]{1,0:T(8,128)(2,1)}, u32[]{:S(2)}) copy-start(bf16[64,1024]{1,0:T(8,128)(2,1)} %param.19) | copy-start | bytes 393220
  2.8 134.9 %copy-start = (bf16[3,128,2048]{2,1,0:T(8,128)(2,1)}, bf16[3,128,2048]{2,1,0:T(8,128)(2,1)S(1)}, u32[]{:S(2)}) copy-start(bf16[3,128,2048]{2,1,0:T(8,128)(2,1)S(1)} %get-tuple-element.392.refs_1_.refs_7_) | copy-start | bytes 4718596
  2.8 134.9 %copy-start.1 = (bf16[3,128,2048]{2,1,0:T(8,128)(2,1)}, bf16[3,128,2048]{2,1,0:T(8,128)(2,1)S(1)}, u32[]{:S(2)}) copy-start(bf16[3,128,2048]{2,1,0:T(8,128)(2,1)S(1)} %get-tuple-element.393.refs_0_.refs_6_) | copy-start | bytes 4718596
  2.9 138.1 %collective-permute-start.1 = (bf16[3,128,2048]{2,1,0:T(8,128)(2,1)S(1)}, bf16[3,128,2048]{2,1,0:T(8,128)(2,1)}, u32[]{:S(2)}, u32[]{:S(2)}) collective-permute-start(bf16[3,128,2048]{2,1,0:T(8,128)(2,1)S(1)} %get-tuple-element.392.refs_1_.refs_7_), channel_id=1, source_target_pairs={{0,4},{8,0},{16,8},{24,16},{28,24},{20,28},{12,20},{4,12},{1,5},{9... | collective-permute-start | bytes 4718600 | tf_op jit(solution)/shard_map/ppermute | solution.py:57
  5.9 135.1 %collective-permute-start = (bf16[3,128,2048]{2,1,0:T(8,128)(2,1)S(1)}, bf16[3,128,2048]{2,1,0:T(8,128)(2,1)}, u32[]{:S(2)}, u32[]{:S(2)}) collective-permute-start(bf16[3,128,2048]{2,1,0:T(8,128)(2,1)S(1)} %get-tuple-element.393.refs_0_.refs_6_), channel_id=1, source_target_pairs={{0,8},{8,16},{16,24},{24,28},{28,20},{20,12},{12,4},{4,0},{1,9},{9... | collective-permute-start | bytes 4718600 | tf_op jit(solution)/shard_map/ppermute | solution.py:57
  141.0 36.9 %collective-permute-start.2 = (bf16[3,128,2048]{2,1,0:T(8,128)(2,1)}, bf16[3,128,2048]{2,1,0:T(8,128)(2,1)S(1)}, u32[]{:S(2)}, u32[]{:S(2)}) collective-permute-start(bf16[3,128,2048]{2,1,0:T(8,128)(2,1)} %collective-permute-done.refs_2_.refs_0_), channel_id=1, source_target_pairs={{0,8},{8,16},{16,24},{24,28},{28,20},{20,12},{12,4},{4,0},{1,9},{9... | collective-permute-start | bytes 4718600 | tf_op jit(solution)/shard_map/ppermute | solution.py:57
  141.6 36.6 %collective-permute-start.3 = (bf16[3,128,2048]{2,1,0:T(8,128)(2,1)}, bf16[3,128,2048]{2,1,0:T(8,128)(2,1)S(1)}, u32[]{:S(2)}, u32[]{:S(2)}) collective-permute-start(bf16[3,128,2048]{2,1,0:T(8,128)(2,1)} %collective-permute-done.1.refs_3_.refs_1_), channel_id=1, source_target_pairs={{0,4},{8,0},{16,8},{24,16},{28,24},{20,28},{12,20},{4,12},{1,5},{9... | collective-permute-start | bytes 4718600 | tf_op jit(solution)/shard_map/ppermute | solution.py:57
  177.9 23.2 %copy-start.4 = (bf16[3,128,2048]{2,1,0:T(8,128)(2,1)}, bf16[3,128,2048]{2,1,0:T(8,128)(2,1)S(1)}, u32[]{:S(2)}) copy-start(bf16[3,128,2048]{2,1,0:T(8,128)(2,1)S(1)} %collective-permute-done.2.refs_4_.refs_0_) | copy-start | bytes 4718596
  178.2 23.0 %copy-start.5 = (bf16[3,128,2048]{2,1,0:T(8,128)(2,1)}, bf16[3,128,2048]{2,1,0:T(8,128)(2,1)S(1)}, u32[]{:S(2)}) copy-start(bf16[3,128,2048]{2,1,0:T(8,128)(2,1)S(1)} %collective-permute-done.3.refs_5_.refs_1_) | copy-start | bytes 4718596
  180.4 16.1 %collective-permute-start.7 = (bf16[256,1024]{1,0:T(8,128)(2,1)}, bf16[256,1024]{1,0:T(8,128)(2,1)}, u32[]{:S(2)}, u32[]{:S(2)}) collective-permute-start(bf16[256,1024]{1,0:T(8,128)(2,1)} %slice.79), channel_id=1, source_target_pairs={{0,4},{4,8},{8,12},{12,20},{1,5},{5,9},{9,13},{13,21},{2,6},{6,10}... | collective-permute-start | bytes 1572872 | tf_op jit(solution)/shard_map/ppermute | solution.py:1594
  184.7 11.8 %collective-permute-start.6 = (bf16[256,1024]{1,0:T(8,128)(2,1)}, bf16[256,1024]{1,0:T(8,128)(2,1)}, u32[]{:S(2)}, u32[]{:S(2)}) collective-permute-start(bf16[256,1024]{1,0:T(8,128)(2,1)} %slice.79), channel_id=1, source_target_pairs={{12,16},{13,17},{14,18},{15,19}} | collective-permute-start | bytes 1572872 | tf_op jit(solution)/shard_map/ppermute | solution.py:1593
  186.1 35.5 %collective-permute-start.4 = (bf16[3,128,2048]{2,1,0:T(8,128)(2,1)S(1)}, bf16[3,128,2048]{2,1,0:T(8,128)(2,1)}, u32[]{:S(2)}, u32[]{:S(2)}) collective-permute-start(bf16[3,128,2048]{2,1,0:T(8,128)(2,1)S(1)} %collective-permute-done.2.refs_4_.refs_0_), channel_id=1, source_target_pairs={{0,8},{8,16},{16,24},{24,28},{28,20},{20,12},{12,4},{4,0},{1,9},{9... | collective-permute-start | bytes 4718600 | tf_op jit(solution)/shard_map/ppermute | solution.py:57
  186.9 41.6 %collective-permute-start.5 = (bf16[3,128,2048]{2,1,0:T(8,128)(2,1)S(1)}, bf16[3,128,2048]{2,1,0:T(8,128)(2,1)}, u32[]{:S(2)}, u32[]{:S(2)}) collective-permute-start(bf16[3,128,2048]{2,1,0:T(8,128)(2,1)S(1)} %collective-permute-done.3.refs_5_.refs_1_), channel_id=1, source_target_pairs={{0,4},{8,0},{16,8},{24,16},{28,24},{20,28},{12,20},{4,12},{1,5},{9... | collective-permute-start | bytes 4718600 | tf_op jit(solution)/shard_map/ppermute | solution.py:57
  198.4 1.5 collective-permute-start.8
  201.2 2.0 collective-permute-start.9
  228.5 35.9 %collective-permute-start.10 = (bf16[3,128,2048]{2,1,0:T(8,128)(2,1)}, bf16[3,128,2048]{2,1,0:T(8,128)(2,1)}, u32[]{:S(2)}, u32[]{:S(2)}) collective-permute-start(bf16[3,128,2048]{2,1,0:T(8,128)(2,1)} %collective-permute-done.4.refs_6_.refs_2_), channel_id=1, source_target_pairs={{0,8},{8,16},{16,24},{24,28},{28,20},{20,12},{12,4},{4,0},{1,9},{9... | collective-permute-start | bytes 4718600 | tf_op jit(solution)/shard_map/ppermute | solution.py:57
  228.5 44.3 %collective-permute-start.11 = (bf16[3,128,2048]{2,1,0:T(8,128)(2,1)}, bf16[3,128,2048]{2,1,0:T(8,128)(2,1)S(1)}, u32[]{:S(2)}, u32[]{:S(2)}) collective-permute-start(bf16[3,128,2048]{2,1,0:T(8,128)(2,1)} %collective-permute-done.5.refs_7_.refs_3_), channel_id=1, source_target_pairs={{0,4},{8,0},{16,8},{24,16},{28,24},{20,28},{12,20},{4,12},{1,5},{9... | collective-permute-start | bytes 4718600 | tf_op jit(solution)/shard_map/ppermute | solution.py:57
  274.0 36.0 %collective-permute-start.12 = (bf16[3,128,2048]{2,1,0:T(8,128)(2,1)}, bf16[3,128,2048]{2,1,0:T(8,128)(2,1)S(1)}, u32[]{:S(2)}, u32[]{:S(2)}) collective-permute-start(bf16[3,128,2048]{2,1,0:T(8,128)(2,1)} %collective-permute-done.10.refs_8_.refs_4_), channel_id=1, source_target_pairs={{0,8},{8,16},{16,24},{24,28},{28,20},{20,12},{12,4},{4,0},{1,9},{9... | collective-permute-start | bytes 4718600 | tf_op jit(solution)/shard_map/ppermute | solution.py:57
  276.5 36.7 %collective-permute-start.13 = (bf16[3,128,2048]{2,1,0:T(8,128)(2,1)}, bf16[3,128,2048]{2,1,0:T(8,128)(2,1)S(1)}, u32[]{:S(2)}, u32[]{:S(2)}) collective-permute-start(bf16[3,128,2048]{2,1,0:T(8,128)(2,1)} %copy-done.6), channel_id=1, source_target_pairs={{0,4},{8,0},{16,8},{24,16},{28,24},{20,28},{12,20},{4,12},{1,5},{9... | collective-permute-start | bytes 4718600 | tf_op jit(solution)/shard_map/ppermute | solution.py:57
  304.9 56.9 %copy-start.30 = (s32[2,4]{1,0:T(2,128)S(1)}, s32[2,4]{1,0:T(2,128)}, u32[]{:S(2)}) copy-start(s32[2,4]{1,0:T(2,128)} %param.17) | copy-start | bytes 100
  310.0 16.0 %copy-start.2 = (bf16[3,128,2048]{2,1,0:T(8,128)(2,1)}, bf16[3,128,2048]{2,1,0:T(8,128)(2,1)S(1)}, u32[]{:S(2)}) copy-start(bf16[3,128,2048]{2,1,0:T(8,128)(2,1)S(1)} %collective-permute-done.12.refs_10_.refs_0_) | copy-start | bytes 4718596
  313.2 12.8 %copy-start.3 = (bf16[3,128,2048]{2,1,0:T(8,128)(2,1)}, bf16[3,128,2048]{2,1,0:T(8,128)(2,1)S(1)}, u32[]{:S(2)}) copy-start(bf16[3,128,2048]{2,1,0:T(8,128)(2,1)S(1)} %collective-permute-done.13.refs_11_.refs_1_) | copy-start | bytes 4718596
  313.2 43.8 %collective-permute-start.14 = (bf16[3,128,2048]{2,1,0:T(8,128)(2,1)S(1)}, bf16[3,128,2048]{2,1,0:T(8,128)(2,1)}, u32[]{:S(2)}, u32[]{:S(2)}) collective-permute-start(bf16[3,128,2048]{2,1,0:T(8,128)(2,1)S(1)} %collective-permute-done.12.refs_10_.refs_0_), channel_id=1, source_target_pairs={{0,8},{8,16},{16,24},{24,28},{28,20},{20,12},{12,4},{4,0},{1,9},{9... | collective-permute-start | bytes 4718600 | tf_op jit(solution)/shard_map/ppermute | solution.py:57
  314.9 44.8 %collective-permute-start.15 = (bf16[3,128,2048]{2,1,0:T(8,128)(2,1)S(1)}, bf16[3,128,2048]{2,1,0:T(8,128)(2,1)}, u32[]{:S(2)}, u32[]{:S(2)}) collective-permute-start(bf16[3,128,2048]{2,1,0:T(8,128)(2,1)S(1)} %collective-permute-done.13.refs_11_.refs_1_), channel_id=1, source_target_pairs={{0,4},{8,0},{16,8},{24,16},{28,24},{20,28},{12,20},{4,12},{1,5},{9... | collective-permute-start | bytes 4718600 | tf_op jit(solution)/shard_map/ppermute | solution.py:57
  359.7 33.2 %collective-permute-start.16 = (bf16[3,128,2048]{2,1,0:T(8,128)(2,1)}, bf16[3,128,2048]{2,1,0:T(8,128)(2,1)S(1)}, u32[]{:S(2)}, u32[]{:S(2)}) collective-permute-start(bf16[3,128,2048]{2,1,0:T(8,128)(2,1)} %collective-permute-done.14.refs_0_.refs_2_), channel_id=1, source_target_pairs={{0,8},{8,16},{16,24},{24,28},{28,20},{20,12},{12,4},{4,0},{1,9},{9... | collective-permute-start | bytes 4718600 | tf_op jit(solution)/shard_map/ppermute | solution.py:57
  360.5 33.3 %collective-permute-start.17 = (bf16[3,128,2048]{2,1,0:T(8,128)(2,1)}, bf16[3,128,2048]{2,1,0:T(8,128)(2,1)S(1)}, u32[]{:S(2)}, u32[]{:S(2)}) collective-permute-start(bf16[3,128,2048]{2,1,0:T(8,128)(2,1)} %collective-permute-done.15.refs_1_.refs_3_), channel_id=1, source_target_pairs={{0,4},{8,0},{16,8},{24,16},{28,24},{20,28},{12,20},{4,12},{1,5},{9... | collective-permute-start | bytes 4718600 | tf_op jit(solution)/shard_map/ppermute | solution.py:57
  482.0 36.6 %collective-permute-start.18 = (bf16[3,128,2048]{2,1,0:T(8,128)(2,1)}, bf16[3,128,2048]{2,1,0:T(8,128)(2,1)S(1)}, u32[]{:S(2)}, u32[]{:S(2)}) collective-permute-start(bf16[3,128,2048]{2,1,0:T(8,128)(2,1)} %get-tuple-element.221), channel_id=1, source_target_pairs={{0,8},{8,16},{16,24},{24,28},{28,20},{20,12},{12,4},{4,0},{1,9},{9... | collective-permute-start | bytes 4718600 | tf_op jit(solution)/shard_map/ppermute | solution.py:57
  482.8 36.4 %collective-permute-start.19 = (bf16[3,128,2048]{2,1,0:T(8,128)(2,1)}, bf16[3,128,2048]{2,1,0:T(8,128)(2,1)S(1)}, u32[]{:S(2)}, u32[]{:S(2)}) collective-permute-start(bf16[3,128,2048]{2,1,0:T(8,128)(2,1)} %get-tuple-element.222), channel_id=1, source_target_pairs={{0,4},{8,0},{16,8},{24,16},{28,24},{20,28},{12,20},{4,12},{1,5},{9... | collective-permute-start | bytes 4718600 | tf_op jit(solution)/shard_map/ppermute | solution.py:57
  519.2 3.5 copy-start.21
  521.4 37.4 %collective-permute-start.21 = (bf16[3,128,2048]{2,1,0:T(8,128)(2,1)S(1)}, bf16[3,128,2048]{2,1,0:T(8,128)(2,1)S(1)}, u32[]{:S(2)}, u32[]{:S(2)}) collective-permute-start(bf16[3,128,2048]{2,1,0:T(8,128)(2,1)S(1)} %add_convert_fusion.10), channel_id=1, source_target_pairs={{0,4},{8,0},{16,8},{24,16},{28,24},{20,28},{12,20},{4,12},{1,5},{9... | collective-permute-start | bytes 4718600 | tf_op jit(solution)/shard_map/ppermute | solution.py:57
  523.3 35.6 %collective-permute-start.20 = (bf16[3,128,2048]{2,1,0:T(8,128)(2,1)S(1)}, bf16[3,128,2048]{2,1,0:T(8,128)(2,1)S(1)}, u32[]{:S(2)}, u32[]{:S(2)}) collective-permute-start(bf16[3,128,2048]{2,1,0:T(8,128)(2,1)S(1)} %add_convert_fusion.11), channel_id=1, source_target_pairs={{0,8},{8,16},{16,24},{24,28},{28,20},{20,12},{12,4},{4,0},{1,9},{9... | collective-permute-start | bytes 4718600 | tf_op jit(solution)/shard_map/ppermute | solution.py:57
  531.6 27.3 %copy-start.20 = (bf16[3,128,2048]{2,1,0:T(8,128)(2,1)S(1)}, bf16[3,128,2048]{2,1,0:T(8,128)(2,1)}, u32[]{:S(2)}) copy-start(bf16[3,128,2048]{2,1,0:T(8,128)(2,1)} %get-tuple-element.259) | copy-start | bytes 4718596
  558.8 1.9 copy-start.18
  559.5 40.3 %collective-permute-start.23 = (bf16[3,128,2048]{2,1,0:T(8,128)(2,1)S(1)}, bf16[3,128,2048]{2,1,0:T(8,128)(2,1)S(1)}, u32[]{:S(2)}, u32[]{:S(2)}) collective-permute-start(bf16[3,128,2048]{2,1,0:T(8,128)(2,1)S(1)} %add_convert_fusion.8), channel_id=1, source_target_pairs={{0,4},{8,0},{16,8},{24,16},{28,24},{20,28},{12,20},{4,12},{1,5},{9... | collective-permute-start | bytes 4718600 | tf_op jit(solution)/shard_map/ppermute | solution.py:57
  561.4 38.4 %collective-permute-start.22 = (bf16[3,128,2048]{2,1,0:T(8,128)(2,1)S(1)}, bf16[3,128,2048]{2,1,0:T(8,128)(2,1)S(1)}, u32[]{:S(2)}, u32[]{:S(2)}) collective-permute-start(bf16[3,128,2048]{2,1,0:T(8,128)(2,1)S(1)} %add_convert_fusion.9), channel_id=1, source_target_pairs={{0,8},{8,16},{16,24},{24,28},{28,20},{20,12},{12,4},{4,0},{1,9},{9... | collective-permute-start | bytes 4718600 | tf_op jit(solution)/shard_map/ppermute | solution.py:57
  599.8 3.5 copy-start.19
  602.0 36.7 %collective-permute-start.25 = (bf16[3,128,2048]{2,1,0:T(8,128)(2,1)S(1)}, bf16[3,128,2048]{2,1,0:T(8,128)(2,1)S(1)}, u32[]{:S(2)}, u32[]{:S(2)}) collective-permute-start(bf16[3,128,2048]{2,1,0:T(8,128)(2,1)S(1)} %add_convert_fusion.6), channel_id=1, source_target_pairs={{0,4},{8,0},{16,8},{24,16},{28,24},{20,28},{12,20},{4,12},{1,5},{9... | collective-permute-start | bytes 4718600 | tf_op jit(solution)/shard_map/ppermute | solution.py:57
  603.9 36.4 %collective-permute-start.24 = (bf16[3,128,2048]{2,1,0:T(8,128)(2,1)S(1)}, bf16[3,128,2048]{2,1,0:T(8,128)(2,1)S(1)}, u32[]{:S(2)}, u32[]{:S(2)}) collective-permute-start(bf16[3,128,2048]{2,1,0:T(8,128)(2,1)S(1)} %add_convert_fusion.7), channel_id=1, source_target_pairs={{0,8},{8,16},{16,24},{24,28},{28,20},{20,12},{12,4},{4,0},{1,9},{9... | collective-permute-start | bytes 4718600 | tf_op jit(solution)/shard_map/ppermute | solution.py:57
  632.4 1.9 copy-start.12
  634.5 2.0 collective-permute-start.26
  636.8 4.4 copy-start.17
  640.4 2.4 copy-start.16
  640.4 4.2 collective-permute-start.29
  641.8 50.6 %collective-permute-start.28 = (bf16[3,128,2048]{2,1,0:T(8,128)(2,1)S(1)}, bf16[3,128,2048]{2,1,0:T(8,128)(2,1)S(1)}, u32[]{:S(2)}, u32[]{:S(2)}) collective-permute-start(bf16[3,128,2048]{2,1,0:T(8,128)(2,1)S(1)} %add_convert_fusion.4), channel_id=1, source_target_pairs={{0,4},{8,0},{16,8},{24,16},{28,24},{20,28},{12,20},{4,12},{1,5},{9... | collective-permute-start | bytes 4718600 | tf_op jit(solution)/shard_map/ppermute | solution.py:57
  643.4 49.0 %collective-permute-start.27 = (bf16[3,128,2048]{2,1,0:T(8,128)(2,1)S(1)}, bf16[3,128,2048]{2,1,0:T(8,128)(2,1)S(1)}, u32[]{:S(2)}, u32[]{:S(2)}) collective-permute-start(bf16[3,128,2048]{2,1,0:T(8,128)(2,1)S(1)} %add_convert_fusion.5), channel_id=1, source_target_pairs={{0,8},{8,16},{16,24},{24,28},{28,20},{20,12},{12,4},{4,0},{1,9},{9... | collective-permute-start | bytes 4718600 | tf_op jit(solution)/shard_map/ppermute | solution.py:57
  644.7 17.3 %collective-permute-start.31 = (bf16[256,1024]{1,0:T(8,128)(2,1)S(1)}, bf16[256,1024]{1,0:T(8,128)(2,1)}, u32[]{:S(2)}, u32[]{:S(2)}) collective-permute-start(bf16[256,1024]{1,0:T(8,128)(2,1)S(1)} %add_convert_fusion.12), channel_id=1, source_target_pairs={{16,12},{17,13},{18,14},{19,15}} | collective-permute-start | bytes 1572872 | tf_op jit(solution)/shard_map/ppermute | solution.py:1746
  646.2 43.8 %collective-permute-start.30 = (bf16[256,1024]{1,0:T(8,128)(2,1)S(1)}, bf16[256,1024]{1,0:T(8,128)(2,1)}, u32[]{:S(2)}, u32[]{:S(2)}) collective-permute-start(bf16[256,1024]{1,0:T(8,128)(2,1)S(1)} %add_convert_fusion.12), channel_id=1, source_target_pairs={{4,0},{8,4},{12,8},{20,12},{5,1},{9,5},{13,9},{21,13},{6,2},{10,6}... | collective-permute-start | bytes 1572872 | tf_op jit(solution)/shard_map/ppermute | solution.py:1745
  662.0 30.4 %copy-start.15 = (bf16[3,128,2048]{2,1,0:T(8,128)(2,1)S(1)}, bf16[3,128,2048]{2,1,0:T(8,128)(2,1)}, u32[]{:S(2)}) copy-start(bf16[3,128,2048]{2,1,0:T(8,128)(2,1)} %get-tuple-element.317) | copy-start | bytes 4718596
  692.5 1.9 copy-start.14
  694.2 4.6 copy-start.23
  694.2 34.6 %collective-permute-start.33 = (bf16[3,128,2048]{2,1,0:T(8,128)(2,1)}, bf16[3,128,2048]{2,1,0:T(8,128)(2,1)}, u32[]{:S(2)}, u32[]{:S(2)}) collective-permute-start(bf16[3,128,2048]{2,1,0:T(8,128)(2,1)} %add_convert_fusion.2), channel_id=1, source_target_pairs={{0,4},{8,0},{16,8},{24,16},{28,24},{20,28},{12,20},{4,12},{1,5},{9... | collective-permute-start | bytes 4718600 | tf_op jit(solution)/shard_map/ppermute | solution.py:57
  696.1 35.6 %collective-permute-start.32 = (bf16[3,128,2048]{2,1,0:T(8,128)(2,1)}, bf16[3,128,2048]{2,1,0:T(8,128)(2,1)}, u32[]{:S(2)}, u32[]{:S(2)}) collective-permute-start(bf16[3,128,2048]{2,1,0:T(8,128)(2,1)} %add_convert_fusion.3), channel_id=1, source_target_pairs={{0,8},{8,16},{16,24},{24,28},{28,20},{20,12},{12,4},{4,0},{1,9},{9... | collective-permute-start | bytes 4718600 | tf_op jit(solution)/shard_map/ppermute | solution.py:57
  699.4 2.2 copy-start.22
  701.7 12.6 %copy-start.31 = (f32[1,256]{1,0:T(1,128)S(1)}, f32[1,256]{1,0:T(1,128)}, u32[]{:S(2)}) copy-start(f32[1,256]{1,0:T(1,128)} %get-tuple-element.334) | copy-start | bytes 3076
  731.7 3.8 copy-start.13
  738.7 131.8 %copy-start.10 = (bf16[3,128,2048]{2,1,0:T(8,128)(2,1)S(1)}, bf16[3,128,2048]{2,1,0:T(8,128)(2,1)}, u32[]{:S(2)}) copy-start(bf16[3,128,2048]{2,1,0:T(8,128)(2,1)} %get-tuple-element.353) | copy-start | bytes 4718596
  738.7 131.8 %copy-start.11 = (bf16[3,128,2048]{2,1,0:T(8,128)(2,1)S(1)}, bf16[3,128,2048]{2,1,0:T(8,128)(2,1)}, u32[]{:S(2)}) copy-start(bf16[3,128,2048]{2,1,0:T(8,128)(2,1)} %get-tuple-element.355) | copy-start | bytes 4718596
  873.6 3.1 copy-start.9
  876.8 1.3 copy-start.26
  876.8 2.0 copy-start.25
  878.1 1.5 copy-start.27
  878.1 2.2 copy-start.24
  (3 other events, 3.5 us)

commit v8 on v7

--- a/solution.py
+++ b/solution.py
@@ -709,13 +709,11 @@
     return [range(first, min(first + many, steps)) for first in range(0, steps, many)]
 
 
-def ffn_forward_kernel(steps, add, last, *refs):
+def ffn_forward_kernel(steps, add, *refs):
     weights, refs = refs[: 2 * steps], refs[2 * steps :]
     if add:
         before, refs = refs[0], refs[1:]
     rows, total, refs = refs[0], refs[1], refs[2:]
-    if last:
-        low_total, refs = refs[0], refs[1:]
     gates, uppers, hiddens, (held, sems) = refs_of((steps, steps, steps, 2), refs)
     load_weights(weights, held, sems)
     units = held.shape[1] // steps
@@ -733,7 +731,7 @@
             hiddens[step][...] = low[:, own]
         term = full_dot(low, held[2, cut])
         running = term if running is None else running + term
-    write_sum(running, total, low_total if last else None)
+    total[...] = running
 
 
 def write_sum(running, total, low_total):
@@ -763,22 +761,22 @@
     return (lambda i: lax.rem(i + half, blocks)), specs, [((many // 2, D), F32), ((many // 2, D), BF16)]
 
 
-def ffn_forward(rows, before, weights, last):
+def ffn_forward(rows, before, weights):
     many = rows.shape[0]
     steps, units = len(weights) // 2, 2 * weights[0].shape[1]
-    at, sums, sum_shapes = sum_specs(many, last)
-    by_row = lambda width: pl.BlockSpec((ROW_BLOCK, width), lambda i: (at(i), 0))
+    by_row = lambda width: pl.BlockSpec((ROW_BLOCK, width), lambda i: (i, 0))
     add = before is not None
     outs = piece(
-        functools.partial(ffn_forward_kernel, steps, add, last),
+        functools.partial(ffn_forward_kernel, steps, add),
         "ffn_forward",
         (many // ROW_BLOCK,),
         [pl.BlockSpec(memory_space=pl.ANY)] * len(weights) + [by_row(D)] * (1 + add),
-        sums + [by_row(units)] * (3 * steps),
-        sum_shapes + [((many, units), F32)] * (2 * steps) + [((many, units), BF16)] * steps,
+        [by_row(D)] + [by_row(units)] * (3 * steps),
+        [((many, D), F32)] + [((many, units), F32)] * (2 * steps) + [((many, units), BF16)] * steps,
         [pltpu.VMEM((3, steps * units, D), BF16), pltpu.SemaphoreType.DMA((len(weights),))],
     )(*weights, *([before] if add else []), rows)
-    return refs_of((len(sums), steps, steps, steps), outs)
+    (total,), gate, upper, hidden = refs_of((1, steps, steps, steps), outs)
+    return total, gate, upper, hidden
 
 
 def ffn_backward_kernel(steps, add, last, *refs):
@@ -827,6 +825,51 @@
         [pltpu.VMEM((3, steps * units, D), BF16), pltpu.SemaphoreType.DMA((len(weights),))],
     )(*weights, *([before] if add else []), rows, *gates, *uppers)
     return refs_of((len(sums), steps, steps), outs)
+
+
+def first_backward_kernel(
+    up_w, down_w, down_rows, rows, gate, upper, hidden, total, grad_gate, grad_upper, up_out, down_out, held, sums, sems
+):
+    load_weights((up_w, down_w), held, sems)
+    at = pl.program_id(0)
+    unused, act_back = jax.vjp(gated_product, gate[...], upper[...])
+    back_gate, back_upper = act_back(right_dot(down_rows[...], held[2]))
+    low_gate, low_upper = back_gate.astype(BF16), back_upper.astype(BF16)
+    grad_gate[...] = low_gate
+    grad_upper[...] = low_upper
+    total[...] = full_dot(low_gate, held[0]) + full_dot(low_upper, held[1])
+    pairs = ((low_gate, rows), (low_upper, rows), (hidden[...], down_rows))
+
+    @pl.when(at == 0)
+    def _():
+        for kind, (left, right) in enumerate(pairs):
+            sums[kind] = left_dot(left, right[...])
+
+    @pl.when(at > 0)
+    def _():
+        for kind, (left, right) in enumerate(pairs):
+            sums[kind] += left_dot(left, right[...])
+
+    @pl.when(at == pl.num_programs(0) - 1)
+    def _():
+        half = up_out.shape[1]
+        up_out[...] = sums[:, :half].astype(BF16)
+        down_out[...] = sums[:, half:].astype(BF16)
+
+
+def first_backward(down_rows, rows, weights, gate, upper, hidden):
+    many, units = gate.shape
+    by_row = lambda width: pl.BlockSpec((ROW_BLOCK, width), lambda i: (i, 0))
+    part = (3, units // 2, D)
+    return piece(
+        first_backward_kernel,
+        "first_backward",
+        (many // ROW_BLOCK,),
+        [pl.BlockSpec(memory_space=pl.ANY)] * 2 + [by_row(D)] * 2 + [by_row(units)] * 3,
+        [by_row(D)] + [by_row(units)] * 2 + [whole(part)] * 2,
+        [((many, D), F32)] + [((many, units), BF16)] * 2 + [(part, BF16)] * 2,
+        [pltpu.VMEM((3, units, D), BF16), pltpu.VMEM((3, units, D), F32), pltpu.SemaphoreType.DMA((2,))],
+    )(*weights, down_rows, rows, gate, upper, hidden)
 
 
 def unit_grads_kernel(grad_gate, grad_upper, hidden, rows, down_rows, up_out, down_out):
@@ -1282,13 +1325,19 @@
 PARTS = 4
 
 
-def middle_kernel(
-    own, low, mixed, layer_in, teacher, mask, scale, gains, gate_w, proj_w,
-    result, grad_after, grad_layer, rows, grad_gate_w, grad_proj_w, grad_gains, squares,
-    own_in, mixed_in, teacher_in, gate_in, proj_in, core_in, pair_low, x_in,
-    result_out, after_out, after_low, mid_low, grad_pl, grad_raw, grad_low,
-    loads, stores, core_send, core_recv, x_send, x_recv, y_send, y_recv, near_send, near_recv, far_send, far_recv,
-):
+def middle_kernel(steps, *refs):
+    weights, inputs, outs, unit_outs, scratch, unit_scratch, sems = refs_of((2 * steps, 10, 8, 3 * steps, 15, 6, 14), refs)
+    before, ffn_rows, mixed, layer_in, teacher, mask, scale, gains, gate_w, proj_w = inputs
+    result, grad_after, grad_layer, rows, grad_gate_w, grad_proj_w, grad_gains, squares = outs
+    (
+        own_in, mixed_in, teacher_in, gate_in, proj_in, core_in, pair_low, x_in,
+        result_out, after_out, after_low, mid_low, grad_pl, grad_raw, grad_low,
+    ) = scratch
+    rows_in, held, low, *unit_sides = unit_scratch
+    (
+        loads, stores, core_send, core_recv, x_send, x_recv, y_send, y_recv, near_send, near_recv, far_send, far_recv,
+        unit_loads, unit_stores,
+    ) = sems
     count = mixed.shape[0]
     cut = count // PARTS
     other_core, other_side = partners()
@@ -1296,17 +1345,44 @@
     def load(number, src, dst):
         return pltpu.make_async_copy(src, dst, loads.at[number])
 
+    units = held.shape[1] // steps
+    weight_loads = [
+        pltpu.make_async_copy(ref, held.at[:, pl.ds(at * units // 2, units // 2)], unit_loads.at[at])
+        for at, ref in enumerate(weights)
+    ]
+    block_loads = [
+        [
+            load(2 * block, ffn_rows.at[pl.ds(block * count, count)], rows_in.at[pl.ds(block * count, count)]),
+            load(2 * block + 1, before.at[pl.ds(block * count, count)], own_in.at[pl.ds(block * count, count)]),
+        ]
+        for block in range(4)
+    ]
     incoming = [
-        load(0, own.at[pl.ds(count, count)], own_in.at[pl.ds(count, count)]),
-        load(1, own.at[pl.ds(0, count)], own_in.at[pl.ds(0, count)]),
-        load(2, mixed, mixed_in),
-        load(3, gate_w, gate_in),
-        load(4, proj_w, proj_in),
-        load(5, teacher, teacher_in),
+        load(8, mixed, mixed_in),
+        load(9, gate_w, gate_in),
+        load(10, proj_w, proj_in),
+        load(11, teacher, teacher_in),
     ]
-    for one in incoming:
+    for one in weight_loads + block_loads[3] + block_loads[1] + block_loads[2] + block_loads[0] + incoming:
         one.start()
     greet((other_core, other_side))
+
+    def forward_block(block):
+        here = slice(block * count, (block + 1) * count)
+        for one in block_loads[block]:
+            one.wait()
+        gate = right_dot(rows_in[here], held[0])
+        upper = right_dot(rows_in[here], held[1])
+        hidden = gated_product(gate, upper).astype(BF16)
+        for side, values in zip(unit_sides, (gate, upper, hidden)):
+            for step in range(steps):
+                side[step, here] = values[:, step * units : (step + 1) * units]
+        return own_in[here] + full_dot(hidden, held[2])
+
+    def unit_store(kind, step):
+        return pltpu.make_async_copy(
+            unit_sides[kind].at[step], unit_outs[kind * steps + step], unit_stores.at[kind * steps + step]
+        )
 
     def remote(src, dst, send, recv, peer):
         return pltpu.make_async_remote_copy(
@@ -1342,16 +1418,25 @@
         src, dst = ((result_out, result), (after_out, grad_after), (grad_low, rows))[number]
         return pltpu.make_async_copy(src.at[here], dst.at[here], stores.at[number, at])
 
-    for block in (1, 0):
-        for at in range(PARTS):
-            core_copy(block, at).start()
-    incoming[0].wait()
+    for one in weight_loads:
+        one.wait()
+    low[count:] = forward_block(3).astype(BF16)
+    for at in range(PARTS):
+        core_copy(1, at).start()
+    own_in[count : 2 * count] = forward_block(1)
     for at in range(PARTS):
         there = pl.ds(count + at * cut, cut)
         core_copy(1, at).wait_recv()
         pair_low[piece_of(at)] = (own_in[there] + core_in[there].astype(F32)).astype(BF16)
         x_copy(at).start()
-    for one in incoming[1:]:
+    low[:count] = forward_block(2).astype(BF16)
+    for at in range(PARTS):
+        core_copy(0, at).start()
+    own_in[:count] = forward_block(0)
+    for kind in range(3):
+        for step in range(steps):
+            unit_store(kind, step).start()
+    for one in incoming:
         one.wait()
     gain_4, gain_5 = gains[4:5], gains[5:6]
     total = jnp.zeros((), F32)
@@ -1413,15 +1498,20 @@
             core_copy(block, at).wait_send()
         for number in range(3):
             kept(number, at).wait()
-
-
-def middle(own, low, mixed, layer_in, teacher, mask, scale, gains, gate_w, proj_w):
+    for kind in range(3):
+        for step in range(steps):
+            unit_store(kind, step).wait()
+
+
+def middle(weights, before, ffn_rows, mixed, layer_in, teacher, mask, scale, gains, gate_w, proj_w):
     count = mixed.shape[0]
+    steps, units = len(weights) // 2, 2 * weights[0].shape[1]
+    sides = [(4 * count, units)] * steps
     dma, vmem = pltpu.SemaphoreType.DMA, pltpu.VMEM
     anywhere, inside = pl.BlockSpec(memory_space=pl.ANY), pl.BlockSpec(memory_space=pltpu.VMEM)
     shape = jax.ShapeDtypeStruct
-    return pl.pallas_call(
-        middle_kernel,
+    outs = pl.pallas_call(
+        functools.partial(middle_kernel, steps),
         out_shape=[
             shape((count, D), F32),
             shape((count, D), F32),
@@ -1431,11 +1521,13 @@
             shape((PLD, D), BF16),
             shape((8, D), F32),
             shape((8, 128), F32),
-        ],
-        in_specs=[anywhere, anywhere, anywhere, inside, anywhere, inside, inside, inside, anywhere, anywhere],
-        out_specs=[anywhere, anywhere, inside, anywhere, inside, inside, inside, inside],
+        ]
+        + [shape(side, F32) for side in sides * 2]
+        + [shape(side, BF16) for side in sides],
+        in_specs=[anywhere] * (2 * steps) + [anywhere, anywhere, anywhere, inside, anywhere, inside, inside, inside, anywhere, anywhere],
+        out_specs=[anywhere, anywhere, inside, anywhere, inside, inside, inside, inside] + [anywhere] * (3 * steps),
         scratch_shapes=[
-            vmem((2 * count, D), F32),
+            vmem((4 * count, D), F32),
             vmem((count, D), F32),
             vmem((count, D), BF16),
             vmem((D, PLD), BF16),
@@ -1450,18 +1542,26 @@
             vmem((count, D), BF16),
             vmem((count, PLD), BF16),
             vmem((count, D), BF16),
-            dma((6,)),
+            vmem((4 * count, D), BF16),
+            vmem((3, steps * units, D), BF16),
+            vmem((2 * count, D), BF16),
+            vmem((steps, 4 * count, units), F32),
+            vmem((steps, 4 * count, units), F32),
+            vmem((steps, 4 * count, units), BF16),
+            dma((12,)),
             dma((3, PARTS)),
             dma((2 * PARTS,)),
             dma((2 * PARTS,)),
         ]
-        + [dma((PARTS,)) for _ in range(8)],
+        + [dma((PARTS,)) for _ in range(8)]
+        + [dma((2 * steps,)), dma((3 * steps,))],
         compiler_params=pltpu.CompilerParams(
             collective_id=3, has_side_effects=True, vmem_limit_bytes=VMEM_LIMIT
         ),
         cost_estimate=LITTLE,
         name="middle",
-    )(own, low, mixed, layer_in, teacher, mask, scale, gains, gate_w, proj_w)
+    )(*weights, before, ffn_rows, mixed, layer_in, teacher, mask, scale, gains, gate_w, proj_w)
+    return refs_of((8, steps, steps, steps), outs)
 
 
 def body(
@@ -1629,21 +1729,21 @@
     def weights_of(steps):
         return [w for k in steps for w in (ups[k], downs[k])]
 
-    def forward_part(running, first, end, last=False):
-        sums, gate, upper, hidden = ffn_forward(ffn_rows, running, weights_of(range(first, end)), last)
+    def forward_part(running, first, end):
+        running, gate, upper, hidden = ffn_forward(ffn_rows, running, weights_of(range(first, end)))
         gates.extend(gate)
         uppers.extend(upper)
         hiddens.extend(hidden)
-        return sums if last else sums[0]
+        return running
 
     running = stage_end(forward_part(None, 0, here))
     then = len(ups)
     pass_on(6)
     running = stage_end(forward_part(running, here, then))
-    own_sum, low_sum = forward_part(running, then, chips, True)
-    result, grad_after, grad_layer_in, grad_down_rows, grad_plg, grad_plp, late_gains, squares = middle(
-        own_sum,
-        low_sum,
+    outs, gate, upper, hidden = middle(
+        weights_of(range(then, chips)),
+        running,
+        ffn_rows,
         mixed,
         per_layer[0],
         teacher[0],
@@ -1653,6 +1753,10 @@
         plg,
         plp,
     )
+    result, grad_after, grad_layer_in, grad_down_rows, grad_plg, grad_plp, late_gains, squares = outs
+    gates.extend(gate)
+    uppers.extend(upper)
+    hiddens.extend(hidden)
     grad_gates, grad_uppers = [None] * chips, [None] * chips
 
     def backward_part(steps, running, last=False):
@@ -1691,8 +1795,14 @@
 
     first = ring_steps[0]
     then = first + 1 + ring_steps[0] + ring_steps[1]
-    running = backward_part(order[:first], None)
-    up_sum, down_sum = unit_grads(order[0])
+    if first == 1 and units % 128 == 0:
+        k = order[0]
+        running, grad_gates[k], grad_uppers[k], up_sum, down_sum = first_backward(
+            grad_down_rows, ffn_rows, weights_of([k]), gates[k], uppers[k], hiddens[k]
+        )
+    else:
+        running = backward_part(order[:first], None)
+        up_sum, down_sum = unit_grads(order[0])
     running = beside(0, lambda: backward_part(order[first:then], running))
     own_sum, low_sum = beside(1, lambda: backward_part(order[then:], running, True))
 

time: 886 us -> 872 us (0.984)
  starting transfers between devices: 51.9 us -> 41.8 us
    pallas_call x4, Pallas kernels: 109 us -> 122 us  [the longest x1 60.6 us: middle(): pl.pallas_call(functools.partial(middle_kernel, steps), out_shape=[shape(...]
    pallas_call x3 -> x2, Pallas kernels: 62.2 us -> 49.6 us  [ffn_backward(): piece(functools.partial(ffn_backward_kernel, steps, add, last), 'ffn_back...]
    ppermute x26, starting transfers between devices: 40.9 us -> 30.7 us  [ring(): return lax.ppermute(value, 'zy', ring_pairs(lax.axis_size('zy'), by))]
    pallas_call x3 -> x2, Pallas kernels: 22.5 us -> 15 us  [unit_grads_of(): piece(unit_grads_kernel, 'unit_grads', (D // width,), [narrow, narrow, na...]
  transfers between devices with their start and end apart: 34 -> 34, of which waited for: 21 -> 22; matrix products, arithmetic and copies ran while one was open for 6% -> 6% of each run, Pallas kernels for 43% -> 44%
where the time goes in v8:
time: 872 us; the launch traced here: 863 us
  Pallas kernels  583 us (67%)
  waiting for transfers between devices  144 us (17%)
  local copies, waits for them, and re-layouts  50.1 us (6%)
  starting transfers between devices  41.8 us (5%)
  other arithmetic  39.6 us (5%)
    pallas_call x1, Pallas kernels, gather_all(): pl.pallas_call(functools.partial(gather_kernel, chips, streams), out_shap...  123 us
    pallas_call x1, Pallas kernels, sum_all(): pl.pallas_call(functools.partial(sum_kernel, chips, streams, (count, 3, c...  122 us
    ppermute x26, waiting for transfers between devices, ring(): return lax.ppermute(value, 'zy', ring_pairs(lax.axis_size('zy'), by))  104 us
    pallas_call x1, Pallas kernels, middle(): pl.pallas_call(functools.partial(middle_kernel, steps), out_shape=[shape(...  60.6 us
    pallas_call x2, Pallas kernels, ffn_backward(): piece(functools.partial(ffn_backward_kernel, steps, add, last), 'ffn_back...  49.6 us
    pallas_call x2, Pallas kernels, ffn_forward(): piece(functools.partial(ffn_forward_kernel, steps, add), 'ffn_forward', (...  43.6 us
    pallas_call x1, Pallas kernels, sum_of_four(): pl.pallas_call(functools.partial(gather_sum_kernel, steps), out_shape=[ja...  36.8 us
    ppermute x26, starting transfers between devices, ring(): return lax.ppermute(value, 'zy', ring_pairs(lax.axis_size('zy'), by))  30.7 us
  transfers between devices with their start and end apart: 34, of which 22 were waited for; matrix products, arithmetic and copies ran while one was open for 6% of the time, Pallas kernels for 44%

profile of v8, /device:TPU:0, one launch (start us, length us, event | category | flops | bytes accessed | tf_op | source)
XLA Modules:
  0.0 863.1 jit_solution(5159059951011698429)
XLA Ops:
  0.7 2.2 fusion.9
  2.9 3.0 collective-permute-start.1
  12.8 2.0 concatenate.23.shard
  14.8 122.9 %gather_all.1.weight.w_out.lleft.lright = bf16[2048,5888]{1,0:T(8,128)(2,1)} custom-call(bf16[64,5888]{1,0:T(8,128)(2,1)} %concatenate.23.shard), custom_call_target="tpu_custom_call" | custom-call | bytes 48234496 | tf_op jit(solution)/shard_map/gather_all/pallas_call | solution.py:220
  137.7 2.0 slice.75
  141.6 1.5 collective-permute-start.3
  146.0 13.5 %make_qkv.1 = (bf16[256,2048]{1,0:T(8,128)(2,1)}, f32[256,3072]{1,0:T(8,128)}, bf16[256,3072]{1,0:T(8,128)(2,1)}) custom-call(bf16[256,2048]{1,0:T(8,128)(2,1)} %bitcast.34, f32[8,2048]{1,0:T(8,128)} %pad_convert_fusion.gains.refs_9_, f32[2,256]{1,0:T(2,128)} %reshape.117.head_gain, f32[256,128]{1,0:T(8,128)} %get-tuple-element.391.cosine, ...), custom_call_target="tpu_custom_call" | custom-call | bytes 1024 | tf_op jit(solution)/shard_map/make_qkv/pallas_call | solution.py:591
  159.4 18.5 %collective-permute-done.2.refs_4_.refs_0_ = bf16[3,128,2048]{2,1,0:T(8,128)(2,1)S(1)} collective-permute-done((bf16[3,128,2048]{2,1,0:T(8,128)(2,1)}, bf16[3,128,2048]{2,1,0:T(8,128)(2,1)S(1)}, u32[]{:S(2)}, u32[]{:S(2)}) %collective-permute-start.2) | collective-permute-done | bytes 1572896 | tf_op jit(solution)/shard_map/ppermute | solution.py:57
  178.2 2.3 slice.79
  180.4 4.2 collective-permute-start.7
  184.6 1.4 collective-permute-start.6
  188.1 8.4 collective-permute-done.7
  196.5 1.9 broadcast_select_fusion.1
  201.3 1.9 collective-permute-done.9
  203.2 2.3 pad_maximum_fusion.1.key.value
  205.5 16.1 %collective-permute-done.4.refs_6_.refs_2_ = bf16[3,128,2048]{2,1,0:T(8,128)(2,1)} collective-permute-done((bf16[3,128,2048]{2,1,0:T(8,128)(2,1)S(1)}, bf16[3,128,2048]{2,1,0:T(8,128)(2,1)}, u32[]{:S(2)}, u32[]{:S(2)}) %collective-permute-start.4) | collective-permute-done | bytes 1572896 | tf_op jit(solution)/shard_map/ppermute | solution.py:57
  221.6 6.9 collective-permute-done.5.refs_7_.refs_3_
  228.5 2.6 collective-permute-start.11
  232.3 19.5 %attend.1 = (bf16[256,2048]{1,0:T(8,128)(2,1)}, f32[256,2048]{1,0:T(8,128)}, f32[256,2048]{1,0:T(8,128)}, bf16[256,2048]{1,0:T(8,128)(2,1)}, bf16[256,128]{1,0:T(8,128)(2,1)}) custom-call(bf16[256,2048]{1,0:T(8,128)(2,1)} %bitcast.35, f32[8,2048]{1,0:T(8,128)} %pad_convert_fusion.gains.refs_9_, bf16[256,2048]{1,0:T(8,128)(2,1)} %get-tuple-element.190.low, ...), custom_call_target="tpu_custom_call" | custom-call | bytes 1024 | tf_op jit(solution)/shard_map/attend/pallas_call | solution.py:655
  251.8 12.6 %collective-permute-done.10.refs_8_.refs_4_ = bf16[3,128,2048]{2,1,0:T(8,128)(2,1)} collective-permute-done((bf16[3,128,2048]{2,1,0:T(8,128)(2,1)}, bf16[3,128,2048]{2,1,0:T(8,128)(2,1)}, u32[]{:S(2)}, u32[]{:S(2)}) %collective-permute-start.10) | collective-permute-done | bytes 1572896 | tf_op jit(solution)/shard_map/ppermute | solution.py:57
  264.4 8.3 collective-permute-done.11.refs_9_.refs_5_
  273.8 2.5 collective-permute-start.12
  277.4 27.5 %spread_rows.1.refs_12_.refs_3_.rows.refs_2_ = bf16[1024,2048]{1,0:T(8,128)(2,1)} custom-call(bf16[256,2048]{1,0:T(8,128)(2,1)} %get-tuple-element.195.own), custom_call_target="tpu_custom_call" | custom-call | bytes 1024 | tf_op jit(solution)/shard_map/spread_rows/pallas_call | solution.py:1182
  304.8 5.1 collective-permute-done.12.refs_10_.refs_0_
  310.0 3.1 collective-permute-done.13.refs_11_.refs_1_
  313.0 1.7 collective-permute-start.14
  315.5 31.0 %ffn_forward.2 = (f32[1024,2048]{1,0:T(8,128)}, f32[1024,256]{1,0:T(8,128)}, f32[1024,256]{1,0:T(8,128)}, f32[1024,256]{1,0:T(8,128)}, f32[1024,256]{1,0:T(8,128...) custom-call(bf16[3,128,2048]{2,1,0:T(8,128)(2,1)} %copy-done.1, ...), custom_call_target="tpu_custom_call" | custom-call | bytes 1024 | tf_op jit(solution)/shard_map/ffn_forward/pallas_call | solution.py:769
  352.5 3.0 fusion.8
  355.5 2.4 reshape.107.refs_11_
  359.2 12.6 %ffn_forward.3 = (f32[1024,2048]{1,0:T(8,128)}, f32[1024,256]{1,0:T(8,128)}, f32[1024,256]{1,0:T(8,128)}, bf16[1024,256]{1,0:T(8,128)(2,1)}) custom-call(bf16[3,128,2048]{2,1,0:T(8,128)(2,1)} %collective-permute-done.14.refs_0_.refs_2_, bf16[3,128,2048]{2,1,0:T(8,128)(2,1)} %collective-permute-done.15.refs_1_.refs_3_, ...), custom_call_target="tpu_custom_call" | custom-call | bytes 1024 | tf_op jit(solution)/shard_map/ffn_forward/pallas_call | solution.py:769
  371.8 10.5 %collective-permute-done.16.refs_0_.refs_4_ = bf16[3,128,2048]{2,1,0:T(8,128)(2,1)S(1)} collective-permute-done((bf16[3,128,2048]{2,1,0:T(8,128)(2,1)}, bf16[3,128,2048]{2,1,0:T(8,128)(2,1)S(1)}, u32[]{:S(2)}, u32[]{:S(2)}) %collective-permute-start.16) | collective-permute-done | bytes 1572896 | tf_op jit(solution)/shard_map/ppermute | solution.py:57
  384.6 60.6 %middle.1 = (f32[256,2048]{1,0:T(8,128)}, f32[256,2048]{1,0:T(8,128)}, f32[256,256]{1,0:T(8,128)}, bf16[1024,2048]{1,0:T(8,128)(2,1)}, bf16[2048,256]{1,0:T(8,12...) custom-call(bf16[3,128,2048]{2,1,0:T(8,128)(2,1)} %copy-done.4, ...), custom_call_target="tpu_custom_call" | custom-call | bytes 1024 | tf_op jit(solution)/shard_map/middle/pallas_call | solution.py:1513
  445.2 18.1 %first_backward.1 = (f32[1024,2048]{1,0:T(8,128)}, bf16[1024,256]{1,0:T(8,128)(2,1)}, bf16[1024,256]{1,0:T(8,128)(2,1)}, bf16[3,128,2048]{2,1,0:T(8,128)(2,1)}, bf16[3,128,2048]{2,1,0:T(8,128)(2,1)}) custom-call(bf16[3,128,2048]{2,1,0:T(8,128)(2,1)} %collective-permute-done.refs_2_.up_w, bf16[3,128,2048]{2,1,0:T(8,128)(2,1)} %collective-permute-done.1.refs_3_.down_w, ...), custom_call_target="tpu_custom_call" | custom-call | bytes 1024 | tf_op jit(solution)/shard_map/first_backward/pallas_call | solution.py:864
  465.4 22.4 %ffn_backward.2 = (f32[1024,2048]{1,0:T(8,128)}, bf16[1024,256]{1,0:T(8,128)(2,1)}, bf16[1024,256]{1,0:T(8,128)(2,1)}, bf16[1024,256]{1,0:T(8,128)(2,1)}, bf16[1...) custom-call(bf16[3,128,2048]{2,1,0:T(8,128)(2,1)} %copy-done.6, ...), custom_call_target="tpu_custom_call" | custom-call | bytes 1024 | tf_op jit(solution)/shard_map/ffn_backward/pallas_call | solution.py:816
  487.8 7.5 unit_grads.2
  495.4 4.9 collective-permute-done.18
  500.7 2.2 add_convert_fusion.10
  505.6 7.5 unit_grads.3
  513.1 27.2 %ffn_backward.3 = (f32[512,2048]{1,0:T(8,128)}, bf16[512,2048]{1,0:T(8,128)(2,1)}, bf16[1024,256]{1,0:T(8,128)(2,1)}, bf16[1024,256]{1,0:T(8,128)(2,1)}, bf16[10...) custom-call(bf16[3,128,2048]{2,1,0:T(8,128)(2,1)} %copy-done.2, ...), custom_call_target="tpu_custom_call" | custom-call | bytes 1024 | tf_op jit(solution)/shard_map/ffn_backward/pallas_call | solution.py:816
  543.9 36.8 %gather_sum.1 = (f32[256,2048]{1,0:T(8,128)}, bf16[3,128,2048]{2,1,0:T(8,128)(2,1)}, bf16[3,128,2048]{2,1,0:T(8,128)(2,1)}, bf16[3,128,2048]{2,1,0:T(8,128)(2,1)...) custom-call(f32[512,2048]{1,0:T(8,128)} %get-tuple-element.252.refs_, ...), custom_call_target="tpu_custom_call" | custom-call | bytes 1024 | tf_op jit(solution)/shard_map/gather_sum/pallas_call | solution.py:1310
  580.8 2.2 add_convert_fusion.6
  585.7 27.8 %attend_back.1 = (f32[256,2048]{1,0:T(8,128)}, bf16[256,128]{1,0:T(8,128)(2,1)}, f32[8,2048]{1,0:T(8,128)}, f32[2048,128]{1,0:T(8,128)}, f32[2048,128]{1,0:T(8,1...) custom-call(f32[8,2048]{1,0:T(8,128)} %pad_convert_fusion.gains.refs_9_, ...), custom_call_target="tpu_custom_call" | custom-call | bytes 1024 | tf_op jit(solution)/shard_map/attend_back/pallas_call | solution.py:954
  613.5 1.7 constant_dynamic-update-slice_fusion.1
  615.7 1.9 collective-permute-done.26
  617.8 1.8 collective-permute-done.25
  619.6 1.7 collective-permute-done.24
  625.8 1.5 collective-permute-start.31
  627.3 1.5 collective-permute-start.30
  628.8 14.4 %query_back.1 = (bf16[2048,2048]{1,0:T(8,128)(2,1)}, f32[256,2048]{1,0:T(8,128)}, f32[1,256]{1,0:T(1,128)}) custom-call(f32[256,2048]{1,0:T(8,128)} %get-tuple-element.300.grad_query, f32[256,3072]{1,0:T(8,128)} %get-tuple-element.301.raw, f32[256,128]{1,0:T(8,128)} %get-tuple-element.391.cosine, f32[256,128]{1,0:T(8,128)} %get-tuple-element.390.sine, ...), custom_call_target="tpu_custom_call" | custom-call | bytes 1024 | tf_op jit(solution)/shard_map/query_back/pallas_call | solution.py:1032
  643.2 27.9 %collective-permute-done.30 = bf16[256,1024]{1,0:T(8,128)(2,1)} collective-permute-done((bf16[256,1024]{1,0:T(8,128)(2,1)S(1)}, bf16[256,1024]{1,0:T(8,128)(2,1)}, u32[]{:S(2)}, u32[]{:S(2)}) %collective-permute-start.30) | collective-permute-done | bytes 524320 | tf_op jit(solution)/shard_map/ppermute | solution.py:1855
  671.1 2.4 convert_add_fusion.grad_kv
  673.5 1.8 add_convert_fusion.2
  675.5 1.7 add_convert_fusion.3
  677.2 1.9 collective-permute-start.32
  682.7 11.8 %key_back.1 = (bf16[2048,1024]{1,0:T(8,128)(2,1)}, f32[256,2048]{1,0:T(8,128)}, f32[1,256]{1,0:T(1,128)}, f32[1,2048]{1,0:T(1,128)}) custom-call(f32[256,1024]{1,0:T(8,128)} %convert_add_fusion.grad_kv, f32[256,3072]{1,0:T(8,128)} %get-tuple-element.301.raw, f32[256,128]{1,0:T(8,128)} %get-tuple-element.391.cosine, f32[256,128]{1,0:T(8,128)} %get-tuple-element.390.sine, ...), custom_call_target="tpu_custom_call" | custom-call | bytes 1024 | tf_op jit(solution)/shard_map/key_back/pallas_call | solution.py:1085
  696.8 5.4 concatenate.28
  702.2 7.7 collective-permute-done.33
  709.9 2.9 collective-permute-done.32
  712.8 3.8 add_convert_fusion.1.refs_5_
  716.6 3.2 add_convert_fusion.refs_6_
  719.8 122.3 %sum_all.1 = (f32[64,2048]{1,0:T(8,128)}, f32[64,1024]{1,0:T(8,128)}, f32[64,2048]{1,0:T(8,128)}, f32[64,768]{1,0:T(8,128)}, f32[8,128]{1,0:T(8,128)}, /*index=5...) custom-call(bf16[8,2,2,64,2048]{4,3,2,1,0:T(8,128)(2,1)} %bitcast.38, bf16[8,2,2,64,1024]{4,3,2,1,0:T(8,128)(2,1)} %bitcast.39, ...), custom_call_target="tpu_custom_call" | custom-call | bytes 24117248 | tf_op jit(solution)/shard_map/sum_all/pallas_call | solution.py:512
  845.2 1.5 fusion.10
  851.2 3.1 add_bitcast_fusion
  854.3 3.1 pad_maximum_fusion
  (179 shorter events, 63.7 us)
Async XLA Ops:
  0.6 5.4 copy-start.32
  0.7 12.1 %copy-start.28 = (bf16[64,2048]{1,0:T(8,128)(2,1)S(1)}, bf16[64,2048]{1,0:T(8,128)(2,1)}, u32[]{:S(2)}) copy-start(bf16[64,2048]{1,0:T(8,128)(2,1)} %param.20) | copy-start | bytes 786436
  0.7 12.1 %copy-start.29 = (bf16[64,1024]{1,0:T(8,128)(2,1)S(1)}, bf16[64,1024]{1,0:T(8,128)(2,1)}, u32[]{:S(2)}) copy-start(bf16[64,1024]{1,0:T(8,128)(2,1)} %param.19) | copy-start | bytes 393220
  2.8 134.9 %copy-start = (bf16[3,128,2048]{2,1,0:T(8,128)(2,1)}, bf16[3,128,2048]{2,1,0:T(8,128)(2,1)S(1)}, u32[]{:S(2)}) copy-start(bf16[3,128,2048]{2,1,0:T(8,128)(2,1)S(1)} %get-tuple-element.384.refs_1_.refs_7_) | copy-start | bytes 4718596
  2.8 134.9 %copy-start.1 = (bf16[3,128,2048]{2,1,0:T(8,128)(2,1)}, bf16[3,128,2048]{2,1,0:T(8,128)(2,1)S(1)}, u32[]{:S(2)}) copy-start(bf16[3,128,2048]{2,1,0:T(8,128)(2,1)S(1)} %get-tuple-element.385.refs_0_.refs_6_) | copy-start | bytes 4718596
  2.9 138.1 %collective-permute-start.1 = (bf16[3,128,2048]{2,1,0:T(8,128)(2,1)S(1)}, bf16[3,128,2048]{2,1,0:T(8,128)(2,1)}, u32[]{:S(2)}, u32[]{:S(2)}) collective-permute-start(bf16[3,128,2048]{2,1,0:T(8,128)(2,1)S(1)} %get-tuple-element.384.refs_1_.refs_7_), channel_id=1, source_target_pairs={{0,4},{8,0},{16,8},{24,16},{28,24},{20,28},{12,20},{4,12},{1,5},{9... | collective-permute-start | bytes 4718600 | tf_op jit(solution)/shard_map/ppermute | solution.py:57
  5.9 135.1 %collective-permute-start = (bf16[3,128,2048]{2,1,0:T(8,128)(2,1)S(1)}, bf16[3,128,2048]{2,1,0:T(8,128)(2,1)}, u32[]{:S(2)}, u32[]{:S(2)}) collective-permute-start(bf16[3,128,2048]{2,1,0:T(8,128)(2,1)S(1)} %get-tuple-element.385.refs_0_.refs_6_), channel_id=1, source_target_pairs={{0,8},{8,16},{16,24},{24,28},{28,20},{20,12},{12,4},{4,0},{1,9},{9... | collective-permute-start | bytes 4718600 | tf_op jit(solution)/shard_map/ppermute | solution.py:57
  141.0 36.9 %collective-permute-start.2 = (bf16[3,128,2048]{2,1,0:T(8,128)(2,1)}, bf16[3,128,2048]{2,1,0:T(8,128)(2,1)S(1)}, u32[]{:S(2)}, u32[]{:S(2)}) collective-permute-start(bf16[3,128,2048]{2,1,0:T(8,128)(2,1)} %collective-permute-done.refs_2_.up_w), channel_id=1, source_target_pairs={{0,8},{8,16},{16,24},{24,28},{28,20},{20,12},{12,4},{4,0},{1,9},{9... | collective-permute-start | bytes 4718600 | tf_op jit(solution)/shard_map/ppermute | solution.py:57
  141.6 36.6 %collective-permute-start.3 = (bf16[3,128,2048]{2,1,0:T(8,128)(2,1)}, bf16[3,128,2048]{2,1,0:T(8,128)(2,1)S(1)}, u32[]{:S(2)}, u32[]{:S(2)}) collective-permute-start(bf16[3,128,2048]{2,1,0:T(8,128)(2,1)} %collective-permute-done.1.refs_3_.down_w), channel_id=1, source_target_pairs={{0,4},{8,0},{16,8},{24,16},{28,24},{20,28},{12,20},{4,12},{1,5},{9... | collective-permute-start | bytes 4718600 | tf_op jit(solution)/shard_map/ppermute | solution.py:57
  177.9 23.2 %copy-start.6 = (bf16[3,128,2048]{2,1,0:T(8,128)(2,1)}, bf16[3,128,2048]{2,1,0:T(8,128)(2,1)S(1)}, u32[]{:S(2)}) copy-start(bf16[3,128,2048]{2,1,0:T(8,128)(2,1)S(1)} %collective-permute-done.2.refs_4_.refs_0_) | copy-start | bytes 4718596
  178.2 23.0 %copy-start.7 = (bf16[3,128,2048]{2,1,0:T(8,128)(2,1)}, bf16[3,128,2048]{2,1,0:T(8,128)(2,1)S(1)}, u32[]{:S(2)}) copy-start(bf16[3,128,2048]{2,1,0:T(8,128)(2,1)S(1)} %collective-permute-done.3.refs_5_.refs_1_) | copy-start | bytes 4718596
  180.4 16.1 %collective-permute-start.7 = (bf16[256,1024]{1,0:T(8,128)(2,1)}, bf16[256,1024]{1,0:T(8,128)(2,1)}, u32[]{:S(2)}, u32[]{:S(2)}) collective-permute-start(bf16[256,1024]{1,0:T(8,128)(2,1)} %slice.79), channel_id=1, source_target_pairs={{0,4},{4,8},{8,12},{12,20},{1,5},{5,9},{9,13},{13,21},{2,6},{6,10}... | collective-permute-start | bytes 1572872 | tf_op jit(solution)/shard_map/ppermute | solution.py:1694
  184.6 11.9 %collective-permute-start.6 = (bf16[256,1024]{1,0:T(8,128)(2,1)}, bf16[256,1024]{1,0:T(8,128)(2,1)}, u32[]{:S(2)}, u32[]{:S(2)}) collective-permute-start(bf16[256,1024]{1,0:T(8,128)(2,1)} %slice.79), channel_id=1, source_target_pairs={{12,16},{13,17},{14,18},{15,19}} | collective-permute-start | bytes 1572872 | tf_op jit(solution)/shard_map/ppermute | solution.py:1693
  186.1 35.5 %collective-permute-start.4 = (bf16[3,128,2048]{2,1,0:T(8,128)(2,1)S(1)}, bf16[3,128,2048]{2,1,0:T(8,128)(2,1)}, u32[]{:S(2)}, u32[]{:S(2)}) collective-permute-start(bf16[3,128,2048]{2,1,0:T(8,128)(2,1)S(1)} %collective-permute-done.2.refs_4_.refs_0_), channel_id=1, source_target_pairs={{0,8},{8,16},{16,24},{24,28},{28,20},{20,12},{12,4},{4,0},{1,9},{9... | collective-permute-start | bytes 4718600 | tf_op jit(solution)/shard_map/ppermute | solution.py:57
  186.9 41.6 %collective-permute-start.5 = (bf16[3,128,2048]{2,1,0:T(8,128)(2,1)S(1)}, bf16[3,128,2048]{2,1,0:T(8,128)(2,1)}, u32[]{:S(2)}, u32[]{:S(2)}) collective-permute-start(bf16[3,128,2048]{2,1,0:T(8,128)(2,1)S(1)} %collective-permute-done.3.refs_5_.refs_1_), channel_id=1, source_target_pairs={{0,4},{8,0},{16,8},{24,16},{28,24},{20,28},{12,20},{4,12},{1,5},{9... | collective-permute-start | bytes 4718600 | tf_op jit(solution)/shard_map/ppermute | solution.py:57
  198.4 1.4 collective-permute-start.8
  201.2 2.0 collective-permute-start.9
  228.5 35.9 %collective-permute-start.10 = (bf16[3,128,2048]{2,1,0:T(8,128)(2,1)}, bf16[3,128,2048]{2,1,0:T(8,128)(2,1)}, u32[]{:S(2)}, u32[]{:S(2)}) collective-permute-start(bf16[3,128,2048]{2,1,0:T(8,128)(2,1)} %collective-permute-done.4.refs_6_.refs_2_), channel_id=1, source_target_pairs={{0,8},{8,16},{16,24},{24,28},{28,20},{20,12},{12,4},{4,0},{1,9},{9... | collective-permute-start | bytes 4718600 | tf_op jit(solution)/shard_map/ppermute | solution.py:57
  228.5 44.2 %collective-permute-start.11 = (bf16[3,128,2048]{2,1,0:T(8,128)(2,1)}, bf16[3,128,2048]{2,1,0:T(8,128)(2,1)S(1)}, u32[]{:S(2)}, u32[]{:S(2)}) collective-permute-start(bf16[3,128,2048]{2,1,0:T(8,128)(2,1)} %collective-permute-done.5.refs_7_.refs_3_), channel_id=1, source_target_pairs={{0,4},{8,0},{16,8},{24,16},{28,24},{20,28},{12,20},{4,12},{1,5},{9... | collective-permute-start | bytes 4718600 | tf_op jit(solution)/shard_map/ppermute | solution.py:57
  273.8 36.1 %collective-permute-start.12 = (bf16[3,128,2048]{2,1,0:T(8,128)(2,1)}, bf16[3,128,2048]{2,1,0:T(8,128)(2,1)S(1)}, u32[]{:S(2)}, u32[]{:S(2)}) collective-permute-start(bf16[3,128,2048]{2,1,0:T(8,128)(2,1)} %collective-permute-done.10.refs_8_.refs_4_), channel_id=1, source_target_pairs={{0,8},{8,16},{16,24},{24,28},{28,20},{20,12},{12,4},{4,0},{1,9},{9... | collective-permute-start | bytes 4718600 | tf_op jit(solution)/shard_map/ppermute | solution.py:57
  276.3 36.7 %collective-permute-start.13 = (bf16[3,128,2048]{2,1,0:T(8,128)(2,1)}, bf16[3,128,2048]{2,1,0:T(8,128)(2,1)S(1)}, u32[]{:S(2)}, u32[]{:S(2)}) collective-permute-start(bf16[3,128,2048]{2,1,0:T(8,128)(2,1)} %copy-done.8), channel_id=1, source_target_pairs={{0,4},{8,0},{16,8},{24,16},{28,24},{20,28},{12,20},{4,12},{1,5},{9... | collective-permute-start | bytes 4718600 | tf_op jit(solution)/shard_map/ppermute | solution.py:57
  304.8 46.3 %copy-start.30 = (s32[2,4]{1,0:T(2,128)S(1)}, s32[2,4]{1,0:T(2,128)}, u32[]{:S(2)}) copy-start(s32[2,4]{1,0:T(2,128)} %param.17) | copy-start | bytes 100
  310.0 5.6 copy-start.2
  313.0 2.5 copy-start.3
  313.0 34.8 %collective-permute-start.14 = (bf16[3,128,2048]{2,1,0:T(8,128)(2,1)S(1)}, bf16[3,128,2048]{2,1,0:T(8,128)(2,1)}, u32[]{:S(2)}, u32[]{:S(2)}) collective-permute-start(bf16[3,128,2048]{2,1,0:T(8,128)(2,1)S(1)} %collective-permute-done.12.refs_10_.refs_0_), channel_id=1, source_target_pairs={{0,8},{8,16},{16,24},{24,28},{28,20},{20,12},{12,4},{4,0},{1,9},{9... | collective-permute-start | bytes 4718600 | tf_op jit(solution)/shard_map/ppermute | solution.py:57
  314.8 34.4 %collective-permute-start.15 = (bf16[3,128,2048]{2,1,0:T(8,128)(2,1)S(1)}, bf16[3,128,2048]{2,1,0:T(8,128)(2,1)}, u32[]{:S(2)}, u32[]{:S(2)}) collective-permute-start(bf16[3,128,2048]{2,1,0:T(8,128)(2,1)S(1)} %collective-permute-done.13.refs_11_.refs_1_), channel_id=1, source_target_pairs={{0,4},{8,0},{16,8},{24,16},{28,24},{20,28},{12,20},{4,12},{1,5},{9... | collective-permute-start | bytes 4718600 | tf_op jit(solution)/shard_map/ppermute | solution.py:57
  349.1 33.1 %collective-permute-start.16 = (bf16[3,128,2048]{2,1,0:T(8,128)(2,1)}, bf16[3,128,2048]{2,1,0:T(8,128)(2,1)S(1)}, u32[]{:S(2)}, u32[]{:S(2)}) collective-permute-start(bf16[3,128,2048]{2,1,0:T(8,128)(2,1)} %collective-permute-done.14.refs_0_.refs_2_), channel_id=1, source_target_pairs={{0,8},{8,16},{16,24},{24,28},{28,20},{20,12},{12,4},{4,0},{1,9},{9... | collective-permute-start | bytes 4718600 | tf_op jit(solution)/shard_map/ppermute | solution.py:57
  350.1 33.1 %collective-permute-start.17 = (bf16[3,128,2048]{2,1,0:T(8,128)(2,1)}, bf16[3,128,2048]{2,1,0:T(8,128)(2,1)S(1)}, u32[]{:S(2)}, u32[]{:S(2)}) collective-permute-start(bf16[3,128,2048]{2,1,0:T(8,128)(2,1)} %collective-permute-done.15.refs_1_.refs_3_), channel_id=1, source_target_pairs={{0,4},{8,0},{16,8},{24,16},{28,24},{20,28},{12,20},{4,12},{1,5},{9... | collective-permute-start | bytes 4718600 | tf_op jit(solution)/shard_map/ppermute | solution.py:57
  382.2 2.4 copy-start.4
  463.3 36.9 %collective-permute-start.18 = (bf16[3,128,2048]{2,1,0:T(8,128)(2,1)}, bf16[3,128,2048]{2,1,0:T(8,128)(2,1)S(1)}, u32[]{:S(2)}, u32[]{:S(2)}) collective-permute-start(bf16[3,128,2048]{2,1,0:T(8,128)(2,1)} %get-tuple-element.213), channel_id=1, source_target_pairs={{0,8},{8,16},{16,24},{24,28},{28,20},{20,12},{12,4},{4,0},{1,9},{9... | collective-permute-start | bytes 4718600 | tf_op jit(solution)/shard_map/ppermute | solution.py:57
  464.1 36.6 %collective-permute-start.19 = (bf16[3,128,2048]{2,1,0:T(8,128)(2,1)}, bf16[3,128,2048]{2,1,0:T(8,128)(2,1)S(1)}, u32[]{:S(2)}, u32[]{:S(2)}) collective-permute-start(bf16[3,128,2048]{2,1,0:T(8,128)(2,1)} %get-tuple-element.214), channel_id=1, source_target_pairs={{0,4},{8,0},{16,8},{24,16},{28,24},{20,28},{12,20},{4,12},{1,5},{9... | collective-permute-start | bytes 4718600 | tf_op jit(solution)/shard_map/ppermute | solution.py:57
  500.7 3.6 copy-start.21
  502.9 37.5 %collective-permute-start.21 = (bf16[3,128,2048]{2,1,0:T(8,128)(2,1)S(1)}, bf16[3,128,2048]{2,1,0:T(8,128)(2,1)S(1)}, u32[]{:S(2)}, u32[]{:S(2)}) collective-permute-start(bf16[3,128,2048]{2,1,0:T(8,128)(2,1)S(1)} %add_convert_fusion.10), channel_id=1, source_target_pairs={{0,4},{8,0},{16,8},{24,16},{28,24},{20,28},{12,20},{4,12},{1,5},{9... | collective-permute-start | bytes 4718600 | tf_op jit(solution)/shard_map/ppermute | solution.py:57
  504.9 35.5 %collective-permute-start.20 = (bf16[3,128,2048]{2,1,0:T(8,128)(2,1)S(1)}, bf16[3,128,2048]{2,1,0:T(8,128)(2,1)S(1)}, u32[]{:S(2)}, u32[]{:S(2)}) collective-permute-start(bf16[3,128,2048]{2,1,0:T(8,128)(2,1)S(1)} %add_convert_fusion.11), channel_id=1, source_target_pairs={{0,8},{8,16},{16,24},{24,28},{28,20},{20,12},{12,4},{4,0},{1,9},{9... | collective-permute-start | bytes 4718600 | tf_op jit(solution)/shard_map/ppermute | solution.py:57
  513.1 27.3 %copy-start.20 = (bf16[3,128,2048]{2,1,0:T(8,128)(2,1)S(1)}, bf16[3,128,2048]{2,1,0:T(8,128)(2,1)}, u32[]{:S(2)}) copy-start(bf16[3,128,2048]{2,1,0:T(8,128)(2,1)} %get-tuple-element.251) | copy-start | bytes 4718596
  540.3 2.1 copy-start.18
  541.0 39.7 %collective-permute-start.23 = (bf16[3,128,2048]{2,1,0:T(8,128)(2,1)S(1)}, bf16[3,128,2048]{2,1,0:T(8,128)(2,1)S(1)}, u32[]{:S(2)}, u32[]{:S(2)}) collective-permute-start(bf16[3,128,2048]{2,1,0:T(8,128)(2,1)S(1)} %add_convert_fusion.8), channel_id=1, source_target_pairs={{0,4},{8,0},{16,8},{24,16},{28,24},{20,28},{12,20},{4,12},{1,5},{9... | collective-permute-start | bytes 4718600 | tf_op jit(solution)/shard_map/ppermute | solution.py:57
  543.0 37.7 %collective-permute-start.22 = (bf16[3,128,2048]{2,1,0:T(8,128)(2,1)S(1)}, bf16[3,128,2048]{2,1,0:T(8,128)(2,1)S(1)}, u32[]{:S(2)}, u32[]{:S(2)}) collective-permute-start(bf16[3,128,2048]{2,1,0:T(8,128)(2,1)S(1)} %add_convert_fusion.9), channel_id=1, source_target_pairs={{0,8},{8,16},{16,24},{24,28},{28,20},{20,12},{12,4},{4,0},{1,9},{9... | collective-permute-start | bytes 4718600 | tf_op jit(solution)/shard_map/ppermute | solution.py:57
  580.8 3.6 copy-start.19
  583.0 36.6 %collective-permute-start.25 = (bf16[3,128,2048]{2,1,0:T(8,128)(2,1)S(1)}, bf16[3,128,2048]{2,1,0:T(8,128)(2,1)S(1)}, u32[]{:S(2)}, u32[]{:S(2)}) collective-permute-start(bf16[3,128,2048]{2,1,0:T(8,128)(2,1)S(1)} %add_convert_fusion.6), channel_id=1, source_target_pairs={{0,4},{8,0},{16,8},{24,16},{28,24},{20,28},{12,20},{4,12},{1,5},{9... | collective-permute-start | bytes 4718600 | tf_op jit(solution)/shard_map/ppermute | solution.py:57
  585.0 36.4 %collective-permute-start.24 = (bf16[3,128,2048]{2,1,0:T(8,128)(2,1)S(1)}, bf16[3,128,2048]{2,1,0:T(8,128)(2,1)S(1)}, u32[]{:S(2)}, u32[]{:S(2)}) collective-permute-start(bf16[3,128,2048]{2,1,0:T(8,128)(2,1)S(1)} %add_convert_fusion.7), channel_id=1, source_target_pairs={{0,8},{8,16},{16,24},{24,28},{28,20},{20,12},{12,4},{4,0},{1,9},{9... | collective-permute-start | bytes 4718600 | tf_op jit(solution)/shard_map/ppermute | solution.py:57
  613.5 1.9 copy-start.12
  615.6 2.0 collective-permute-start.26
  617.8 4.5 copy-start.17
  621.4 2.4 copy-start.16
  621.4 4.2 collective-permute-start.29
  622.9 50.6 %collective-permute-start.28 = (bf16[3,128,2048]{2,1,0:T(8,128)(2,1)S(1)}, bf16[3,128,2048]{2,1,0:T(8,128)(2,1)S(1)}, u32[]{:S(2)}, u32[]{:S(2)}) collective-permute-start(bf16[3,128,2048]{2,1,0:T(8,128)(2,1)S(1)} %add_convert_fusion.4), channel_id=1, source_target_pairs={{0,4},{8,0},{16,8},{24,16},{28,24},{20,28},{12,20},{4,12},{1,5},{9... | collective-permute-start | bytes 4718600 | tf_op jit(solution)/shard_map/ppermute | solution.py:57
  624.5 49.0 %collective-permute-start.27 = (bf16[3,128,2048]{2,1,0:T(8,128)(2,1)S(1)}, bf16[3,128,2048]{2,1,0:T(8,128)(2,1)S(1)}, u32[]{:S(2)}, u32[]{:S(2)}) collective-permute-start(bf16[3,128,2048]{2,1,0:T(8,128)(2,1)S(1)} %add_convert_fusion.5), channel_id=1, source_target_pairs={{0,8},{8,16},{16,24},{24,28},{28,20},{20,12},{12,4},{4,0},{1,9},{9... | collective-permute-start | bytes 4718600 | tf_op jit(solution)/shard_map/ppermute | solution.py:57
  625.8 17.4 %collective-permute-start.31 = (bf16[256,1024]{1,0:T(8,128)(2,1)S(1)}, bf16[256,1024]{1,0:T(8,128)(2,1)}, u32[]{:S(2)}, u32[]{:S(2)}) collective-permute-start(bf16[256,1024]{1,0:T(8,128)(2,1)S(1)} %add_convert_fusion.12), channel_id=1, source_target_pairs={{16,12},{17,13},{18,14},{19,15}} | collective-permute-start | bytes 1572872 | tf_op jit(solution)/shard_map/ppermute | solution.py:1856
  627.3 43.8 %collective-permute-start.30 = (bf16[256,1024]{1,0:T(8,128)(2,1)S(1)}, bf16[256,1024]{1,0:T(8,128)(2,1)}, u32[]{:S(2)}, u32[]{:S(2)}) collective-permute-start(bf16[256,1024]{1,0:T(8,128)(2,1)S(1)} %add_convert_fusion.12), channel_id=1, source_target_pairs={{4,0},{8,4},{12,8},{20,12},{5,1},{9,5},{13,9},{21,13},{6,2},{10,6}... | collective-permute-start | bytes 1572872 | tf_op jit(solution)/shard_map/ppermute | solution.py:1855
  643.2 30.3 %copy-start.15 = (bf16[3,128,2048]{2,1,0:T(8,128)(2,1)S(1)}, bf16[3,128,2048]{2,1,0:T(8,128)(2,1)}, u32[]{:S(2)}) copy-start(bf16[3,128,2048]{2,1,0:T(8,128)(2,1)} %get-tuple-element.309) | copy-start | bytes 4718596
  673.5 2.0 copy-start.14
  675.3 4.6 copy-start.23
  675.3 34.6 %collective-permute-start.33 = (bf16[3,128,2048]{2,1,0:T(8,128)(2,1)}, bf16[3,128,2048]{2,1,0:T(8,128)(2,1)}, u32[]{:S(2)}, u32[]{:S(2)}) collective-permute-start(bf16[3,128,2048]{2,1,0:T(8,128)(2,1)} %add_convert_fusion.2), channel_id=1, source_target_pairs={{0,4},{8,0},{16,8},{24,16},{28,24},{20,28},{12,20},{4,12},{1,5},{9... | collective-permute-start | bytes 4718600 | tf_op jit(solution)/shard_map/ppermute | solution.py:57
  677.2 35.6 %collective-permute-start.32 = (bf16[3,128,2048]{2,1,0:T(8,128)(2,1)}, bf16[3,128,2048]{2,1,0:T(8,128)(2,1)}, u32[]{:S(2)}, u32[]{:S(2)}) collective-permute-start(bf16[3,128,2048]{2,1,0:T(8,128)(2,1)} %add_convert_fusion.3), channel_id=1, source_target_pairs={{0,8},{8,16},{16,24},{24,28},{28,20},{20,12},{12,4},{4,0},{1,9},{9... | collective-permute-start | bytes 4718600 | tf_op jit(solution)/shard_map/ppermute | solution.py:57
  680.4 2.2 copy-start.22
  682.7 12.5 %copy-start.31 = (f32[1,256]{1,0:T(1,128)S(1)}, f32[1,256]{1,0:T(1,128)}, u32[]{:S(2)}) copy-start(f32[1,256]{1,0:T(1,128)} %get-tuple-element.326) | copy-start | bytes 3076
  712.8 3.8 copy-start.13
  719.8 131.4 %copy-start.10 = (bf16[3,128,2048]{2,1,0:T(8,128)(2,1)S(1)}, bf16[3,128,2048]{2,1,0:T(8,128)(2,1)}, u32[]{:S(2)}) copy-start(bf16[3,128,2048]{2,1,0:T(8,128)(2,1)} %get-tuple-element.345) | copy-start | bytes 4718596
  719.8 131.4 %copy-start.11 = (bf16[3,128,2048]{2,1,0:T(8,128)(2,1)S(1)}, bf16[3,128,2048]{2,1,0:T(8,128)(2,1)}, u32[]{:S(2)}) copy-start(bf16[3,128,2048]{2,1,0:T(8,128)(2,1)} %get-tuple-element.347) | copy-start | bytes 4718596
  854.3 3.1 copy-start.9
  857.5 2.0 copy-start.25
  858.8 1.5 copy-start.27
  858.8 2.2 copy-start.24
  (3 other events, 3.8 us)

commit v9 on v8

--- a/solution.py
+++ b/solution.py
@@ -240,9 +240,9 @@
 
 
 def sum_kernel(chips, streams, counts, *refs):
-    arrays, (tile, up_sum, down_sum), outs, (tile_out, up_in, down_in), held, core_in, ring_in, x_in, tiles, sems = refs_of(counts, refs)
+    arrays, (tile, *unit_refs), outs, (tile_out, up_in, down_in), held, core_in, ring_in, x_in, tiles, sems = refs_of(counts, refs)
     load_sem, core_send, core_recv, ring_send, ring_recv, x_send, x_recv, tile_send, tile_recv, hop_send, hop_recv = sems
-    tile_pairs, tile_ring = tiles
+    tile_pairs, tile_ring, hop_sums, hop_terms = tiles
     chip = lax.axis_index("zy")
     core = lax.axis_index("core")
     side = lax.axis_index("fsdp")
@@ -315,14 +315,32 @@
         for i in range(len(arrays))
     ]
 
+    loads += [
+        pltpu.make_async_copy(ref, held_in.at[way], load_sem.at[len(arrays) + 2 * i + way])
+        for i, held_in in enumerate((hop_sums, hop_terms))
+        for way, ref in enumerate(unit_refs[2 * i : 2 * i + 2])
+    ]
+
     def send_cores(turn, carry):
         for number in numbers:
             core_copy(number, turn).start()
         return carry
 
     def hop_copy(way, kind):
-        src, dst = ((up_sum, up_in), (down_sum, down_in))[way]
-        return remote(src.at[kind], dst.at[kind], hop_send.at[way, kind], hop_recv.at[way, kind], neighbour(1 - 2 * way))
+        return remote(
+            hop_sums.at[way, kind],
+            (up_in, down_in)[way].at[kind],
+            hop_send.at[way, kind],
+            hop_recv.at[way, kind],
+            neighbour(1 - 2 * way),
+        )
+
+    def hop_on(kind):
+        for way in range(2):
+            hop_sums[way, kind] = (
+                hop_sums[way, kind].astype(F32) + hop_terms[way, kind].astype(F32)
+            ).astype(BF16)
+            hop_copy(way, kind).start()
 
     def tile_copy(src, dst, number, peer):
         return remote(src, dst, tile_send.at[number], tile_recv.at[number], peer)
@@ -379,8 +397,7 @@
 
             @pl.when(turn == 1 + kind)
             def _(kind=kind):
-                for way in range(2):
-                    hop_copy(way, kind).start()
+                hop_on(kind)
 
         @pl.when(turn < chips)
         def _():
@@ -485,7 +502,7 @@
     return groups
 
 
-def sum_all(arrays, firsts, tile, up_sum, down_sum, chips):
+def sum_all(arrays, firsts, tile, arrived, terms, chips):
     rows = arrays[0].shape[0] // (4 * chips)
     streams = []
     for i, (array, first) in enumerate(zip(arrays, firsts)):
@@ -504,21 +521,22 @@
         + [vmem((chips - 1, 1 if first else 2, rows, width), BF16) for _, _, width, _, first in streams]
         + [vmem((chips if first else 1, rows, width), BF16) for _, _, width, _, first in streams]
         + [vmem((3, 8, 128), F32), vmem((chips, 8, 128), F32)]
-        + [dma((count,))]
+        + [vmem((2,) + terms[0].shape, BF16)] * 2
+        + [dma((count + 4,))]
         + [dma((number, chips)) for _ in range(6)]
         + [dma((chips + 1,)) for _ in range(2)]
         + [dma((2, 3)) for _ in range(2)]
     )
     return pl.pallas_call(
         functools.partial(
-            sum_kernel, chips, streams, (count, 3, count, 3, count, count, number, number, 2, 11)
+            sum_kernel, chips, streams, (count, 5, count, 3, count, count, number, number, 4, 11)
         ),
         out_shape=[jax.ShapeDtypeStruct((rows, a.shape[1]), F32) for a in arrays]
         + [jax.ShapeDtypeStruct((8, 128), F32)]
-        + [jax.ShapeDtypeStruct(up_sum.shape, BF16)] * 2,
+        + [jax.ShapeDtypeStruct(terms[0].shape, BF16)] * 2,
         in_specs=[pl.BlockSpec(memory_space=pl.ANY)] * count
         + [pl.BlockSpec(memory_space=pltpu.VMEM)]
-        + [pl.BlockSpec(memory_space=pl.ANY)] * 2,
+        + [pl.BlockSpec(memory_space=pl.ANY)] * 4,
         out_specs=[pl.BlockSpec(memory_space=pltpu.VMEM)] * (count + 1) + [pl.BlockSpec(memory_space=pl.ANY)] * 2,
         scratch_shapes=scratch,
         compiler_params=pltpu.CompilerParams(
@@ -528,7 +546,7 @@
             flops=0, bytes_accessed=sum(2 * a.size for a in arrays), transcendentals=0
         ),
         name="sum_all",
-    )(*[a.reshape(chips, 2, 2, rows, a.shape[1]) for a in arrays], tile, up_sum, down_sum)
+    )(*[a.reshape(chips, 2, 2, rows, a.shape[1]) for a in arrays], tile, *arrived, *terms)
 
 
 LITTLE = pl.CostEstimate(flops=0, bytes_accessed=1024, transcendentals=0)
@@ -1777,9 +1795,10 @@
     order = list(range(1, chips)) + [0]
     ring_steps = shares(chips - 2, 6)
     done = 0
+    last_sums = None
 
     def beside(stage, work):
-        nonlocal done, up_sum, down_sum
+        nonlocal done, up_sum, down_sum, last_sums
         values = None
         for step in range(ring_steps[stage]):
             up_in = ring(up_sum, 1)
@@ -1789,6 +1808,7 @@
             done += 1
             terms = unit_grads(order[done])
             (up_in, down_in), terms, values = tie((up_in, down_in), terms, values)
+            last_sums = (up_in, down_in), terms
             up_sum = (up_in.astype(F32) + terms[0].astype(F32)).astype(BF16)
             down_sum = (down_in.astype(F32) + terms[1].astype(F32)).astype(BF16)
         return work() if values is None else values
@@ -1885,8 +1905,7 @@
         [grad_wq, grad_wkv, grad_wo, rest_back],
         (D, 2 * key_cols, D - 512, 0),
         squares,
-        up_sum,
-        down_sum,
+        *last_sums,
         chips,
     )
     grad_ffn = jnp.concatenate(

time: 872 us -> 867 us (level)
  transfers between devices with their start and end apart: 34 -> 34, of which waited for: 22 -> 22; matrix products, arithmetic and copies ran while one was open for 6% -> 6% of each run, Pallas kernels for 44% -> 45%
where the time goes in v9:
time: 867 us; the launch traced here: 858 us
  Pallas kernels  585 us (67%)
  waiting for transfers between devices  144 us (17%)
  local copies, waits for them, and re-layouts  50.1 us (6%)
  starting transfers between devices  41.8 us (5%)
  other arithmetic  32.7 us (4%)
    pallas_call x1, Pallas kernels, sum_all(): pl.pallas_call(functools.partial(sum_kernel, chips, streams, (count, 5, c...  124 us
    pallas_call x1, Pallas kernels, gather_all(): pl.pallas_call(functools.partial(gather_kernel, chips, streams), out_shap...  123 us
    ppermute x26, waiting for transfers between devices, ring(): return lax.ppermute(value, 'zy', ring_pairs(lax.axis_size('zy'), by))  104 us
    pallas_call x1, Pallas kernels, middle(): pl.pallas_call(functools.partial(middle_kernel, steps), out_shape=[shape(...  60.6 us
    pallas_call x2, Pallas kernels, ffn_backward(): piece(functools.partial(ffn_backward_kernel, steps, add, last), 'ffn_back...  49.6 us
    pallas_call x2, Pallas kernels, ffn_forward(): piece(functools.partial(ffn_forward_kernel, steps, add), 'ffn_forward', (...  43.6 us
    pallas_call x1, Pallas kernels, sum_of_four(): pl.pallas_call(functools.partial(gather_sum_kernel, steps), out_shape=[ja...  36.8 us
    ppermute x26, starting transfers between devices, ring(): return lax.ppermute(value, 'zy', ring_pairs(lax.axis_size('zy'), by))  30.7 us
  transfers between devices with their start and end apart: 34, of which 22 were waited for; matrix products, arithmetic and copies ran while one was open for 6% of the time, Pallas kernels for 45%

profile of v9, /device:TPU:0, one launch (start us, length us, event | category | flops | bytes accessed | tf_op | source)
XLA Modules:
  0.0 858.0 jit_solution(13842464111916307995)
XLA Ops:
  0.7 2.2 fusion.9
  2.9 3.0 collective-permute-start.1
  12.8 2.0 concatenate.23.shard
  14.8 122.9 %gather_all.1.weight.w_out.lleft.lright = bf16[2048,5888]{1,0:T(8,128)(2,1)} custom-call(bf16[64,5888]{1,0:T(8,128)(2,1)} %concatenate.23.shard), custom_call_target="tpu_custom_call" | custom-call | bytes 48234496 | tf_op jit(solution)/shard_map/gather_all/pallas_call | solution.py:220
  137.7 2.0 slice.75
  141.6 1.5 collective-permute-start.3
  146.0 13.5 %make_qkv.1 = (bf16[256,2048]{1,0:T(8,128)(2,1)}, f32[256,3072]{1,0:T(8,128)}, bf16[256,3072]{1,0:T(8,128)(2,1)}) custom-call(bf16[256,2048]{1,0:T(8,128)(2,1)} %bitcast.34, f32[8,2048]{1,0:T(8,128)} %pad_convert_fusion.gains.refs_9_, f32[2,256]{1,0:T(2,128)} %reshape.117.head_gain, f32[256,128]{1,0:T(8,128)} %get-tuple-element.391.cosine, ...), custom_call_target="tpu_custom_call" | custom-call | bytes 1024 | tf_op jit(solution)/shard_map/make_qkv/pallas_call | solution.py:609
  159.4 18.5 %collective-permute-done.2.refs_4_.refs_0_ = bf16[3,128,2048]{2,1,0:T(8,128)(2,1)S(1)} collective-permute-done((bf16[3,128,2048]{2,1,0:T(8,128)(2,1)}, bf16[3,128,2048]{2,1,0:T(8,128)(2,1)S(1)}, u32[]{:S(2)}, u32[]{:S(2)}) %collective-permute-start.2) | collective-permute-done | bytes 1572896 | tf_op jit(solution)/shard_map/ppermute | solution.py:57
  178.2 2.3 slice.79
  180.4 4.2 collective-permute-start.7
  184.6 1.5 collective-permute-start.6
  188.1 8.4 collective-permute-done.7
  196.5 1.9 broadcast_select_fusion.1
  198.4 1.5 collective-permute-start.8
  201.3 1.9 collective-permute-done.9
  203.2 2.3 pad_maximum_fusion.1.key.value
  205.5 16.1 %collective-permute-done.4.refs_6_.refs_2_ = bf16[3,128,2048]{2,1,0:T(8,128)(2,1)} collective-permute-done((bf16[3,128,2048]{2,1,0:T(8,128)(2,1)S(1)}, bf16[3,128,2048]{2,1,0:T(8,128)(2,1)}, u32[]{:S(2)}, u32[]{:S(2)}) %collective-permute-start.4) | collective-permute-done | bytes 1572896 | tf_op jit(solution)/shard_map/ppermute | solution.py:57
  221.6 6.9 collective-permute-done.5.refs_7_.refs_3_
  228.5 2.6 collective-permute-start.11
  232.3 19.5 %attend.1 = (bf16[256,2048]{1,0:T(8,128)(2,1)}, f32[256,2048]{1,0:T(8,128)}, f32[256,2048]{1,0:T(8,128)}, bf16[256,2048]{1,0:T(8,128)(2,1)}, bf16[256,128]{1,0:T(8,128)(2,1)}) custom-call(bf16[256,2048]{1,0:T(8,128)(2,1)} %bitcast.35, f32[8,2048]{1,0:T(8,128)} %pad_convert_fusion.gains.refs_9_, bf16[256,2048]{1,0:T(8,128)(2,1)} %get-tuple-element.190.low, ...), custom_call_target="tpu_custom_call" | custom-call | bytes 1024 | tf_op jit(solution)/shard_map/attend/pallas_call | solution.py:673
  251.8 12.6 %collective-permute-done.10.refs_8_.refs_4_ = bf16[3,128,2048]{2,1,0:T(8,128)(2,1)} collective-permute-done((bf16[3,128,2048]{2,1,0:T(8,128)(2,1)}, bf16[3,128,2048]{2,1,0:T(8,128)(2,1)}, u32[]{:S(2)}, u32[]{:S(2)}) %collective-permute-start.10) | collective-permute-done | bytes 1572896 | tf_op jit(solution)/shard_map/ppermute | solution.py:57
  264.4 8.3 collective-permute-done.11.refs_9_.refs_5_
  273.8 2.5 collective-permute-start.12
  277.4 27.5 %spread_rows.1.refs_12_.refs_3_.rows.refs_2_ = bf16[1024,2048]{1,0:T(8,128)(2,1)} custom-call(bf16[256,2048]{1,0:T(8,128)(2,1)} %get-tuple-element.195.own), custom_call_target="tpu_custom_call" | custom-call | bytes 1024 | tf_op jit(solution)/shard_map/spread_rows/pallas_call | solution.py:1200
  304.8 5.1 collective-permute-done.12.refs_10_.refs_0_
  310.0 3.1 collective-permute-done.13.refs_11_.refs_1_
  313.0 1.7 collective-permute-start.14
  315.5 31.0 %ffn_forward.2 = (f32[1024,2048]{1,0:T(8,128)}, f32[1024,256]{1,0:T(8,128)}, f32[1024,256]{1,0:T(8,128)}, f32[1024,256]{1,0:T(8,128)}, f32[1024,256]{1,0:T(8,128...) custom-call(bf16[3,128,2048]{2,1,0:T(8,128)(2,1)} %copy-done.1, ...), custom_call_target="tpu_custom_call" | custom-call | bytes 1024 | tf_op jit(solution)/shard_map/ffn_forward/pallas_call | solution.py:787
  352.5 3.0 fusion.8
  355.5 2.4 reshape.107.refs_11_
  359.2 12.6 %ffn_forward.3 = (f32[1024,2048]{1,0:T(8,128)}, f32[1024,256]{1,0:T(8,128)}, f32[1024,256]{1,0:T(8,128)}, bf16[1024,256]{1,0:T(8,128)(2,1)}) custom-call(bf16[3,128,2048]{2,1,0:T(8,128)(2,1)} %collective-permute-done.14.refs_0_.refs_2_, bf16[3,128,2048]{2,1,0:T(8,128)(2,1)} %collective-permute-done.15.refs_1_.refs_3_, ...), custom_call_target="tpu_custom_call" | custom-call | bytes 1024 | tf_op jit(solution)/shard_map/ffn_forward/pallas_call | solution.py:787
  371.8 10.4 %collective-permute-done.16.refs_0_.refs_4_ = bf16[3,128,2048]{2,1,0:T(8,128)(2,1)S(1)} collective-permute-done((bf16[3,128,2048]{2,1,0:T(8,128)(2,1)}, bf16[3,128,2048]{2,1,0:T(8,128)(2,1)S(1)}, u32[]{:S(2)}, u32[]{:S(2)}) %collective-permute-start.16) | collective-permute-done | bytes 1572896 | tf_op jit(solution)/shard_map/ppermute | solution.py:57
  384.7 60.6 %middle.1 = (f32[256,2048]{1,0:T(8,128)}, f32[256,2048]{1,0:T(8,128)}, f32[256,256]{1,0:T(8,128)}, bf16[1024,2048]{1,0:T(8,128)(2,1)}, bf16[2048,256]{1,0:T(8,12...) custom-call(bf16[3,128,2048]{2,1,0:T(8,128)(2,1)} %copy-done.4, ...), custom_call_target="tpu_custom_call" | custom-call | bytes 1024 | tf_op jit(solution)/shard_map/middle/pallas_call | solution.py:1531
  445.2 18.1 %first_backward.1 = (f32[1024,2048]{1,0:T(8,128)}, bf16[1024,256]{1,0:T(8,128)(2,1)}, bf16[1024,256]{1,0:T(8,128)(2,1)}, bf16[3,128,2048]{2,1,0:T(8,128)(2,1)}, bf16[3,128,2048]{2,1,0:T(8,128)(2,1)}) custom-call(bf16[3,128,2048]{2,1,0:T(8,128)(2,1)} %collective-permute-done.refs_2_.up_w, bf16[3,128,2048]{2,1,0:T(8,128)(2,1)} %collective-permute-done.1.refs_3_.down_w, ...), custom_call_target="tpu_custom_call" | custom-call | bytes 1024 | tf_op jit(solution)/shard_map/first_backward/pallas_call | solution.py:882
  465.4 22.4 %ffn_backward.2 = (f32[1024,2048]{1,0:T(8,128)}, bf16[1024,256]{1,0:T(8,128)(2,1)}, bf16[1024,256]{1,0:T(8,128)(2,1)}, bf16[1024,256]{1,0:T(8,128)(2,1)}, bf16[1...) custom-call(bf16[3,128,2048]{2,1,0:T(8,128)(2,1)} %copy-done.6, ...), custom_call_target="tpu_custom_call" | custom-call | bytes 1024 | tf_op jit(solution)/shard_map/ffn_backward/pallas_call | solution.py:834
  487.9 7.5 unit_grads.2
  495.4 4.9 collective-permute-done.18
  500.7 2.2 add_convert_fusion.8
  505.6 7.5 unit_grads.3
  513.1 27.2 %ffn_backward.3 = (f32[512,2048]{1,0:T(8,128)}, bf16[512,2048]{1,0:T(8,128)(2,1)}, bf16[1024,256]{1,0:T(8,128)(2,1)}, bf16[1024,256]{1,0:T(8,128)(2,1)}, bf16[10...) custom-call(bf16[3,128,2048]{2,1,0:T(8,128)(2,1)} %copy-done.2, ...), custom_call_target="tpu_custom_call" | custom-call | bytes 1024 | tf_op jit(solution)/shard_map/ffn_backward/pallas_call | solution.py:834
  543.9 36.8 %gather_sum.1 = (f32[256,2048]{1,0:T(8,128)}, bf16[3,128,2048]{2,1,0:T(8,128)(2,1)}, bf16[3,128,2048]{2,1,0:T(8,128)(2,1)}, bf16[3,128,2048]{2,1,0:T(8,128)(2,1)...) custom-call(f32[512,2048]{1,0:T(8,128)} %get-tuple-element.252.refs_, ...), custom_call_target="tpu_custom_call" | custom-call | bytes 1024 | tf_op jit(solution)/shard_map/gather_sum/pallas_call | solution.py:1328
  580.8 2.2 add_convert_fusion.4
  583.0 1.4 collective-permute-start.25
  585.7 27.7 %attend_back.1 = (f32[256,2048]{1,0:T(8,128)}, bf16[256,128]{1,0:T(8,128)(2,1)}, f32[8,2048]{1,0:T(8,128)}, f32[2048,128]{1,0:T(8,128)}, f32[2048,128]{1,0:T(8,1...) custom-call(f32[8,2048]{1,0:T(8,128)} %pad_convert_fusion.gains.refs_9_, ...), custom_call_target="tpu_custom_call" | custom-call | bytes 1024 | tf_op jit(solution)/shard_map/attend_back/pallas_call | solution.py:972
  613.4 1.7 constant_dynamic-update-slice_fusion.1
  615.6 1.9 collective-permute-done.26
  617.8 1.8 collective-permute-done.25
  619.6 1.8 collective-permute-done.24
  625.8 1.5 collective-permute-start.31
  627.4 1.5 collective-permute-start.30
  628.8 14.4 %query_back.1 = (bf16[2048,2048]{1,0:T(8,128)(2,1)}, f32[256,2048]{1,0:T(8,128)}, f32[1,256]{1,0:T(1,128)}) custom-call(f32[256,2048]{1,0:T(8,128)} %get-tuple-element.300.grad_query, f32[256,3072]{1,0:T(8,128)} %get-tuple-element.301.raw, f32[256,128]{1,0:T(8,128)} %get-tuple-element.391.cosine, f32[256,128]{1,0:T(8,128)} %get-tuple-element.390.sine, ...), custom_call_target="tpu_custom_call" | custom-call | bytes 1024 | tf_op jit(solution)/shard_map/query_back/pallas_call | solution.py:1050
  643.2 27.9 %collective-permute-done.30 = bf16[256,1024]{1,0:T(8,128)(2,1)} collective-permute-done((bf16[256,1024]{1,0:T(8,128)(2,1)S(1)}, bf16[256,1024]{1,0:T(8,128)(2,1)}, u32[]{:S(2)}, u32[]{:S(2)}) %collective-permute-start.30) | collective-permute-done | bytes 524320 | tf_op jit(solution)/shard_map/ppermute | solution.py:1875
  671.1 2.4 convert_add_fusion.grad_kv
  673.6 1.8 add_convert_fusion
  675.5 1.8 add_convert_fusion.1
  677.3 1.9 collective-permute-start.32
  682.9 11.8 %key_back.1 = (bf16[2048,1024]{1,0:T(8,128)(2,1)}, f32[256,2048]{1,0:T(8,128)}, f32[1,256]{1,0:T(1,128)}, f32[1,2048]{1,0:T(1,128)}) custom-call(f32[256,1024]{1,0:T(8,128)} %convert_add_fusion.grad_kv, f32[256,3072]{1,0:T(8,128)} %get-tuple-element.301.raw, f32[256,128]{1,0:T(8,128)} %get-tuple-element.391.cosine, f32[256,128]{1,0:T(8,128)} %get-tuple-element.390.sine, ...), custom_call_target="tpu_custom_call" | custom-call | bytes 1024 | tf_op jit(solution)/shard_map/key_back/pallas_call | solution.py:1103
  696.9 5.5 concatenate.28
  702.4 7.6 collective-permute-done.33.refs_6_
  710.0 3.0 collective-permute-done.32.refs_5_
  712.9 124.0 %sum_all.1 = (f32[64,2048]{1,0:T(8,128)}, f32[64,1024]{1,0:T(8,128)}, f32[64,2048]{1,0:T(8,128)}, f32[64,768]{1,0:T(8,128)}, f32[8,128]{1,0:T(8,128)}, /*index=5...) custom-call(bf16[8,2,2,64,2048]{4,3,2,1,0:T(8,128)(2,1)} %bitcast.38, bf16[8,2,2,64,1024]{4,3,2,1,0:T(8,128)(2,1)} %bitcast.39, ...), custom_call_target="tpu_custom_call" | custom-call | bytes 24117248 | tf_op jit(solution)/shard_map/sum_all/pallas_call | solution.py:530
  840.1 1.5 fusion.10
  846.1 3.1 add_bitcast_fusion
  849.2 3.1 pad_maximum_fusion
  (175 shorter events, 60.8 us)
Async XLA Ops:
  0.6 5.4 copy-start.31
  0.7 12.1 %copy-start.27 = (bf16[64,2048]{1,0:T(8,128)(2,1)S(1)}, bf16[64,2048]{1,0:T(8,128)(2,1)}, u32[]{:S(2)}) copy-start(bf16[64,2048]{1,0:T(8,128)(2,1)} %param.20) | copy-start | bytes 786436
  0.7 12.1 %copy-start.28 = (bf16[64,1024]{1,0:T(8,128)(2,1)S(1)}, bf16[64,1024]{1,0:T(8,128)(2,1)}, u32[]{:S(2)}) copy-start(bf16[64,1024]{1,0:T(8,128)(2,1)} %param.19) | copy-start | bytes 393220
  2.8 134.9 %copy-start = (bf16[3,128,2048]{2,1,0:T(8,128)(2,1)}, bf16[3,128,2048]{2,1,0:T(8,128)(2,1)S(1)}, u32[]{:S(2)}) copy-start(bf16[3,128,2048]{2,1,0:T(8,128)(2,1)S(1)} %get-tuple-element.384.refs_1_.refs_7_) | copy-start | bytes 4718596
  2.8 134.9 %copy-start.1 = (bf16[3,128,2048]{2,1,0:T(8,128)(2,1)}, bf16[3,128,2048]{2,1,0:T(8,128)(2,1)S(1)}, u32[]{:S(2)}) copy-start(bf16[3,128,2048]{2,1,0:T(8,128)(2,1)S(1)} %get-tuple-element.385.refs_0_.refs_6_) | copy-start | bytes 4718596
  2.9 138.1 %collective-permute-start.1 = (bf16[3,128,2048]{2,1,0:T(8,128)(2,1)S(1)}, bf16[3,128,2048]{2,1,0:T(8,128)(2,1)}, u32[]{:S(2)}, u32[]{:S(2)}) collective-permute-start(bf16[3,128,2048]{2,1,0:T(8,128)(2,1)S(1)} %get-tuple-element.384.refs_1_.refs_7_), channel_id=1, source_target_pairs={{0,4},{8,0},{16,8},{24,16},{28,24},{20,28},{12,20},{4,12},{1,5},{9... | collective-permute-start | bytes 4718600 | tf_op jit(solution)/shard_map/ppermute | solution.py:57
  5.9 135.1 %collective-permute-start = (bf16[3,128,2048]{2,1,0:T(8,128)(2,1)S(1)}, bf16[3,128,2048]{2,1,0:T(8,128)(2,1)}, u32[]{:S(2)}, u32[]{:S(2)}) collective-permute-start(bf16[3,128,2048]{2,1,0:T(8,128)(2,1)S(1)} %get-tuple-element.385.refs_0_.refs_6_), channel_id=1, source_target_pairs={{0,8},{8,16},{16,24},{24,28},{28,20},{20,12},{12,4},{4,0},{1,9},{9... | collective-permute-start | bytes 4718600 | tf_op jit(solution)/shard_map/ppermute | solution.py:57
  141.0 36.9 %collective-permute-start.2 = (bf16[3,128,2048]{2,1,0:T(8,128)(2,1)}, bf16[3,128,2048]{2,1,0:T(8,128)(2,1)S(1)}, u32[]{:S(2)}, u32[]{:S(2)}) collective-permute-start(bf16[3,128,2048]{2,1,0:T(8,128)(2,1)} %collective-permute-done.refs_2_.up_w), channel_id=1, source_target_pairs={{0,8},{8,16},{16,24},{24,28},{28,20},{20,12},{12,4},{4,0},{1,9},{9... | collective-permute-start | bytes 4718600 | tf_op jit(solution)/shard_map/ppermute | solution.py:57
  141.6 36.6 %collective-permute-start.3 = (bf16[3,128,2048]{2,1,0:T(8,128)(2,1)}, bf16[3,128,2048]{2,1,0:T(8,128)(2,1)S(1)}, u32[]{:S(2)}, u32[]{:S(2)}) collective-permute-start(bf16[3,128,2048]{2,1,0:T(8,128)(2,1)} %collective-permute-done.1.refs_3_.down_w), channel_id=1, source_target_pairs={{0,4},{8,0},{16,8},{24,16},{28,24},{20,28},{12,20},{4,12},{1,5},{9... | collective-permute-start | bytes 4718600 | tf_op jit(solution)/shard_map/ppermute | solution.py:57
  177.9 23.2 %copy-start.6 = (bf16[3,128,2048]{2,1,0:T(8,128)(2,1)}, bf16[3,128,2048]{2,1,0:T(8,128)(2,1)S(1)}, u32[]{:S(2)}) copy-start(bf16[3,128,2048]{2,1,0:T(8,128)(2,1)S(1)} %collective-permute-done.2.refs_4_.refs_0_) | copy-start | bytes 4718596
  178.2 23.0 %copy-start.7 = (bf16[3,128,2048]{2,1,0:T(8,128)(2,1)}, bf16[3,128,2048]{2,1,0:T(8,128)(2,1)S(1)}, u32[]{:S(2)}) copy-start(bf16[3,128,2048]{2,1,0:T(8,128)(2,1)S(1)} %collective-permute-done.3.refs_5_.refs_1_) | copy-start | bytes 4718596
  180.4 16.1 %collective-permute-start.7 = (bf16[256,1024]{1,0:T(8,128)(2,1)}, bf16[256,1024]{1,0:T(8,128)(2,1)}, u32[]{:S(2)}, u32[]{:S(2)}) collective-permute-start(bf16[256,1024]{1,0:T(8,128)(2,1)} %slice.79), channel_id=1, source_target_pairs={{0,4},{4,8},{8,12},{12,20},{1,5},{5,9},{9,13},{13,21},{2,6},{6,10}... | collective-permute-start | bytes 1572872 | tf_op jit(solution)/shard_map/ppermute | solution.py:1712
  184.6 11.9 %collective-permute-start.6 = (bf16[256,1024]{1,0:T(8,128)(2,1)}, bf16[256,1024]{1,0:T(8,128)(2,1)}, u32[]{:S(2)}, u32[]{:S(2)}) collective-permute-start(bf16[256,1024]{1,0:T(8,128)(2,1)} %slice.79), channel_id=1, source_target_pairs={{12,16},{13,17},{14,18},{15,19}} | collective-permute-start | bytes 1572872 | tf_op jit(solution)/shard_map/ppermute | solution.py:1711
  186.1 35.5 %collective-permute-start.4 = (bf16[3,128,2048]{2,1,0:T(8,128)(2,1)S(1)}, bf16[3,128,2048]{2,1,0:T(8,128)(2,1)}, u32[]{:S(2)}, u32[]{:S(2)}) collective-permute-start(bf16[3,128,2048]{2,1,0:T(8,128)(2,1)S(1)} %collective-permute-done.2.refs_4_.refs_0_), channel_id=1, source_target_pairs={{0,8},{8,16},{16,24},{24,28},{28,20},{20,12},{12,4},{4,0},{1,9},{9... | collective-permute-start | bytes 4718600 | tf_op jit(solution)/shard_map/ppermute | solution.py:57
  186.9 41.6 %collective-permute-start.5 = (bf16[3,128,2048]{2,1,0:T(8,128)(2,1)S(1)}, bf16[3,128,2048]{2,1,0:T(8,128)(2,1)}, u32[]{:S(2)}, u32[]{:S(2)}) collective-permute-start(bf16[3,128,2048]{2,1,0:T(8,128)(2,1)S(1)} %collective-permute-done.3.refs_5_.refs_1_), channel_id=1, source_target_pairs={{0,4},{8,0},{16,8},{24,16},{28,24},{20,28},{12,20},{4,12},{1,5},{9... | collective-permute-start | bytes 4718600 | tf_op jit(solution)/shard_map/ppermute | solution.py:57
  198.4 1.5 collective-permute-start.8
  201.2 2.0 collective-permute-start.9
  228.5 35.9 %collective-permute-start.10 = (bf16[3,128,2048]{2,1,0:T(8,128)(2,1)}, bf16[3,128,2048]{2,1,0:T(8,128)(2,1)}, u32[]{:S(2)}, u32[]{:S(2)}) collective-permute-start(bf16[3,128,2048]{2,1,0:T(8,128)(2,1)} %collective-permute-done.4.refs_6_.refs_2_), channel_id=1, source_target_pairs={{0,8},{8,16},{16,24},{24,28},{28,20},{20,12},{12,4},{4,0},{1,9},{9... | collective-permute-start | bytes 4718600 | tf_op jit(solution)/shard_map/ppermute | solution.py:57
  228.5 44.2 %collective-permute-start.11 = (bf16[3,128,2048]{2,1,0:T(8,128)(2,1)}, bf16[3,128,2048]{2,1,0:T(8,128)(2,1)S(1)}, u32[]{:S(2)}, u32[]{:S(2)}) collective-permute-start(bf16[3,128,2048]{2,1,0:T(8,128)(2,1)} %collective-permute-done.5.refs_7_.refs_3_), channel_id=1, source_target_pairs={{0,4},{8,0},{16,8},{24,16},{28,24},{20,28},{12,20},{4,12},{1,5},{9... | collective-permute-start | bytes 4718600 | tf_op jit(solution)/shard_map/ppermute | solution.py:57
  273.8 36.1 %collective-permute-start.12 = (bf16[3,128,2048]{2,1,0:T(8,128)(2,1)}, bf16[3,128,2048]{2,1,0:T(8,128)(2,1)S(1)}, u32[]{:S(2)}, u32[]{:S(2)}) collective-permute-start(bf16[3,128,2048]{2,1,0:T(8,128)(2,1)} %collective-permute-done.10.refs_8_.refs_4_), channel_id=1, source_target_pairs={{0,8},{8,16},{16,24},{24,28},{28,20},{20,12},{12,4},{4,0},{1,9},{9... | collective-permute-start | bytes 4718600 | tf_op jit(solution)/shard_map/ppermute | solution.py:57
  276.3 36.8 %collective-permute-start.13 = (bf16[3,128,2048]{2,1,0:T(8,128)(2,1)}, bf16[3,128,2048]{2,1,0:T(8,128)(2,1)S(1)}, u32[]{:S(2)}, u32[]{:S(2)}) collective-permute-start(bf16[3,128,2048]{2,1,0:T(8,128)(2,1)} %copy-done.8), channel_id=1, source_target_pairs={{0,4},{8,0},{16,8},{24,16},{28,24},{20,28},{12,20},{4,12},{1,5},{9... | collective-permute-start | bytes 4718600 | tf_op jit(solution)/shard_map/ppermute | solution.py:57
  304.8 46.4 %copy-start.29 = (s32[2,4]{1,0:T(2,128)S(1)}, s32[2,4]{1,0:T(2,128)}, u32[]{:S(2)}) copy-start(s32[2,4]{1,0:T(2,128)} %param.17) | copy-start | bytes 100
  310.0 5.6 copy-start.2
  313.0 2.5 copy-start.3
  313.0 34.8 %collective-permute-start.14 = (bf16[3,128,2048]{2,1,0:T(8,128)(2,1)S(1)}, bf16[3,128,2048]{2,1,0:T(8,128)(2,1)}, u32[]{:S(2)}, u32[]{:S(2)}) collective-permute-start(bf16[3,128,2048]{2,1,0:T(8,128)(2,1)S(1)} %collective-permute-done.12.refs_10_.refs_0_), channel_id=1, source_target_pairs={{0,8},{8,16},{16,24},{24,28},{28,20},{20,12},{12,4},{4,0},{1,9},{9... | collective-permute-start | bytes 4718600 | tf_op jit(solution)/shard_map/ppermute | solution.py:57
  314.8 34.4 %collective-permute-start.15 = (bf16[3,128,2048]{2,1,0:T(8,128)(2,1)S(1)}, bf16[3,128,2048]{2,1,0:T(8,128)(2,1)}, u32[]{:S(2)}, u32[]{:S(2)}) collective-permute-start(bf16[3,128,2048]{2,1,0:T(8,128)(2,1)S(1)} %collective-permute-done.13.refs_11_.refs_1_), channel_id=1, source_target_pairs={{0,4},{8,0},{16,8},{24,16},{28,24},{20,28},{12,20},{4,12},{1,5},{9... | collective-permute-start | bytes 4718600 | tf_op jit(solution)/shard_map/ppermute | solution.py:57
  349.2 33.1 %collective-permute-start.16 = (bf16[3,128,2048]{2,1,0:T(8,128)(2,1)}, bf16[3,128,2048]{2,1,0:T(8,128)(2,1)S(1)}, u32[]{:S(2)}, u32[]{:S(2)}) collective-permute-start(bf16[3,128,2048]{2,1,0:T(8,128)(2,1)} %collective-permute-done.14.refs_0_.refs_2_), channel_id=1, source_target_pairs={{0,8},{8,16},{16,24},{24,28},{28,20},{20,12},{12,4},{4,0},{1,9},{9... | collective-permute-start | bytes 4718600 | tf_op jit(solution)/shard_map/ppermute | solution.py:57
  350.1 33.1 %collective-permute-start.17 = (bf16[3,128,2048]{2,1,0:T(8,128)(2,1)}, bf16[3,128,2048]{2,1,0:T(8,128)(2,1)S(1)}, u32[]{:S(2)}, u32[]{:S(2)}) collective-permute-start(bf16[3,128,2048]{2,1,0:T(8,128)(2,1)} %collective-permute-done.15.refs_1_.refs_3_), channel_id=1, source_target_pairs={{0,4},{8,0},{16,8},{24,16},{28,24},{20,28},{12,20},{4,12},{1,5},{9... | collective-permute-start | bytes 4718600 | tf_op jit(solution)/shard_map/ppermute | solution.py:57
  382.3 2.4 copy-start.4
  383.3 1.4 copy-start.5
  463.4 36.9 %collective-permute-start.18 = (bf16[3,128,2048]{2,1,0:T(8,128)(2,1)}, bf16[3,128,2048]{2,1,0:T(8,128)(2,1)S(1)}, u32[]{:S(2)}, u32[]{:S(2)}) collective-permute-start(bf16[3,128,2048]{2,1,0:T(8,128)(2,1)} %get-tuple-element.213), channel_id=1, source_target_pairs={{0,8},{8,16},{16,24},{24,28},{28,20},{20,12},{12,4},{4,0},{1,9},{9... | collective-permute-start | bytes 4718600 | tf_op jit(solution)/shard_map/ppermute | solution.py:57
  464.1 36.6 %collective-permute-start.19 = (bf16[3,128,2048]{2,1,0:T(8,128)(2,1)}, bf16[3,128,2048]{2,1,0:T(8,128)(2,1)S(1)}, u32[]{:S(2)}, u32[]{:S(2)}) collective-permute-start(bf16[3,128,2048]{2,1,0:T(8,128)(2,1)} %get-tuple-element.214), channel_id=1, source_target_pairs={{0,4},{8,0},{16,8},{24,16},{28,24},{20,28},{12,20},{4,12},{1,5},{9... | collective-permute-start | bytes 4718600 | tf_op jit(solution)/shard_map/ppermute | solution.py:57
  500.7 3.6 copy-start.20
  502.9 37.5 %collective-permute-start.21 = (bf16[3,128,2048]{2,1,0:T(8,128)(2,1)S(1)}, bf16[3,128,2048]{2,1,0:T(8,128)(2,1)S(1)}, u32[]{:S(2)}, u32[]{:S(2)}) collective-permute-start(bf16[3,128,2048]{2,1,0:T(8,128)(2,1)S(1)} %add_convert_fusion.8), channel_id=1, source_target_pairs={{0,4},{8,0},{16,8},{24,16},{28,24},{20,28},{12,20},{4,12},{1,5},{9... | collective-permute-start | bytes 4718600 | tf_op jit(solution)/shard_map/ppermute | solution.py:57
  504.9 35.4 %collective-permute-start.20 = (bf16[3,128,2048]{2,1,0:T(8,128)(2,1)S(1)}, bf16[3,128,2048]{2,1,0:T(8,128)(2,1)S(1)}, u32[]{:S(2)}, u32[]{:S(2)}) collective-permute-start(bf16[3,128,2048]{2,1,0:T(8,128)(2,1)S(1)} %add_convert_fusion.9), channel_id=1, source_target_pairs={{0,8},{8,16},{16,24},{24,28},{28,20},{20,12},{12,4},{4,0},{1,9},{9... | collective-permute-start | bytes 4718600 | tf_op jit(solution)/shard_map/ppermute | solution.py:57
  513.1 27.3 %copy-start.19 = (bf16[3,128,2048]{2,1,0:T(8,128)(2,1)S(1)}, bf16[3,128,2048]{2,1,0:T(8,128)(2,1)}, u32[]{:S(2)}) copy-start(bf16[3,128,2048]{2,1,0:T(8,128)(2,1)} %get-tuple-element.251) | copy-start | bytes 4718596
  540.3 2.1 copy-start.17
  541.0 39.7 %collective-permute-start.23 = (bf16[3,128,2048]{2,1,0:T(8,128)(2,1)S(1)}, bf16[3,128,2048]{2,1,0:T(8,128)(2,1)S(1)}, u32[]{:S(2)}, u32[]{:S(2)}) collective-permute-start(bf16[3,128,2048]{2,1,0:T(8,128)(2,1)S(1)} %add_convert_fusion.6), channel_id=1, source_target_pairs={{0,4},{8,0},{16,8},{24,16},{28,24},{20,28},{12,20},{4,12},{1,5},{9... | collective-permute-start | bytes 4718600 | tf_op jit(solution)/shard_map/ppermute | solution.py:57
  543.0 37.7 %collective-permute-start.22 = (bf16[3,128,2048]{2,1,0:T(8,128)(2,1)S(1)}, bf16[3,128,2048]{2,1,0:T(8,128)(2,1)S(1)}, u32[]{:S(2)}, u32[]{:S(2)}) collective-permute-start(bf16[3,128,2048]{2,1,0:T(8,128)(2,1)S(1)} %add_convert_fusion.7), channel_id=1, source_target_pairs={{0,8},{8,16},{16,24},{24,28},{28,20},{20,12},{12,4},{4,0},{1,9},{9... | collective-permute-start | bytes 4718600 | tf_op jit(solution)/shard_map/ppermute | solution.py:57
  580.8 3.6 copy-start.18
  583.0 36.7 %collective-permute-start.25 = (bf16[3,128,2048]{2,1,0:T(8,128)(2,1)S(1)}, bf16[3,128,2048]{2,1,0:T(8,128)(2,1)S(1)}, u32[]{:S(2)}, u32[]{:S(2)}) collective-permute-start(bf16[3,128,2048]{2,1,0:T(8,128)(2,1)S(1)} %add_convert_fusion.4), channel_id=1, source_target_pairs={{0,4},{8,0},{16,8},{24,16},{28,24},{20,28},{12,20},{4,12},{1,5},{9... | collective-permute-start | bytes 4718600 | tf_op jit(solution)/shard_map/ppermute | solution.py:57
  585.0 36.4 %collective-permute-start.24 = (bf16[3,128,2048]{2,1,0:T(8,128)(2,1)S(1)}, bf16[3,128,2048]{2,1,0:T(8,128)(2,1)S(1)}, u32[]{:S(2)}, u32[]{:S(2)}) collective-permute-start(bf16[3,128,2048]{2,1,0:T(8,128)(2,1)S(1)} %add_convert_fusion.5), channel_id=1, source_target_pairs={{0,8},{8,16},{16,24},{24,28},{28,20},{20,12},{12,4},{4,0},{1,9},{9... | collective-permute-start | bytes 4718600 | tf_op jit(solution)/shard_map/ppermute | solution.py:57
  613.4 1.9 copy-start.12
  615.5 2.0 collective-permute-start.26
  617.8 4.5 copy-start.16
  621.5 2.5 copy-start.15
  621.5 4.2 collective-permute-start.29
  622.9 50.6 %collective-permute-start.28 = (bf16[3,128,2048]{2,1,0:T(8,128)(2,1)S(1)}, bf16[3,128,2048]{2,1,0:T(8,128)(2,1)S(1)}, u32[]{:S(2)}, u32[]{:S(2)}) collective-permute-start(bf16[3,128,2048]{2,1,0:T(8,128)(2,1)S(1)} %add_convert_fusion.2), channel_id=1, source_target_pairs={{0,4},{8,0},{16,8},{24,16},{28,24},{20,28},{12,20},{4,12},{1,5},{9... | collective-permute-start | bytes 4718600 | tf_op jit(solution)/shard_map/ppermute | solution.py:57
  624.5 49.0 %collective-permute-start.27 = (bf16[3,128,2048]{2,1,0:T(8,128)(2,1)S(1)}, bf16[3,128,2048]{2,1,0:T(8,128)(2,1)S(1)}, u32[]{:S(2)}, u32[]{:S(2)}) collective-permute-start(bf16[3,128,2048]{2,1,0:T(8,128)(2,1)S(1)} %add_convert_fusion.3), channel_id=1, source_target_pairs={{0,8},{8,16},{16,24},{24,28},{28,20},{20,12},{12,4},{4,0},{1,9},{9... | collective-permute-start | bytes 4718600 | tf_op jit(solution)/shard_map/ppermute | solution.py:57
  625.8 17.4 %collective-permute-start.31 = (bf16[256,1024]{1,0:T(8,128)(2,1)S(1)}, bf16[256,1024]{1,0:T(8,128)(2,1)}, u32[]{:S(2)}, u32[]{:S(2)}) collective-permute-start(bf16[256,1024]{1,0:T(8,128)(2,1)S(1)} %add_convert_fusion.10), channel_id=1, source_target_pairs={{16,12},{17,13},{18,14},{19,15}} | collective-permute-start | bytes 1572872 | tf_op jit(solution)/shard_map/ppermute | solution.py:1876
  627.4 43.8 %collective-permute-start.30 = (bf16[256,1024]{1,0:T(8,128)(2,1)S(1)}, bf16[256,1024]{1,0:T(8,128)(2,1)}, u32[]{:S(2)}, u32[]{:S(2)}) collective-permute-start(bf16[256,1024]{1,0:T(8,128)(2,1)S(1)} %add_convert_fusion.10), channel_id=1, source_target_pairs={{4,0},{8,4},{12,8},{20,12},{5,1},{9,5},{13,9},{21,13},{6,2},{10,6}... | collective-permute-start | bytes 1572872 | tf_op jit(solution)/shard_map/ppermute | solution.py:1875
  643.2 30.4 %copy-start.14 = (bf16[3,128,2048]{2,1,0:T(8,128)(2,1)S(1)}, bf16[3,128,2048]{2,1,0:T(8,128)(2,1)}, u32[]{:S(2)}) copy-start(bf16[3,128,2048]{2,1,0:T(8,128)(2,1)} %get-tuple-element.309) | copy-start | bytes 4718596
  673.6 1.9 copy-start.13
  675.4 4.7 copy-start.22
  675.4 34.6 %collective-permute-start.33 = (bf16[3,128,2048]{2,1,0:T(8,128)(2,1)}, bf16[3,128,2048]{2,1,0:T(8,128)(2,1)}, u32[]{:S(2)}, u32[]{:S(2)}) collective-permute-start(bf16[3,128,2048]{2,1,0:T(8,128)(2,1)} %add_convert_fusion), channel_id=1, source_target_pairs={{0,4},{8,0},{16,8},{24,16},{28,24},{20,28},{12,20},{4,12},{1,5},{9... | collective-permute-start | bytes 4718600 | tf_op jit(solution)/shard_map/ppermute | solution.py:57
  677.3 35.6 %collective-permute-start.32 = (bf16[3,128,2048]{2,1,0:T(8,128)(2,1)}, bf16[3,128,2048]{2,1,0:T(8,128)(2,1)}, u32[]{:S(2)}, u32[]{:S(2)}) collective-permute-start(bf16[3,128,2048]{2,1,0:T(8,128)(2,1)} %add_convert_fusion.1), channel_id=1, source_target_pairs={{0,8},{8,16},{16,24},{24,28},{28,20},{20,12},{12,4},{4,0},{1,9},{9... | collective-permute-start | bytes 4718600 | tf_op jit(solution)/shard_map/ppermute | solution.py:57
  680.6 2.2 copy-start.21
  682.8 12.5 %copy-start.30 = (f32[1,256]{1,0:T(1,128)S(1)}, f32[1,256]{1,0:T(1,128)}, u32[]{:S(2)}) copy-start(f32[1,256]{1,0:T(1,128)} %get-tuple-element.326) | copy-start | bytes 3076
  712.9 133.1 %copy-start.10 = (bf16[3,128,2048]{2,1,0:T(8,128)(2,1)S(1)}, bf16[3,128,2048]{2,1,0:T(8,128)(2,1)}, u32[]{:S(2)}) copy-start(bf16[3,128,2048]{2,1,0:T(8,128)(2,1)} %get-tuple-element.345) | copy-start | bytes 4718596
  712.9 133.1 %copy-start.11 = (bf16[3,128,2048]{2,1,0:T(8,128)(2,1)S(1)}, bf16[3,128,2048]{2,1,0:T(8,128)(2,1)}, u32[]{:S(2)}) copy-start(bf16[3,128,2048]{2,1,0:T(8,128)(2,1)} %get-tuple-element.347) | copy-start | bytes 4718596
  849.2 3.1 copy-start.9
  852.4 2.0 copy-start.24
  853.7 1.5 copy-start.26
  853.7 2.2 copy-start.23
  (2 other events, 2.5 us)

commit v10 on v9

--- a/solution.py
+++ b/solution.py
@@ -1277,11 +1277,8 @@
         core_copy(1, at).wait_recv()
         pair_low[pl.ds(at * cut, cut)] = (own[there] + core_in[there].astype(F32)).astype(BF16)
         x_copy(at).start()
-    for at in range(CUTS):
-        here = pl.ds(at * cut, cut)
-        next_piece(CUTS + at)
-        core_copy(0, at).wait_recv()
-        out[here] = own[here] + core_in[here].astype(F32)
+    for number in range(CUTS + FLYING, 2 * CUTS):
+        core_copy(*pieces[number]).start()
     if steps:
         for load in loads:
             load.wait()
@@ -1301,10 +1298,12 @@
                 store(step, way).start()
     for at in range(CUTS):
         here = pl.ds(at * cut, cut)
+        core_copy(0, at).wait_recv()
         x_copy(at).wait_recv()
-        out[here] += x_in[here].astype(F32)
+        out[here] = own[here] + core_in[here].astype(F32) + x_in[here].astype(F32)
     for at in range(CUTS):
         x_copy(at).wait_send()
+        core_copy(0, at).wait_send()
     for step in range(steps):
         for way in range(2):
             store(step, way).wait()

time: 867 us -> 864 us (level)
  transfers between devices with their start and end apart: 34 -> 34, of which waited for: 22 -> 23; matrix products, arithmetic and copies ran while one was open for 6% -> 6% of each run, Pallas kernels for 45% -> 44%
where the time goes in v10:
time: 864 us; the launch traced here: 855 us
  Pallas kernels  583 us (67%)
  waiting for transfers between devices  144 us (17%)
  local copies, waits for them, and re-layouts  50.1 us (6%)
  starting transfers between devices  41.8 us (5%)
  other arithmetic  32.7 us (4%)
    pallas_call x1, Pallas kernels, sum_all(): pl.pallas_call(functools.partial(sum_kernel, chips, streams, (count, 5, c...  126 us
    pallas_call x1, Pallas kernels, gather_all(): pl.pallas_call(functools.partial(gather_kernel, chips, streams), out_shap...  123 us
    ppermute x26, waiting for transfers between devices, ring(): return lax.ppermute(value, 'zy', ring_pairs(lax.axis_size('zy'), by))  104 us
    pallas_call x1, Pallas kernels, middle(): pl.pallas_call(functools.partial(middle_kernel, steps), out_shape=[shape(...  60.6 us
    pallas_call x2, Pallas kernels, ffn_backward(): piece(functools.partial(ffn_backward_kernel, steps, add, last), 'ffn_back...  49.6 us
    pallas_call x2, Pallas kernels, ffn_forward(): piece(functools.partial(ffn_forward_kernel, steps, add), 'ffn_forward', (...  43.6 us
    pallas_call x1, Pallas kernels, sum_of_four(): pl.pallas_call(functools.partial(gather_sum_kernel, steps), out_shape=[ja...  32 us
    ppermute x26, starting transfers between devices, ring(): return lax.ppermute(value, 'zy', ring_pairs(lax.axis_size('zy'), by))  30.7 us
  transfers between devices with their start and end apart: 34, of which 23 were waited for; matrix products, arithmetic and copies ran while one was open for 6% of the time, Pallas kernels for 44%

profile of v10, /device:TPU:0, one launch (start us, length us, event | category | flops | bytes accessed | tf_op | source)
XLA Modules:
  0.0 855.2 jit_solution(12837303636488707149)
XLA Ops:
  0.7 2.2 fusion.9
  2.9 3.0 collective-permute-start.1
  12.8 2.0 concatenate.23.shard
  14.8 122.9 %gather_all.1.weight.w_out.lleft.lright = bf16[2048,5888]{1,0:T(8,128)(2,1)} custom-call(bf16[64,5888]{1,0:T(8,128)(2,1)} %concatenate.23.shard), custom_call_target="tpu_custom_call" | custom-call | bytes 48234496 | tf_op jit(solution)/shard_map/gather_all/pallas_call | solution.py:220
  137.7 2.0 slice.75
  141.6 1.5 collective-permute-start.3
  146.0 13.5 %make_qkv.1 = (bf16[256,2048]{1,0:T(8,128)(2,1)}, f32[256,3072]{1,0:T(8,128)}, bf16[256,3072]{1,0:T(8,128)(2,1)}) custom-call(bf16[256,2048]{1,0:T(8,128)(2,1)} %bitcast.34, f32[8,2048]{1,0:T(8,128)} %pad_convert_fusion.gains.refs_9_, f32[2,256]{1,0:T(2,128)} %reshape.117.head_gain, f32[256,128]{1,0:T(8,128)} %get-tuple-element.391.cosine, ...), custom_call_target="tpu_custom_call" | custom-call | bytes 1024 | tf_op jit(solution)/shard_map/make_qkv/pallas_call | solution.py:609
  159.4 18.5 %collective-permute-done.2.refs_4_.refs_0_ = bf16[3,128,2048]{2,1,0:T(8,128)(2,1)S(1)} collective-permute-done((bf16[3,128,2048]{2,1,0:T(8,128)(2,1)}, bf16[3,128,2048]{2,1,0:T(8,128)(2,1)S(1)}, u32[]{:S(2)}, u32[]{:S(2)}) %collective-permute-start.2) | collective-permute-done | bytes 1572896 | tf_op jit(solution)/shard_map/ppermute | solution.py:57
  178.2 2.3 slice.79
  180.4 4.2 collective-permute-start.7
  184.6 1.5 collective-permute-start.6
  188.1 8.4 collective-permute-done.7
  196.5 1.9 broadcast_select_fusion.1
  198.4 1.5 collective-permute-start.8
  201.3 1.9 collective-permute-done.9
  203.2 2.3 pad_maximum_fusion.1.key.value
  205.5 16.1 %collective-permute-done.4.refs_6_.refs_2_ = bf16[3,128,2048]{2,1,0:T(8,128)(2,1)} collective-permute-done((bf16[3,128,2048]{2,1,0:T(8,128)(2,1)S(1)}, bf16[3,128,2048]{2,1,0:T(8,128)(2,1)}, u32[]{:S(2)}, u32[]{:S(2)}) %collective-permute-start.4) | collective-permute-done | bytes 1572896 | tf_op jit(solution)/shard_map/ppermute | solution.py:57
  221.6 6.9 collective-permute-done.5.refs_7_.refs_3_
  228.5 2.6 collective-permute-start.11
  232.3 19.5 %attend.1 = (bf16[256,2048]{1,0:T(8,128)(2,1)}, f32[256,2048]{1,0:T(8,128)}, f32[256,2048]{1,0:T(8,128)}, bf16[256,2048]{1,0:T(8,128)(2,1)}, bf16[256,128]{1,0:T(8,128)(2,1)}) custom-call(bf16[256,2048]{1,0:T(8,128)(2,1)} %bitcast.35, f32[8,2048]{1,0:T(8,128)} %pad_convert_fusion.gains.refs_9_, bf16[256,2048]{1,0:T(8,128)(2,1)} %get-tuple-element.190.low, ...), custom_call_target="tpu_custom_call" | custom-call | bytes 1024 | tf_op jit(solution)/shard_map/attend/pallas_call | solution.py:673
  251.8 12.6 %collective-permute-done.10.refs_8_.refs_4_ = bf16[3,128,2048]{2,1,0:T(8,128)(2,1)} collective-permute-done((bf16[3,128,2048]{2,1,0:T(8,128)(2,1)}, bf16[3,128,2048]{2,1,0:T(8,128)(2,1)}, u32[]{:S(2)}, u32[]{:S(2)}) %collective-permute-start.10) | collective-permute-done | bytes 1572896 | tf_op jit(solution)/shard_map/ppermute | solution.py:57
  264.4 8.3 collective-permute-done.11.refs_9_.refs_5_
  273.8 2.5 collective-permute-start.12
  277.4 27.5 %spread_rows.1.refs_12_.refs_3_.rows.refs_2_ = bf16[1024,2048]{1,0:T(8,128)(2,1)} custom-call(bf16[256,2048]{1,0:T(8,128)(2,1)} %get-tuple-element.195.own), custom_call_target="tpu_custom_call" | custom-call | bytes 1024 | tf_op jit(solution)/shard_map/spread_rows/pallas_call | solution.py:1200
  304.8 5.1 collective-permute-done.12.refs_10_.refs_0_
  310.0 3.1 collective-permute-done.13.refs_11_.refs_1_
  313.0 1.7 collective-permute-start.14
  315.5 31.0 %ffn_forward.2 = (f32[1024,2048]{1,0:T(8,128)}, f32[1024,256]{1,0:T(8,128)}, f32[1024,256]{1,0:T(8,128)}, f32[1024,256]{1,0:T(8,128)}, f32[1024,256]{1,0:T(8,128...) custom-call(bf16[3,128,2048]{2,1,0:T(8,128)(2,1)} %copy-done.1, ...), custom_call_target="tpu_custom_call" | custom-call | bytes 1024 | tf_op jit(solution)/shard_map/ffn_forward/pallas_call | solution.py:787
  352.5 3.0 fusion.8
  355.5 2.4 reshape.107.refs_11_
  359.2 12.6 %ffn_forward.3 = (f32[1024,2048]{1,0:T(8,128)}, f32[1024,256]{1,0:T(8,128)}, f32[1024,256]{1,0:T(8,128)}, bf16[1024,256]{1,0:T(8,128)(2,1)}) custom-call(bf16[3,128,2048]{2,1,0:T(8,128)(2,1)} %collective-permute-done.14.refs_0_.refs_2_, bf16[3,128,2048]{2,1,0:T(8,128)(2,1)} %collective-permute-done.15.refs_1_.refs_3_, ...), custom_call_target="tpu_custom_call" | custom-call | bytes 1024 | tf_op jit(solution)/shard_map/ffn_forward/pallas_call | solution.py:787
  371.8 10.4 %collective-permute-done.16.refs_0_.refs_4_ = bf16[3,128,2048]{2,1,0:T(8,128)(2,1)S(1)} collective-permute-done((bf16[3,128,2048]{2,1,0:T(8,128)(2,1)}, bf16[3,128,2048]{2,1,0:T(8,128)(2,1)S(1)}, u32[]{:S(2)}, u32[]{:S(2)}) %collective-permute-start.16) | collective-permute-done | bytes 1572896 | tf_op jit(solution)/shard_map/ppermute | solution.py:57
  384.7 60.6 %middle.1 = (f32[256,2048]{1,0:T(8,128)}, f32[256,2048]{1,0:T(8,128)}, f32[256,256]{1,0:T(8,128)}, bf16[1024,2048]{1,0:T(8,128)(2,1)}, bf16[2048,256]{1,0:T(8,12...) custom-call(bf16[3,128,2048]{2,1,0:T(8,128)(2,1)} %copy-done.4, ...), custom_call_target="tpu_custom_call" | custom-call | bytes 1024 | tf_op jit(solution)/shard_map/middle/pallas_call | solution.py:1530
  445.2 18.1 %first_backward.1 = (f32[1024,2048]{1,0:T(8,128)}, bf16[1024,256]{1,0:T(8,128)(2,1)}, bf16[1024,256]{1,0:T(8,128)(2,1)}, bf16[3,128,2048]{2,1,0:T(8,128)(2,1)}, bf16[3,128,2048]{2,1,0:T(8,128)(2,1)}) custom-call(bf16[3,128,2048]{2,1,0:T(8,128)(2,1)} %collective-permute-done.refs_2_.up_w, bf16[3,128,2048]{2,1,0:T(8,128)(2,1)} %collective-permute-done.1.refs_3_.down_w, ...), custom_call_target="tpu_custom_call" | custom-call | bytes 1024 | tf_op jit(solution)/shard_map/first_backward/pallas_call | solution.py:882
  465.4 22.4 %ffn_backward.2 = (f32[1024,2048]{1,0:T(8,128)}, bf16[1024,256]{1,0:T(8,128)(2,1)}, bf16[1024,256]{1,0:T(8,128)(2,1)}, bf16[1024,256]{1,0:T(8,128)(2,1)}, bf16[1...) custom-call(bf16[3,128,2048]{2,1,0:T(8,128)(2,1)} %copy-done.6, ...), custom_call_target="tpu_custom_call" | custom-call | bytes 1024 | tf_op jit(solution)/shard_map/ffn_backward/pallas_call | solution.py:834
  487.9 7.5 unit_grads.2
  495.4 4.9 collective-permute-done.18
  500.7 2.2 add_convert_fusion.8
  502.9 1.4 collective-permute-start.21
  505.6 7.5 unit_grads.3
  513.1 27.2 %ffn_backward.3 = (f32[512,2048]{1,0:T(8,128)}, bf16[512,2048]{1,0:T(8,128)(2,1)}, bf16[1024,256]{1,0:T(8,128)(2,1)}, bf16[1024,256]{1,0:T(8,128)(2,1)}, bf16[10...) custom-call(bf16[3,128,2048]{2,1,0:T(8,128)(2,1)} %copy-done.2, ...), custom_call_target="tpu_custom_call" | custom-call | bytes 1024 | tf_op jit(solution)/shard_map/ffn_backward/pallas_call | solution.py:834
  543.9 32.0 %gather_sum.1 = (f32[256,2048]{1,0:T(8,128)}, bf16[3,128,2048]{2,1,0:T(8,128)(2,1)}, bf16[3,128,2048]{2,1,0:T(8,128)(2,1)}, bf16[3,128,2048]{2,1,0:T(8,128)(2,1)...) custom-call(f32[512,2048]{1,0:T(8,128)} %get-tuple-element.252.refs_, ...), custom_call_target="tpu_custom_call" | custom-call | bytes 1024 | tf_op jit(solution)/shard_map/gather_sum/pallas_call | solution.py:1327
  576.0 1.9 collective-permute-done.22
  578.0 2.2 add_convert_fusion.4
  582.9 27.7 %attend_back.1 = (f32[256,2048]{1,0:T(8,128)}, bf16[256,128]{1,0:T(8,128)(2,1)}, f32[8,2048]{1,0:T(8,128)}, f32[2048,128]{1,0:T(8,128)}, f32[2048,128]{1,0:T(8,1...) custom-call(f32[8,2048]{1,0:T(8,128)} %pad_convert_fusion.gains.refs_9_, ...), custom_call_target="tpu_custom_call" | custom-call | bytes 1024 | tf_op jit(solution)/shard_map/attend_back/pallas_call | solution.py:972
  610.7 1.7 constant_dynamic-update-slice_fusion.1
  612.8 1.9 collective-permute-done.26
  615.0 1.6 collective-permute-done.24
  621.1 1.5 collective-permute-start.31
  622.6 1.5 collective-permute-start.30
  624.1 14.4 %query_back.1 = (bf16[2048,2048]{1,0:T(8,128)(2,1)}, f32[256,2048]{1,0:T(8,128)}, f32[1,256]{1,0:T(1,128)}) custom-call(f32[256,2048]{1,0:T(8,128)} %get-tuple-element.300.grad_query, f32[256,3072]{1,0:T(8,128)} %get-tuple-element.301.raw, f32[256,128]{1,0:T(8,128)} %get-tuple-element.391.cosine, f32[256,128]{1,0:T(8,128)} %get-tuple-element.390.sine, ...), custom_call_target="tpu_custom_call" | custom-call | bytes 1024 | tf_op jit(solution)/shard_map/query_back/pallas_call | solution.py:1050
  638.5 27.7 %collective-permute-done.30 = bf16[256,1024]{1,0:T(8,128)(2,1)} collective-permute-done((bf16[256,1024]{1,0:T(8,128)(2,1)S(1)}, bf16[256,1024]{1,0:T(8,128)(2,1)}, u32[]{:S(2)}, u32[]{:S(2)}) %collective-permute-start.30) | collective-permute-done | bytes 524320 | tf_op jit(solution)/shard_map/ppermute | solution.py:1874
  666.2 2.4 convert_add_fusion.grad_kv
  668.6 1.8 add_convert_fusion
  670.5 1.8 add_convert_fusion.1
  672.3 1.9 collective-permute-start.32
  677.9 11.8 %key_back.1 = (bf16[2048,1024]{1,0:T(8,128)(2,1)}, f32[256,2048]{1,0:T(8,128)}, f32[1,256]{1,0:T(1,128)}, f32[1,2048]{1,0:T(1,128)}) custom-call(f32[256,1024]{1,0:T(8,128)} %convert_add_fusion.grad_kv, f32[256,3072]{1,0:T(8,128)} %get-tuple-element.301.raw, f32[256,128]{1,0:T(8,128)} %get-tuple-element.391.cosine, f32[256,128]{1,0:T(8,128)} %get-tuple-element.390.sine, ...), custom_call_target="tpu_custom_call" | custom-call | bytes 1024 | tf_op jit(solution)/shard_map/key_back/pallas_call | solution.py:1103
  692.0 5.5 concatenate.28
  697.4 7.4 collective-permute-done.33.refs_6_
  704.8 2.9 collective-permute-done.32.refs_5_
  707.7 126.5 %sum_all.1 = (f32[64,2048]{1,0:T(8,128)}, f32[64,1024]{1,0:T(8,128)}, f32[64,2048]{1,0:T(8,128)}, f32[64,768]{1,0:T(8,128)}, f32[8,128]{1,0:T(8,128)}, /*index=5...) custom-call(bf16[8,2,2,64,2048]{4,3,2,1,0:T(8,128)(2,1)} %bitcast.38, bf16[8,2,2,64,1024]{4,3,2,1,0:T(8,128)(2,1)} %bitcast.39, ...), custom_call_target="tpu_custom_call" | custom-call | bytes 24117248 | tf_op jit(solution)/shard_map/sum_all/pallas_call | solution.py:530
  837.3 1.5 fusion.10
  843.3 3.1 add_bitcast_fusion
  846.4 3.1 pad_maximum_fusion
  (175 shorter events, 60.9 us)
Async XLA Ops:
  0.6 5.4 copy-start.31
  0.7 12.1 %copy-start.27 = (bf16[64,2048]{1,0:T(8,128)(2,1)S(1)}, bf16[64,2048]{1,0:T(8,128)(2,1)}, u32[]{:S(2)}) copy-start(bf16[64,2048]{1,0:T(8,128)(2,1)} %param.20) | copy-start | bytes 786436
  0.7 12.1 %copy-start.28 = (bf16[64,1024]{1,0:T(8,128)(2,1)S(1)}, bf16[64,1024]{1,0:T(8,128)(2,1)}, u32[]{:S(2)}) copy-start(bf16[64,1024]{1,0:T(8,128)(2,1)} %param.19) | copy-start | bytes 393220
  2.8 134.9 %copy-start = (bf16[3,128,2048]{2,1,0:T(8,128)(2,1)}, bf16[3,128,2048]{2,1,0:T(8,128)(2,1)S(1)}, u32[]{:S(2)}) copy-start(bf16[3,128,2048]{2,1,0:T(8,128)(2,1)S(1)} %get-tuple-element.384.refs_1_.refs_7_) | copy-start | bytes 4718596
  2.8 134.9 %copy-start.1 = (bf16[3,128,2048]{2,1,0:T(8,128)(2,1)}, bf16[3,128,2048]{2,1,0:T(8,128)(2,1)S(1)}, u32[]{:S(2)}) copy-start(bf16[3,128,2048]{2,1,0:T(8,128)(2,1)S(1)} %get-tuple-element.385.refs_0_.refs_6_) | copy-start | bytes 4718596
  2.9 138.1 %collective-permute-start.1 = (bf16[3,128,2048]{2,1,0:T(8,128)(2,1)S(1)}, bf16[3,128,2048]{2,1,0:T(8,128)(2,1)}, u32[]{:S(2)}, u32[]{:S(2)}) collective-permute-start(bf16[3,128,2048]{2,1,0:T(8,128)(2,1)S(1)} %get-tuple-element.384.refs_1_.refs_7_), channel_id=1, source_target_pairs={{0,4},{8,0},{16,8},{24,16},{28,24},{20,28},{12,20},{4,12},{1,5},{9... | collective-permute-start | bytes 4718600 | tf_op jit(solution)/shard_map/ppermute | solution.py:57
  5.9 135.1 %collective-permute-start = (bf16[3,128,2048]{2,1,0:T(8,128)(2,1)S(1)}, bf16[3,128,2048]{2,1,0:T(8,128)(2,1)}, u32[]{:S(2)}, u32[]{:S(2)}) collective-permute-start(bf16[3,128,2048]{2,1,0:T(8,128)(2,1)S(1)} %get-tuple-element.385.refs_0_.refs_6_), channel_id=1, source_target_pairs={{0,8},{8,16},{16,24},{24,28},{28,20},{20,12},{12,4},{4,0},{1,9},{9... | collective-permute-start | bytes 4718600 | tf_op jit(solution)/shard_map/ppermute | solution.py:57
  141.0 36.9 %collective-permute-start.2 = (bf16[3,128,2048]{2,1,0:T(8,128)(2,1)}, bf16[3,128,2048]{2,1,0:T(8,128)(2,1)S(1)}, u32[]{:S(2)}, u32[]{:S(2)}) collective-permute-start(bf16[3,128,2048]{2,1,0:T(8,128)(2,1)} %collective-permute-done.refs_2_.up_w), channel_id=1, source_target_pairs={{0,8},{8,16},{16,24},{24,28},{28,20},{20,12},{12,4},{4,0},{1,9},{9... | collective-permute-start | bytes 4718600 | tf_op jit(solution)/shard_map/ppermute | solution.py:57
  141.6 36.6 %collective-permute-start.3 = (bf16[3,128,2048]{2,1,0:T(8,128)(2,1)}, bf16[3,128,2048]{2,1,0:T(8,128)(2,1)S(1)}, u32[]{:S(2)}, u32[]{:S(2)}) collective-permute-start(bf16[3,128,2048]{2,1,0:T(8,128)(2,1)} %collective-permute-done.1.refs_3_.down_w), channel_id=1, source_target_pairs={{0,4},{8,0},{16,8},{24,16},{28,24},{20,28},{12,20},{4,12},{1,5},{9... | collective-permute-start | bytes 4718600 | tf_op jit(solution)/shard_map/ppermute | solution.py:57
  177.9 23.2 %copy-start.6 = (bf16[3,128,2048]{2,1,0:T(8,128)(2,1)}, bf16[3,128,2048]{2,1,0:T(8,128)(2,1)S(1)}, u32[]{:S(2)}) copy-start(bf16[3,128,2048]{2,1,0:T(8,128)(2,1)S(1)} %collective-permute-done.2.refs_4_.refs_0_) | copy-start | bytes 4718596
  178.2 23.0 %copy-start.7 = (bf16[3,128,2048]{2,1,0:T(8,128)(2,1)}, bf16[3,128,2048]{2,1,0:T(8,128)(2,1)S(1)}, u32[]{:S(2)}) copy-start(bf16[3,128,2048]{2,1,0:T(8,128)(2,1)S(1)} %collective-permute-done.3.refs_5_.refs_1_) | copy-start | bytes 4718596
  180.4 16.1 %collective-permute-start.7 = (bf16[256,1024]{1,0:T(8,128)(2,1)}, bf16[256,1024]{1,0:T(8,128)(2,1)}, u32[]{:S(2)}, u32[]{:S(2)}) collective-permute-start(bf16[256,1024]{1,0:T(8,128)(2,1)} %slice.79), channel_id=1, source_target_pairs={{0,4},{4,8},{8,12},{12,20},{1,5},{5,9},{9,13},{13,21},{2,6},{6,10}... | collective-permute-start | bytes 1572872 | tf_op jit(solution)/shard_map/ppermute | solution.py:1711
  184.6 11.9 %collective-permute-start.6 = (bf16[256,1024]{1,0:T(8,128)(2,1)}, bf16[256,1024]{1,0:T(8,128)(2,1)}, u32[]{:S(2)}, u32[]{:S(2)}) collective-permute-start(bf16[256,1024]{1,0:T(8,128)(2,1)} %slice.79), channel_id=1, source_target_pairs={{12,16},{13,17},{14,18},{15,19}} | collective-permute-start | bytes 1572872 | tf_op jit(solution)/shard_map/ppermute | solution.py:1710
  186.1 35.5 %collective-permute-start.4 = (bf16[3,128,2048]{2,1,0:T(8,128)(2,1)S(1)}, bf16[3,128,2048]{2,1,0:T(8,128)(2,1)}, u32[]{:S(2)}, u32[]{:S(2)}) collective-permute-start(bf16[3,128,2048]{2,1,0:T(8,128)(2,1)S(1)} %collective-permute-done.2.refs_4_.refs_0_), channel_id=1, source_target_pairs={{0,8},{8,16},{16,24},{24,28},{28,20},{20,12},{12,4},{4,0},{1,9},{9... | collective-permute-start | bytes 4718600 | tf_op jit(solution)/shard_map/ppermute | solution.py:57
  186.9 41.6 %collective-permute-start.5 = (bf16[3,128,2048]{2,1,0:T(8,128)(2,1)S(1)}, bf16[3,128,2048]{2,1,0:T(8,128)(2,1)}, u32[]{:S(2)}, u32[]{:S(2)}) collective-permute-start(bf16[3,128,2048]{2,1,0:T(8,128)(2,1)S(1)} %collective-permute-done.3.refs_5_.refs_1_), channel_id=1, source_target_pairs={{0,4},{8,0},{16,8},{24,16},{28,24},{20,28},{12,20},{4,12},{1,5},{9... | collective-permute-start | bytes 4718600 | tf_op jit(solution)/shard_map/ppermute | solution.py:57
  198.4 1.5 collective-permute-start.8
  201.2 2.0 collective-permute-start.9
  228.5 35.9 %collective-permute-start.10 = (bf16[3,128,2048]{2,1,0:T(8,128)(2,1)}, bf16[3,128,2048]{2,1,0:T(8,128)(2,1)}, u32[]{:S(2)}, u32[]{:S(2)}) collective-permute-start(bf16[3,128,2048]{2,1,0:T(8,128)(2,1)} %collective-permute-done.4.refs_6_.refs_2_), channel_id=1, source_target_pairs={{0,8},{8,16},{16,24},{24,28},{28,20},{20,12},{12,4},{4,0},{1,9},{9... | collective-permute-start | bytes 4718600 | tf_op jit(solution)/shard_map/ppermute | solution.py:57
  228.5 44.2 %collective-permute-start.11 = (bf16[3,128,2048]{2,1,0:T(8,128)(2,1)}, bf16[3,128,2048]{2,1,0:T(8,128)(2,1)S(1)}, u32[]{:S(2)}, u32[]{:S(2)}) collective-permute-start(bf16[3,128,2048]{2,1,0:T(8,128)(2,1)} %collective-permute-done.5.refs_7_.refs_3_), channel_id=1, source_target_pairs={{0,4},{8,0},{16,8},{24,16},{28,24},{20,28},{12,20},{4,12},{1,5},{9... | collective-permute-start | bytes 4718600 | tf_op jit(solution)/shard_map/ppermute | solution.py:57
  273.8 36.1 %collective-permute-start.12 = (bf16[3,128,2048]{2,1,0:T(8,128)(2,1)}, bf16[3,128,2048]{2,1,0:T(8,128)(2,1)S(1)}, u32[]{:S(2)}, u32[]{:S(2)}) collective-permute-start(bf16[3,128,2048]{2,1,0:T(8,128)(2,1)} %collective-permute-done.10.refs_8_.refs_4_), channel_id=1, source_target_pairs={{0,8},{8,16},{16,24},{24,28},{28,20},{20,12},{12,4},{4,0},{1,9},{9... | collective-permute-start | bytes 4718600 | tf_op jit(solution)/shard_map/ppermute | solution.py:57
  276.3 36.8 %collective-permute-start.13 = (bf16[3,128,2048]{2,1,0:T(8,128)(2,1)}, bf16[3,128,2048]{2,1,0:T(8,128)(2,1)S(1)}, u32[]{:S(2)}, u32[]{:S(2)}) collective-permute-start(bf16[3,128,2048]{2,1,0:T(8,128)(2,1)} %copy-done.8), channel_id=1, source_target_pairs={{0,4},{8,0},{16,8},{24,16},{28,24},{20,28},{12,20},{4,12},{1,5},{9... | collective-permute-start | bytes 4718600 | tf_op jit(solution)/shard_map/ppermute | solution.py:57
  304.8 46.4 %copy-start.29 = (s32[2,4]{1,0:T(2,128)S(1)}, s32[2,4]{1,0:T(2,128)}, u32[]{:S(2)}) copy-start(s32[2,4]{1,0:T(2,128)} %param.17) | copy-start | bytes 100
  310.0 5.6 copy-start.2
  313.0 2.5 copy-start.3
  313.0 34.8 %collective-permute-start.14 = (bf16[3,128,2048]{2,1,0:T(8,128)(2,1)S(1)}, bf16[3,128,2048]{2,1,0:T(8,128)(2,1)}, u32[]{:S(2)}, u32[]{:S(2)}) collective-permute-start(bf16[3,128,2048]{2,1,0:T(8,128)(2,1)S(1)} %collective-permute-done.12.refs_10_.refs_0_), channel_id=1, source_target_pairs={{0,8},{8,16},{16,24},{24,28},{28,20},{20,12},{12,4},{4,0},{1,9},{9... | collective-permute-start | bytes 4718600 | tf_op jit(solution)/shard_map/ppermute | solution.py:57
  314.8 34.4 %collective-permute-start.15 = (bf16[3,128,2048]{2,1,0:T(8,128)(2,1)S(1)}, bf16[3,128,2048]{2,1,0:T(8,128)(2,1)}, u32[]{:S(2)}, u32[]{:S(2)}) collective-permute-start(bf16[3,128,2048]{2,1,0:T(8,128)(2,1)S(1)} %collective-permute-done.13.refs_11_.refs_1_), channel_id=1, source_target_pairs={{0,4},{8,0},{16,8},{24,16},{28,24},{20,28},{12,20},{4,12},{1,5},{9... | collective-permute-start | bytes 4718600 | tf_op jit(solution)/shard_map/ppermute | solution.py:57
  349.2 33.1 %collective-permute-start.16 = (bf16[3,128,2048]{2,1,0:T(8,128)(2,1)}, bf16[3,128,2048]{2,1,0:T(8,128)(2,1)S(1)}, u32[]{:S(2)}, u32[]{:S(2)}) collective-permute-start(bf16[3,128,2048]{2,1,0:T(8,128)(2,1)} %collective-permute-done.14.refs_0_.refs_2_), channel_id=1, source_target_pairs={{0,8},{8,16},{16,24},{24,28},{28,20},{20,12},{12,4},{4,0},{1,9},{9... | collective-permute-start | bytes 4718600 | tf_op jit(solution)/shard_map/ppermute | solution.py:57
  350.1 33.1 %collective-permute-start.17 = (bf16[3,128,2048]{2,1,0:T(8,128)(2,1)}, bf16[3,128,2048]{2,1,0:T(8,128)(2,1)S(1)}, u32[]{:S(2)}, u32[]{:S(2)}) collective-permute-start(bf16[3,128,2048]{2,1,0:T(8,128)(2,1)} %collective-permute-done.15.refs_1_.refs_3_), channel_id=1, source_target_pairs={{0,4},{8,0},{16,8},{24,16},{28,24},{20,28},{12,20},{4,12},{1,5},{9... | collective-permute-start | bytes 4718600 | tf_op jit(solution)/shard_map/ppermute | solution.py:57
  382.3 2.4 copy-start.4
  383.3 1.4 copy-start.5
  463.4 36.9 %collective-permute-start.18 = (bf16[3,128,2048]{2,1,0:T(8,128)(2,1)}, bf16[3,128,2048]{2,1,0:T(8,128)(2,1)S(1)}, u32[]{:S(2)}, u32[]{:S(2)}) collective-permute-start(bf16[3,128,2048]{2,1,0:T(8,128)(2,1)} %get-tuple-element.213), channel_id=1, source_target_pairs={{0,8},{8,16},{16,24},{24,28},{28,20},{20,12},{12,4},{4,0},{1,9},{9... | collective-permute-start | bytes 4718600 | tf_op jit(solution)/shard_map/ppermute | solution.py:57
  464.1 36.6 %collective-permute-start.19 = (bf16[3,128,2048]{2,1,0:T(8,128)(2,1)}, bf16[3,128,2048]{2,1,0:T(8,128)(2,1)S(1)}, u32[]{:S(2)}, u32[]{:S(2)}) collective-permute-start(bf16[3,128,2048]{2,1,0:T(8,128)(2,1)} %get-tuple-element.214), channel_id=1, source_target_pairs={{0,4},{8,0},{16,8},{24,16},{28,24},{20,28},{12,20},{4,12},{1,5},{9... | collective-permute-start | bytes 4718600 | tf_op jit(solution)/shard_map/ppermute | solution.py:57
  500.7 3.6 copy-start.20
  502.9 37.5 %collective-permute-start.21 = (bf16[3,128,2048]{2,1,0:T(8,128)(2,1)S(1)}, bf16[3,128,2048]{2,1,0:T(8,128)(2,1)S(1)}, u32[]{:S(2)}, u32[]{:S(2)}) collective-permute-start(bf16[3,128,2048]{2,1,0:T(8,128)(2,1)S(1)} %add_convert_fusion.8), channel_id=1, source_target_pairs={{0,4},{8,0},{16,8},{24,16},{28,24},{20,28},{12,20},{4,12},{1,5},{9... | collective-permute-start | bytes 4718600 | tf_op jit(solution)/shard_map/ppermute | solution.py:57
  504.9 35.4 %collective-permute-start.20 = (bf16[3,128,2048]{2,1,0:T(8,128)(2,1)S(1)}, bf16[3,128,2048]{2,1,0:T(8,128)(2,1)S(1)}, u32[]{:S(2)}, u32[]{:S(2)}) collective-permute-start(bf16[3,128,2048]{2,1,0:T(8,128)(2,1)S(1)} %add_convert_fusion.9), channel_id=1, source_target_pairs={{0,8},{8,16},{16,24},{24,28},{28,20},{20,12},{12,4},{4,0},{1,9},{9... | collective-permute-start | bytes 4718600 | tf_op jit(solution)/shard_map/ppermute | solution.py:57
  513.1 27.3 %copy-start.19 = (bf16[3,128,2048]{2,1,0:T(8,128)(2,1)S(1)}, bf16[3,128,2048]{2,1,0:T(8,128)(2,1)}, u32[]{:S(2)}) copy-start(bf16[3,128,2048]{2,1,0:T(8,128)(2,1)} %get-tuple-element.251) | copy-start | bytes 4718596
  540.3 2.1 copy-start.17
  541.0 35.0 %collective-permute-start.23 = (bf16[3,128,2048]{2,1,0:T(8,128)(2,1)S(1)}, bf16[3,128,2048]{2,1,0:T(8,128)(2,1)S(1)}, u32[]{:S(2)}, u32[]{:S(2)}) collective-permute-start(bf16[3,128,2048]{2,1,0:T(8,128)(2,1)S(1)} %add_convert_fusion.6), channel_id=1, source_target_pairs={{0,4},{8,0},{16,8},{24,16},{28,24},{20,28},{12,20},{4,12},{1,5},{9... | collective-permute-start | bytes 4718600 | tf_op jit(solution)/shard_map/ppermute | solution.py:57
  543.0 34.9 %collective-permute-start.22 = (bf16[3,128,2048]{2,1,0:T(8,128)(2,1)S(1)}, bf16[3,128,2048]{2,1,0:T(8,128)(2,1)S(1)}, u32[]{:S(2)}, u32[]{:S(2)}) collective-permute-start(bf16[3,128,2048]{2,1,0:T(8,128)(2,1)S(1)} %add_convert_fusion.7), channel_id=1, source_target_pairs={{0,8},{8,16},{16,24},{24,28},{28,20},{20,12},{12,4},{4,0},{1,9},{9... | collective-permute-start | bytes 4718600 | tf_op jit(solution)/shard_map/ppermute | solution.py:57
  578.0 3.2 copy-start.18
  580.2 34.8 %collective-permute-start.25 = (bf16[3,128,2048]{2,1,0:T(8,128)(2,1)S(1)}, bf16[3,128,2048]{2,1,0:T(8,128)(2,1)S(1)}, u32[]{:S(2)}, u32[]{:S(2)}) collective-permute-start(bf16[3,128,2048]{2,1,0:T(8,128)(2,1)S(1)} %add_convert_fusion.4), channel_id=1, source_target_pairs={{0,4},{8,0},{16,8},{24,16},{28,24},{20,28},{12,20},{4,12},{1,5},{9... | collective-permute-start | bytes 4718600 | tf_op jit(solution)/shard_map/ppermute | solution.py:57
  581.8 34.8 %collective-permute-start.24 = (bf16[3,128,2048]{2,1,0:T(8,128)(2,1)S(1)}, bf16[3,128,2048]{2,1,0:T(8,128)(2,1)S(1)}, u32[]{:S(2)}, u32[]{:S(2)}) collective-permute-start(bf16[3,128,2048]{2,1,0:T(8,128)(2,1)S(1)} %add_convert_fusion.5), channel_id=1, source_target_pairs={{0,8},{8,16},{16,24},{24,28},{28,20},{20,12},{12,4},{4,0},{1,9},{9... | collective-permute-start | bytes 4718600 | tf_op jit(solution)/shard_map/ppermute | solution.py:57
  610.7 1.9 copy-start.12
  612.8 2.0 collective-permute-start.26
  615.0 2.5 copy-start.16
  616.7 2.5 copy-start.15
  616.7 4.2 collective-permute-start.29
  618.2 50.4 %collective-permute-start.28 = (bf16[3,128,2048]{2,1,0:T(8,128)(2,1)S(1)}, bf16[3,128,2048]{2,1,0:T(8,128)(2,1)S(1)}, u32[]{:S(2)}, u32[]{:S(2)}) collective-permute-start(bf16[3,128,2048]{2,1,0:T(8,128)(2,1)S(1)} %add_convert_fusion.2), channel_id=1, source_target_pairs={{0,4},{8,0},{16,8},{24,16},{28,24},{20,28},{12,20},{4,12},{1,5},{9... | collective-permute-start | bytes 4718600 | tf_op jit(solution)/shard_map/ppermute | solution.py:57
  619.8 48.8 %collective-permute-start.27 = (bf16[3,128,2048]{2,1,0:T(8,128)(2,1)S(1)}, bf16[3,128,2048]{2,1,0:T(8,128)(2,1)S(1)}, u32[]{:S(2)}, u32[]{:S(2)}) collective-permute-start(bf16[3,128,2048]{2,1,0:T(8,128)(2,1)S(1)} %add_convert_fusion.3), channel_id=1, source_target_pairs={{0,8},{8,16},{16,24},{24,28},{28,20},{20,12},{12,4},{4,0},{1,9},{9... | collective-permute-start | bytes 4718600 | tf_op jit(solution)/shard_map/ppermute | solution.py:57
  621.1 17.4 %collective-permute-start.31 = (bf16[256,1024]{1,0:T(8,128)(2,1)S(1)}, bf16[256,1024]{1,0:T(8,128)(2,1)}, u32[]{:S(2)}, u32[]{:S(2)}) collective-permute-start(bf16[256,1024]{1,0:T(8,128)(2,1)S(1)} %add_convert_fusion.10), channel_id=1, source_target_pairs={{16,12},{17,13},{18,14},{19,15}} | collective-permute-start | bytes 1572872 | tf_op jit(solution)/shard_map/ppermute | solution.py:1875
  622.6 43.6 %collective-permute-start.30 = (bf16[256,1024]{1,0:T(8,128)(2,1)S(1)}, bf16[256,1024]{1,0:T(8,128)(2,1)}, u32[]{:S(2)}, u32[]{:S(2)}) collective-permute-start(bf16[256,1024]{1,0:T(8,128)(2,1)S(1)} %add_convert_fusion.10), channel_id=1, source_target_pairs={{4,0},{8,4},{12,8},{20,12},{5,1},{9,5},{13,9},{21,13},{6,2},{10,6}... | collective-permute-start | bytes 1572872 | tf_op jit(solution)/shard_map/ppermute | solution.py:1874
  638.5 30.2 %copy-start.14 = (bf16[3,128,2048]{2,1,0:T(8,128)(2,1)S(1)}, bf16[3,128,2048]{2,1,0:T(8,128)(2,1)}, u32[]{:S(2)}) copy-start(bf16[3,128,2048]{2,1,0:T(8,128)(2,1)} %get-tuple-element.309) | copy-start | bytes 4718596
  668.6 1.9 copy-start.13
  670.4 4.7 copy-start.22
  670.4 34.4 %collective-permute-start.33 = (bf16[3,128,2048]{2,1,0:T(8,128)(2,1)}, bf16[3,128,2048]{2,1,0:T(8,128)(2,1)}, u32[]{:S(2)}, u32[]{:S(2)}) collective-permute-start(bf16[3,128,2048]{2,1,0:T(8,128)(2,1)} %add_convert_fusion), channel_id=1, source_target_pairs={{0,4},{8,0},{16,8},{24,16},{28,24},{20,28},{12,20},{4,12},{1,5},{9... | collective-permute-start | bytes 4718600 | tf_op jit(solution)/shard_map/ppermute | solution.py:57
  672.3 35.3 %collective-permute-start.32 = (bf16[3,128,2048]{2,1,0:T(8,128)(2,1)}, bf16[3,128,2048]{2,1,0:T(8,128)(2,1)}, u32[]{:S(2)}, u32[]{:S(2)}) collective-permute-start(bf16[3,128,2048]{2,1,0:T(8,128)(2,1)} %add_convert_fusion.1), channel_id=1, source_target_pairs={{0,8},{8,16},{16,24},{24,28},{28,20},{20,12},{12,4},{4,0},{1,9},{9... | collective-permute-start | bytes 4718600 | tf_op jit(solution)/shard_map/ppermute | solution.py:57
  675.6 2.2 copy-start.21
  677.9 12.5 %copy-start.30 = (f32[1,256]{1,0:T(1,128)S(1)}, f32[1,256]{1,0:T(1,128)}, u32[]{:S(2)}) copy-start(f32[1,256]{1,0:T(1,128)} %get-tuple-element.326) | copy-start | bytes 3076
  707.7 135.6 %copy-start.10 = (bf16[3,128,2048]{2,1,0:T(8,128)(2,1)S(1)}, bf16[3,128,2048]{2,1,0:T(8,128)(2,1)}, u32[]{:S(2)}) copy-start(bf16[3,128,2048]{2,1,0:T(8,128)(2,1)} %get-tuple-element.345) | copy-start | bytes 4718596
  707.7 135.6 %copy-start.11 = (bf16[3,128,2048]{2,1,0:T(8,128)(2,1)S(1)}, bf16[3,128,2048]{2,1,0:T(8,128)(2,1)}, u32[]{:S(2)}) copy-start(bf16[3,128,2048]{2,1,0:T(8,128)(2,1)} %get-tuple-element.347) | copy-start | bytes 4718596
  846.4 3.1 copy-start.9
  849.6 2.0 copy-start.24
  850.9 1.5 copy-start.26
  850.9 2.2 copy-start.23
  (2 other events, 2.5 us)
